TPU v7x, 32 devices: a whole 2x2x4 slice. The times are simulated.
32 devices in a mesh: groups: 2 (over y), space: 16 (over z, x, core).
Axes of the slice: x: 2, y: 2, z: 4, core: 2. Of those that a mesh axis runs over, the one named last changes fastest.
Arguments:
- latent: float32 [131072], P(('groups', 'space')), parts along dimension 0, may hold values from -6 to 6
- responses: int32 [131072], P(('groups', 'space')), parts along dimension 0, may hold values from 0 to 1
- probes: float32 [32, 131072], P(None, ('groups', 'space')), parts along dimension 1
- prior_diag: float32 [131072], P(('groups', 'space')), parts along dimension 0, may hold values from 0.5 to 8
- factor: bfloat16 [1024, 4, 128, 128], P(('groups', 'space')), parts along dimension 0, may hold values from -0.25 to 0.25
- cond_ids: int32 [1024, 3], P(('groups', 'space')), parts along dimension 0, may hold values from 0 to 510, as said below
- inducing_map: bfloat16 [131072, 256], P(('groups', 'space')), parts along dimension 0, may hold values from -0.375 to 0.375
- inner_inverse: float32 [512, 256], P('groups'), parts along dimension 0
Outputs:
- solution: float32 [33, 131072], P(None, ('groups', 'space')), parts along dimension 1
- residual: float32 [33, 131072], P(None, ('groups', 'space')), parts along dimension 1
- next_direction: float32 [33, 131072], P(None, ('groups', 'space')), parts along dimension 1
There are 2 independent parts, one for each index of `groups`. A program takes and returns all parts, laid end to end along the dimension named above; each array names one. Nothing has to cross between parts.
Inputs may be any that keep to these rules, and one draw needn't show every extreme that they name: `cond_ids`: each id of block b lies from max(b - 64, 0) to max(b - 1, 0); the first block of every device names, as its third id, the block 64 before it where that exists.
All inputs are finite; a program needn't handle non-finite values.
Results may differ from a plain program's by a relative error of at most 0.006.
Values may be sent and summed in bfloat16 or wider, within the bound.
No kernel may reach another device: no remote copies, remote signals or barrier semaphores. Data moves between devices by JAX's collectives and lax.ppermute only.
A program may use at most 64 MiB of HBM per device.

v0:
```python
import jax
import jax.numpy as jnp
from jax import lax
from jax.sharding import PartitionSpec as P


def passed_along(block, axis, distance):
    devices = range(lax.axis_size(axis))
    route = [(i - distance, i) for i in devices if i - distance in devices]
    return lax.ppermute(block, axis, route)


def precondition(field, inv_diag, inducing_map, inner_inverse):
    scaled_f = field * inv_diag
    scaled = scaled_f.astype(jnp.bfloat16)
    partial_sum = jnp.dot(scaled, inducing_map, preferred_element_type=jnp.float32)
    summed = lax.psum(partial_sum, "space")
    coeffs = jnp.dot(summed, inner_inverse, precision=lax.Precision.HIGHEST).astype(jnp.bfloat16)
    correction = lax.dot_general(
        coeffs, inducing_map, (((1,), (1,)), ((), ())), preferred_element_type=jnp.float32
    )
    smoothed = scaled_f + correction * inv_diag
    energy = lax.psum(jnp.sum(field * smoothed, axis=1), "space")
    return (smoothed, energy)


def apply_hessian(direction, weights, factor, cond_ids):
    columns, point_count = direction.shape
    block_count, _, block_size, _ = factor.shape
    position = lax.axis_index("space")
    rounded = direction.astype(jnp.bfloat16)
    prev_near = passed_along(rounded, "space", 1)
    prev_far = passed_along(rounded, "space", 2)
    neighbourhood = jnp.concatenate([prev_far, prev_near, rounded], axis=1).reshape(
        columns, 3 * block_count, block_size
    )
    local_ids = cond_ids - (position - 2) * block_count
    picked = jnp.take(neighbourhood, local_ids, axis=1)
    own_blocks = rounded.reshape(columns, block_count, 1, block_size)
    chosen = jnp.concatenate([own_blocks, picked], axis=2)
    image = jnp.einsum("bkij,cbkj->cbi", factor, chosen, preferred_element_type=jnp.float32)
    imaged = image.astype(jnp.bfloat16)
    transposed = jnp.einsum("bkij,cbi->cbkj", factor, imaged, preferred_element_type=jnp.float32)
    slots = jnp.arange(3 * block_count, dtype=jnp.int32)
    onehot = (local_ids[:, :, None] == slots[None, None, :]).astype(jnp.float32)
    spread = jnp.einsum(
        "cbkj,bks->csj", transposed[:, :, 1:], onehot, precision=lax.Precision.HIGHEST
    )
    far_part = spread[:, :block_count].reshape(columns, point_count)
    near_part = spread[:, block_count : 2 * block_count].reshape(columns, point_count)
    mine_part = spread[:, 2 * block_count :].reshape(columns, point_count)
    own_part = transposed[:, :, 0].reshape(columns, point_count)
    from_near = passed_along(near_part.astype(jnp.bfloat16), "space", -1).astype(near_part.dtype)
    from_far = passed_along(far_part.astype(jnp.bfloat16), "space", -2).astype(far_part.dtype)
    summed = own_part + mine_part + from_near + from_far
    hess_dir = summed + weights * direction
    curve_sum = lax.psum(jnp.sum(direction * hess_dir, axis=1), "space")
    return (hess_dir, curve_sum)


def body(latent, responses, probes, prior_diag, factor, cond_ids, inducing_map, inner_inverse):
    probability = jax.nn.sigmoid(latent)
    weights = probability * (1.0 - probability)
    first_column = responses.astype(jnp.float32) - probability
    right_side = jnp.concatenate([first_column[None, :], probes], axis=0)
    inv_diag = 1.0 / (weights + prior_diag)
    direction, energy = precondition(right_side, inv_diag, inducing_map, inner_inverse)
    hess_dir, curve_sum = apply_hessian(direction, weights, factor, cond_ids)
    step_length = (energy / curve_sum)[:, None]
    solution = step_length * direction
    residual = right_side - step_length * hess_dir
    smoothed, energy_next = precondition(residual, inv_diag, inducing_map, inner_inverse)
    next_direction = smoothed + (energy_next / energy)[:, None] * direction
    return (solution, residual, next_direction)


def solution(mesh):
    return jax.shard_map(
        body,
        mesh=mesh,
        in_specs=(
            P(("groups", "space")),
            P(("groups", "space")),
            P(None, ("groups", "space")),
            P(("groups", "space")),
            P(("groups", "space"), None, None, None),
            P(("groups", "space"), None),
            P(("groups", "space"), None),
            P("groups", None),
        ),
        out_specs=(
            P(None, ("groups", "space")),
            P(None, ("groups", "space")),
            P(None, ("groups", "space")),
        ),
        check_vma=False,
    )
```

profile of v0, /device:TPU:0, one launch (start us, length us, event | category | flops | bytes accessed | tf_op | source)
XLA Modules:
  0.0 239.3 jit_solution(1672347668578215679)
XLA Ops:
  0.6 0.0 copy-start
  0.6 0.0 copy-start.1
  0.7 1.5 subtract_multiply_fusion
  2.2 0.2 copy-done
  2.4 1.5 fusion.22
  3.8 63.0 %psum.35 = f32[33,256]{1,0:T(8,128)S(1)} all-reduce(f32[33,256]{1,0:T(8,128)S(1)} %fusion.22), channel_id=1, replica_groups=mesh['groups'=2,'space'=16] {'space'}, use_global_device_ids=true, to_apply=%region_0.0 | all-reduce | flops 8448 | bytes 67584 | tf_op jit(solution)/shard_map/psum | solution.py:17
  66.8 0.2 convolution_convert_fusion.1
  67.1 2.2 fusion.33
  69.3 2.0 collective-permute-start.1
  71.3 2.0 collective-permute-start
  73.3 1.2 compare_and_fusion
  74.5 0.6 copy-done.8
  75.1 0.6 compare_select_fusion
  75.7 1.3 copy.16
  77.0 1.4 copy.17
  78.4 1.4 reshape.34
  79.7 1.0 copy.25
  80.8 0.8 copy.19
  81.6 1.3 pad_clamp_fusion
  82.9 1.2 pad_maximum_fusion
  84.2 0.2 copy.26
  84.3 0.1 slice.30
  84.4 1.3 copy.18
  85.7 3.0 %gather_fusion = bf16[96,33,128]{2,1,0:T(8,128)(2,1)} fusion(bf16[33,96,128]{2,0,1:T(8,128)(2,1)} %copy.18, s32[1024]{0:T(1024)} %pad_clamp_fusion), kind=kCustom, calls=%fused_computation | custom fusion | bytes 1622400 | tf_op jit(solution)/shard_map/jit(_take)/gather | solution.py:38
  88.8 2.3 select_bitcast_fusion
  91.1 7.4 %convolution_bitcast_fusion = f32[33,32,4,128]{3,0,2,1:T(8,128)} fusion(bf16[32,4,128,128]{3,2,1,0:T(8,128)(2,1)} %param.12, bf16[33,32,3,128]{3,0,2,1:T(8,128)(2,1)} %select_bitcast_fusion, bf16[33,32,1,128]{3,0,2,1:T(8,128)(2,1)} %copy.19), kind=kOutput, calls=%fused_computation.5 | convolution fusion | flops 277499904 | bytes 7438336 | tf_op jit(solution)/shard_map/bkij,cbi->cbkj/dot_general | solution.py:43
  98.6 1.5 slice-done
  100.1 1.2 fusion.34
  101.4 0.1 copy.29
  101.5 0.1 copy.30
  101.7 1.3 collective-permute-start.3
  103.0 1.3 collective-permute-start.2
  104.3 0.1 copy.38
  104.4 0.1 pad.8
  104.5 0.4 copy.27
  104.9 0.1 pad.9
  105.0 0.4 copy.28
  105.4 5.3 %collective-permute-done.3 = bf16[33,4096]{1,0:T(8,128)(2,1)S(1)} collective-permute-done((bf16[33,4096]{1,0:T(8,128)(2,1)S(1)}, bf16[33,4096]{1,0:T(8,128)(2,1)S(1)}, u32[]{:S(2)}, u32[]{:S(2)}) %collective-permute-start.3) | collective-permute-done | bytes 270368 | tf_op jit(solution)/shard_map/ppermute | solution.py:10
  110.7 1.8 multiply_reduce_fusion.1
  112.5 32.9 %all-reduce = (f32[33]{0:T(128)S(1)}, f32[33]{0:T(128)S(1)}) all-reduce(f32[33]{0:T(128)} %get-tuple-element.4, f32[33]{0:T(128)} %get-tuple-element.3), channel_id=1, replica_groups=mesh['groups'=2,'space'=16] {'space'}, use_global_device_ids=true, to_apply=%region_2.0 | all-reduce | flops 66 | bytes 528 | tf_op jit(solution)/shard_map/psum | solution.py:23
  145.4 0.5 copy-done.12
  145.9 1.2 multiply_subtract_fusion
  147.2 0.4 fusion.23
  147.6 57.7 %psum.38 = f32[33,256]{1,0:T(8,128)S(1)} all-reduce(f32[33,256]{1,0:T(8,128)S(1)} %fusion.23), channel_id=1, replica_groups=mesh['groups'=2,'space'=16] {'space'}, use_global_device_ids=true, to_apply=%region_5.6 | all-reduce | flops 8448 | bytes 67584 | tf_op jit(solution)/shard_map/psum | solution.py:17
  205.3 0.2 convolution_convert_fusion
  205.6 1.7 multiply_reduce_fusion
  207.3 29.5 %psum.39 = f32[33]{0:T(128)S(1)} all-reduce(f32[33]{0:T(128)S(1)} %get-tuple-element.21), channel_id=1, replica_groups=mesh['groups'=2,'space'=16] {'space'}, use_global_device_ids=true, to_apply=%region_7.8 | all-reduce | flops 33 | bytes 264 | tf_op jit(solution)/shard_map/psum | solution.py:23
  236.8 2.5 %multiply_add_fusion = (f32[33,4096]{1,0:T(8,128)}, f32[33,4096]{1,0:T(8,128)}) fusion(f32[33,4096]{1,0:T(8,128)} %get-tuple-element.22, f32[33,4096]{1,0:T(8,128)} %copy-done.3, f32[33]{0:T(128)S(1)} %div.15, f32[33]{0:T(128)S(1)} %copy-done.11), kind=kLoop, calls=%fused_computation.21 | loop fusion | flops 405504 | bytes 2162952 | tf_op jit(solution)/shard_map/add | solution.py:73
  (36 shorter events, 0.2 us)
Async XLA Ops:
  0.6 1.7 copy-start
  0.6 66.4 %copy-start.1 = (f32[32,4096]{1,0:T(8,128)S(1)}, f32[32,4096]{1,0:T(8,128)}, u32[]{:S(2)}) copy-start(f32[32,4096]{1,0:T(8,128)} %param.10) | copy-start | bytes 1572868
  0.7 66.2 %copy-start.4 = (f32[256,256]{1,0:T(8,128)S(1)}, f32[256,256]{1,0:T(8,128)}, u32[]{:S(2)}) copy-start(f32[256,256]{1,0:T(8,128)} %param.15) | copy-start | bytes 786436
  2.2 64.6 %copy-start.5 = (f32[4096]{0:T(1024)}, f32[4096]{0:T(1024)S(1)}, u32[]{:S(2)}) copy-start(f32[4096]{0:T(1024)S(1)} %get-tuple-element.16) | copy-start | bytes 49156
  69.3 41.4 %copy-start.3 = (f32[33,4096]{1,0:T(8,128)}, f32[33,4096]{1,0:T(8,128)S(1)}, u32[]{:S(2)}) copy-start(f32[33,4096]{1,0:T(8,128)S(1)} %get-tuple-element.18) | copy-start | bytes 1622020
  69.3 13.6 %collective-permute-start.1 = (bf16[33,4096]{1,0:T(8,128)(2,1)}, bf16[33,4096]{1,0:T(8,128)(2,1)}, u32[]{:S(2)}, u32[]{:S(2)}) collective-permute-start(bf16[33,4096]{1,0:T(8,128)(2,1)} %get-tuple-element.17), channel_id=1, source_target_pairs={{0,1},{1,2},{2,3},{3,4},{4,5},{5,6},{6,7},{7,8},{8,9},{9,10},{10,1... | collective-permute-start | bytes 811016 | tf_op jit(solution)/shard_map/ppermute | solution.py:10
  71.3 11.6 %collective-permute-start = (bf16[33,4096]{1,0:T(8,128)(2,1)}, bf16[33,4096]{1,0:T(8,128)(2,1)}, u32[]{:S(2)}, u32[]{:S(2)}) collective-permute-start(bf16[33,4096]{1,0:T(8,128)(2,1)} %get-tuple-element.17), channel_id=1, source_target_pairs={{0,2},{1,3},{2,4},{3,5},{4,6},{5,7},{6,8},{7,9},{8,10},{9,11},{10,... | collective-permute-start | bytes 811016 | tf_op jit(solution)/shard_map/ppermute | solution.py:10
  74.5 0.6 copy-start.8
  98.5 1.5 slice-start
  98.6 1.5 copy-start.9
  101.3 3.0 %slice-start.1 = ((f32[33,32,4,128]{3,0,2,1:T(8,128)}), f32[33,32,1,128]{3,0,2,1:T(8,128)S(1)}, s32[]{:S(2)}) async-start(f32[33,32,4,128]{3,0,2,1:T(8,128)} %convolution_bitcast_fusion), calls=%async_computation.1 | async-start | bytes 1310720 | tf_op jit(solution)/shard_map/slice | solution.py:52
  101.7 9.0 %collective-permute-start.3 = (bf16[33,4096]{1,0:T(8,128)(2,1)S(1)}, bf16[33,4096]{1,0:T(8,128)(2,1)S(1)}, u32[]{:S(2)}, u32[]{:S(2)}) collective-permute-start(bf16[33,4096]{1,0:T(8,128)(2,1)S(1)} %bitcast.86), channel_id=1, source_target_pairs={{2,0},{3,1},{4,2},{5,3},{6,4},{7,5},{8,6},{9,7},{10,8},{11,9},{12,... | collective-permute-start | bytes 811016 | tf_op jit(solution)/shard_map/ppermute | solution.py:10
  103.0 7.7 %collective-permute-start.2 = (bf16[33,4096]{1,0:T(8,128)(2,1)S(1)}, bf16[33,4096]{1,0:T(8,128)(2,1)S(1)}, u32[]{:S(2)}, u32[]{:S(2)}) collective-permute-start(bf16[33,4096]{1,0:T(8,128)(2,1)S(1)} %bitcast.85), channel_id=1, source_target_pairs={{1,0},{2,1},{3,2},{4,3},{5,4},{6,5},{7,6},{8,7},{9,8},{10,9},{11,1... | collective-permute-start | bytes 811016 | tf_op jit(solution)/shard_map/ppermute | solution.py:10
  104.8 5.8 %copy-start.6 = (f32[4096]{0:T(1024)S(1)}, f32[4096]{0:T(1024)}, u32[]{:S(2)}) copy-start(f32[4096]{0:T(1024)} %copy-done.5) | copy-start | bytes 49156
  104.9 5.8 %copy-start.7 = (f32[4096]{0:T(1024)S(1)}, f32[4096]{0:T(1024)}, u32[]{:S(2)}) copy-start(f32[4096]{0:T(1024)} %get-tuple-element.14) | copy-start | bytes 49156
  145.4 0.5 copy-start.12
  145.9 1.2 copy-start.10
  147.2 60.1 %copy-start.2 = (f32[33,4096]{1,0:T(8,128)}, f32[33,4096]{1,0:T(8,128)S(1)}, u32[]{:S(2)}) copy-start(f32[33,4096]{1,0:T(8,128)S(1)} %multiply_subtract_fusion) | copy-start | bytes 1622020
  147.6 89.1 %copy-start.13 = (f32[33]{0:T(128)S(1)}, f32[33]{0:T(128)}, u32[]{:S(2)}) copy-start(f32[33]{0:T(128)} %copy-done.12) | copy-start | bytes 400
  147.6 89.1 %copy-start.11 = (f32[33]{0:T(128)S(1)}, f32[33]{0:T(128)}, u32[]{:S(2)}) copy-start(f32[33]{0:T(128)} %copy-done.10) | copy-start | bytes 400
where the time goes:
time: 240 us; the launch traced here: 239 us
  blocking collectives  183 us (76%)
  local copies, waits for them, and re-layouts  14.8 us (6%)
  matrix products  14.8 us (6%)
  other arithmetic  13.7 us (6%)
  starting transfers between devices  6.61 us (3%)
  waiting for transfers between devices  5.27 us (2%)
    psum x2, blocking collectives, precondition(): summed = lax.psum(partial_sum, 'space')  121 us
    psum x2, blocking collectives, precondition(): energy = lax.psum(jnp.sum(field * smoothed, axis=1), 'space')  62.4 us
    dot_general x1, matrix products, apply_hessian(): jnp.einsum('bkij,cbi->cbkj', factor, imaged, preferred_element_type=jnp.f...  7.44 us
    ppermute x4, starting transfers between devices, passed_along(): return lax.ppermute(block, axis, route)  6.61 us
    ppermute x4, waiting for transfers between devices, passed_along(): return lax.ppermute(block, axis, route)  5.27 us
  transfers between devices with their start and end apart: 4, of which 1 were waited for; matrix products, arithmetic and copies ran while one was open for 4% of the time, Pallas kernels for 0%

commit v1 on v0

v1 whole, which is shorter than its diff:
```python
import functools

import jax
import jax.numpy as jnp
from jax import lax
from jax.experimental import pallas as pl
from jax.experimental.pallas import tpu as pltpu
from jax.sharding import PartitionSpec as P

F32, BF16 = jnp.float32, jnp.bfloat16
PAIR = 2


def shifted(block, axis, distance):
    devices = range(lax.axis_size(axis))
    route = [(i - distance, i) for i in devices if i - distance in devices]
    return lax.ppermute(block, axis, route)


def total(x, axis):
    n = lax.axis_size(axis)
    if n & (n - 1):
        return lax.psum(x, axis)
    step = 1
    while step < n:
        partners = [m * step for m in range(1, 4) if m * step < n]
        got = [lax.ppermute(x, axis, [(i, i ^ d) for i in range(n)]) for d in partners]
        for y in got:
            x = x + y
        step *= 4
    return x


def eye(rows, lanes):
    return lax.broadcasted_iota(jnp.int32, (rows, lanes), 0) == lax.broadcasted_iota(jnp.int32, (rows, lanes), 1)


def as_row(column, lanes):
    return jnp.sum(jnp.where(eye(column.shape[0], lanes), column, 0.0), axis=0, keepdims=True)


def as_column(row, rows):
    return jnp.sum(jnp.where(eye(rows, row.shape[1]), row, 0.0), axis=1, keepdims=True)


def point_terms(latent, prior):
    probability = 1.0 / (1.0 + jnp.exp(-latent))
    weights = probability * (1.0 - probability)
    return probability, weights, 1.0 / (weights + prior)


def right_side_of(probes_ref, gradient, b, bs, rows):
    count = probes_ref.shape[0]
    return jnp.concatenate(
        [probes_ref[:, b * bs : (b + 1) * bs], jnp.broadcast_to(gradient[b : b + 1], (rows - count, bs))], axis=0
    )


def project_kernel(rows, latent_ref, responses_ref, prior_ref, probes_ref, map_ref, out_ref):
    blocks, bs = latent_ref.shape
    count = probes_ref.shape[0]
    probability, _, inv_diag = point_terms(latent_ref[...], prior_ref[...])
    gradient = responses_ref[...].astype(F32) - probability
    energy = jnp.zeros((rows, bs), F32)
    summed = jnp.zeros((rows, map_ref.shape[1]), F32)
    for b in range(0, blocks, PAIR):
        parts = []
        for c in range(b, b + PAIR):
            field = right_side_of(probes_ref, gradient, c, bs, rows)
            scaled = field * inv_diag[c : c + 1]
            energy += field * scaled
            parts.append(scaled.astype(BF16))
        summed += jnp.dot(
            jnp.concatenate(parts, axis=1), map_ref[b * bs : (b + PAIR) * bs], preferred_element_type=F32
        )
    out_ref[...] = summed
    out_ref[count + 1 : count + 2] = as_row(jnp.sum(energy, axis=1, keepdims=True), map_ref.shape[1])


def direction_kernel(
    rows, sums_ref, inner_ref, latent_ref, responses_ref, prior_ref, probes_ref, map_ref, dir_ref, msg_ref, grad_ref
):
    blocks, bs = latent_ref.shape
    count = probes_ref.shape[0]
    probability, _, inv_diag = point_terms(latent_ref[...], prior_ref[...])
    gradient = responses_ref[...].astype(F32) - probability
    coeffs = jnp.dot(sums_ref[...], inner_ref[...], precision=lax.Precision.HIGHEST).astype(BF16)
    for b in range(0, blocks, PAIR):
        correction = lax.dot_general(
            coeffs, map_ref[b * bs : (b + PAIR) * bs], (((1,), (1,)), ((), ())), preferred_element_type=F32
        )
        for c in range(b, b + PAIR):
            field = right_side_of(probes_ref, gradient, c, bs, rows)
            direction = (field + correction[:, (c - b) * bs : (c - b + 1) * bs]) * inv_diag[c : c + 1]
            dir_ref[c] = direction
            msg_ref[c] = direction[:count].astype(BF16)
            grad_ref[c : c + 1] = direction[count : count + 1]
    msg_ref[blocks] = grad_ref[...].astype(BF16)


def hessian_kernel(
    rows, ids_ref, factor_ref, far_ref, near_ref, own_ref, back_far_ref, back_near_ref, back_own_ref, curve_ref,
    around_ref, around_grad_ref, image_ref, total_ref, grad_ref,
):
    blocks, taps, bs, _ = factor_ref.shape
    count = around_ref.shape[1]
    tall = image_ref.shape[1]
    for i, ref in enumerate((far_ref, near_ref, own_ref)):
        around_ref[i * blocks : (i + 1) * blocks] = ref[:blocks]
        around_grad_ref[i * blocks : (i + 1) * blocks] = ref[blocks].astype(F32)
    total_ref[...] = jnp.zeros_like(total_ref)
    curve = jnp.zeros((rows, bs), F32)
    for b in range(blocks):
        image = jnp.zeros((tall, bs), F32)
        for k in range(taps):
            at = 2 * blocks + b if k == 0 else ids_ref[b, k - 1]
            last = jnp.broadcast_to(around_grad_ref[pl.ds(at, 1), :], (tall - count, bs)).astype(BF16)
            chosen = jnp.concatenate([around_ref[at], last], axis=0)
            image += lax.dot_general(
                chosen, factor_ref[b, k], (((1,), (1,)), ((), ())), preferred_element_type=F32
            )
        rounded = image.astype(BF16)
        image_ref[b] = rounded
        curve += (image * rounded.astype(F32))[:rows]
    curve_ref[...] = curve
    for b in range(blocks):
        rounded = image_ref[b]
        for k in range(taps):
            at = 2 * blocks + b if k == 0 else ids_ref[b, k - 1]
            back = jnp.dot(rounded, factor_ref[b, k], preferred_element_type=F32)
            total_ref[at] += back[:rows]
    for i, ref in enumerate((back_far_ref, back_near_ref)):
        for b in range(blocks):
            ref[b] = total_ref[i * blocks + b, :count].astype(BF16)
            grad_ref[b : b + 1] = total_ref[i * blocks + b, count : count + 1]
        ref[blocks] = grad_ref[...].astype(BF16)
    back_own_ref[...] = total_ref[2 * blocks :]


def combine_kernel(
    rows, own_ref, near_ref, far_ref, curve_ref, dir_ref, latent_ref, responses_ref, prior_ref, probes_ref, map_ref,
    hess_ref, out_ref,
):
    blocks, bs = latent_ref.shape
    count = probes_ref.shape[0]
    lanes = map_ref.shape[1]
    probability, weights, inv_diag = point_terms(latent_ref[...], prior_ref[...])
    gradient = responses_ref[...].astype(F32) - probability
    from_grad = near_ref[blocks].astype(F32) + far_ref[blocks].astype(F32)
    curve = curve_ref[...]
    cross = jnp.zeros((rows, bs), F32)
    square = jnp.zeros((rows, bs), F32)
    summed = jnp.zeros((rows, lanes), F32)
    for b in range(0, blocks, PAIR):
        parts = []
        for c in range(b, b + PAIR):
            came = jnp.concatenate(
                [
                    near_ref[c].astype(F32) + far_ref[c].astype(F32),
                    jnp.broadcast_to(from_grad[c : c + 1], (rows - count, bs)),
                ],
                axis=0,
            )
            direction = dir_ref[c]
            weighted = weights[c : c + 1] * direction
            hess = own_ref[c] + came + weighted
            hess_ref[c] = hess
            scaled = hess * inv_diag[c : c + 1]
            curve += weighted * direction
            cross += right_side_of(probes_ref, gradient, c, bs, rows) * scaled
            square += hess * scaled
            parts.append(scaled.astype(BF16))
        summed += jnp.dot(
            jnp.concatenate(parts, axis=1), map_ref[b * bs : (b + PAIR) * bs], preferred_element_type=F32
        )
    out_ref[...] = summed
    for i, acc in enumerate((curve, cross, square)):
        out_ref[count + 1 + i : count + 2 + i] = as_row(jnp.sum(acc, axis=1, keepdims=True), lanes)


def finish_kernel(
    rows, sums_ref, hess_sums_ref, inner_ref, dir_ref, hess_ref, latent_ref, responses_ref, prior_ref, probes_ref,
    map_ref, solution_ref, residual_ref, next_ref,
):
    blocks, bs = latent_ref.shape
    count = probes_ref.shape[0]
    probability, _, inv_diag = point_terms(latent_ref[...], prior_ref[...])
    gradient = responses_ref[...].astype(F32) - probability
    sums, hess_sums, inner = sums_ref[...], hess_sums_ref[...], inner_ref[...]
    column = lambda x, i: as_column(x[count + 1 + i : count + 2 + i], rows)
    coeffs = jnp.dot(sums, inner, precision=lax.Precision.HIGHEST).astype(BF16)
    plain = column(sums, 0)
    energy = plain + jnp.sum(coeffs.astype(F32) * sums, axis=1, keepdims=True)
    step = energy / column(hess_sums, 0)
    left = sums - step * hess_sums
    coeffs = jnp.dot(left, inner, precision=lax.Precision.HIGHEST).astype(BF16)
    plain_next = plain - 2.0 * step * column(hess_sums, 1) + step * step * column(hess_sums, 2)
    energy_next = plain_next + jnp.sum(coeffs.astype(F32) * left, axis=1, keepdims=True)
    ratio = energy_next / energy
    for b in range(0, blocks, PAIR):
        correction = lax.dot_general(
            coeffs, map_ref[b * bs : (b + PAIR) * bs], (((1,), (1,)), ((), ())), preferred_element_type=F32
        )
        for c in range(b, b + PAIR):
            at = slice(c * bs, (c + 1) * bs)
            direction = dir_ref[c]
            residual = right_side_of(probes_ref, gradient, c, bs, rows) - step * hess_ref[c]
            smoothed = (residual + correction[:, (c - b) * bs : (c - b + 1) * bs]) * inv_diag[c : c + 1]
            for ref, value in (
                (solution_ref, step * direction),
                (residual_ref, residual),
                (next_ref, smoothed + ratio * direction),
            ):
                ref[0:1, at] = value[count : count + 1]
                ref[1 : count + 1, at] = value[:count]


def call(kernel, outs, scratch=(), scalars=0, count=0, **kw):
    vmem = pl.BlockSpec(memory_space=pltpu.VMEM)
    smem = pl.BlockSpec(memory_space=pltpu.SMEM)
    shapes = tuple(jax.ShapeDtypeStruct(s, t) for s, t in outs)
    return pl.pallas_call(
        kernel,
        out_shape=shapes if len(shapes) > 1 else shapes[0],
        in_specs=[smem] * scalars + [vmem] * (count - scalars),
        out_specs=(vmem,) * len(shapes) if len(shapes) > 1 else vmem,
        scratch_shapes=scratch,
        compiler_params=pltpu.CompilerParams(vmem_limit_bytes=48 * 1024 * 1024),
    )


def body(latent, responses, probes, prior_diag, factor, cond_ids, inducing_map, inner_inverse):
    blocks, _, bs, _ = factor.shape
    count = probes.shape[0]
    inducing = inducing_map.shape[1]
    rows = count + 8
    tall = count + 16
    by_block = lambda x: x.reshape(blocks, bs)
    points = (by_block(latent), by_block(responses), by_block(prior_diag), probes, inducing_map)
    partial = call(functools.partial(project_kernel, rows), [((rows, inducing), F32)], count=5)(*points)
    sums = total(partial, "space")
    packed = (blocks + 1, count, bs)
    field = (blocks, rows, bs)
    direction, rounded = call(
        functools.partial(direction_kernel, rows), [(field, F32), (packed, BF16)], [pltpu.VMEM((blocks, bs), F32)], count=7
    )(sums, inner_inverse, *points)
    near = shifted(rounded, "space", 1)
    far = shifted(rounded, "space", 2)
    local_ids = cond_ids - (lax.axis_index("space") - 2) * blocks
    back_far, back_near, back_own, curve = call(
        functools.partial(hessian_kernel, rows),
        [(packed, BF16), (packed, BF16), (field, F32), ((rows, bs), F32)],
        [
            pltpu.VMEM((3 * blocks, count, bs), BF16),
            pltpu.VMEM((3 * blocks, bs), F32),
            pltpu.VMEM((blocks, tall, bs), BF16),
            pltpu.VMEM((3 * blocks, rows, bs), F32),
            pltpu.VMEM((blocks, bs), F32),
        ],
        scalars=1,
        count=5,
    )(local_ids, factor, far, near, rounded)
    from_near = shifted(back_near, "space", -1)
    from_far = shifted(back_far, "space", -2)
    hess, partial = call(
        functools.partial(combine_kernel, rows), [(field, F32), ((rows, inducing), F32)], count=10
    )(back_own, from_near, from_far, curve, direction, *points)
    hess_sums = total(partial, "space")
    whole = (count + 1, blocks * bs)
    return call(functools.partial(finish_kernel, rows), [(whole, F32)] * 3, count=10)(
        sums, hess_sums, inner_inverse, direction, hess, *points
    )


def solution(mesh):
    return jax.shard_map(
        body,
        mesh=mesh,
        in_specs=(
            P(("groups", "space")),
            P(("groups", "space")),
            P(None, ("groups", "space")),
            P(("groups", "space")),
            P(("groups", "space"), None, None, None),
            P(("groups", "space"), None),
            P(("groups", "space"), None),
            P("groups", None),
        ),
        out_specs=(
            P(None, ("groups", "space")),
            P(None, ("groups", "space")),
            P(None, ("groups", "space")),
        ),
        check_vma=False,
    )
```

time: 240 us -> 73.6 us (0.31)
  blocking collectives: 183 us -> 0 us
  waiting for transfers between devices: 5.27 us -> 31.5 us
  starting transfers between devices: 6.61 us -> 23.2 us
  matrix products: 14.8 us -> 0 us
  other arithmetic: 13.7 us -> 0.06 us
  Pallas kernels: 0 us -> 11.8 us
  local copies, waits for them, and re-layouts: 14.8 us -> 5.85 us
    psum x4 -> x0, blocking collectives: 183 us -> none  [the longest x2 121 us: precondition(): summed = lax.psum(partial_sum, 'space')]
    ppermute x4 -> x16, waiting for transfers between devices: 5.27 us -> 31.5 us  [the longest x4 18.4 us: shifted(): return lax.ppermute(block, axis, route)]
    ppermute x4 -> x16, starting transfers between devices: 6.61 us -> 23.2 us  [the longest x12 14.9 us: total(): lax.ppermute(x, axis, [(i, i ^ d) for i in range(n)])]
    dot_general x8 -> x0, matrix products: 14.8 us -> none  [the longest x1 7.44 us: apply_hessian(): jnp.einsum('bkij,cbi->cbkj', factor, imaged, preferred_element_type=jnp.f...]
    pallas_call x0 -> x5, Pallas kernels: none -> 11.8 us  [the longest x1 6.73 us: body(): call(functools.partial(hessian_kernel, rows), [(packed, BF16), (packed, B...]
    gather x1 -> x0, local copies, waits for them, and re-layouts: 3.04 us -> none  [apply_hessian(): picked = jnp.take(neighbourhood, local_ids, axis=1)]
    select_n x2 -> x0, other arithmetic: 2.92 us -> none  [apply_hessian(): picked = jnp.take(neighbourhood, local_ids, axis=1)]
    add x1 -> x4, other arithmetic: 2.52 us -> 0.05 us  [total(): x = x + y]
  transfers between devices with their start and end apart: 4 -> 16, of which waited for: 1 -> 12; matrix products, arithmetic and copies ran while one was open for 4% -> 0% of each run, Pallas kernels for 0% -> 0%
where the time goes in v1:
time: 73.6 us; the launch traced here: 73.1 us
  waiting for transfers between devices  31.5 us (43%)
  starting transfers between devices  23.2 us (32%)
  Pallas kernels  11.8 us (16%)
  local copies, waits for them, and re-layouts  5.85 us (8%)
  between operations  0.78 us (1%)
    ppermute x4, waiting for transfers between devices, shifted(): return lax.ppermute(block, axis, route)  18.4 us
    ppermute x12, starting transfers between devices, total(): lax.ppermute(x, axis, [(i, i ^ d) for i in range(n)])  14.9 us
    ppermute x12, waiting for transfers between devices, total(): lax.ppermute(x, axis, [(i, i ^ d) for i in range(n)])  13.1 us
    ppermute x4, starting transfers between devices, shifted(): return lax.ppermute(block, axis, route)  8.27 us
    pallas_call x1, Pallas kernels, body(): call(functools.partial(hessian_kernel, rows), [(packed, BF16), (packed, B...  6.73 us
    unnamed x27, local copies, waits for them, and re-layouts  5.85 us
    pallas_call x1, Pallas kernels, body(): call(functools.partial(finish_kernel, rows), [(whole, F32)] * 3, count=10)  2.28 us
    pallas_call x1, Pallas kernels, body(): call(functools.partial(direction_kernel, rows), [(field, F32), (packed, B...  1.76 us
  transfers between devices with their start and end apart: 16, of which 12 were waited for; matrix products, arithmetic and copies ran while one was open for 0% of the time, Pallas kernels for 0%

profile of v1, /device:TPU:0, one launch (start us, length us, event | category | flops | bytes accessed | tf_op | source)
XLA Modules:
  0.0 73.1 jit_solution(3446248967151246954)
XLA Ops:
  0.6 0.0 copy-start
  0.7 1.6 %copy-done = bf16[4096,256]{1,0:T(8,128)(2,1)S(1)} copy-done((bf16[4096,256]{1,0:T(8,128)(2,1)S(1)}, bf16[4096,256]{1,0:T(8,128)(2,1)}, u32[]{:S(2)}) %copy-start) | copy-done | bytes 2097176
  2.2 1.0 %copy-done.2 = f32[32,4096]{1,0:T(8,128)S(1)} copy-done((f32[32,4096]{1,0:T(8,128)S(1)}, f32[32,4096]{1,0:T(8,128)}, u32[]{:S(2)}) %copy-start.2) | copy-done | bytes 524312
  3.3 0.7 copy-done.6
  4.0 0.7 copy-done.8
  4.7 0.7 copy-done.10
  5.4 0.5 shard_map.103
  5.9 0.0 copy-start.1
  5.9 0.0 copy-start.3
  6.0 2.4 %collective-permute-start.2 = (f32[40,256]{1,0:T(8,128)S(1)}, f32[40,256]{1,0:T(8,128)S(1)}, u32[]{:S(2)}, u32[]{:S(2)}) collective-permute-start(f32[40,256]{1,0:T(8,128)S(1)} %shard_map.103), channel_id=1, source_target_pairs={{0,3},{1,2},{2,1},{3,0},{4,7},{5,6},{6,5},{7,4},{8,11},{9,10},{10,... | collective-permute-start | bytes 122888 | tf_op jit(solution)/shard_map/ppermute | solution.py:27
  8.4 0.6 collective-permute-start.1
  9.0 0.0 collective-permute-start
  9.1 1.3 %collective-permute-done.2 = f32[40,256]{1,0:T(8,128)S(1)} collective-permute-done((f32[40,256]{1,0:T(8,128)S(1)}, f32[40,256]{1,0:T(8,128)S(1)}, u32[]{:S(2)}, u32[]{:S(2)}) %collective-permute-start.2) | collective-permute-done | bytes 40992 | tf_op jit(solution)/shard_map/ppermute | solution.py:27
  10.4 2.2 %collective-permute-done.1 = f32[40,256]{1,0:T(8,128)S(1)} collective-permute-done((f32[40,256]{1,0:T(8,128)S(1)}, f32[40,256]{1,0:T(8,128)S(1)}, u32[]{:S(2)}, u32[]{:S(2)}) %collective-permute-start.1) | collective-permute-done | bytes 40992 | tf_op jit(solution)/shard_map/ppermute | solution.py:27
  12.6 0.0 collective-permute-done
  12.6 3.7 %collective-permute-start.5 = (f32[40,256]{1,0:T(8,128)S(1)}, f32[40,256]{1,0:T(8,128)S(1)}, u32[]{:S(2)}, u32[]{:S(2)}) collective-permute-start(f32[40,256]{1,0:T(8,128)S(1)} %add_add_fusion.3), channel_id=1, source_target_pairs={{0,12},{1,13},{2,14},{3,15},{4,8},{5,9},{6,10},{7,11},{8,4},{9,5},... | collective-permute-start | bytes 122888 | tf_op jit(solution)/shard_map/ppermute | solution.py:27
  16.2 0.0 collective-permute-start.4
  16.2 0.8 %collective-permute-start.3 = (f32[40,256]{1,0:T(8,128)S(1)}, f32[40,256]{1,0:T(8,128)S(1)}, u32[]{:S(2)}, u32[]{:S(2)}) collective-permute-start(f32[40,256]{1,0:T(8,128)S(1)} %add_add_fusion.3), channel_id=1, source_target_pairs={{0,4},{1,5},{2,6},{3,7},{4,0},{5,1},{6,2},{7,3},{8,12},{9,13},{10,... | collective-permute-start | bytes 122888 | tf_op jit(solution)/shard_map/ppermute | solution.py:27
  17.0 1.6 %collective-permute-done.5 = f32[40,256]{1,0:T(8,128)S(1)} collective-permute-done((f32[40,256]{1,0:T(8,128)S(1)}, f32[40,256]{1,0:T(8,128)S(1)}, u32[]{:S(2)}, u32[]{:S(2)}) %collective-permute-start.5) | collective-permute-done | bytes 40992 | tf_op jit(solution)/shard_map/ppermute | solution.py:27
  18.6 2.5 %collective-permute-done.4 = f32[40,256]{1,0:T(8,128)S(1)} collective-permute-done((f32[40,256]{1,0:T(8,128)S(1)}, f32[40,256]{1,0:T(8,128)S(1)}, u32[]{:S(2)}, u32[]{:S(2)}) %collective-permute-start.4) | collective-permute-done | bytes 40992 | tf_op jit(solution)/shard_map/ppermute | solution.py:27
  21.1 0.0 collective-permute-done.3
  21.2 0.0 copy-start.4
  21.2 0.9 %copy-done.4 = f32[256,256]{1,0:T(8,128)S(1)} copy-done((f32[256,256]{1,0:T(8,128)S(1)}, f32[256,256]{1,0:T(8,128)}, u32[]{:S(2)}) %copy-start.4) | copy-done | bytes 262168
  22.1 1.8 %shard_map.104 = (f32[32,40,128]{2,1,0:T(8,128)S(1)}, bf16[33,32,128]{2,1,0:T(8,128)(2,1)}) custom-call(f32[40,256]{1,0:T(8,128)S(1)} %add_add_fusion.2.sums_ref, f32[256,256]{1,0:T(8,128)S(1)} %copy-done.4, f32[32,128]{1,0:T(8,128)S(1)} %bitcast.4, s32[32,128]{1,0:T(8,128)S(1)} %bitcast.8, f32[32,128]{1,0:T(8,128)S(1)} %bitcast.12, ...), custom_call_target="tpu_custom_call" | custom-call | tf_op jit(solution)/shard_map/pallas_call | solution.py:244
  23.9 2.0 %collective-permute-start.7 = (bf16[33,32,128]{2,1,0:T(8,128)(2,1)}, bf16[33,32,128]{2,1,0:T(8,128)(2,1)}, u32[]{:S(2)}, u32[]{:S(2)}) collective-permute-start(bf16[33,32,128]{2,1,0:T(8,128)(2,1)} %get-tuple-element.11.own_ref), channel_id=1, source_target_pairs={{0,1},{1,2},{2,3},{3,4},{4,5},{5,6},{6,7},{7,8},{8,9},{9,10},{10,1... | collective-permute-start | bytes 811016 | tf_op jit(solution)/shard_map/ppermute | solution.py:17
  25.9 3.7 %collective-permute-start.6 = (bf16[33,32,128]{2,1,0:T(8,128)(2,1)}, bf16[33,32,128]{2,1,0:T(8,128)(2,1)}, u32[]{:S(2)}, u32[]{:S(2)}) collective-permute-start(bf16[33,32,128]{2,1,0:T(8,128)(2,1)} %get-tuple-element.11.own_ref), channel_id=1, source_target_pairs={{0,2},{1,3},{2,4},{3,5},{4,6},{5,7},{6,8},{7,9},{8,10},{9,11},{10,... | collective-permute-start | bytes 811016 | tf_op jit(solution)/shard_map/ppermute | solution.py:17
  29.6 0.1 copy.12
  29.7 0.0 collective-permute-done.7.near_ref
  29.7 6.4 %collective-permute-done.6.far_ref = bf16[33,32,128]{2,1,0:T(8,128)(2,1)} collective-permute-done((bf16[33,32,128]{2,1,0:T(8,128)(2,1)}, bf16[33,32,128]{2,1,0:T(8,128)(2,1)}, u32[]{:S(2)}, u32[]{:S(2)}) %collective-permute-start.6) | collective-permute-done | bytes 270368 | tf_op jit(solution)/shard_map/ppermute | solution.py:17
  36.1 6.7 %shard_map.105 = (bf16[33,32,128]{2,1,0:T(8,128)(2,1)S(1)}, bf16[33,32,128]{2,1,0:T(8,128)(2,1)S(1)}, f32[32,40,128]{2,1,0:T(8,128)S(1)}, f32[40,128]{1,0:T(8,128)S(1)}) custom-call(s32[32,3]{1,0:T(8,128)S(1)} %broadcast_subtract_fusion.ids_ref, bf16[32,4,128,128]{3,2,1,0:T(8,128)(2,1)} %factor_ref.1, bf16[33,32,128]{2,1,0:T(8,128)(2,1)} %collective-permute-done.6.far_ref, ...), custom_call_target="tpu_custom_call" | custom-call | tf_op jit(solution)/shard_map/pallas_call | solution.py:250
  42.8 1.3 %collective-permute-start.8 = (bf16[33,32,128]{2,1,0:T(8,128)(2,1)S(1)}, bf16[33,32,128]{2,1,0:T(8,128)(2,1)S(1)}, u32[]{:S(2)}, u32[]{:S(2)}) collective-permute-start(bf16[33,32,128]{2,1,0:T(8,128)(2,1)S(1)} %get-tuple-element.13), channel_id=1, source_target_pairs={{1,0},{2,1},{3,2},{4,3},{5,4},{6,5},{7,6},{8,7},{9,8},{10,9},{11,1... | collective-permute-start | bytes 811016 | tf_op jit(solution)/shard_map/ppermute | solution.py:17
  44.1 1.3 %collective-permute-start.9 = (bf16[33,32,128]{2,1,0:T(8,128)(2,1)S(1)}, bf16[33,32,128]{2,1,0:T(8,128)(2,1)S(1)}, u32[]{:S(2)}, u32[]{:S(2)}) collective-permute-start(bf16[33,32,128]{2,1,0:T(8,128)(2,1)S(1)} %get-tuple-element.14), channel_id=1, source_target_pairs={{2,0},{3,1},{4,2},{5,3},{6,4},{7,5},{8,6},{9,7},{10,8},{11,9},{12,... | collective-permute-start | bytes 811016 | tf_op jit(solution)/shard_map/ppermute | solution.py:17
  45.4 0.8 %collective-permute-done.8.near_ref = bf16[33,32,128]{2,1,0:T(8,128)(2,1)S(1)} collective-permute-done((bf16[33,32,128]{2,1,0:T(8,128)(2,1)S(1)}, bf16[33,32,128]{2,1,0:T(8,128)(2,1)S(1)}, u32[]{:S(2)}, u32[]{:S(2)}) %collective-permute-start.8) | collective-permute-done | bytes 270368 | tf_op jit(solution)/shard_map/ppermute | solution.py:17
  46.3 11.1 %collective-permute-done.9.far_ref = bf16[33,32,128]{2,1,0:T(8,128)(2,1)S(1)} collective-permute-done((bf16[33,32,128]{2,1,0:T(8,128)(2,1)S(1)}, bf16[33,32,128]{2,1,0:T(8,128)(2,1)S(1)}, u32[]{:S(2)}, u32[]{:S(2)}) %collective-permute-start.9) | collective-permute-done | bytes 270368 | tf_op jit(solution)/shard_map/ppermute | solution.py:17
  57.5 0.6 shard_map.106
  58.0 1.3 %collective-permute-start.12 = (f32[40,256]{1,0:T(8,128)S(1)}, f32[40,256]{1,0:T(8,128)S(1)}, u32[]{:S(2)}, u32[]{:S(2)}) collective-permute-start(f32[40,256]{1,0:T(8,128)S(1)} %get-tuple-element.17), channel_id=1, source_target_pairs={{0,3},{1,2},{2,1},{3,0},{4,7},{5,6},{6,5},{7,4},{8,11},{9,10},{10,... | collective-permute-start | bytes 122888 | tf_op jit(solution)/shard_map/ppermute | solution.py:27
  59.3 1.5 %collective-permute-start.11 = (f32[40,256]{1,0:T(8,128)S(1)}, f32[40,256]{1,0:T(8,128)S(1)}, u32[]{:S(2)}, u32[]{:S(2)}) collective-permute-start(f32[40,256]{1,0:T(8,128)S(1)} %get-tuple-element.17), channel_id=1, source_target_pairs={{0,2},{1,3},{2,0},{3,1},{4,6},{5,7},{6,4},{7,5},{8,10},{9,11},{10,... | collective-permute-start | bytes 122888 | tf_op jit(solution)/shard_map/ppermute | solution.py:27
  60.8 0.0 collective-permute-start.10
  60.9 0.6 collective-permute-done.12
  61.5 1.8 %collective-permute-done.11 = f32[40,256]{1,0:T(8,128)S(1)} collective-permute-done((f32[40,256]{1,0:T(8,128)S(1)}, f32[40,256]{1,0:T(8,128)S(1)}, u32[]{:S(2)}, u32[]{:S(2)}) %collective-permute-start.11) | collective-permute-done | bytes 40992 | tf_op jit(solution)/shard_map/ppermute | solution.py:27
  63.3 0.0 collective-permute-done.10
  63.4 2.2 %collective-permute-start.15 = (f32[40,256]{1,0:T(8,128)S(1)}, f32[40,256]{1,0:T(8,128)S(1)}, u32[]{:S(2)}, u32[]{:S(2)}) collective-permute-start(f32[40,256]{1,0:T(8,128)S(1)} %add_add_fusion.1), channel_id=1, source_target_pairs={{0,12},{1,13},{2,14},{3,15},{4,8},{5,9},{6,10},{7,11},{8,4},{9,5},... | collective-permute-start | bytes 122888 | tf_op jit(solution)/shard_map/ppermute | solution.py:27
  65.5 0.5 collective-permute-start.14
  66.1 1.8 %collective-permute-start.13 = (f32[40,256]{1,0:T(8,128)S(1)}, f32[40,256]{1,0:T(8,128)S(1)}, u32[]{:S(2)}, u32[]{:S(2)}) collective-permute-start(f32[40,256]{1,0:T(8,128)S(1)} %add_add_fusion.1), channel_id=1, source_target_pairs={{0,4},{1,5},{2,6},{3,7},{4,0},{5,1},{6,2},{7,3},{8,12},{9,13},{10,... | collective-permute-start | bytes 122888 | tf_op jit(solution)/shard_map/ppermute | solution.py:27
  67.8 1.6 %collective-permute-done.15 = f32[40,256]{1,0:T(8,128)S(1)} collective-permute-done((f32[40,256]{1,0:T(8,128)S(1)}, f32[40,256]{1,0:T(8,128)S(1)}, u32[]{:S(2)}, u32[]{:S(2)}) %collective-permute-start.15) | collective-permute-done | bytes 40992 | tf_op jit(solution)/shard_map/ppermute | solution.py:27
  69.4 1.1 %collective-permute-done.14 = f32[40,256]{1,0:T(8,128)S(1)} collective-permute-done((f32[40,256]{1,0:T(8,128)S(1)}, f32[40,256]{1,0:T(8,128)S(1)}, u32[]{:S(2)}, u32[]{:S(2)}) %collective-permute-start.14) | collective-permute-done | bytes 40992 | tf_op jit(solution)/shard_map/ppermute | solution.py:27
  70.5 0.3 collective-permute-done.13
  70.8 2.3 %shard_map.107 = (f32[33,4096]{1,0:T(8,128)}, f32[33,4096]{1,0:T(8,128)}, f32[33,4096]{1,0:T(8,128)}) custom-call(f32[40,256]{1,0:T(8,128)S(1)} %add_add_fusion.2.sums_ref, f32[40,256]{1,0:T(8,128)S(1)} %add_add_fusion.hess_sums_ref, f32[256,256]{1,0:T(8,128)S(1)} %copy-done.5, f32[32,40,128]{2,1,0:T(8,128)S(1)} %get-tuple-element.16.dir_ref, ...), custom_call_target="tpu_custom_call" | custom-call | tf_op jit(solution)/shard_map/pallas_call | solution.py:270
  (21 shorter events, 0.1 us)
Async XLA Ops:
  0.6 28.9 %copy-start.12 = (s32[32,3]{0,1:T(4,128)S(1)}, s32[32,3]{0,1:T(4,128)}, u32[]{:S(2)}) copy-start(s32[32,3]{0,1:T(4,128)} %param.13) | copy-start | bytes 1156
  0.6 1.6 %copy-start = (bf16[4096,256]{1,0:T(8,128)(2,1)S(1)}, bf16[4096,256]{1,0:T(8,128)(2,1)}, u32[]{:S(2)}) copy-start(bf16[4096,256]{1,0:T(8,128)(2,1)} %map_ref.7) | copy-start | bytes 6291460
  2.2 1.0 %copy-start.2 = (f32[32,4096]{1,0:T(8,128)S(1)}, f32[32,4096]{1,0:T(8,128)}, u32[]{:S(2)}) copy-start(f32[32,4096]{1,0:T(8,128)} %probes_ref.7) | copy-start | bytes 1572868
  3.3 0.7 copy-start.6
  4.0 0.7 copy-start.8
  4.7 0.7 copy-start.10
  5.4 52.0 %copy-start.7 = (f32[4096]{0:T(1024)S(1)}, f32[4096]{0:T(1024)}, u32[]{:S(2)}) copy-start(f32[4096]{0:T(1024)} %param.8) | copy-start | bytes 49156
  5.4 52.0 %copy-start.9 = (s32[4096]{0:T(1024)S(1)}, s32[4096]{0:T(1024)}, u32[]{:S(2)}) copy-start(s32[4096]{0:T(1024)} %param.9) | copy-start | bytes 49156
  5.4 52.0 %copy-start.11 = (f32[4096]{0:T(1024)S(1)}, f32[4096]{0:T(1024)}, u32[]{:S(2)}) copy-start(f32[4096]{0:T(1024)} %param.11) | copy-start | bytes 49156
  5.9 51.5 %copy-start.1 = (bf16[4096,256]{1,0:T(8,128)(2,1)S(1)}, bf16[4096,256]{1,0:T(8,128)(2,1)}, u32[]{:S(2)}) copy-start(bf16[4096,256]{1,0:T(8,128)(2,1)} %map_ref.7) | copy-start | bytes 6291460
  5.9 51.5 %copy-start.3 = (f32[32,4096]{1,0:T(8,128)S(1)}, f32[32,4096]{1,0:T(8,128)}, u32[]{:S(2)}) copy-start(f32[32,4096]{1,0:T(8,128)} %probes_ref.7) | copy-start | bytes 1572868
  6.0 4.4 %collective-permute-start.2 = (f32[40,256]{1,0:T(8,128)S(1)}, f32[40,256]{1,0:T(8,128)S(1)}, u32[]{:S(2)}, u32[]{:S(2)}) collective-permute-start(f32[40,256]{1,0:T(8,128)S(1)} %shard_map.103), channel_id=1, source_target_pairs={{0,3},{1,2},{2,1},{3,0},{4,7},{5,6},{6,5},{7,4},{8,11},{9,10},{10,... | collective-permute-start | bytes 122888 | tf_op jit(solution)/shard_map/ppermute | solution.py:27
  8.4 4.1 %collective-permute-start.1 = (f32[40,256]{1,0:T(8,128)S(1)}, f32[40,256]{1,0:T(8,128)S(1)}, u32[]{:S(2)}, u32[]{:S(2)}) collective-permute-start(f32[40,256]{1,0:T(8,128)S(1)} %shard_map.103), channel_id=1, source_target_pairs={{0,2},{1,3},{2,0},{3,1},{4,6},{5,7},{6,4},{7,5},{8,10},{9,11},{10,... | collective-permute-start | bytes 122888 | tf_op jit(solution)/shard_map/ppermute | solution.py:27
  9.0 3.5 %collective-permute-start = (f32[40,256]{1,0:T(8,128)S(1)}, f32[40,256]{1,0:T(8,128)S(1)}, u32[]{:S(2)}, u32[]{:S(2)}) collective-permute-start(f32[40,256]{1,0:T(8,128)S(1)} %shard_map.103), channel_id=1, source_target_pairs={{0,1},{1,0},{2,3},{3,2},{4,5},{5,4},{6,7},{7,6},{8,9},{9,8},{10,11... | collective-permute-start | bytes 122888 | tf_op jit(solution)/shard_map/ppermute | solution.py:27
  12.6 6.0 %collective-permute-start.5 = (f32[40,256]{1,0:T(8,128)S(1)}, f32[40,256]{1,0:T(8,128)S(1)}, u32[]{:S(2)}, u32[]{:S(2)}) collective-permute-start(f32[40,256]{1,0:T(8,128)S(1)} %add_add_fusion.3), channel_id=1, source_target_pairs={{0,12},{1,13},{2,14},{3,15},{4,8},{5,9},{6,10},{7,11},{8,4},{9,5},... | collective-permute-start | bytes 122888 | tf_op jit(solution)/shard_map/ppermute | solution.py:27
  16.2 4.9 %collective-permute-start.4 = (f32[40,256]{1,0:T(8,128)S(1)}, f32[40,256]{1,0:T(8,128)S(1)}, u32[]{:S(2)}, u32[]{:S(2)}) collective-permute-start(f32[40,256]{1,0:T(8,128)S(1)} %add_add_fusion.3), channel_id=1, source_target_pairs={{0,8},{1,9},{2,10},{3,11},{4,12},{5,13},{6,14},{7,15},{8,0},{9,1},... | collective-permute-start | bytes 122888 | tf_op jit(solution)/shard_map/ppermute | solution.py:27
  16.2 4.9 %collective-permute-start.3 = (f32[40,256]{1,0:T(8,128)S(1)}, f32[40,256]{1,0:T(8,128)S(1)}, u32[]{:S(2)}, u32[]{:S(2)}) collective-permute-start(f32[40,256]{1,0:T(8,128)S(1)} %add_add_fusion.3), channel_id=1, source_target_pairs={{0,4},{1,5},{2,6},{3,7},{4,0},{5,1},{6,2},{7,3},{8,12},{9,13},{10,... | collective-permute-start | bytes 122888 | tf_op jit(solution)/shard_map/ppermute | solution.py:27
  21.2 1.0 %copy-start.4 = (f32[256,256]{1,0:T(8,128)S(1)}, f32[256,256]{1,0:T(8,128)}, u32[]{:S(2)}) copy-start(f32[256,256]{1,0:T(8,128)} %inner_ref.3) | copy-start | bytes 786436
  23.9 5.8 %collective-permute-start.7 = (bf16[33,32,128]{2,1,0:T(8,128)(2,1)}, bf16[33,32,128]{2,1,0:T(8,128)(2,1)}, u32[]{:S(2)}, u32[]{:S(2)}) collective-permute-start(bf16[33,32,128]{2,1,0:T(8,128)(2,1)} %get-tuple-element.11.own_ref), channel_id=1, source_target_pairs={{0,1},{1,2},{2,3},{3,4},{4,5},{5,6},{6,7},{7,8},{8,9},{9,10},{10,1... | collective-permute-start | bytes 811016 | tf_op jit(solution)/shard_map/ppermute | solution.py:17
  25.9 10.2 %collective-permute-start.6 = (bf16[33,32,128]{2,1,0:T(8,128)(2,1)}, bf16[33,32,128]{2,1,0:T(8,128)(2,1)}, u32[]{:S(2)}, u32[]{:S(2)}) collective-permute-start(bf16[33,32,128]{2,1,0:T(8,128)(2,1)} %get-tuple-element.11.own_ref), channel_id=1, source_target_pairs={{0,2},{1,3},{2,4},{3,5},{4,6},{5,7},{6,8},{7,9},{8,10},{9,11},{10,... | collective-permute-start | bytes 811016 | tf_op jit(solution)/shard_map/ppermute | solution.py:17
  29.7 41.2 %copy-start.5 = (f32[256,256]{1,0:T(8,128)S(1)}, f32[256,256]{1,0:T(8,128)}, u32[]{:S(2)}) copy-start(f32[256,256]{1,0:T(8,128)} %inner_ref.3) | copy-start | bytes 786436
  42.8 3.4 %collective-permute-start.8 = (bf16[33,32,128]{2,1,0:T(8,128)(2,1)S(1)}, bf16[33,32,128]{2,1,0:T(8,128)(2,1)S(1)}, u32[]{:S(2)}, u32[]{:S(2)}) collective-permute-start(bf16[33,32,128]{2,1,0:T(8,128)(2,1)S(1)} %get-tuple-element.13), channel_id=1, source_target_pairs={{1,0},{2,1},{3,2},{4,3},{5,4},{6,5},{7,6},{8,7},{9,8},{10,9},{11,1... | collective-permute-start | bytes 811016 | tf_op jit(solution)/shard_map/ppermute | solution.py:17
  44.1 13.3 %collective-permute-start.9 = (bf16[33,32,128]{2,1,0:T(8,128)(2,1)S(1)}, bf16[33,32,128]{2,1,0:T(8,128)(2,1)S(1)}, u32[]{:S(2)}, u32[]{:S(2)}) collective-permute-start(bf16[33,32,128]{2,1,0:T(8,128)(2,1)S(1)} %get-tuple-element.14), channel_id=1, source_target_pairs={{2,0},{3,1},{4,2},{5,3},{6,4},{7,5},{8,6},{9,7},{10,8},{11,9},{12,... | collective-permute-start | bytes 811016 | tf_op jit(solution)/shard_map/ppermute | solution.py:17
  58.0 3.5 %collective-permute-start.12 = (f32[40,256]{1,0:T(8,128)S(1)}, f32[40,256]{1,0:T(8,128)S(1)}, u32[]{:S(2)}, u32[]{:S(2)}) collective-permute-start(f32[40,256]{1,0:T(8,128)S(1)} %get-tuple-element.17), channel_id=1, source_target_pairs={{0,3},{1,2},{2,1},{3,0},{4,7},{5,6},{6,5},{7,4},{8,11},{9,10},{10,... | collective-permute-start | bytes 122888 | tf_op jit(solution)/shard_map/ppermute | solution.py:27
  59.3 4.0 %collective-permute-start.11 = (f32[40,256]{1,0:T(8,128)S(1)}, f32[40,256]{1,0:T(8,128)S(1)}, u32[]{:S(2)}, u32[]{:S(2)}) collective-permute-start(f32[40,256]{1,0:T(8,128)S(1)} %get-tuple-element.17), channel_id=1, source_target_pairs={{0,2},{1,3},{2,0},{3,1},{4,6},{5,7},{6,4},{7,5},{8,10},{9,11},{10,... | collective-permute-start | bytes 122888 | tf_op jit(solution)/shard_map/ppermute | solution.py:27
  60.8 2.5 %collective-permute-start.10 = (f32[40,256]{1,0:T(8,128)S(1)}, f32[40,256]{1,0:T(8,128)S(1)}, u32[]{:S(2)}, u32[]{:S(2)}) collective-permute-start(f32[40,256]{1,0:T(8,128)S(1)} %get-tuple-element.17), channel_id=1, source_target_pairs={{0,1},{1,0},{2,3},{3,2},{4,5},{5,4},{6,7},{7,6},{8,9},{9,8},{10,11... | collective-permute-start | bytes 122888 | tf_op jit(solution)/shard_map/ppermute | solution.py:27
  63.4 6.0 %collective-permute-start.15 = (f32[40,256]{1,0:T(8,128)S(1)}, f32[40,256]{1,0:T(8,128)S(1)}, u32[]{:S(2)}, u32[]{:S(2)}) collective-permute-start(f32[40,256]{1,0:T(8,128)S(1)} %add_add_fusion.1), channel_id=1, source_target_pairs={{0,12},{1,13},{2,14},{3,15},{4,8},{5,9},{6,10},{7,11},{8,4},{9,5},... | collective-permute-start | bytes 122888 | tf_op jit(solution)/shard_map/ppermute | solution.py:27
  65.5 5.0 %collective-permute-start.14 = (f32[40,256]{1,0:T(8,128)S(1)}, f32[40,256]{1,0:T(8,128)S(1)}, u32[]{:S(2)}, u32[]{:S(2)}) collective-permute-start(f32[40,256]{1,0:T(8,128)S(1)} %add_add_fusion.1), channel_id=1, source_target_pairs={{0,8},{1,9},{2,10},{3,11},{4,12},{5,13},{6,14},{7,15},{8,0},{9,1},... | collective-permute-start | bytes 122888 | tf_op jit(solution)/shard_map/ppermute | solution.py:27
  66.1 4.8 %collective-permute-start.13 = (f32[40,256]{1,0:T(8,128)S(1)}, f32[40,256]{1,0:T(8,128)S(1)}, u32[]{:S(2)}, u32[]{:S(2)}) collective-permute-start(f32[40,256]{1,0:T(8,128)S(1)} %add_add_fusion.1), channel_id=1, source_target_pairs={{0,4},{1,5},{2,6},{3,7},{4,0},{5,1},{6,2},{7,3},{8,12},{9,13},{10,... | collective-permute-start | bytes 122888 | tf_op jit(solution)/shard_map/ppermute | solution.py:27

commit v2 on v1

v2 whole, which is shorter than its diff:
```python
import functools

import jax
import jax.numpy as jnp
from jax import lax
from jax.experimental import pallas as pl
from jax.experimental.pallas import tpu as pltpu
from jax.sharding import PartitionSpec as P

F32, BF16 = jnp.float32, jnp.bfloat16
PAIR = 2
MAP_PARTS = 4
FACTOR_PARTS = 8


def shifted(block, axis, distance):
    devices = range(lax.axis_size(axis))
    route = [(i - distance, i) for i in devices if i - distance in devices]
    return lax.ppermute(block, axis, route)


def total(x, axis):
    n = lax.axis_size(axis)
    if n & (n - 1):
        return lax.psum(x, axis)
    step = 1
    while step < n:
        partners = [m * step for m in range(1, 4) if m * step < n]
        got = [lax.ppermute(x, axis, [(i, i ^ d) for i in range(n)]) for d in partners]
        for y in got:
            x = x + y
        step *= 4
    return x


def eye(rows, lanes):
    return lax.broadcasted_iota(jnp.int32, (rows, lanes), 0) == lax.broadcasted_iota(jnp.int32, (rows, lanes), 1)


def as_row(column, lanes):
    return jnp.sum(jnp.where(eye(column.shape[0], lanes), column, 0.0), axis=0, keepdims=True)


def as_column(row, rows):
    return jnp.sum(jnp.where(eye(rows, row.shape[1]), row, 0.0), axis=1, keepdims=True)


def right_side_of(probes_ref, gradient_ref, b, bs, rows):
    count = probes_ref.shape[0]
    return jnp.concatenate(
        [probes_ref[:, b * bs : (b + 1) * bs], jnp.broadcast_to(gradient_ref[b : b + 1], (rows - count, bs))], axis=0
    )


def project_kernel(
    rows, latent_hbm, responses_hbm, prior_hbm, probes_hbm, map_hbm, inner_hbm, out_ref, terms_ref, probes_ref, map_ref,
    inner_ref, latent_ref, responses_ref, prior_ref, sems,
):
    blocks, bs = latent_ref.shape
    count = probes_ref.shape[0]
    points = map_ref.shape[0]
    part = points // MAP_PARTS
    cut = lambda ref, i: ref.at[i * part : (i + 1) * part]
    pairs = [(latent_hbm, latent_ref), (responses_hbm, responses_ref), (prior_hbm, prior_ref), (probes_hbm, probes_ref)]
    pairs += [(cut(map_hbm, i), cut(map_ref, i)) for i in range(MAP_PARTS)] + [(inner_hbm, inner_ref)]
    copies = [pltpu.make_async_copy(a, b, sems.at[i]) for i, (a, b) in enumerate(pairs)]
    for copy in copies:
        copy.start()
    for copy in copies[:3]:
        copy.wait()
    probability = 1.0 / (1.0 + jnp.exp(-latent_ref[...]))
    weights = probability * (1.0 - probability)
    gradient_ref, weights_ref, inv_diag_ref = terms_ref.at[0], terms_ref.at[1], terms_ref.at[2]
    gradient_ref[...] = responses_ref[...].astype(F32) - probability
    weights_ref[...] = weights
    inv_diag_ref[...] = 1.0 / (weights + prior_ref[...])
    copies[3].wait()
    energy = jnp.zeros((rows, bs), F32)
    summed = jnp.zeros((rows, map_ref.shape[1]), F32)
    for b in range(0, blocks, PAIR):
        if b * bs % part == 0:
            copies[4 + b * bs // part].wait()
        parts = []
        for c in range(b, b + PAIR):
            field = right_side_of(probes_ref, gradient_ref, c, bs, rows)
            scaled = field * inv_diag_ref[c : c + 1]
            energy += field * scaled
            parts.append(scaled.astype(BF16))
        summed += jnp.dot(
            jnp.concatenate(parts, axis=1), map_ref[b * bs : (b + PAIR) * bs], preferred_element_type=F32
        )
    out_ref[...] = summed
    out_ref[count + 1 : count + 2] = as_row(jnp.sum(energy, axis=1, keepdims=True), map_ref.shape[1])
    copies[-1].wait()


def direction_kernel(
    rows, sums_ref, inner_ref, terms_ref, probes_ref, map_ref, dir_ref, msg_ref, product_ref, grad_ref
):
    _, blocks, bs = terms_ref.shape
    count = probes_ref.shape[0]
    gradient_ref, inv_diag_ref = terms_ref.at[0], terms_ref.at[2]
    product = jnp.dot(sums_ref[...], inner_ref[...], precision=lax.Precision.HIGHEST)
    product_ref[...] = product
    coeffs = product.astype(BF16)
    for b in range(0, blocks, PAIR):
        correction = lax.dot_general(
            coeffs, map_ref[b * bs : (b + PAIR) * bs], (((1,), (1,)), ((), ())), preferred_element_type=F32
        )
        for c in range(b, b + PAIR):
            field = right_side_of(probes_ref, gradient_ref, c, bs, rows)
            direction = (field + correction[:, (c - b) * bs : (c - b + 1) * bs]) * inv_diag_ref[c : c + 1]
            dir_ref[c] = direction
            msg_ref[c] = direction[:count].astype(BF16)
            grad_ref[c : c + 1] = direction[count : count + 1]
    msg_ref[blocks] = grad_ref[...].astype(BF16)


def hessian_kernel(
    rows, ids_ref, factor_hbm, far_ref, near_ref, own_ref, back_far_ref, back_near_ref, back_own_ref, curve_ref,
    around_ref, around_grad_ref, image_ref, total_ref, grad_ref, factor_ref, sems,
):
    blocks, taps, bs, _ = factor_ref.shape
    part = blocks // FACTOR_PARTS
    cut = lambda ref, i: ref.at[i * part : (i + 1) * part]
    copies = [
        pltpu.make_async_copy(cut(factor_hbm, i), cut(factor_ref, i), sems.at[i]) for i in range(FACTOR_PARTS)
    ]
    for copy in copies:
        copy.start()
    count = around_ref.shape[1]
    tall = image_ref.shape[1]
    for i, ref in enumerate((far_ref, near_ref, own_ref)):
        around_ref[i * blocks : (i + 1) * blocks] = ref[:blocks]
        around_grad_ref[i * blocks : (i + 1) * blocks] = ref[blocks].astype(F32)
    total_ref[...] = jnp.zeros_like(total_ref)
    curve = jnp.zeros((rows, bs), F32)
    for b in range(blocks):
        if b % part == 0:
            copies[b // part].wait()
        chosen = []
        for k in range(taps):
            at = 2 * blocks + b if k == 0 else ids_ref[b, k - 1]
            last = jnp.broadcast_to(around_grad_ref[pl.ds(at, 1), :], (tall - count, bs)).astype(BF16)
            chosen.append(jnp.concatenate([around_ref[at], last], axis=0))
        side_by_side = jnp.concatenate([factor_ref[b, k] for k in range(taps)], axis=1)
        image = lax.dot_general(
            jnp.concatenate(chosen, axis=1), side_by_side, (((1,), (1,)), ((), ())), preferred_element_type=F32
        )
        rounded = image.astype(BF16)
        image_ref[b] = rounded
        curve += (image * rounded.astype(F32))[:rows]
    curve_ref[...] = curve
    for b in range(blocks):
        side_by_side = jnp.concatenate([factor_ref[b, k] for k in range(taps)], axis=1)
        back = jnp.dot(image_ref[b], side_by_side, preferred_element_type=F32)
        for k in range(taps):
            at = 2 * blocks + b if k == 0 else ids_ref[b, k - 1]
            total_ref[at] += back[:rows, k * bs : (k + 1) * bs]
    for i, ref in enumerate((back_far_ref, back_near_ref)):
        for b in range(blocks):
            ref[b] = total_ref[i * blocks + b, :count].astype(BF16)
            grad_ref[b : b + 1] = total_ref[i * blocks + b, count : count + 1]
        ref[blocks] = grad_ref[...].astype(BF16)
    back_own_ref[...] = total_ref[2 * blocks :]


def combine_kernel(
    rows, own_ref, near_ref, far_ref, curve_ref, dir_ref, terms_ref, probes_ref, map_ref, hess_ref, out_ref
):
    _, blocks, bs = terms_ref.shape
    count = probes_ref.shape[0]
    lanes = map_ref.shape[1]
    gradient_ref, weights_ref, inv_diag_ref = terms_ref.at[0], terms_ref.at[1], terms_ref.at[2]
    from_grad = near_ref[blocks].astype(F32) + far_ref[blocks].astype(F32)
    curve = curve_ref[...]
    cross = jnp.zeros((rows, bs), F32)
    square = jnp.zeros((rows, bs), F32)
    summed = jnp.zeros((rows, lanes), F32)
    for b in range(0, blocks, PAIR):
        parts = []
        for c in range(b, b + PAIR):
            came = jnp.concatenate(
                [
                    near_ref[c].astype(F32) + far_ref[c].astype(F32),
                    jnp.broadcast_to(from_grad[c : c + 1], (rows - count, bs)),
                ],
                axis=0,
            )
            direction = dir_ref[c]
            weighted = weights_ref[c : c + 1] * direction
            hess = own_ref[c] + came + weighted
            hess_ref[c] = hess
            scaled = hess * inv_diag_ref[c : c + 1]
            curve += weighted * direction
            cross += right_side_of(probes_ref, gradient_ref, c, bs, rows) * scaled
            square += hess * scaled
            parts.append(scaled.astype(BF16))
        summed += jnp.dot(
            jnp.concatenate(parts, axis=1), map_ref[b * bs : (b + PAIR) * bs], preferred_element_type=F32
        )
    out_ref[...] = summed
    for i, acc in enumerate((curve, cross, square)):
        out_ref[count + 1 + i : count + 2 + i] = as_row(jnp.sum(acc, axis=1, keepdims=True), lanes)


def finish_kernel(
    rows, sums_ref, product_ref, hess_sums_ref, inner_ref, dir_ref, hess_ref, terms_ref, probes_ref, map_ref,
    solution_ref, residual_ref, next_ref,
):
    _, blocks, bs = terms_ref.shape
    count = probes_ref.shape[0]
    gradient_ref, inv_diag_ref = terms_ref.at[0], terms_ref.at[2]
    sums, product, hess_sums = sums_ref[...], product_ref[...], hess_sums_ref[...]
    column = lambda x, i: as_column(x[count + 1 + i : count + 2 + i], rows)
    coeffs = product.astype(BF16)
    plain = column(sums, 0)
    energy = plain + jnp.sum(coeffs.astype(F32) * sums, axis=1, keepdims=True)
    step = energy / column(hess_sums, 0)
    left = sums - step * hess_sums
    hess_product = jnp.dot(hess_sums, inner_ref[...], precision=lax.Precision.HIGHEST)
    coeffs = (product - step * hess_product).astype(BF16)
    plain_next = plain - 2.0 * step * column(hess_sums, 1) + step * step * column(hess_sums, 2)
    energy_next = plain_next + jnp.sum(coeffs.astype(F32) * left, axis=1, keepdims=True)
    ratio = energy_next / energy
    for b in range(0, blocks, PAIR):
        correction = lax.dot_general(
            coeffs, map_ref[b * bs : (b + PAIR) * bs], (((1,), (1,)), ((), ())), preferred_element_type=F32
        )
        for c in range(b, b + PAIR):
            at = slice(c * bs, (c + 1) * bs)
            direction = dir_ref[c]
            residual = right_side_of(probes_ref, gradient_ref, c, bs, rows) - step * hess_ref[c]
            smoothed = (residual + correction[:, (c - b) * bs : (c - b + 1) * bs]) * inv_diag_ref[c : c + 1]
            for ref, value in (
                (solution_ref, step * direction),
                (residual_ref, residual),
                (next_ref, smoothed + ratio * direction),
            ):
                ref[0:1, at] = value[count : count + 1]
                ref[1 : count + 1, at] = value[:count]


def call(kernel, ins, outs, scratch=(), limit=16, keep=True):
    spec = lambda space: pl.BlockSpec(memory_space=space)
    shapes = tuple((pltpu.VMEM if keep else jax.ShapeDtypeStruct)(s, t) for s, t in outs)
    specs = (spec(pltpu.VMEM),) * len(shapes)
    return pl.pallas_call(
        kernel,
        out_shape=shapes if len(shapes) > 1 else shapes[0],
        in_specs=[spec(space) for space in ins],
        out_specs=specs if len(shapes) > 1 else specs[0],
        scratch_shapes=scratch,
        compiler_params=pltpu.CompilerParams(vmem_limit_bytes=limit * 1024 * 1024),
    )


def in_hbm(x):
    return pltpu.with_memory_space_constraint(x, pltpu.HBM)


def body(latent, responses, probes, prior_diag, factor, cond_ids, inducing_map, inner_inverse):
    blocks, _, bs, _ = factor.shape
    count = probes.shape[0]
    rows, tall = count + 8, count + 16
    by_block = lambda x: x.reshape(blocks, bs)
    sum_shape = ((rows, inducing_map.shape[1]), F32)
    field = ((blocks, rows, bs), F32)
    packed = ((blocks + 1, count, bs), BF16)
    vmem, smem = pltpu.VMEM, pltpu.SMEM
    partial, terms, probes, inducing_map, inner_inverse = call(
        functools.partial(project_kernel, rows),
        [pl.ANY] * 6,
        [sum_shape, ((3, blocks, bs), F32), (probes.shape, F32), (inducing_map.shape, BF16), (inner_inverse.shape, F32)],
        [
            vmem((blocks, bs), F32),
            vmem((blocks, bs), jnp.int32),
            vmem((blocks, bs), F32),
            pltpu.SemaphoreType.DMA((5 + MAP_PARTS,)),
        ],
    )(*map(in_hbm, (by_block(latent), by_block(responses), by_block(prior_diag), probes, inducing_map, inner_inverse)))
    points = (terms, probes, inducing_map)
    sums = total(partial, "space")
    direction, rounded, product = call(
        functools.partial(direction_kernel, rows), [vmem] * 5, [field, packed, sum_shape], [vmem((blocks, bs), F32)]
    )(sums, inner_inverse, *points)
    near = shifted(rounded, "space", 1)
    far = shifted(rounded, "space", 2)
    local_ids = cond_ids - (lax.axis_index("space") - 2) * blocks
    back_far, back_near, back_own, curve = call(
        functools.partial(hessian_kernel, rows),
        [smem, pl.ANY] + [vmem] * 3,
        [packed, packed, field, ((rows, bs), F32)],
        [
            vmem((3 * blocks, count, bs), BF16),
            vmem((3 * blocks, bs), F32),
            vmem((blocks, tall, bs), BF16),
            vmem((3 * blocks, rows, bs), F32),
            vmem((blocks, bs), F32),
            vmem(factor.shape, BF16),
            pltpu.SemaphoreType.DMA((FACTOR_PARTS,)),
        ],
    )(local_ids, in_hbm(factor), far, near, rounded)
    from_near = shifted(back_near, "space", -1)
    from_far = shifted(back_far, "space", -2)
    hess, partial = call(functools.partial(combine_kernel, rows), [vmem] * 8, [field, sum_shape])(
        back_own, from_near, from_far, curve, direction, *points
    )
    hess_sums = total(partial, "space")
    whole = ((count + 1, blocks * bs), F32)
    return call(functools.partial(finish_kernel, rows), [vmem] * 9, [whole] * 3, keep=False)(
        sums, product, hess_sums, inner_inverse, direction, hess, *points
    )


def solution(mesh):
    return jax.shard_map(
        body,
        mesh=mesh,
        in_specs=(
            P(("groups", "space")),
            P(("groups", "space")),
            P(None, ("groups", "space")),
            P(("groups", "space")),
            P(("groups", "space"), None, None, None),
            P(("groups", "space"), None),
            P(("groups", "space"), None),
            P("groups", None),
        ),
        out_specs=(
            P(None, ("groups", "space")),
            P(None, ("groups", "space")),
            P(None, ("groups", "space")),
        ),
        check_vma=False,
    )
```

time: 73.6 us -> 68.6 us (0.932)
  local copies, waits for them, and re-layouts: 5.85 us -> 1.4 us
    unnamed x27 -> x13, local copies, waits for them, and re-layouts: 5.85 us -> 1.4 us
  transfers between devices with their start and end apart: 16 -> 16, of which waited for: 12 -> 12; matrix products, arithmetic and copies ran while one was open for 0% -> 1% of each run, Pallas kernels for 0% -> 0%
where the time goes in v2:
time: 68.6 us; the launch traced here: 68.3 us
  waiting for transfers between devices  30.8 us (45%)
  starting transfers between devices  23.2 us (34%)
  Pallas kernels  12.2 us (18%)
  local copies, waits for them, and re-layouts  1.4 us (2%)
  between operations  0.73 us (1%)
    ppermute x4, waiting for transfers between devices, shifted(): return lax.ppermute(block, axis, route)  17.7 us
    ppermute x12, starting transfers between devices, total(): lax.ppermute(x, axis, [(i, i ^ d) for i in range(n)])  14.9 us
    ppermute x12, waiting for transfers between devices, total(): lax.ppermute(x, axis, [(i, i ^ d) for i in range(n)])  13.1 us
    ppermute x4, starting transfers between devices, shifted(): return lax.ppermute(block, axis, route)  8.28 us
    pallas_call x1, Pallas kernels, body(): call(functools.partial(hessian_kernel, rows), [smem, pl.ANY] + [vmem] * 3...  5.5 us
    pallas_call x1, Pallas kernels, body(): call(functools.partial(finish_kernel, rows), [vmem] * 9, [whole] * 3, kee...  2.23 us
    pallas_call x1, Pallas kernels, body(): call(functools.partial(project_kernel, rows), [pl.ANY] * 6, [sum_shape, (...  2.15 us
    pallas_call x1, Pallas kernels, body(): call(functools.partial(direction_kernel, rows), [vmem] * 5, [field, packe...  1.76 us
  transfers between devices with their start and end apart: 16, of which 12 were waited for; matrix products, arithmetic and copies ran while one was open for 1% of the time, Pallas kernels for 0%

profile of v2, /device:TPU:0, one launch (start us, length us, event | category | flops | bytes accessed | tf_op | source)
XLA Modules:
  0.0 68.3 jit_solution(4298591603018971911)
XLA Ops:
  0.6 2.2 %shard_map.103 = (f32[40,256]{1,0:T(8,128)S(1)}, f32[3,32,128]{2,1,0:T(8,128)S(1)}, f32[32,4096]{1,0:T(8,128)S(1)}, bf16[4096,256]{1,0:T(8,128)(2,1)S(1)}, f32[256,256]{1,0:T(8,128)S(1)}) custom-call(f32[32,128]{1,0:T(8,128)} %bitcast.3, s32[32,128]{1,0:T(8,128)} %bitcast.4, f32[32,128]{1,0:T(8,128)} %bitcast.5, f32[32,4096]{1,0:T(8,128)} %probes_hbm.1, ...), custom_call_target="tpu_custom_call" | custom-call | tf_op jit(solution)/shard_map/pallas_call | solution.py:271
  2.8 0.0 copy-start
  2.8 2.4 %collective-permute-start.2 = (f32[40,256]{1,0:T(8,128)S(1)}, f32[40,256]{1,0:T(8,128)S(1)}, u32[]{:S(2)}, u32[]{:S(2)}) collective-permute-start(f32[40,256]{1,0:T(8,128)S(1)} %get-tuple-element.17), channel_id=1, source_target_pairs={{0,3},{1,2},{2,1},{3,0},{4,7},{5,6},{6,5},{7,4},{8,11},{9,10},{10,... | collective-permute-start | bytes 122888 | tf_op jit(solution)/shard_map/ppermute | solution.py:29
  5.2 0.6 collective-permute-start.1
  5.9 0.0 collective-permute-start
  5.9 1.3 %collective-permute-done.2 = f32[40,256]{1,0:T(8,128)S(1)} collective-permute-done((f32[40,256]{1,0:T(8,128)S(1)}, f32[40,256]{1,0:T(8,128)S(1)}, u32[]{:S(2)}, u32[]{:S(2)}) %collective-permute-start.2) | collective-permute-done | bytes 40992 | tf_op jit(solution)/shard_map/ppermute | solution.py:29
  7.2 2.2 %collective-permute-done.1 = f32[40,256]{1,0:T(8,128)S(1)} collective-permute-done((f32[40,256]{1,0:T(8,128)S(1)}, f32[40,256]{1,0:T(8,128)S(1)}, u32[]{:S(2)}, u32[]{:S(2)}) %collective-permute-start.1) | collective-permute-done | bytes 40992 | tf_op jit(solution)/shard_map/ppermute | solution.py:29
  9.4 0.0 collective-permute-done
  9.4 3.7 %collective-permute-start.5 = (f32[40,256]{1,0:T(8,128)S(1)}, f32[40,256]{1,0:T(8,128)S(1)}, u32[]{:S(2)}, u32[]{:S(2)}) collective-permute-start(f32[40,256]{1,0:T(8,128)S(1)} %add_add_fusion.3), channel_id=1, source_target_pairs={{0,12},{1,13},{2,14},{3,15},{4,8},{5,9},{6,10},{7,11},{8,4},{9,5},... | collective-permute-start | bytes 122888 | tf_op jit(solution)/shard_map/ppermute | solution.py:29
  13.1 0.0 collective-permute-start.4
  13.1 0.8 %collective-permute-start.3 = (f32[40,256]{1,0:T(8,128)S(1)}, f32[40,256]{1,0:T(8,128)S(1)}, u32[]{:S(2)}, u32[]{:S(2)}) collective-permute-start(f32[40,256]{1,0:T(8,128)S(1)} %add_add_fusion.3), channel_id=1, source_target_pairs={{0,4},{1,5},{2,6},{3,7},{4,0},{5,1},{6,2},{7,3},{8,12},{9,13},{10,... | collective-permute-start | bytes 122888 | tf_op jit(solution)/shard_map/ppermute | solution.py:29
  13.9 1.6 %collective-permute-done.5 = f32[40,256]{1,0:T(8,128)S(1)} collective-permute-done((f32[40,256]{1,0:T(8,128)S(1)}, f32[40,256]{1,0:T(8,128)S(1)}, u32[]{:S(2)}, u32[]{:S(2)}) %collective-permute-start.5) | collective-permute-done | bytes 40992 | tf_op jit(solution)/shard_map/ppermute | solution.py:29
  15.5 2.5 %collective-permute-done.4 = f32[40,256]{1,0:T(8,128)S(1)} collective-permute-done((f32[40,256]{1,0:T(8,128)S(1)}, f32[40,256]{1,0:T(8,128)S(1)}, u32[]{:S(2)}, u32[]{:S(2)}) %collective-permute-start.4) | collective-permute-done | bytes 40992 | tf_op jit(solution)/shard_map/ppermute | solution.py:29
  18.0 0.0 collective-permute-done.3
  18.0 0.0 copy-start.2
  18.0 0.0 copy-done
  18.0 1.8 %shard_map.104 = (f32[32,40,128]{2,1,0:T(8,128)S(1)}, bf16[33,32,128]{2,1,0:T(8,128)(2,1)}, f32[40,256]{1,0:T(8,128)S(1)}) custom-call(f32[40,256]{1,0:T(8,128)S(1)} %add_add_fusion.2.sums_ref, f32[256,256]{1,0:T(8,128)S(1)} %get-tuple-element.18.inner_ref, f32[3,32,128]{2,1,0:T(8,128)S(1)} %get-tuple-element.19.terms_ref, ...), custom_call_target="tpu_custom_call" | custom-call | tf_op jit(solution)/shard_map/pallas_call | solution.py:284
  19.8 0.0 copy-done.2
  19.8 0.6 copy-done.4
  20.4 2.0 %collective-permute-start.7 = (bf16[33,32,128]{2,1,0:T(8,128)(2,1)}, bf16[33,32,128]{2,1,0:T(8,128)(2,1)}, u32[]{:S(2)}, u32[]{:S(2)}) collective-permute-start(bf16[33,32,128]{2,1,0:T(8,128)(2,1)} %get-tuple-element.23.own_ref), channel_id=1, source_target_pairs={{0,1},{1,2},{2,3},{3,4},{4,5},{5,6},{6,7},{7,8},{8,9},{9,10},{10,1... | collective-permute-start | bytes 811016 | tf_op jit(solution)/shard_map/ppermute | solution.py:19
  22.4 3.7 %collective-permute-start.6 = (bf16[33,32,128]{2,1,0:T(8,128)(2,1)}, bf16[33,32,128]{2,1,0:T(8,128)(2,1)}, u32[]{:S(2)}, u32[]{:S(2)}) collective-permute-start(bf16[33,32,128]{2,1,0:T(8,128)(2,1)} %get-tuple-element.23.own_ref), channel_id=1, source_target_pairs={{0,2},{1,3},{2,4},{3,5},{4,6},{5,7},{6,8},{7,9},{8,10},{9,11},{10,... | collective-permute-start | bytes 811016 | tf_op jit(solution)/shard_map/ppermute | solution.py:19
  26.1 0.8 %copy.12 = s32[32,3]{1,0:T(8,128)S(1)} copy(s32[32,3]{0,1:T(4,128)} %param.13) | data formatting | bytes 768 | tf_op args[5]
  26.9 0.0 copy-start.1
  26.9 0.0 collective-permute-done.7.near_ref
  26.9 5.8 %collective-permute-done.6.far_ref = bf16[33,32,128]{2,1,0:T(8,128)(2,1)} collective-permute-done((bf16[33,32,128]{2,1,0:T(8,128)(2,1)}, bf16[33,32,128]{2,1,0:T(8,128)(2,1)}, u32[]{:S(2)}, u32[]{:S(2)}) %collective-permute-start.6) | collective-permute-done | bytes 270368 | tf_op jit(solution)/shard_map/ppermute | solution.py:19
  32.6 5.5 %shard_map.105 = (bf16[33,32,128]{2,1,0:T(8,128)(2,1)S(1)}, bf16[33,32,128]{2,1,0:T(8,128)(2,1)S(1)}, f32[32,40,128]{2,1,0:T(8,128)S(1)}, f32[40,128]{1,0:T(8,128)S(1)}) custom-call(s32[32,3]{1,0:T(8,128)S(1)} %broadcast_subtract_fusion.ids_ref, bf16[32,4,128,128]{3,2,1,0:T(8,128)(2,1)} %factor_hbm.1, bf16[33,32,128]{2,1,0:T(8,128)(2,1)} %collective-permute-done.6.far_ref, ...), custom_call_target="tpu_custom_call" | custom-call | tf_op jit(solution)/shard_map/pallas_call | solution.py:290
  38.1 1.3 %collective-permute-start.8 = (bf16[33,32,128]{2,1,0:T(8,128)(2,1)S(1)}, bf16[33,32,128]{2,1,0:T(8,128)(2,1)S(1)}, u32[]{:S(2)}, u32[]{:S(2)}) collective-permute-start(bf16[33,32,128]{2,1,0:T(8,128)(2,1)S(1)} %get-tuple-element.25), channel_id=1, source_target_pairs={{1,0},{2,1},{3,2},{4,3},{5,4},{6,5},{7,6},{8,7},{9,8},{10,9},{11,1... | collective-permute-start | bytes 811016 | tf_op jit(solution)/shard_map/ppermute | solution.py:19
  39.4 1.3 %collective-permute-start.9 = (bf16[33,32,128]{2,1,0:T(8,128)(2,1)S(1)}, bf16[33,32,128]{2,1,0:T(8,128)(2,1)S(1)}, u32[]{:S(2)}, u32[]{:S(2)}) collective-permute-start(bf16[33,32,128]{2,1,0:T(8,128)(2,1)S(1)} %get-tuple-element.26), channel_id=1, source_target_pairs={{2,0},{3,1},{4,2},{5,3},{6,4},{7,5},{8,6},{9,7},{10,8},{11,9},{12,... | collective-permute-start | bytes 811016 | tf_op jit(solution)/shard_map/ppermute | solution.py:19
  40.7 0.8 %collective-permute-done.8.near_ref = bf16[33,32,128]{2,1,0:T(8,128)(2,1)S(1)} collective-permute-done((bf16[33,32,128]{2,1,0:T(8,128)(2,1)S(1)}, bf16[33,32,128]{2,1,0:T(8,128)(2,1)S(1)}, u32[]{:S(2)}, u32[]{:S(2)}) %collective-permute-start.8) | collective-permute-done | bytes 270368 | tf_op jit(solution)/shard_map/ppermute | solution.py:19
  41.6 11.1 %collective-permute-done.9.far_ref = bf16[33,32,128]{2,1,0:T(8,128)(2,1)S(1)} collective-permute-done((bf16[33,32,128]{2,1,0:T(8,128)(2,1)S(1)}, bf16[33,32,128]{2,1,0:T(8,128)(2,1)S(1)}, u32[]{:S(2)}, u32[]{:S(2)}) %collective-permute-start.9) | collective-permute-done | bytes 270368 | tf_op jit(solution)/shard_map/ppermute | solution.py:19
  52.7 0.0 copy-done.1
  52.7 0.0 copy-start.3
  52.7 0.5 shard_map.106
  53.2 1.3 %collective-permute-start.12 = (f32[40,256]{1,0:T(8,128)S(1)}, f32[40,256]{1,0:T(8,128)S(1)}, u32[]{:S(2)}, u32[]{:S(2)}) collective-permute-start(f32[40,256]{1,0:T(8,128)S(1)} %get-tuple-element.29), channel_id=1, source_target_pairs={{0,3},{1,2},{2,1},{3,0},{4,7},{5,6},{6,5},{7,4},{8,11},{9,10},{10,... | collective-permute-start | bytes 122888 | tf_op jit(solution)/shard_map/ppermute | solution.py:29
  54.5 1.5 %collective-permute-start.11 = (f32[40,256]{1,0:T(8,128)S(1)}, f32[40,256]{1,0:T(8,128)S(1)}, u32[]{:S(2)}, u32[]{:S(2)}) collective-permute-start(f32[40,256]{1,0:T(8,128)S(1)} %get-tuple-element.29), channel_id=1, source_target_pairs={{0,2},{1,3},{2,0},{3,1},{4,6},{5,7},{6,4},{7,5},{8,10},{9,11},{10,... | collective-permute-start | bytes 122888 | tf_op jit(solution)/shard_map/ppermute | solution.py:29
  56.0 0.0 collective-permute-start.10
  56.1 0.7 collective-permute-done.12
  56.7 1.8 %collective-permute-done.11 = f32[40,256]{1,0:T(8,128)S(1)} collective-permute-done((f32[40,256]{1,0:T(8,128)S(1)}, f32[40,256]{1,0:T(8,128)S(1)}, u32[]{:S(2)}, u32[]{:S(2)}) %collective-permute-start.11) | collective-permute-done | bytes 40992 | tf_op jit(solution)/shard_map/ppermute | solution.py:29
  58.5 0.0 collective-permute-done.10
  58.6 2.2 %collective-permute-start.15 = (f32[40,256]{1,0:T(8,128)S(1)}, f32[40,256]{1,0:T(8,128)S(1)}, u32[]{:S(2)}, u32[]{:S(2)}) collective-permute-start(f32[40,256]{1,0:T(8,128)S(1)} %add_add_fusion.1), channel_id=1, source_target_pairs={{0,12},{1,13},{2,14},{3,15},{4,8},{5,9},{6,10},{7,11},{8,4},{9,5},... | collective-permute-start | bytes 122888 | tf_op jit(solution)/shard_map/ppermute | solution.py:29
  60.7 0.5 collective-permute-start.14
  61.3 1.8 %collective-permute-start.13 = (f32[40,256]{1,0:T(8,128)S(1)}, f32[40,256]{1,0:T(8,128)S(1)}, u32[]{:S(2)}, u32[]{:S(2)}) collective-permute-start(f32[40,256]{1,0:T(8,128)S(1)} %add_add_fusion.1), channel_id=1, source_target_pairs={{0,4},{1,5},{2,6},{3,7},{4,0},{5,1},{6,2},{7,3},{8,12},{9,13},{10,... | collective-permute-start | bytes 122888 | tf_op jit(solution)/shard_map/ppermute | solution.py:29
  63.0 1.6 %collective-permute-done.15 = f32[40,256]{1,0:T(8,128)S(1)} collective-permute-done((f32[40,256]{1,0:T(8,128)S(1)}, f32[40,256]{1,0:T(8,128)S(1)}, u32[]{:S(2)}, u32[]{:S(2)}) %collective-permute-start.15) | collective-permute-done | bytes 40992 | tf_op jit(solution)/shard_map/ppermute | solution.py:29
  64.6 1.1 %collective-permute-done.14 = f32[40,256]{1,0:T(8,128)S(1)} collective-permute-done((f32[40,256]{1,0:T(8,128)S(1)}, f32[40,256]{1,0:T(8,128)S(1)}, u32[]{:S(2)}, u32[]{:S(2)}) %collective-permute-start.14) | collective-permute-done | bytes 40992 | tf_op jit(solution)/shard_map/ppermute | solution.py:29
  65.7 0.3 collective-permute-done.13
  66.0 0.0 copy-done.3
  66.0 0.0 copy-done.5
  66.0 2.2 %shard_map.107 = (f32[33,4096]{1,0:T(8,128)}, f32[33,4096]{1,0:T(8,128)}, f32[33,4096]{1,0:T(8,128)}) custom-call(f32[40,256]{1,0:T(8,128)S(1)} %copy-done.3, f32[40,256]{1,0:T(8,128)S(1)} %copy-done.5, f32[40,256]{1,0:T(8,128)S(1)} %add_add_fusion.hess_sums_ref, f32[256,256]{1,0:T(8,128)S(1)} %get-tuple-element.18.inner_ref, ...), custom_call_target="tpu_custom_call" | custom-call | tf_op jit(solution)/shard_map/pallas_call | solution.py:311
  (7 shorter events, 0.1 us)
Async XLA Ops:
  2.8 15.2 %copy-start = (f32[3,32,128]{2,1,0:T(8,128)}, f32[3,32,128]{2,1,0:T(8,128)S(1)}, u32[]{:S(2)}) copy-start(f32[3,32,128]{2,1,0:T(8,128)S(1)} %get-tuple-element.19.terms_ref) | copy-start | bytes 147460
  2.8 4.4 %collective-permute-start.2 = (f32[40,256]{1,0:T(8,128)S(1)}, f32[40,256]{1,0:T(8,128)S(1)}, u32[]{:S(2)}, u32[]{:S(2)}) collective-permute-start(f32[40,256]{1,0:T(8,128)S(1)} %get-tuple-element.17), channel_id=1, source_target_pairs={{0,3},{1,2},{2,1},{3,0},{4,7},{5,6},{6,5},{7,4},{8,11},{9,10},{10,... | collective-permute-start | bytes 122888 | tf_op jit(solution)/shard_map/ppermute | solution.py:29
  5.2 4.1 %collective-permute-start.1 = (f32[40,256]{1,0:T(8,128)S(1)}, f32[40,256]{1,0:T(8,128)S(1)}, u32[]{:S(2)}, u32[]{:S(2)}) collective-permute-start(f32[40,256]{1,0:T(8,128)S(1)} %get-tuple-element.17), channel_id=1, source_target_pairs={{0,2},{1,3},{2,0},{3,1},{4,6},{5,7},{6,4},{7,5},{8,10},{9,11},{10,... | collective-permute-start | bytes 122888 | tf_op jit(solution)/shard_map/ppermute | solution.py:29
  5.9 3.5 %collective-permute-start = (f32[40,256]{1,0:T(8,128)S(1)}, f32[40,256]{1,0:T(8,128)S(1)}, u32[]{:S(2)}, u32[]{:S(2)}) collective-permute-start(f32[40,256]{1,0:T(8,128)S(1)} %get-tuple-element.17), channel_id=1, source_target_pairs={{0,1},{1,0},{2,3},{3,2},{4,5},{5,4},{6,7},{7,6},{8,9},{9,8},{10,11... | collective-permute-start | bytes 122888 | tf_op jit(solution)/shard_map/ppermute | solution.py:29
  9.4 6.0 %collective-permute-start.5 = (f32[40,256]{1,0:T(8,128)S(1)}, f32[40,256]{1,0:T(8,128)S(1)}, u32[]{:S(2)}, u32[]{:S(2)}) collective-permute-start(f32[40,256]{1,0:T(8,128)S(1)} %add_add_fusion.3), channel_id=1, source_target_pairs={{0,12},{1,13},{2,14},{3,15},{4,8},{5,9},{6,10},{7,11},{8,4},{9,5},... | collective-permute-start | bytes 122888 | tf_op jit(solution)/shard_map/ppermute | solution.py:29
  13.1 4.9 %collective-permute-start.4 = (f32[40,256]{1,0:T(8,128)S(1)}, f32[40,256]{1,0:T(8,128)S(1)}, u32[]{:S(2)}, u32[]{:S(2)}) collective-permute-start(f32[40,256]{1,0:T(8,128)S(1)} %add_add_fusion.3), channel_id=1, source_target_pairs={{0,8},{1,9},{2,10},{3,11},{4,12},{5,13},{6,14},{7,15},{8,0},{9,1},... | collective-permute-start | bytes 122888 | tf_op jit(solution)/shard_map/ppermute | solution.py:29
  13.1 4.9 %collective-permute-start.3 = (f32[40,256]{1,0:T(8,128)S(1)}, f32[40,256]{1,0:T(8,128)S(1)}, u32[]{:S(2)}, u32[]{:S(2)}) collective-permute-start(f32[40,256]{1,0:T(8,128)S(1)} %add_add_fusion.3), channel_id=1, source_target_pairs={{0,4},{1,5},{2,6},{3,7},{4,0},{5,1},{6,2},{7,3},{8,12},{9,13},{10,... | collective-permute-start | bytes 122888 | tf_op jit(solution)/shard_map/ppermute | solution.py:29
  18.0 1.8 %copy-start.2 = (f32[40,256]{1,0:T(8,128)}, f32[40,256]{1,0:T(8,128)S(1)}, u32[]{:S(2)}) copy-start(f32[40,256]{1,0:T(8,128)S(1)} %add_add_fusion.2.sums_ref) | copy-start | bytes 122884
  19.8 0.6 copy-start.4
  20.4 6.5 %collective-permute-start.7 = (bf16[33,32,128]{2,1,0:T(8,128)(2,1)}, bf16[33,32,128]{2,1,0:T(8,128)(2,1)}, u32[]{:S(2)}, u32[]{:S(2)}) collective-permute-start(bf16[33,32,128]{2,1,0:T(8,128)(2,1)} %get-tuple-element.23.own_ref), channel_id=1, source_target_pairs={{0,1},{1,2},{2,3},{3,4},{4,5},{5,6},{6,7},{7,8},{8,9},{9,10},{10,1... | collective-permute-start | bytes 811016 | tf_op jit(solution)/shard_map/ppermute | solution.py:19
  22.4 10.2 %collective-permute-start.6 = (bf16[33,32,128]{2,1,0:T(8,128)(2,1)}, bf16[33,32,128]{2,1,0:T(8,128)(2,1)}, u32[]{:S(2)}, u32[]{:S(2)}) collective-permute-start(bf16[33,32,128]{2,1,0:T(8,128)(2,1)} %get-tuple-element.23.own_ref), channel_id=1, source_target_pairs={{0,2},{1,3},{2,4},{3,5},{4,6},{5,7},{6,8},{7,9},{8,10},{9,11},{10,... | collective-permute-start | bytes 811016 | tf_op jit(solution)/shard_map/ppermute | solution.py:19
  26.9 25.8 %copy-start.1 = (f32[3,32,128]{2,1,0:T(8,128)S(1)}, f32[3,32,128]{2,1,0:T(8,128)}, u32[]{:S(2)}) copy-start(f32[3,32,128]{2,1,0:T(8,128)} %copy-done) | copy-start | bytes 147460
  38.1 3.4 %collective-permute-start.8 = (bf16[33,32,128]{2,1,0:T(8,128)(2,1)S(1)}, bf16[33,32,128]{2,1,0:T(8,128)(2,1)S(1)}, u32[]{:S(2)}, u32[]{:S(2)}) collective-permute-start(bf16[33,32,128]{2,1,0:T(8,128)(2,1)S(1)} %get-tuple-element.25), channel_id=1, source_target_pairs={{1,0},{2,1},{3,2},{4,3},{5,4},{6,5},{7,6},{8,7},{9,8},{10,9},{11,1... | collective-permute-start | bytes 811016 | tf_op jit(solution)/shard_map/ppermute | solution.py:19
  39.4 13.2 %collective-permute-start.9 = (bf16[33,32,128]{2,1,0:T(8,128)(2,1)S(1)}, bf16[33,32,128]{2,1,0:T(8,128)(2,1)S(1)}, u32[]{:S(2)}, u32[]{:S(2)}) collective-permute-start(bf16[33,32,128]{2,1,0:T(8,128)(2,1)S(1)} %get-tuple-element.26), channel_id=1, source_target_pairs={{2,0},{3,1},{4,2},{5,3},{6,4},{7,5},{8,6},{9,7},{10,8},{11,9},{12,... | collective-permute-start | bytes 811016 | tf_op jit(solution)/shard_map/ppermute | solution.py:19
  52.7 13.3 %copy-start.3 = (f32[40,256]{1,0:T(8,128)S(1)}, f32[40,256]{1,0:T(8,128)}, u32[]{:S(2)}) copy-start(f32[40,256]{1,0:T(8,128)} %copy-done.2) | copy-start | bytes 122884
  52.7 13.4 %copy-start.5 = (f32[40,256]{1,0:T(8,128)S(1)}, f32[40,256]{1,0:T(8,128)}, u32[]{:S(2)}) copy-start(f32[40,256]{1,0:T(8,128)} %copy-done.4) | copy-start | bytes 122884
  53.2 3.5 %collective-permute-start.12 = (f32[40,256]{1,0:T(8,128)S(1)}, f32[40,256]{1,0:T(8,128)S(1)}, u32[]{:S(2)}, u32[]{:S(2)}) collective-permute-start(f32[40,256]{1,0:T(8,128)S(1)} %get-tuple-element.29), channel_id=1, source_target_pairs={{0,3},{1,2},{2,1},{3,0},{4,7},{5,6},{6,5},{7,4},{8,11},{9,10},{10,... | collective-permute-start | bytes 122888 | tf_op jit(solution)/shard_map/ppermute | solution.py:29
  54.5 4.0 %collective-permute-start.11 = (f32[40,256]{1,0:T(8,128)S(1)}, f32[40,256]{1,0:T(8,128)S(1)}, u32[]{:S(2)}, u32[]{:S(2)}) collective-permute-start(f32[40,256]{1,0:T(8,128)S(1)} %get-tuple-element.29), channel_id=1, source_target_pairs={{0,2},{1,3},{2,0},{3,1},{4,6},{5,7},{6,4},{7,5},{8,10},{9,11},{10,... | collective-permute-start | bytes 122888 | tf_op jit(solution)/shard_map/ppermute | solution.py:29
  56.0 2.5 %collective-permute-start.10 = (f32[40,256]{1,0:T(8,128)S(1)}, f32[40,256]{1,0:T(8,128)S(1)}, u32[]{:S(2)}, u32[]{:S(2)}) collective-permute-start(f32[40,256]{1,0:T(8,128)S(1)} %get-tuple-element.29), channel_id=1, source_target_pairs={{0,1},{1,0},{2,3},{3,2},{4,5},{5,4},{6,7},{7,6},{8,9},{9,8},{10,11... | collective-permute-start | bytes 122888 | tf_op jit(solution)/shard_map/ppermute | solution.py:29
  58.6 6.0 %collective-permute-start.15 = (f32[40,256]{1,0:T(8,128)S(1)}, f32[40,256]{1,0:T(8,128)S(1)}, u32[]{:S(2)}, u32[]{:S(2)}) collective-permute-start(f32[40,256]{1,0:T(8,128)S(1)} %add_add_fusion.1), channel_id=1, source_target_pairs={{0,12},{1,13},{2,14},{3,15},{4,8},{5,9},{6,10},{7,11},{8,4},{9,5},... | collective-permute-start | bytes 122888 | tf_op jit(solution)/shard_map/ppermute | solution.py:29
  60.7 5.0 %collective-permute-start.14 = (f32[40,256]{1,0:T(8,128)S(1)}, f32[40,256]{1,0:T(8,128)S(1)}, u32[]{:S(2)}, u32[]{:S(2)}) collective-permute-start(f32[40,256]{1,0:T(8,128)S(1)} %add_add_fusion.1), channel_id=1, source_target_pairs={{0,8},{1,9},{2,10},{3,11},{4,12},{5,13},{6,14},{7,15},{8,0},{9,1},... | collective-permute-start | bytes 122888 | tf_op jit(solution)/shard_map/ppermute | solution.py:29
  61.3 4.7 %collective-permute-start.13 = (f32[40,256]{1,0:T(8,128)S(1)}, f32[40,256]{1,0:T(8,128)S(1)}, u32[]{:S(2)}, u32[]{:S(2)}) collective-permute-start(f32[40,256]{1,0:T(8,128)S(1)} %add_add_fusion.1), channel_id=1, source_target_pairs={{0,4},{1,5},{2,6},{3,7},{4,0},{5,1},{6,2},{7,3},{8,12},{9,13},{10,... | collective-permute-start | bytes 122888 | tf_op jit(solution)/shard_map/ppermute | solution.py:29

commit v3 on v2

--- a/solution.py
+++ b/solution.py
@@ -10,7 +10,6 @@
 F32, BF16 = jnp.float32, jnp.bfloat16
 PAIR = 2
 MAP_PARTS = 4
-FACTOR_PARTS = 8
 
 
 def shifted(block, axis, distance):
@@ -19,16 +18,42 @@
     return lax.ppermute(block, axis, route)
 
 
-def total(x, axis):
+def write_message(msg_ref, x):
+    top = x.shape[0] - 8
+    tail = x[top:]
+    high = tail.astype(BF16).astype(F32)
+    middle = (tail - high).astype(BF16).astype(F32)
+    low = tail - high - middle
+    first = lax.broadcasted_iota(jnp.int32, tail.shape, 0) < 4
+    msg_ref[:top] = x[:top].astype(BF16)
+    msg_ref[top:] = jnp.concatenate([high, jnp.where(first, middle, pltpu.roll(low, 4, 0))], axis=0).astype(BF16)
+
+
+def read_message(msg_ref):
+    x = msg_ref[...].astype(F32)
+    rest = x[-8:]
+    first = lax.broadcasted_iota(jnp.int32, rest.shape, 0) < 4
+    return jnp.concatenate([x[:-16], x[-16:-8] + jnp.where(first, rest + pltpu.roll(rest, 4, 0), 0.0)], axis=0)
+
+
+def add_kernel(x_ref, *refs):
+    *msg_refs, out_ref, msg_ref = refs
+    x = x_ref[...]
+    for ref in msg_refs:
+        x = x + read_message(ref)
+    out_ref[...] = x
+    write_message(msg_ref, x)
+
+
+def total(x, msg, axis):
     n = lax.axis_size(axis)
     if n & (n - 1):
         return lax.psum(x, axis)
     step = 1
     while step < n:
         partners = [m * step for m in range(1, 4) if m * step < n]
-        got = [lax.ppermute(x, axis, [(i, i ^ d) for i in range(n)]) for d in partners]
-        for y in got:
-            x = x + y
+        got = [lax.ppermute(msg, axis, [(i, i ^ d) for i in range(n)]) for d in partners]
+        x, msg = call(add_kernel, [pltpu.VMEM] * (1 + len(got)), [(x.shape, F32), (msg.shape, BF16)])(x, *got)
         step *= 4
     return x
 
@@ -53,8 +78,8 @@
 
 
 def project_kernel(
-    rows, latent_hbm, responses_hbm, prior_hbm, probes_hbm, map_hbm, inner_hbm, out_ref, terms_ref, probes_ref, map_ref,
-    inner_ref, latent_ref, responses_ref, prior_ref, sems,
+    rows, latent_hbm, responses_hbm, prior_hbm, probes_hbm, map_hbm, inner_hbm, out_ref, msg_ref, terms_ref, probes_ref,
+    map_ref, inner_ref, latent_ref, responses_ref, prior_ref, sems,
 ):
     blocks, bs = latent_ref.shape
     count = probes_ref.shape[0]
@@ -91,12 +116,16 @@
         )
     out_ref[...] = summed
     out_ref[count + 1 : count + 2] = as_row(jnp.sum(energy, axis=1, keepdims=True), map_ref.shape[1])
+    write_message(msg_ref, out_ref[...])
     copies[-1].wait()
 
 
 def direction_kernel(
-    rows, sums_ref, inner_ref, terms_ref, probes_ref, map_ref, dir_ref, msg_ref, product_ref, grad_ref
-):
+    rows, sums_ref, inner_ref, terms_ref, probes_ref, map_ref, factor_hbm, dir_ref, msg_ref, product_ref, factor_ref,
+    grad_ref, sem,
+):
+    copy = pltpu.make_async_copy(factor_hbm, factor_ref, sem)
+    copy.start()
     _, blocks, bs = terms_ref.shape
     count = probes_ref.shape[0]
     gradient_ref, inv_diag_ref = terms_ref.at[0], terms_ref.at[2]
@@ -114,20 +143,14 @@
             msg_ref[c] = direction[:count].astype(BF16)
             grad_ref[c : c + 1] = direction[count : count + 1]
     msg_ref[blocks] = grad_ref[...].astype(BF16)
+    copy.wait()
 
 
 def hessian_kernel(
-    rows, ids_ref, factor_hbm, far_ref, near_ref, own_ref, back_far_ref, back_near_ref, back_own_ref, curve_ref,
-    around_ref, around_grad_ref, image_ref, total_ref, grad_ref, factor_ref, sems,
+    rows, ids_ref, factor_ref, near_ref, far_ref, own_ref, back_far_ref, back_near_ref, back_own_ref, curve_ref,
+    around_ref, around_grad_ref, image_ref, total_ref, grad_ref,
 ):
     blocks, taps, bs, _ = factor_ref.shape
-    part = blocks // FACTOR_PARTS
-    cut = lambda ref, i: ref.at[i * part : (i + 1) * part]
-    copies = [
-        pltpu.make_async_copy(cut(factor_hbm, i), cut(factor_ref, i), sems.at[i]) for i in range(FACTOR_PARTS)
-    ]
-    for copy in copies:
-        copy.start()
     count = around_ref.shape[1]
     tall = image_ref.shape[1]
     for i, ref in enumerate((far_ref, near_ref, own_ref)):
@@ -136,8 +159,6 @@
     total_ref[...] = jnp.zeros_like(total_ref)
     curve = jnp.zeros((rows, bs), F32)
     for b in range(blocks):
-        if b % part == 0:
-            copies[b // part].wait()
         chosen = []
         for k in range(taps):
             at = 2 * blocks + b if k == 0 else ids_ref[b, k - 1]
@@ -166,7 +187,7 @@
 
 
 def combine_kernel(
-    rows, own_ref, near_ref, far_ref, curve_ref, dir_ref, terms_ref, probes_ref, map_ref, hess_ref, out_ref
+    rows, own_ref, far_ref, near_ref, curve_ref, dir_ref, terms_ref, probes_ref, map_ref, hess_ref, out_ref, msg_ref
 ):
     _, blocks, bs = terms_ref.shape
     count = probes_ref.shape[0]
@@ -202,6 +223,7 @@
     out_ref[...] = summed
     for i, acc in enumerate((curve, cross, square)):
         out_ref[count + 1 + i : count + 2 + i] = as_row(jnp.sum(acc, axis=1, keepdims=True), lanes)
+    write_message(msg_ref, out_ref[...])
 
 
 def finish_kernel(
@@ -259,19 +281,31 @@
     return pltpu.with_memory_space_constraint(x, pltpu.HBM)
 
 
+def in_vmem(x):
+    return pltpu.with_memory_space_constraint(x, pltpu.VMEM)
+
+
 def body(latent, responses, probes, prior_diag, factor, cond_ids, inducing_map, inner_inverse):
     blocks, _, bs, _ = factor.shape
     count = probes.shape[0]
     rows, tall = count + 8, count + 16
     by_block = lambda x: x.reshape(blocks, bs)
     sum_shape = ((rows, inducing_map.shape[1]), F32)
+    sum_msg = ((tall, inducing_map.shape[1]), BF16)
     field = ((blocks, rows, bs), F32)
     packed = ((blocks + 1, count, bs), BF16)
     vmem, smem = pltpu.VMEM, pltpu.SMEM
-    partial, terms, probes, inducing_map, inner_inverse = call(
+    partial, msg, terms, probes, inducing_map, inner_inverse = call(
         functools.partial(project_kernel, rows),
         [pl.ANY] * 6,
-        [sum_shape, ((3, blocks, bs), F32), (probes.shape, F32), (inducing_map.shape, BF16), (inner_inverse.shape, F32)],
+        [
+            sum_shape,
+            sum_msg,
+            ((3, blocks, bs), F32),
+            (probes.shape, F32),
+            (inducing_map.shape, BF16),
+            (inner_inverse.shape, F32),
+        ],
         [
             vmem((blocks, bs), F32),
             vmem((blocks, bs), jnp.int32),
@@ -280,16 +314,19 @@
         ],
     )(*map(in_hbm, (by_block(latent), by_block(responses), by_block(prior_diag), probes, inducing_map, inner_inverse)))
     points = (terms, probes, inducing_map)
-    sums = total(partial, "space")
-    direction, rounded, product = call(
-        functools.partial(direction_kernel, rows), [vmem] * 5, [field, packed, sum_shape], [vmem((blocks, bs), F32)]
-    )(sums, inner_inverse, *points)
+    sums = total(partial, msg, "space")
+    direction, rounded, product, factor = call(
+        functools.partial(direction_kernel, rows),
+        [vmem] * 5 + [pl.ANY],
+        [field, packed, sum_shape, (factor.shape, BF16)],
+        [vmem((blocks, bs), F32), pltpu.SemaphoreType.DMA],
+    )(sums, inner_inverse, *points, in_hbm(factor))
+    far = shifted(rounded, "space", 2)
     near = shifted(rounded, "space", 1)
-    far = shifted(rounded, "space", 2)
     local_ids = cond_ids - (lax.axis_index("space") - 2) * blocks
     back_far, back_near, back_own, curve = call(
         functools.partial(hessian_kernel, rows),
-        [smem, pl.ANY] + [vmem] * 3,
+        [smem] + [vmem] * 4,
         [packed, packed, field, ((rows, bs), F32)],
         [
             vmem((3 * blocks, count, bs), BF16),
@@ -297,19 +334,17 @@
             vmem((blocks, tall, bs), BF16),
             vmem((3 * blocks, rows, bs), F32),
             vmem((blocks, bs), F32),
-            vmem(factor.shape, BF16),
-            pltpu.SemaphoreType.DMA((FACTOR_PARTS,)),
         ],
-    )(local_ids, in_hbm(factor), far, near, rounded)
+    )(local_ids, factor, near, far, rounded)
+    from_far = shifted(back_far, "space", -2)
     from_near = shifted(back_near, "space", -1)
-    from_far = shifted(back_far, "space", -2)
-    hess, partial = call(functools.partial(combine_kernel, rows), [vmem] * 8, [field, sum_shape])(
-        back_own, from_near, from_far, curve, direction, *points
-    )
-    hess_sums = total(partial, "space")
+    hess, partial, msg = call(functools.partial(combine_kernel, rows), [vmem] * 8, [field, sum_shape, sum_msg])(
+        back_own, from_far, from_near, curve, direction, *points
+    )
+    hess_sums = total(partial, msg, "space")
     whole = ((count + 1, blocks * bs), F32)
     return call(functools.partial(finish_kernel, rows), [vmem] * 9, [whole] * 3, keep=False)(
-        sums, product, hess_sums, inner_inverse, direction, hess, *points
+        *map(in_vmem, (sums, product, hess_sums, inner_inverse, direction, hess, *points))
     )
 
 

time: 68.6 us -> 69.6 us (1.015)
  waiting for transfers between devices: 30.8 us -> 25.4 us
  local copies, waits for them, and re-layouts: 1.4 us -> 5.55 us
  starting transfers between devices: 23.2 us -> 24.4 us
  Pallas kernels: 12.2 us -> 13.2 us
    ppermute x4, waiting for transfers between devices: 17.7 us -> 11.9 us  [shifted(): return lax.ppermute(block, axis, route)]
    unnamed x13 -> x17, local copies, waits for them, and re-layouts: 1.4 us -> 5.55 us
    ppermute x12, starting transfers between devices: 14.9 us -> 16.4 us  [total(): lax.ppermute(msg, axis, [(i, i ^ d) for i in range(n)])]
    pallas_call x3 -> x7, Pallas kernels: 9.41 us -> 10.4 us  [the longest x1 3.92 us: body(): call(functools.partial(hessian_kernel, rows), [smem] + [vmem] * 4, [packe...]
  transfers between devices with their start and end apart: 16 -> 16, of which waited for: 12 -> 11; matrix products, arithmetic and copies ran while one was open for 1% -> 1% of each run, Pallas kernels for 0% -> 0%
where the time goes in v3:
time: 69.6 us; the launch traced here: 69.3 us
  waiting for transfers between devices  25.4 us (36%)
  starting transfers between devices  24.4 us (35%)
  Pallas kernels  13.2 us (19%)
  local copies, waits for them, and re-layouts  5.55 us (8%)
  between operations  0.72 us (1%)
    ppermute x12, starting transfers between devices, total(): lax.ppermute(msg, axis, [(i, i ^ d) for i in range(n)])  16.4 us
    ppermute x12, waiting for transfers between devices, total(): lax.ppermute(msg, axis, [(i, i ^ d) for i in range(n)])  13.4 us
    ppermute x4, waiting for transfers between devices, shifted(): return lax.ppermute(block, axis, route)  11.9 us
    ppermute x4, starting transfers between devices, shifted(): return lax.ppermute(block, axis, route)  7.97 us
    unnamed x17, local copies, waits for them, and re-layouts  5.55 us
    pallas_call x1, Pallas kernels, body(): call(functools.partial(hessian_kernel, rows), [smem] + [vmem] * 4, [packe...  3.92 us
    pallas_call x1, Pallas kernels, body(): call(functools.partial(direction_kernel, rows), [vmem] * 5 + [pl.ANY], [f...  3.02 us
    pallas_call x1, Pallas kernels, body(): call(functools.partial(finish_kernel, rows), [vmem] * 9, [whole] * 3, kee...  2.23 us
  transfers between devices with their start and end apart: 16, of which 11 were waited for; matrix products, arithmetic and copies ran while one was open for 1% of the time, Pallas kernels for 0%

profile of v3, /device:TPU:0, one launch (start us, length us, event | category | flops | bytes accessed | tf_op | source)
XLA Modules:
  0.0 69.3 jit_solution(3874935381888724693)
XLA Ops:
  0.6 2.2 %shard_map.103 = (f32[40,256]{1,0:T(8,128)S(1)}, bf16[48,256]{1,0:T(8,128)(2,1)S(1)}, f32[3,32,128]{2,1,0:T(8,128)S(1)}, f32[32,4096]{1,0:T(8,128)S(1)}, bf16[40...) custom-call(f32[32,128]{1,0:T(8,128)} %bitcast.3, s32[32,128]{1,0:T(8,128)} %bitcast.4, f32[32,128]{1,0:T(8,128)} %bitcast.5, ...), custom_call_target="tpu_custom_call" | custom-call | tf_op jit(solution)/shard_map/pallas_call | solution.py:298
  2.8 0.0 copy-start.2
  2.8 2.4 %collective-permute-start.2 = (bf16[48,256]{1,0:T(8,128)(2,1)S(1)}, bf16[48,256]{1,0:T(8,128)(2,1)S(1)}, u32[]{:S(2)}, u32[]{:S(2)}) collective-permute-start(bf16[48,256]{1,0:T(8,128)(2,1)S(1)} %get-tuple-element.27), channel_id=1, source_target_pairs={{0,3},{1,2},{2,1},{3,0},{4,7},{5,6},{6,5},{7,4},{8,11},{9,10},{10,... | collective-permute-start | bytes 73736 | tf_op jit(solution)/shard_map/ppermute | solution.py:55
  5.3 0.6 collective-permute-start.1
  5.9 0.0 collective-permute-start
  5.9 0.9 %collective-permute-done.2.refs_2_ = bf16[48,256]{1,0:T(8,128)(2,1)S(1)} collective-permute-done((bf16[48,256]{1,0:T(8,128)(2,1)S(1)}, bf16[48,256]{1,0:T(8,128)(2,1)S(1)}, u32[]{:S(2)}, u32[]{:S(2)}) %collective-permute-start.2) | collective-permute-done | bytes 24608 | tf_op jit(solution)/shard_map/ppermute | solution.py:55
  6.9 2.2 %collective-permute-done.1.refs_1_ = bf16[48,256]{1,0:T(8,128)(2,1)S(1)} collective-permute-done((bf16[48,256]{1,0:T(8,128)(2,1)S(1)}, bf16[48,256]{1,0:T(8,128)(2,1)S(1)}, u32[]{:S(2)}, u32[]{:S(2)}) %collective-permute-start.1) | collective-permute-done | bytes 24608 | tf_op jit(solution)/shard_map/ppermute | solution.py:55
  9.1 0.0 collective-permute-done.refs_0_
  9.1 3.7 %collective-permute-start.5 = (bf16[48,256]{1,0:T(8,128)(2,1)S(1)}, bf16[48,256]{1,0:T(8,128)(2,1)S(1)}, u32[]{:S(2)}, u32[]{:S(2)}) collective-permute-start(bf16[48,256]{1,0:T(8,128)(2,1)S(1)} %get-tuple-element.29), channel_id=1, source_target_pairs={{0,12},{1,13},{2,14},{3,15},{4,8},{5,9},{6,10},{7,11},{8,4},{9,5},... | collective-permute-start | bytes 73736 | tf_op jit(solution)/shard_map/ppermute | solution.py:55
  12.8 0.0 collective-permute-start.4
  12.8 0.8 %collective-permute-start.3 = (bf16[48,256]{1,0:T(8,128)(2,1)S(1)}, bf16[48,256]{1,0:T(8,128)(2,1)S(1)}, u32[]{:S(2)}, u32[]{:S(2)}) collective-permute-start(bf16[48,256]{1,0:T(8,128)(2,1)S(1)} %get-tuple-element.29), channel_id=1, source_target_pairs={{0,4},{1,5},{2,6},{3,7},{4,0},{5,1},{6,2},{7,3},{8,12},{9,13},{10,... | collective-permute-start | bytes 73736 | tf_op jit(solution)/shard_map/ppermute | solution.py:55
  13.6 1.5 %collective-permute-done.5.refs_2_ = bf16[48,256]{1,0:T(8,128)(2,1)S(1)} collective-permute-done((bf16[48,256]{1,0:T(8,128)(2,1)S(1)}, bf16[48,256]{1,0:T(8,128)(2,1)S(1)}, u32[]{:S(2)}, u32[]{:S(2)}) %collective-permute-start.5) | collective-permute-done | bytes 24608 | tf_op jit(solution)/shard_map/ppermute | solution.py:55
  15.1 2.4 %collective-permute-done.4.refs_1_ = bf16[48,256]{1,0:T(8,128)(2,1)S(1)} collective-permute-done((bf16[48,256]{1,0:T(8,128)(2,1)S(1)}, bf16[48,256]{1,0:T(8,128)(2,1)S(1)}, u32[]{:S(2)}, u32[]{:S(2)}) %collective-permute-start.4) | collective-permute-done | bytes 24608 | tf_op jit(solution)/shard_map/ppermute | solution.py:55
  17.5 0.0 collective-permute-done.3.refs_0_
  17.5 0.6 shard_map.105
  18.2 3.0 %shard_map.106 = (f32[32,40,128]{2,1,0:T(8,128)S(1)}, bf16[33,32,128]{2,1,0:T(8,128)(2,1)}, f32[40,256]{1,0:T(8,128)S(1)}, bf16[32,4,128,128]{3,2,1,0:T(8,128)(2,1)S(1)}) custom-call(f32[40,256]{1,0:T(8,128)S(1)} %get-tuple-element.30.sums_ref, f32[256,256]{1,0:T(8,128)S(1)} %get-tuple-element.31.inner_ref, f32[3,32,128]{2,1,0:T(8,128)S(1)} %get-tuple-element.32.terms_ref, ...), custom_call_target="tpu_custom_call" | custom-call | tf_op jit(solution)/shard_map/pallas_call | solution.py:318
  21.2 0.0 copy-done.2
  21.2 0.0 copy-start
  21.2 2.0 %copy-done = bf16[32,4,128,128]{3,2,1,0:T(8,128)(2,1)} copy-done((bf16[32,4,128,128]{3,2,1,0:T(8,128)(2,1)}, bf16[32,4,128,128]{3,2,1,0:T(8,128)(2,1)S(1)}, u32[]{:S(2)}) %copy-start) | copy-done | bytes 4194328
  23.2 0.6 copy-done.6
  23.8 0.0 copy-done.4
  23.8 3.4 %collective-permute-start.7 = (bf16[33,32,128]{2,1,0:T(8,128)(2,1)}, bf16[33,32,128]{2,1,0:T(8,128)(2,1)}, u32[]{:S(2)}, u32[]{:S(2)}) collective-permute-start(bf16[33,32,128]{2,1,0:T(8,128)(2,1)} %get-tuple-element.37.own_ref), channel_id=1, source_target_pairs={{0,2},{1,3},{2,4},{3,5},{4,6},{5,7},{6,8},{7,9},{8,10},{9,11},{10,... | collective-permute-start | bytes 811016 | tf_op jit(solution)/shard_map/ppermute | solution.py:18
  27.2 2.0 %collective-permute-start.6 = (bf16[33,32,128]{2,1,0:T(8,128)(2,1)}, bf16[33,32,128]{2,1,0:T(8,128)(2,1)}, u32[]{:S(2)}, u32[]{:S(2)}) collective-permute-start(bf16[33,32,128]{2,1,0:T(8,128)(2,1)} %get-tuple-element.37.own_ref), channel_id=1, source_target_pairs={{0,1},{1,2},{2,3},{3,4},{4,5},{5,6},{6,7},{7,8},{8,9},{9,10},{10,1... | collective-permute-start | bytes 811016 | tf_op jit(solution)/shard_map/ppermute | solution.py:18
  29.2 0.8 %copy.12 = s32[32,3]{1,0:T(8,128)S(1)} copy(s32[32,3]{0,1:T(4,128)} %param.13) | data formatting | bytes 768 | tf_op args[5]
  29.9 2.8 %collective-permute-done.7.far_ref = bf16[33,32,128]{2,1,0:T(8,128)(2,1)} collective-permute-done((bf16[33,32,128]{2,1,0:T(8,128)(2,1)}, bf16[33,32,128]{2,1,0:T(8,128)(2,1)}, u32[]{:S(2)}, u32[]{:S(2)}) %collective-permute-start.7) | collective-permute-done | bytes 270368 | tf_op jit(solution)/shard_map/ppermute | solution.py:18
  32.7 0.0 collective-permute-done.6.near_ref
  32.7 2.2 %copy-done.1 = bf16[32,4,128,128]{3,2,1,0:T(8,128)(2,1)S(1)} copy-done((bf16[32,4,128,128]{3,2,1,0:T(8,128)(2,1)S(1)}, bf16[32,4,128,128]{3,2,1,0:T(8,128)(2,1)}, u32[]{:S(2)}) %copy-start.1) | copy-done | bytes 4194328
  34.9 3.9 %shard_map.107 = (bf16[33,32,128]{2,1,0:T(8,128)(2,1)S(1)}, bf16[33,32,128]{2,1,0:T(8,128)(2,1)S(1)}, f32[32,40,128]{2,1,0:T(8,128)S(1)}, f32[40,128]{1,0:T(8,128)S(1)}) custom-call(s32[32,3]{1,0:T(8,128)S(1)} %broadcast_subtract_fusion.ids_ref, bf16[32,4,128,128]{3,2,1,0:T(8,128)(2,1)S(1)} %copy-done.1, ...), custom_call_target="tpu_custom_call" | custom-call | tf_op jit(solution)/shard_map/pallas_call | solution.py:327
  38.9 1.3 %collective-permute-start.8 = (bf16[33,32,128]{2,1,0:T(8,128)(2,1)S(1)}, bf16[33,32,128]{2,1,0:T(8,128)(2,1)S(1)}, u32[]{:S(2)}, u32[]{:S(2)}) collective-permute-start(bf16[33,32,128]{2,1,0:T(8,128)(2,1)S(1)} %get-tuple-element.39), channel_id=1, source_target_pairs={{2,0},{3,1},{4,2},{5,3},{6,4},{7,5},{8,6},{9,7},{10,8},{11,9},{12,... | collective-permute-start | bytes 811016 | tf_op jit(solution)/shard_map/ppermute | solution.py:18
  40.2 1.3 %collective-permute-start.9 = (bf16[33,32,128]{2,1,0:T(8,128)(2,1)S(1)}, bf16[33,32,128]{2,1,0:T(8,128)(2,1)S(1)}, u32[]{:S(2)}, u32[]{:S(2)}) collective-permute-start(bf16[33,32,128]{2,1,0:T(8,128)(2,1)S(1)} %get-tuple-element.40), channel_id=1, source_target_pairs={{1,0},{2,1},{3,2},{4,3},{5,4},{6,5},{7,6},{8,7},{9,8},{10,9},{11,1... | collective-permute-start | bytes 811016 | tf_op jit(solution)/shard_map/ppermute | solution.py:18
  41.5 9.1 %collective-permute-done.8.far_ref = bf16[33,32,128]{2,1,0:T(8,128)(2,1)S(1)} collective-permute-done((bf16[33,32,128]{2,1,0:T(8,128)(2,1)S(1)}, bf16[33,32,128]{2,1,0:T(8,128)(2,1)S(1)}, u32[]{:S(2)}, u32[]{:S(2)}) %collective-permute-start.8) | collective-permute-done | bytes 270368 | tf_op jit(solution)/shard_map/ppermute | solution.py:18
  50.6 0.0 collective-permute-done.9.near_ref
  50.6 0.0 copy-done.3
  50.6 0.6 shard_map.108
  51.2 3.7 %collective-permute-start.12 = (bf16[48,256]{1,0:T(8,128)(2,1)S(1)}, bf16[48,256]{1,0:T(8,128)(2,1)S(1)}, u32[]{:S(2)}, u32[]{:S(2)}) collective-permute-start(bf16[48,256]{1,0:T(8,128)(2,1)S(1)} %get-tuple-element.44), channel_id=1, source_target_pairs={{0,3},{1,2},{2,1},{3,0},{4,7},{5,6},{6,5},{7,4},{8,11},{9,10},{10,... | collective-permute-start | bytes 73736 | tf_op jit(solution)/shard_map/ppermute | solution.py:55
  54.9 0.7 collective-permute-start.11
  55.6 0.0 collective-permute-start.10
  55.6 0.8 %collective-permute-done.12.refs_2_ = bf16[48,256]{1,0:T(8,128)(2,1)S(1)} collective-permute-done((bf16[48,256]{1,0:T(8,128)(2,1)S(1)}, bf16[48,256]{1,0:T(8,128)(2,1)S(1)}, u32[]{:S(2)}, u32[]{:S(2)}) %collective-permute-start.12) | collective-permute-done | bytes 24608 | tf_op jit(solution)/shard_map/ppermute | solution.py:55
  56.4 2.3 %collective-permute-done.11.refs_1_ = bf16[48,256]{1,0:T(8,128)(2,1)S(1)} collective-permute-done((bf16[48,256]{1,0:T(8,128)(2,1)S(1)}, bf16[48,256]{1,0:T(8,128)(2,1)S(1)}, u32[]{:S(2)}, u32[]{:S(2)}) %collective-permute-start.11) | collective-permute-done | bytes 24608 | tf_op jit(solution)/shard_map/ppermute | solution.py:55
  58.7 0.0 collective-permute-done.10.refs_0_
  58.7 0.8 %collective-permute-start.15 = (bf16[48,256]{1,0:T(8,128)(2,1)S(1)}, bf16[48,256]{1,0:T(8,128)(2,1)S(1)}, u32[]{:S(2)}, u32[]{:S(2)}) collective-permute-start(bf16[48,256]{1,0:T(8,128)(2,1)S(1)} %get-tuple-element.46), channel_id=1, source_target_pairs={{0,12},{1,13},{2,14},{3,15},{4,8},{5,9},{6,10},{7,11},{8,4},{9,5},... | collective-permute-start | bytes 73736 | tf_op jit(solution)/shard_map/ppermute | solution.py:55
  59.5 3.1 %collective-permute-start.14 = (bf16[48,256]{1,0:T(8,128)(2,1)S(1)}, bf16[48,256]{1,0:T(8,128)(2,1)S(1)}, u32[]{:S(2)}, u32[]{:S(2)}) collective-permute-start(bf16[48,256]{1,0:T(8,128)(2,1)S(1)} %get-tuple-element.46), channel_id=1, source_target_pairs={{0,8},{1,9},{2,10},{3,11},{4,12},{5,13},{6,14},{7,15},{8,0},{9,1},... | collective-permute-start | bytes 73736 | tf_op jit(solution)/shard_map/ppermute | solution.py:55
  62.6 0.6 collective-permute-start.13
  63.2 1.3 %collective-permute-done.15.refs_2_ = bf16[48,256]{1,0:T(8,128)(2,1)S(1)} collective-permute-done((bf16[48,256]{1,0:T(8,128)(2,1)S(1)}, bf16[48,256]{1,0:T(8,128)(2,1)S(1)}, u32[]{:S(2)}, u32[]{:S(2)}) %collective-permute-start.15) | collective-permute-done | bytes 24608 | tf_op jit(solution)/shard_map/ppermute | solution.py:55
  64.5 0.4 collective-permute-done.14.refs_1_
  64.9 1.5 %collective-permute-done.13.refs_0_ = bf16[48,256]{1,0:T(8,128)(2,1)S(1)} collective-permute-done((bf16[48,256]{1,0:T(8,128)(2,1)S(1)}, bf16[48,256]{1,0:T(8,128)(2,1)S(1)}, u32[]{:S(2)}, u32[]{:S(2)}) %collective-permute-start.13) | collective-permute-done | bytes 24608 | tf_op jit(solution)/shard_map/ppermute | solution.py:55
  66.4 0.6 shard_map.110
  67.0 2.2 %shard_map.111 = (f32[33,4096]{1,0:T(8,128)}, f32[33,4096]{1,0:T(8,128)}, f32[33,4096]{1,0:T(8,128)}) custom-call(f32[40,256]{1,0:T(8,128)S(1)} %copy-done.5, f32[40,256]{1,0:T(8,128)S(1)} %copy-done.7, f32[40,256]{1,0:T(8,128)S(1)} %get-tuple-element.47.hess_sums_ref, f32[256,256]{1,0:T(8,128)S(1)} %get-tuple-element.31.inner_ref, ...), custom_call_target="tpu_custom_call" | custom-call | tf_op jit(solution)/shard_map/pallas_call | solution.py:346
  (11 shorter events, 0.1 us)
Async XLA Ops:
  2.8 18.4 %copy-start.2 = (f32[3,32,128]{2,1,0:T(8,128)}, f32[3,32,128]{2,1,0:T(8,128)S(1)}, u32[]{:S(2)}) copy-start(f32[3,32,128]{2,1,0:T(8,128)S(1)} %get-tuple-element.32.terms_ref) | copy-start | bytes 147460
  2.8 4.0 %collective-permute-start.2 = (bf16[48,256]{1,0:T(8,128)(2,1)S(1)}, bf16[48,256]{1,0:T(8,128)(2,1)S(1)}, u32[]{:S(2)}, u32[]{:S(2)}) collective-permute-start(bf16[48,256]{1,0:T(8,128)(2,1)S(1)} %get-tuple-element.27), channel_id=1, source_target_pairs={{0,3},{1,2},{2,1},{3,0},{4,7},{5,6},{6,5},{7,4},{8,11},{9,10},{10,... | collective-permute-start | bytes 73736 | tf_op jit(solution)/shard_map/ppermute | solution.py:55
  5.3 3.8 %collective-permute-start.1 = (bf16[48,256]{1,0:T(8,128)(2,1)S(1)}, bf16[48,256]{1,0:T(8,128)(2,1)S(1)}, u32[]{:S(2)}, u32[]{:S(2)}) collective-permute-start(bf16[48,256]{1,0:T(8,128)(2,1)S(1)} %get-tuple-element.27), channel_id=1, source_target_pairs={{0,2},{1,3},{2,0},{3,1},{4,6},{5,7},{6,4},{7,5},{8,10},{9,11},{10,... | collective-permute-start | bytes 73736 | tf_op jit(solution)/shard_map/ppermute | solution.py:55
  5.9 3.2 %collective-permute-start = (bf16[48,256]{1,0:T(8,128)(2,1)S(1)}, bf16[48,256]{1,0:T(8,128)(2,1)S(1)}, u32[]{:S(2)}, u32[]{:S(2)}) collective-permute-start(bf16[48,256]{1,0:T(8,128)(2,1)S(1)} %get-tuple-element.27), channel_id=1, source_target_pairs={{0,1},{1,0},{2,3},{3,2},{4,5},{5,4},{6,7},{7,6},{8,9},{9,8},{10,11... | collective-permute-start | bytes 73736 | tf_op jit(solution)/shard_map/ppermute | solution.py:55
  9.1 6.0 %collective-permute-start.5 = (bf16[48,256]{1,0:T(8,128)(2,1)S(1)}, bf16[48,256]{1,0:T(8,128)(2,1)S(1)}, u32[]{:S(2)}, u32[]{:S(2)}) collective-permute-start(bf16[48,256]{1,0:T(8,128)(2,1)S(1)} %get-tuple-element.29), channel_id=1, source_target_pairs={{0,12},{1,13},{2,14},{3,15},{4,8},{5,9},{6,10},{7,11},{8,4},{9,5},... | collective-permute-start | bytes 73736 | tf_op jit(solution)/shard_map/ppermute | solution.py:55
  12.8 4.7 %collective-permute-start.4 = (bf16[48,256]{1,0:T(8,128)(2,1)S(1)}, bf16[48,256]{1,0:T(8,128)(2,1)S(1)}, u32[]{:S(2)}, u32[]{:S(2)}) collective-permute-start(bf16[48,256]{1,0:T(8,128)(2,1)S(1)} %get-tuple-element.29), channel_id=1, source_target_pairs={{0,8},{1,9},{2,10},{3,11},{4,12},{5,13},{6,14},{7,15},{8,0},{9,1},... | collective-permute-start | bytes 73736 | tf_op jit(solution)/shard_map/ppermute | solution.py:55
  12.8 4.7 %collective-permute-start.3 = (bf16[48,256]{1,0:T(8,128)(2,1)S(1)}, bf16[48,256]{1,0:T(8,128)(2,1)S(1)}, u32[]{:S(2)}, u32[]{:S(2)}) collective-permute-start(bf16[48,256]{1,0:T(8,128)(2,1)S(1)} %get-tuple-element.29), channel_id=1, source_target_pairs={{0,4},{1,5},{2,6},{3,7},{4,0},{5,1},{6,2},{7,3},{8,12},{9,13},{10,... | collective-permute-start | bytes 73736 | tf_op jit(solution)/shard_map/ppermute | solution.py:55
  18.2 5.6 %copy-start.4 = (f32[40,256]{1,0:T(8,128)}, f32[40,256]{1,0:T(8,128)S(1)}, u32[]{:S(2)}) copy-start(f32[40,256]{1,0:T(8,128)S(1)} %get-tuple-element.30.sums_ref) | copy-start | bytes 122884
  21.2 2.0 %copy-start = (bf16[32,4,128,128]{3,2,1,0:T(8,128)(2,1)}, bf16[32,4,128,128]{3,2,1,0:T(8,128)(2,1)S(1)}, u32[]{:S(2)}) copy-start(bf16[32,4,128,128]{3,2,1,0:T(8,128)(2,1)S(1)} %get-tuple-element.36.factor_ref) | copy-start | bytes 12582916
  23.2 0.6 copy-start.6
  23.8 8.9 %collective-permute-start.7 = (bf16[33,32,128]{2,1,0:T(8,128)(2,1)}, bf16[33,32,128]{2,1,0:T(8,128)(2,1)}, u32[]{:S(2)}, u32[]{:S(2)}) collective-permute-start(bf16[33,32,128]{2,1,0:T(8,128)(2,1)} %get-tuple-element.37.own_ref), channel_id=1, source_target_pairs={{0,2},{1,3},{2,4},{3,5},{4,6},{5,7},{6,8},{7,9},{8,10},{9,11},{10,... | collective-permute-start | bytes 811016 | tf_op jit(solution)/shard_map/ppermute | solution.py:18
  27.2 5.6 %collective-permute-start.6 = (bf16[33,32,128]{2,1,0:T(8,128)(2,1)}, bf16[33,32,128]{2,1,0:T(8,128)(2,1)}, u32[]{:S(2)}, u32[]{:S(2)}) collective-permute-start(bf16[33,32,128]{2,1,0:T(8,128)(2,1)} %get-tuple-element.37.own_ref), channel_id=1, source_target_pairs={{0,1},{1,2},{2,3},{3,4},{4,5},{5,6},{6,7},{7,8},{8,9},{9,10},{10,1... | collective-permute-start | bytes 811016 | tf_op jit(solution)/shard_map/ppermute | solution.py:18
  32.7 2.2 %copy-start.1 = (bf16[32,4,128,128]{3,2,1,0:T(8,128)(2,1)S(1)}, bf16[32,4,128,128]{3,2,1,0:T(8,128)(2,1)}, u32[]{:S(2)}) copy-start(bf16[32,4,128,128]{3,2,1,0:T(8,128)(2,1)} %copy-done) | copy-start | bytes 12582916
  34.9 15.7 %copy-start.3 = (f32[3,32,128]{2,1,0:T(8,128)S(1)}, f32[3,32,128]{2,1,0:T(8,128)}, u32[]{:S(2)}) copy-start(f32[3,32,128]{2,1,0:T(8,128)} %copy-done.2) | copy-start | bytes 147460
  34.9 32.1 %copy-start.5 = (f32[40,256]{1,0:T(8,128)S(1)}, f32[40,256]{1,0:T(8,128)}, u32[]{:S(2)}) copy-start(f32[40,256]{1,0:T(8,128)} %copy-done.4) | copy-start | bytes 122884
  34.9 32.1 %copy-start.7 = (f32[40,256]{1,0:T(8,128)S(1)}, f32[40,256]{1,0:T(8,128)}, u32[]{:S(2)}) copy-start(f32[40,256]{1,0:T(8,128)} %copy-done.6) | copy-start | bytes 122884
  38.9 11.7 %collective-permute-start.8 = (bf16[33,32,128]{2,1,0:T(8,128)(2,1)S(1)}, bf16[33,32,128]{2,1,0:T(8,128)(2,1)S(1)}, u32[]{:S(2)}, u32[]{:S(2)}) collective-permute-start(bf16[33,32,128]{2,1,0:T(8,128)(2,1)S(1)} %get-tuple-element.39), channel_id=1, source_target_pairs={{2,0},{3,1},{4,2},{5,3},{6,4},{7,5},{8,6},{9,7},{10,8},{11,9},{12,... | collective-permute-start | bytes 811016 | tf_op jit(solution)/shard_map/ppermute | solution.py:18
  40.2 10.4 %collective-permute-start.9 = (bf16[33,32,128]{2,1,0:T(8,128)(2,1)S(1)}, bf16[33,32,128]{2,1,0:T(8,128)(2,1)S(1)}, u32[]{:S(2)}, u32[]{:S(2)}) collective-permute-start(bf16[33,32,128]{2,1,0:T(8,128)(2,1)S(1)} %get-tuple-element.40), channel_id=1, source_target_pairs={{1,0},{2,1},{3,2},{4,3},{5,4},{6,5},{7,6},{8,7},{9,8},{10,9},{11,1... | collective-permute-start | bytes 811016 | tf_op jit(solution)/shard_map/ppermute | solution.py:18
  51.2 5.2 %collective-permute-start.12 = (bf16[48,256]{1,0:T(8,128)(2,1)S(1)}, bf16[48,256]{1,0:T(8,128)(2,1)S(1)}, u32[]{:S(2)}, u32[]{:S(2)}) collective-permute-start(bf16[48,256]{1,0:T(8,128)(2,1)S(1)} %get-tuple-element.44), channel_id=1, source_target_pairs={{0,3},{1,2},{2,1},{3,0},{4,7},{5,6},{6,5},{7,4},{8,11},{9,10},{10,... | collective-permute-start | bytes 73736 | tf_op jit(solution)/shard_map/ppermute | solution.py:55
  54.9 3.8 %collective-permute-start.11 = (bf16[48,256]{1,0:T(8,128)(2,1)S(1)}, bf16[48,256]{1,0:T(8,128)(2,1)S(1)}, u32[]{:S(2)}, u32[]{:S(2)}) collective-permute-start(bf16[48,256]{1,0:T(8,128)(2,1)S(1)} %get-tuple-element.44), channel_id=1, source_target_pairs={{0,2},{1,3},{2,0},{3,1},{4,6},{5,7},{6,4},{7,5},{8,10},{9,11},{10,... | collective-permute-start | bytes 73736 | tf_op jit(solution)/shard_map/ppermute | solution.py:55
  55.6 3.1 %collective-permute-start.10 = (bf16[48,256]{1,0:T(8,128)(2,1)S(1)}, bf16[48,256]{1,0:T(8,128)(2,1)S(1)}, u32[]{:S(2)}, u32[]{:S(2)}) collective-permute-start(bf16[48,256]{1,0:T(8,128)(2,1)S(1)} %get-tuple-element.44), channel_id=1, source_target_pairs={{0,1},{1,0},{2,3},{3,2},{4,5},{5,4},{6,7},{7,6},{8,9},{9,8},{10,11... | collective-permute-start | bytes 73736 | tf_op jit(solution)/shard_map/ppermute | solution.py:55
  58.7 5.8 %collective-permute-start.15 = (bf16[48,256]{1,0:T(8,128)(2,1)S(1)}, bf16[48,256]{1,0:T(8,128)(2,1)S(1)}, u32[]{:S(2)}, u32[]{:S(2)}) collective-permute-start(bf16[48,256]{1,0:T(8,128)(2,1)S(1)} %get-tuple-element.46), channel_id=1, source_target_pairs={{0,12},{1,13},{2,14},{3,15},{4,8},{5,9},{6,10},{7,11},{8,4},{9,5},... | collective-permute-start | bytes 73736 | tf_op jit(solution)/shard_map/ppermute | solution.py:55
  59.5 5.4 %collective-permute-start.14 = (bf16[48,256]{1,0:T(8,128)(2,1)S(1)}, bf16[48,256]{1,0:T(8,128)(2,1)S(1)}, u32[]{:S(2)}, u32[]{:S(2)}) collective-permute-start(bf16[48,256]{1,0:T(8,128)(2,1)S(1)} %get-tuple-element.46), channel_id=1, source_target_pairs={{0,8},{1,9},{2,10},{3,11},{4,12},{5,13},{6,14},{7,15},{8,0},{9,1},... | collective-permute-start | bytes 73736 | tf_op jit(solution)/shard_map/ppermute | solution.py:55
  62.6 3.8 %collective-permute-start.13 = (bf16[48,256]{1,0:T(8,128)(2,1)S(1)}, bf16[48,256]{1,0:T(8,128)(2,1)S(1)}, u32[]{:S(2)}, u32[]{:S(2)}) collective-permute-start(bf16[48,256]{1,0:T(8,128)(2,1)S(1)} %get-tuple-element.46), channel_id=1, source_target_pairs={{0,4},{1,5},{2,6},{3,7},{4,0},{5,1},{6,2},{7,3},{8,12},{9,13},{10,... | collective-permute-start | bytes 73736 | tf_op jit(solution)/shard_map/ppermute | solution.py:55

commit v4 on v3

--- a/solution.py
+++ b/solution.py
@@ -36,13 +36,14 @@
     return jnp.concatenate([x[:-16], x[-16:-8] + jnp.where(first, rest + pltpu.roll(rest, 4, 0), 0.0)], axis=0)
 
 
-def add_kernel(x_ref, *refs):
-    *msg_refs, out_ref, msg_ref = refs
+def add_kernel(count, x_ref, *refs):
+    *in_refs, out_ref = refs[:count]
     x = x_ref[...]
-    for ref in msg_refs:
+    for ref in in_refs:
         x = x + read_message(ref)
     out_ref[...] = x
-    write_message(msg_ref, x)
+    for ref in refs[count:]:
+        write_message(ref, x)
 
 
 def total(x, msg, axis):
@@ -53,8 +54,13 @@
     while step < n:
         partners = [m * step for m in range(1, 4) if m * step < n]
         got = [lax.ppermute(msg, axis, [(i, i ^ d) for i in range(n)]) for d in partners]
-        x, msg = call(add_kernel, [pltpu.VMEM] * (1 + len(got)), [(x.shape, F32), (msg.shape, BF16)])(x, *got)
         step *= 4
+        add = functools.partial(add_kernel, len(got) + 1)
+        ins = [pltpu.VMEM] * (len(got) + 1)
+        if step < n:
+            x, msg = call(add, ins, [(x.shape, F32), (msg.shape, BF16)])(x, *got)
+        else:
+            x = call(add, ins, [(x.shape, F32)])(x, *got)
     return x
 
 
@@ -156,12 +162,13 @@
     for i, ref in enumerate((far_ref, near_ref, own_ref)):
         around_ref[i * blocks : (i + 1) * blocks] = ref[:blocks]
         around_grad_ref[i * blocks : (i + 1) * blocks] = ref[blocks].astype(F32)
+    first = (lax.axis_index("space") - 2) * blocks
     total_ref[...] = jnp.zeros_like(total_ref)
     curve = jnp.zeros((rows, bs), F32)
     for b in range(blocks):
         chosen = []
         for k in range(taps):
-            at = 2 * blocks + b if k == 0 else ids_ref[b, k - 1]
+            at = 2 * blocks + b if k == 0 else ids_ref[k - 1, b] - first
             last = jnp.broadcast_to(around_grad_ref[pl.ds(at, 1), :], (tall - count, bs)).astype(BF16)
             chosen.append(jnp.concatenate([around_ref[at], last], axis=0))
         side_by_side = jnp.concatenate([factor_ref[b, k] for k in range(taps)], axis=1)
@@ -176,7 +183,7 @@
         side_by_side = jnp.concatenate([factor_ref[b, k] for k in range(taps)], axis=1)
         back = jnp.dot(image_ref[b], side_by_side, preferred_element_type=F32)
         for k in range(taps):
-            at = 2 * blocks + b if k == 0 else ids_ref[b, k - 1]
+            at = 2 * blocks + b if k == 0 else ids_ref[k - 1, b] - first
             total_ref[at] += back[:rows, k * bs : (k + 1) * bs]
     for i, ref in enumerate((back_far_ref, back_near_ref)):
         for b in range(blocks):
@@ -323,7 +330,6 @@
     )(sums, inner_inverse, *points, in_hbm(factor))
     far = shifted(rounded, "space", 2)
     near = shifted(rounded, "space", 1)
-    local_ids = cond_ids - (lax.axis_index("space") - 2) * blocks
     back_far, back_near, back_own, curve = call(
         functools.partial(hessian_kernel, rows),
         [smem] + [vmem] * 4,
@@ -335,7 +341,7 @@
             vmem((3 * blocks, rows, bs), F32),
             vmem((blocks, bs), F32),
         ],
-    )(local_ids, factor, near, far, rounded)
+    )(cond_ids.T, factor, near, far, rounded)
     from_far = shifted(back_far, "space", -2)
     from_near = shifted(back_near, "space", -1)
     hess, partial, msg = call(functools.partial(combine_kernel, rows), [vmem] * 8, [field, sum_shape, sum_msg])(

time: 69.6 us -> 62.9 us (0.904)
  local copies, waits for them, and re-layouts: 5.55 us -> 0.01 us
  waiting for transfers between devices: 25.4 us -> 27.2 us
  Pallas kernels: 13.2 us -> 11.6 us
  starting transfers between devices: 24.4 us -> 23 us
    unnamed x17 -> x2, local copies, waits for them, and re-layouts: 5.55 us -> 0.01 us
    ppermute x4, waiting for transfers between devices: 11.9 us -> 13.8 us  [shifted(): return lax.ppermute(block, axis, route)]
    ppermute x4, starting transfers between devices: 7.97 us -> 6.58 us  [shifted(): return lax.ppermute(block, axis, route)]
    pallas_call x4, Pallas kernels: 1.33 us -> 0.09 us  [the longest x2 0.06 us: total(): x, msg = call(add, ins, [(x.shape, F32), (msg.shape, BF16)])(x, *got)]
  transfers between devices with their start and end apart: 16 -> 16, of which waited for: 11 -> 11; matrix products, arithmetic and copies ran while one was open for 1% -> 0% of each run, Pallas kernels for 0% -> 0%
where the time goes in v4:
time: 62.9 us; the launch traced here: 62.6 us
  waiting for transfers between devices  27.2 us (43%)
  starting transfers between devices  23 us (37%)
  Pallas kernels  11.6 us (18%)
  between operations  0.72 us (1%)
    ppermute x12, starting transfers between devices, total(): lax.ppermute(msg, axis, [(i, i ^ d) for i in range(n)])  16.4 us
    ppermute x4, waiting for transfers between devices, shifted(): return lax.ppermute(block, axis, route)  13.8 us
    ppermute x12, waiting for transfers between devices, total(): lax.ppermute(msg, axis, [(i, i ^ d) for i in range(n)])  13.4 us
    ppermute x4, starting transfers between devices, shifted(): return lax.ppermute(block, axis, route)  6.58 us
    pallas_call x1, Pallas kernels, body(): call(functools.partial(hessian_kernel, rows), [smem] + [vmem] * 4, [packe...  3.33 us
    pallas_call x1, Pallas kernels, body(): call(functools.partial(direction_kernel, rows), [vmem] * 5 + [pl.ANY], [f...  3.12 us
    pallas_call x1, Pallas kernels, body(): call(functools.partial(finish_kernel, rows), [vmem] * 9, [whole] * 3, kee...  2.3 us
    pallas_call x1, Pallas kernels, body(): call(functools.partial(project_kernel, rows), [pl.ANY] * 6, [sum_shape, s...  2.17 us
  transfers between devices with their start and end apart: 16, of which 11 were waited for; matrix products, arithmetic and copies ran while one was open for 0% of the time, Pallas kernels for 0%

profile of v4, /device:TPU:0, one launch (start us, length us, event | category | flops | bytes accessed | tf_op | source)
XLA Modules:
  0.0 62.6 jit_solution(3905799444143682427)
XLA Ops:
  0.6 2.2 %shard_map.103 = (f32[40,256]{1,0:T(8,128)S(1)}, bf16[48,256]{1,0:T(8,128)(2,1)S(1)}, f32[3,32,128]{2,1,0:T(8,128)S(1)}, f32[32,4096]{1,0:T(8,128)S(1)}, bf16[40...) custom-call(f32[32,128]{1,0:T(8,128)} %bitcast.5, s32[32,128]{1,0:T(8,128)} %bitcast.6, f32[32,128]{1,0:T(8,128)} %bitcast.7, ...), custom_call_target="tpu_custom_call" | custom-call | tf_op jit(solution)/shard_map/pallas_call | solution.py:305
  2.8 0.0 copy-start
  2.8 2.4 %collective-permute-start.2 = (bf16[48,256]{1,0:T(8,128)(2,1)S(1)}, bf16[48,256]{1,0:T(8,128)(2,1)S(1)}, u32[]{:S(2)}, u32[]{:S(2)}) collective-permute-start(bf16[48,256]{1,0:T(8,128)(2,1)S(1)} %get-tuple-element.25), channel_id=1, source_target_pairs={{0,3},{1,2},{2,1},{3,0},{4,7},{5,6},{6,5},{7,4},{8,11},{9,10},{10,... | collective-permute-start | bytes 73736 | tf_op jit(solution)/shard_map/ppermute | solution.py:56
  5.3 0.6 %collective-permute-start.1 = (bf16[48,256]{1,0:T(8,128)(2,1)S(1)}, bf16[48,256]{1,0:T(8,128)(2,1)S(1)}, u32[]{:S(2)}, u32[]{:S(2)}) collective-permute-start(bf16[48,256]{1,0:T(8,128)(2,1)S(1)} %get-tuple-element.25), channel_id=1, source_target_pairs={{0,2},{1,3},{2,0},{3,1},{4,6},{5,7},{6,4},{7,5},{8,10},{9,11},{10,... | collective-permute-start | bytes 73736 | tf_op jit(solution)/shard_map/ppermute | solution.py:56
  5.9 0.0 collective-permute-start
  5.9 0.9 %collective-permute-done.2.refs_2_ = bf16[48,256]{1,0:T(8,128)(2,1)S(1)} collective-permute-done((bf16[48,256]{1,0:T(8,128)(2,1)S(1)}, bf16[48,256]{1,0:T(8,128)(2,1)S(1)}, u32[]{:S(2)}, u32[]{:S(2)}) %collective-permute-start.2) | collective-permute-done | bytes 24608 | tf_op jit(solution)/shard_map/ppermute | solution.py:56
  6.9 2.2 %collective-permute-done.1.refs_1_ = bf16[48,256]{1,0:T(8,128)(2,1)S(1)} collective-permute-done((bf16[48,256]{1,0:T(8,128)(2,1)S(1)}, bf16[48,256]{1,0:T(8,128)(2,1)S(1)}, u32[]{:S(2)}, u32[]{:S(2)}) %collective-permute-start.1) | collective-permute-done | bytes 24608 | tf_op jit(solution)/shard_map/ppermute | solution.py:56
  9.1 0.0 collective-permute-done.refs_0_
  9.1 3.7 %collective-permute-start.5 = (bf16[48,256]{1,0:T(8,128)(2,1)S(1)}, bf16[48,256]{1,0:T(8,128)(2,1)S(1)}, u32[]{:S(2)}, u32[]{:S(2)}) collective-permute-start(bf16[48,256]{1,0:T(8,128)(2,1)S(1)} %get-tuple-element.27), channel_id=1, source_target_pairs={{0,12},{1,13},{2,14},{3,15},{4,8},{5,9},{6,10},{7,11},{8,4},{9,5},... | collective-permute-start | bytes 73736 | tf_op jit(solution)/shard_map/ppermute | solution.py:56
  12.8 0.0 collective-permute-start.4
  12.8 0.8 %collective-permute-start.3 = (bf16[48,256]{1,0:T(8,128)(2,1)S(1)}, bf16[48,256]{1,0:T(8,128)(2,1)S(1)}, u32[]{:S(2)}, u32[]{:S(2)}) collective-permute-start(bf16[48,256]{1,0:T(8,128)(2,1)S(1)} %get-tuple-element.27), channel_id=1, source_target_pairs={{0,4},{1,5},{2,6},{3,7},{4,0},{5,1},{6,2},{7,3},{8,12},{9,13},{10,... | collective-permute-start | bytes 73736 | tf_op jit(solution)/shard_map/ppermute | solution.py:56
  13.6 1.5 %collective-permute-done.5.refs_2_ = bf16[48,256]{1,0:T(8,128)(2,1)S(1)} collective-permute-done((bf16[48,256]{1,0:T(8,128)(2,1)S(1)}, bf16[48,256]{1,0:T(8,128)(2,1)S(1)}, u32[]{:S(2)}, u32[]{:S(2)}) %collective-permute-start.5) | collective-permute-done | bytes 24608 | tf_op jit(solution)/shard_map/ppermute | solution.py:56
  15.1 2.4 %collective-permute-done.4.refs_1_ = bf16[48,256]{1,0:T(8,128)(2,1)S(1)} collective-permute-done((bf16[48,256]{1,0:T(8,128)(2,1)S(1)}, bf16[48,256]{1,0:T(8,128)(2,1)S(1)}, u32[]{:S(2)}, u32[]{:S(2)}) %collective-permute-start.4) | collective-permute-done | bytes 24608 | tf_op jit(solution)/shard_map/ppermute | solution.py:56
  17.5 0.0 collective-permute-done.3.refs_0_
  17.5 3.1 %shard_map.106 = (f32[32,40,128]{2,1,0:T(8,128)S(1)}, bf16[33,32,128]{2,1,0:T(8,128)(2,1)S(1)}, f32[40,256]{1,0:T(8,128)S(1)}, bf16[32,4,128,128]{3,2,1,0:T(8,128)(2,1)S(1)}) custom-call(f32[40,256]{1,0:T(8,128)S(1)} %shard_map.105.sums_ref, f32[256,256]{1,0:T(8,128)S(1)} %get-tuple-element.28.inner_ref, f32[3,32,128]{2,1,0:T(8,128)S(1)} %get-tuple-element.29.terms_ref, ...), custom_call_target="tpu_custom_call" | custom-call | tf_op jit(solution)/shard_map/pallas_call | solution.py:325
  20.7 2.7 %collective-permute-start.7 = (bf16[33,32,128]{2,1,0:T(8,128)(2,1)S(1)}, bf16[33,32,128]{2,1,0:T(8,128)(2,1)S(1)}, u32[]{:S(2)}, u32[]{:S(2)}) collective-permute-start(bf16[33,32,128]{2,1,0:T(8,128)(2,1)S(1)} %get-tuple-element.34.own_ref), channel_id=1, source_target_pairs={{0,2},{1,3},{2,4},{3,5},{4,6},{5,7},{6,8},{7,9},{8,10},{9,11},{10,... | collective-permute-start | bytes 811016 | tf_op jit(solution)/shard_map/ppermute | solution.py:18
  23.4 1.3 %collective-permute-start.6 = (bf16[33,32,128]{2,1,0:T(8,128)(2,1)S(1)}, bf16[33,32,128]{2,1,0:T(8,128)(2,1)S(1)}, u32[]{:S(2)}, u32[]{:S(2)}) collective-permute-start(bf16[33,32,128]{2,1,0:T(8,128)(2,1)S(1)} %get-tuple-element.34.own_ref), channel_id=1, source_target_pairs={{0,1},{1,2},{2,3},{3,4},{4,5},{5,6},{6,7},{7,8},{8,9},{9,10},{10,1... | collective-permute-start | bytes 811016 | tf_op jit(solution)/shard_map/ppermute | solution.py:18
  24.7 4.6 %collective-permute-done.7.far_ref = bf16[33,32,128]{2,1,0:T(8,128)(2,1)S(1)} collective-permute-done((bf16[33,32,128]{2,1,0:T(8,128)(2,1)S(1)}, bf16[33,32,128]{2,1,0:T(8,128)(2,1)S(1)}, u32[]{:S(2)}, u32[]{:S(2)}) %collective-permute-start.7) | collective-permute-done | bytes 270368 | tf_op jit(solution)/shard_map/ppermute | solution.py:18
  29.3 0.0 collective-permute-done.6.near_ref
  29.3 0.0 copy-done
  29.3 3.3 %shard_map.107 = (bf16[33,32,128]{2,1,0:T(8,128)(2,1)S(1)}, bf16[33,32,128]{2,1,0:T(8,128)(2,1)S(1)}, f32[32,40,128]{2,1,0:T(8,128)S(1)}, f32[40,128]{1,0:T(8,128)S(1)}) custom-call(s32[3,32]{1,0:T(4,128)S(1)} %bitcast.4, bf16[32,4,128,128]{3,2,1,0:T(8,128)(2,1)S(1)} %get-tuple-element.33.factor_ref, ...), custom_call_target="tpu_custom_call" | custom-call | tf_op jit(solution)/shard_map/pallas_call | solution.py:333
  32.7 1.3 %collective-permute-start.8 = (bf16[33,32,128]{2,1,0:T(8,128)(2,1)S(1)}, bf16[33,32,128]{2,1,0:T(8,128)(2,1)S(1)}, u32[]{:S(2)}, u32[]{:S(2)}) collective-permute-start(bf16[33,32,128]{2,1,0:T(8,128)(2,1)S(1)} %get-tuple-element.36), channel_id=1, source_target_pairs={{2,0},{3,1},{4,2},{5,3},{6,4},{7,5},{8,6},{9,7},{10,8},{11,9},{12,... | collective-permute-start | bytes 811016 | tf_op jit(solution)/shard_map/ppermute | solution.py:18
  34.0 1.3 %collective-permute-start.9 = (bf16[33,32,128]{2,1,0:T(8,128)(2,1)S(1)}, bf16[33,32,128]{2,1,0:T(8,128)(2,1)S(1)}, u32[]{:S(2)}, u32[]{:S(2)}) collective-permute-start(bf16[33,32,128]{2,1,0:T(8,128)(2,1)S(1)} %get-tuple-element.37), channel_id=1, source_target_pairs={{1,0},{2,1},{3,2},{4,3},{5,4},{6,5},{7,6},{8,7},{9,8},{10,9},{11,1... | collective-permute-start | bytes 811016 | tf_op jit(solution)/shard_map/ppermute | solution.py:18
  35.3 9.1 %collective-permute-done.8.far_ref = bf16[33,32,128]{2,1,0:T(8,128)(2,1)S(1)} collective-permute-done((bf16[33,32,128]{2,1,0:T(8,128)(2,1)S(1)}, bf16[33,32,128]{2,1,0:T(8,128)(2,1)S(1)}, u32[]{:S(2)}, u32[]{:S(2)}) %collective-permute-start.8) | collective-permute-done | bytes 270368 | tf_op jit(solution)/shard_map/ppermute | solution.py:18
  44.4 0.0 collective-permute-done.9.near_ref
  44.4 0.6 %shard_map.108 = (f32[32,40,128]{2,1,0:T(8,128)S(1)}, f32[40,256]{1,0:T(8,128)S(1)}, bf16[48,256]{1,0:T(8,128)(2,1)S(1)}) custom-call(f32[32,40,128]{2,1,0:T(8,128)S(1)} %get-tuple-element.35.own_ref, bf16[33,32,128]{2,1,0:T(8,128)(2,1)S(1)} %collective-permute-done.8.far_ref, bf16[33,32,128]{2,1,0:T(8,128)(2,1)S(1)} %collective-permute-done.9.near_ref, ...), custom_call_target="tpu_custom_call" | custom-call | tf_op jit(solution)/shard_map/pallas_call | solution.py:347
  45.0 3.7 %collective-permute-start.12 = (bf16[48,256]{1,0:T(8,128)(2,1)S(1)}, bf16[48,256]{1,0:T(8,128)(2,1)S(1)}, u32[]{:S(2)}, u32[]{:S(2)}) collective-permute-start(bf16[48,256]{1,0:T(8,128)(2,1)S(1)} %get-tuple-element.41), channel_id=1, source_target_pairs={{0,3},{1,2},{2,1},{3,0},{4,7},{5,6},{6,5},{7,4},{8,11},{9,10},{10,... | collective-permute-start | bytes 73736 | tf_op jit(solution)/shard_map/ppermute | solution.py:56
  48.7 0.7 %collective-permute-start.11 = (bf16[48,256]{1,0:T(8,128)(2,1)S(1)}, bf16[48,256]{1,0:T(8,128)(2,1)S(1)}, u32[]{:S(2)}, u32[]{:S(2)}) collective-permute-start(bf16[48,256]{1,0:T(8,128)(2,1)S(1)} %get-tuple-element.41), channel_id=1, source_target_pairs={{0,2},{1,3},{2,0},{3,1},{4,6},{5,7},{6,4},{7,5},{8,10},{9,11},{10,... | collective-permute-start | bytes 73736 | tf_op jit(solution)/shard_map/ppermute | solution.py:56
  49.4 0.0 collective-permute-start.10
  49.4 0.8 %collective-permute-done.12.refs_2_ = bf16[48,256]{1,0:T(8,128)(2,1)S(1)} collective-permute-done((bf16[48,256]{1,0:T(8,128)(2,1)S(1)}, bf16[48,256]{1,0:T(8,128)(2,1)S(1)}, u32[]{:S(2)}, u32[]{:S(2)}) %collective-permute-start.12) | collective-permute-done | bytes 24608 | tf_op jit(solution)/shard_map/ppermute | solution.py:56
  50.3 2.3 %collective-permute-done.11.refs_1_ = bf16[48,256]{1,0:T(8,128)(2,1)S(1)} collective-permute-done((bf16[48,256]{1,0:T(8,128)(2,1)S(1)}, bf16[48,256]{1,0:T(8,128)(2,1)S(1)}, u32[]{:S(2)}, u32[]{:S(2)}) %collective-permute-start.11) | collective-permute-done | bytes 24608 | tf_op jit(solution)/shard_map/ppermute | solution.py:56
  52.6 0.0 collective-permute-done.10.refs_0_
  52.6 0.8 %collective-permute-start.15 = (bf16[48,256]{1,0:T(8,128)(2,1)S(1)}, bf16[48,256]{1,0:T(8,128)(2,1)S(1)}, u32[]{:S(2)}, u32[]{:S(2)}) collective-permute-start(bf16[48,256]{1,0:T(8,128)(2,1)S(1)} %get-tuple-element.43), channel_id=1, source_target_pairs={{0,12},{1,13},{2,14},{3,15},{4,8},{5,9},{6,10},{7,11},{8,4},{9,5},... | collective-permute-start | bytes 73736 | tf_op jit(solution)/shard_map/ppermute | solution.py:56
  53.4 3.1 %collective-permute-start.14 = (bf16[48,256]{1,0:T(8,128)(2,1)S(1)}, bf16[48,256]{1,0:T(8,128)(2,1)S(1)}, u32[]{:S(2)}, u32[]{:S(2)}) collective-permute-start(bf16[48,256]{1,0:T(8,128)(2,1)S(1)} %get-tuple-element.43), channel_id=1, source_target_pairs={{0,8},{1,9},{2,10},{3,11},{4,12},{5,13},{6,14},{7,15},{8,0},{9,1},... | collective-permute-start | bytes 73736 | tf_op jit(solution)/shard_map/ppermute | solution.py:56
  56.4 0.6 collective-permute-start.13
  57.0 1.3 %collective-permute-done.15.refs_2_ = bf16[48,256]{1,0:T(8,128)(2,1)S(1)} collective-permute-done((bf16[48,256]{1,0:T(8,128)(2,1)S(1)}, bf16[48,256]{1,0:T(8,128)(2,1)S(1)}, u32[]{:S(2)}, u32[]{:S(2)}) %collective-permute-start.15) | collective-permute-done | bytes 24608 | tf_op jit(solution)/shard_map/ppermute | solution.py:56
  58.4 0.4 collective-permute-done.14.refs_1_
  58.8 1.5 %collective-permute-done.13.refs_0_ = bf16[48,256]{1,0:T(8,128)(2,1)S(1)} collective-permute-done((bf16[48,256]{1,0:T(8,128)(2,1)S(1)}, bf16[48,256]{1,0:T(8,128)(2,1)S(1)}, u32[]{:S(2)}, u32[]{:S(2)}) %collective-permute-start.13) | collective-permute-done | bytes 24608 | tf_op jit(solution)/shard_map/ppermute | solution.py:56
  60.3 2.3 %shard_map.111 = (f32[33,4096]{1,0:T(8,128)}, f32[33,4096]{1,0:T(8,128)}, f32[33,4096]{1,0:T(8,128)}) custom-call(f32[40,256]{1,0:T(8,128)S(1)} %shard_map.105.sums_ref, f32[40,256]{1,0:T(8,128)S(1)} %get-tuple-element.32.product_ref, f32[40,256]{1,0:T(8,128)S(1)} %shard_map.110.hess_sums_ref, f32[256,256]{1,0:T(8,128)S(1)} %get-tuple-element.28.inner_ref, ...), custom_call_target="tpu_custom_call" | custom-call | tf_op jit(solution)/shard_map/pallas_call | solution.py:352
  (4 shorter events, 0.1 us)
Async XLA Ops:
  2.8 26.5 %copy-start = (s32[32,3]{0,1:T(4,128)S(1)}, s32[32,3]{0,1:T(4,128)}, u32[]{:S(2)}) copy-start(s32[32,3]{0,1:T(4,128)} %param.13) | copy-start | bytes 1156
  2.8 4.0 %collective-permute-start.2 = (bf16[48,256]{1,0:T(8,128)(2,1)S(1)}, bf16[48,256]{1,0:T(8,128)(2,1)S(1)}, u32[]{:S(2)}, u32[]{:S(2)}) collective-permute-start(bf16[48,256]{1,0:T(8,128)(2,1)S(1)} %get-tuple-element.25), channel_id=1, source_target_pairs={{0,3},{1,2},{2,1},{3,0},{4,7},{5,6},{6,5},{7,4},{8,11},{9,10},{10,... | collective-permute-start | bytes 73736 | tf_op jit(solution)/shard_map/ppermute | solution.py:56
  5.3 3.8 %collective-permute-start.1 = (bf16[48,256]{1,0:T(8,128)(2,1)S(1)}, bf16[48,256]{1,0:T(8,128)(2,1)S(1)}, u32[]{:S(2)}, u32[]{:S(2)}) collective-permute-start(bf16[48,256]{1,0:T(8,128)(2,1)S(1)} %get-tuple-element.25), channel_id=1, source_target_pairs={{0,2},{1,3},{2,0},{3,1},{4,6},{5,7},{6,4},{7,5},{8,10},{9,11},{10,... | collective-permute-start | bytes 73736 | tf_op jit(solution)/shard_map/ppermute | solution.py:56
  5.9 3.2 %collective-permute-start = (bf16[48,256]{1,0:T(8,128)(2,1)S(1)}, bf16[48,256]{1,0:T(8,128)(2,1)S(1)}, u32[]{:S(2)}, u32[]{:S(2)}) collective-permute-start(bf16[48,256]{1,0:T(8,128)(2,1)S(1)} %get-tuple-element.25), channel_id=1, source_target_pairs={{0,1},{1,0},{2,3},{3,2},{4,5},{5,4},{6,7},{7,6},{8,9},{9,8},{10,11... | collective-permute-start | bytes 73736 | tf_op jit(solution)/shard_map/ppermute | solution.py:56
  9.1 6.0 %collective-permute-start.5 = (bf16[48,256]{1,0:T(8,128)(2,1)S(1)}, bf16[48,256]{1,0:T(8,128)(2,1)S(1)}, u32[]{:S(2)}, u32[]{:S(2)}) collective-permute-start(bf16[48,256]{1,0:T(8,128)(2,1)S(1)} %get-tuple-element.27), channel_id=1, source_target_pairs={{0,12},{1,13},{2,14},{3,15},{4,8},{5,9},{6,10},{7,11},{8,4},{9,5},... | collective-permute-start | bytes 73736 | tf_op jit(solution)/shard_map/ppermute | solution.py:56
  12.8 4.7 %collective-permute-start.4 = (bf16[48,256]{1,0:T(8,128)(2,1)S(1)}, bf16[48,256]{1,0:T(8,128)(2,1)S(1)}, u32[]{:S(2)}, u32[]{:S(2)}) collective-permute-start(bf16[48,256]{1,0:T(8,128)(2,1)S(1)} %get-tuple-element.27), channel_id=1, source_target_pairs={{0,8},{1,9},{2,10},{3,11},{4,12},{5,13},{6,14},{7,15},{8,0},{9,1},... | collective-permute-start | bytes 73736 | tf_op jit(solution)/shard_map/ppermute | solution.py:56
  12.8 4.7 %collective-permute-start.3 = (bf16[48,256]{1,0:T(8,128)(2,1)S(1)}, bf16[48,256]{1,0:T(8,128)(2,1)S(1)}, u32[]{:S(2)}, u32[]{:S(2)}) collective-permute-start(bf16[48,256]{1,0:T(8,128)(2,1)S(1)} %get-tuple-element.27), channel_id=1, source_target_pairs={{0,4},{1,5},{2,6},{3,7},{4,0},{5,1},{6,2},{7,3},{8,12},{9,13},{10,... | collective-permute-start | bytes 73736 | tf_op jit(solution)/shard_map/ppermute | solution.py:56
  20.7 8.7 %collective-permute-start.7 = (bf16[33,32,128]{2,1,0:T(8,128)(2,1)S(1)}, bf16[33,32,128]{2,1,0:T(8,128)(2,1)S(1)}, u32[]{:S(2)}, u32[]{:S(2)}) collective-permute-start(bf16[33,32,128]{2,1,0:T(8,128)(2,1)S(1)} %get-tuple-element.34.own_ref), channel_id=1, source_target_pairs={{0,2},{1,3},{2,4},{3,5},{4,6},{5,7},{6,8},{7,9},{8,10},{9,11},{10,... | collective-permute-start | bytes 811016 | tf_op jit(solution)/shard_map/ppermute | solution.py:18
  23.4 6.0 %collective-permute-start.6 = (bf16[33,32,128]{2,1,0:T(8,128)(2,1)S(1)}, bf16[33,32,128]{2,1,0:T(8,128)(2,1)S(1)}, u32[]{:S(2)}, u32[]{:S(2)}) collective-permute-start(bf16[33,32,128]{2,1,0:T(8,128)(2,1)S(1)} %get-tuple-element.34.own_ref), channel_id=1, source_target_pairs={{0,1},{1,2},{2,3},{3,4},{4,5},{5,6},{6,7},{7,8},{8,9},{9,10},{10,1... | collective-permute-start | bytes 811016 | tf_op jit(solution)/shard_map/ppermute | solution.py:18
  32.7 11.7 %collective-permute-start.8 = (bf16[33,32,128]{2,1,0:T(8,128)(2,1)S(1)}, bf16[33,32,128]{2,1,0:T(8,128)(2,1)S(1)}, u32[]{:S(2)}, u32[]{:S(2)}) collective-permute-start(bf16[33,32,128]{2,1,0:T(8,128)(2,1)S(1)} %get-tuple-element.36), channel_id=1, source_target_pairs={{2,0},{3,1},{4,2},{5,3},{6,4},{7,5},{8,6},{9,7},{10,8},{11,9},{12,... | collective-permute-start | bytes 811016 | tf_op jit(solution)/shard_map/ppermute | solution.py:18
  34.0 10.4 %collective-permute-start.9 = (bf16[33,32,128]{2,1,0:T(8,128)(2,1)S(1)}, bf16[33,32,128]{2,1,0:T(8,128)(2,1)S(1)}, u32[]{:S(2)}, u32[]{:S(2)}) collective-permute-start(bf16[33,32,128]{2,1,0:T(8,128)(2,1)S(1)} %get-tuple-element.37), channel_id=1, source_target_pairs={{1,0},{2,1},{3,2},{4,3},{5,4},{6,5},{7,6},{8,7},{9,8},{10,9},{11,1... | collective-permute-start | bytes 811016 | tf_op jit(solution)/shard_map/ppermute | solution.py:18
  45.0 5.2 %collective-permute-start.12 = (bf16[48,256]{1,0:T(8,128)(2,1)S(1)}, bf16[48,256]{1,0:T(8,128)(2,1)S(1)}, u32[]{:S(2)}, u32[]{:S(2)}) collective-permute-start(bf16[48,256]{1,0:T(8,128)(2,1)S(1)} %get-tuple-element.41), channel_id=1, source_target_pairs={{0,3},{1,2},{2,1},{3,0},{4,7},{5,6},{6,5},{7,4},{8,11},{9,10},{10,... | collective-permute-start | bytes 73736 | tf_op jit(solution)/shard_map/ppermute | solution.py:56
  48.7 3.8 %collective-permute-start.11 = (bf16[48,256]{1,0:T(8,128)(2,1)S(1)}, bf16[48,256]{1,0:T(8,128)(2,1)S(1)}, u32[]{:S(2)}, u32[]{:S(2)}) collective-permute-start(bf16[48,256]{1,0:T(8,128)(2,1)S(1)} %get-tuple-element.41), channel_id=1, source_target_pairs={{0,2},{1,3},{2,0},{3,1},{4,6},{5,7},{6,4},{7,5},{8,10},{9,11},{10,... | collective-permute-start | bytes 73736 | tf_op jit(solution)/shard_map/ppermute | solution.py:56
  49.4 3.1 %collective-permute-start.10 = (bf16[48,256]{1,0:T(8,128)(2,1)S(1)}, bf16[48,256]{1,0:T(8,128)(2,1)S(1)}, u32[]{:S(2)}, u32[]{:S(2)}) collective-permute-start(bf16[48,256]{1,0:T(8,128)(2,1)S(1)} %get-tuple-element.41), channel_id=1, source_target_pairs={{0,1},{1,0},{2,3},{3,2},{4,5},{5,4},{6,7},{7,6},{8,9},{9,8},{10,11... | collective-permute-start | bytes 73736 | tf_op jit(solution)/shard_map/ppermute | solution.py:56
  52.6 5.8 %collective-permute-start.15 = (bf16[48,256]{1,0:T(8,128)(2,1)S(1)}, bf16[48,256]{1,0:T(8,128)(2,1)S(1)}, u32[]{:S(2)}, u32[]{:S(2)}) collective-permute-start(bf16[48,256]{1,0:T(8,128)(2,1)S(1)} %get-tuple-element.43), channel_id=1, source_target_pairs={{0,12},{1,13},{2,14},{3,15},{4,8},{5,9},{6,10},{7,11},{8,4},{9,5},... | collective-permute-start | bytes 73736 | tf_op jit(solution)/shard_map/ppermute | solution.py:56
  53.4 5.4 %collective-permute-start.14 = (bf16[48,256]{1,0:T(8,128)(2,1)S(1)}, bf16[48,256]{1,0:T(8,128)(2,1)S(1)}, u32[]{:S(2)}, u32[]{:S(2)}) collective-permute-start(bf16[48,256]{1,0:T(8,128)(2,1)S(1)} %get-tuple-element.43), channel_id=1, source_target_pairs={{0,8},{1,9},{2,10},{3,11},{4,12},{5,13},{6,14},{7,15},{8,0},{9,1},... | collective-permute-start | bytes 73736 | tf_op jit(solution)/shard_map/ppermute | solution.py:56
  56.4 3.8 %collective-permute-start.13 = (bf16[48,256]{1,0:T(8,128)(2,1)S(1)}, bf16[48,256]{1,0:T(8,128)(2,1)S(1)}, u32[]{:S(2)}, u32[]{:S(2)}) collective-permute-start(bf16[48,256]{1,0:T(8,128)(2,1)S(1)} %get-tuple-element.43), channel_id=1, source_target_pairs={{0,4},{1,5},{2,6},{3,7},{4,0},{5,1},{6,2},{7,3},{8,12},{9,13},{10,... | collective-permute-start | bytes 73736 | tf_op jit(solution)/shard_map/ppermute | solution.py:56

commit v5 on v4

--- a/solution.py
+++ b/solution.py
@@ -12,10 +12,18 @@
 MAP_PARTS = 4
 
 
-def shifted(block, axis, distance):
+def shifted(block, axis, distance, parity):
     devices = range(lax.axis_size(axis))
-    route = [(i - distance, i) for i in devices if i - distance in devices]
+    route = [(i - distance, i) for i in devices if i % 2 == parity and i - distance in devices]
     return lax.ppermute(block, axis, route)
+
+
+def swapped(block, axis):
+    return lax.ppermute(block, axis, [(i, i ^ 1) for i in range(lax.axis_size(axis))])
+
+
+def is_even(axis):
+    return lax.rem(lax.axis_index(axis), 2) == 0
 
 
 def write_message(msg_ref, x):
@@ -36,17 +44,17 @@
     return jnp.concatenate([x[:-16], x[-16:-8] + jnp.where(first, rest + pltpu.roll(rest, 4, 0), 0.0)], axis=0)
 
 
-def add_kernel(count, x_ref, *refs):
-    *in_refs, out_ref = refs[:count]
+def add_kernel(count, held, x_ref, *refs):
+    in_refs, (out_ref, *msg_refs) = refs[: count - 1], refs[count - 1 + held :]
     x = x_ref[...]
     for ref in in_refs:
         x = x + read_message(ref)
     out_ref[...] = x
-    for ref in refs[count:]:
+    for ref in msg_refs:
         write_message(ref, x)
 
 
-def total(x, msg, axis):
+def total(x, msg, axis, held=()):
     n = lax.axis_size(axis)
     if n & (n - 1):
         return lax.psum(x, axis)
@@ -55,12 +63,13 @@
         partners = [m * step for m in range(1, 4) if m * step < n]
         got = [lax.ppermute(msg, axis, [(i, i ^ d) for i in range(n)]) for d in partners]
         step *= 4
-        add = functools.partial(add_kernel, len(got) + 1)
-        ins = [pltpu.VMEM] * (len(got) + 1)
+        add = functools.partial(add_kernel, len(got) + 1, len(held))
+        ins = [pltpu.VMEM] * (len(got) + 1) + [pl.ANY] * len(held)
         if step < n:
-            x, msg = call(add, ins, [(x.shape, F32), (msg.shape, BF16)])(x, *got)
+            x, msg = call(add, ins, [(x.shape, F32), (msg.shape, BF16)])(x, *got, *held)
         else:
-            x = call(add, ins, [(x.shape, F32)])(x, *got)
+            x = call(add, ins, [(x.shape, F32)])(x, *got, *held)
+        held = ()
     return x
 
 
@@ -127,11 +136,8 @@
 
 
 def direction_kernel(
-    rows, sums_ref, inner_ref, terms_ref, probes_ref, map_ref, factor_hbm, dir_ref, msg_ref, product_ref, factor_ref,
-    grad_ref, sem,
+    rows, sums_ref, inner_ref, terms_ref, probes_ref, map_ref, dir_ref, msg_ref, product_ref, grad_ref
 ):
-    copy = pltpu.make_async_copy(factor_hbm, factor_ref, sem)
-    copy.start()
     _, blocks, bs = terms_ref.shape
     count = probes_ref.shape[0]
     gradient_ref, inv_diag_ref = terms_ref.at[0], terms_ref.at[2]
@@ -149,42 +155,81 @@
             msg_ref[c] = direction[:count].astype(BF16)
             grad_ref[c : c + 1] = direction[count : count + 1]
     msg_ref[blocks] = grad_ref[...].astype(BF16)
+
+
+def load_kernel(factor_hbm, after_ref, factor_ref, sem):
+    copy = pltpu.make_async_copy(factor_hbm, factor_ref, sem)
+    copy.start()
     copy.wait()
 
 
+def tall_block(refs, grads, at, tall):
+    probe_rows = refs[at]
+    last = jnp.broadcast_to(grads[pl.ds(at, 1), :], (tall - probe_rows.shape[0], probe_rows.shape[1]))
+    return jnp.concatenate([probe_rows, last.astype(BF16)], axis=0)
+
+
+def own_image_kernel(tall, own_ref, factor_ref, image_ref, again_ref, grad_ref):
+    blocks = factor_ref.shape[0]
+    again_ref[...] = own_ref[...]
+    grad_ref[...] = own_ref[blocks].astype(F32)
+    for b in range(blocks):
+        image_ref[b] = lax.dot_general(
+            tall_block(own_ref, grad_ref, b, tall),
+            factor_ref[b, 0],
+            (((1,), (1,)), ((), ())),
+            preferred_element_type=F32,
+        )
+
+
+def pass_on_kernel(own_ref, far_ref, out_ref):
+    @pl.when(is_even("space"))
+    def _():
+        out_ref[...] = own_ref[...]
+
+    @pl.when(jnp.logical_not(is_even("space")))
+    def _():
+        out_ref[...] = far_ref[...]
+
+
+def join_kernel(back_far_ref, got_ref, out_ref):
+    out_ref[...] = (back_far_ref[...].astype(F32) + got_ref[...].astype(F32)).astype(BF16)
+
+
+def own_back_kernel(rows, image_ref, factor_ref, out_ref):
+    for b in range(factor_ref.shape[0]):
+        out_ref[b] = jnp.dot(image_ref[b], factor_ref[b, 0], preferred_element_type=F32)[:rows]
+
+
 def hessian_kernel(
-    rows, ids_ref, factor_ref, near_ref, far_ref, own_ref, back_far_ref, back_near_ref, back_own_ref, curve_ref,
-    around_ref, around_grad_ref, image_ref, total_ref, grad_ref,
+    rows, ids_ref, factor_ref, own_image_ref, near_ref, far_even_ref, far_odd_ref, own_ref, back_far_ref, back_near_ref,
+    back_own_ref, curve_ref, image_ref, around_ref, around_grad_ref, total_ref, grad_ref,
 ):
     blocks, taps, bs, _ = factor_ref.shape
     count = around_ref.shape[1]
     tall = image_ref.shape[1]
-    for i, ref in enumerate((far_ref, near_ref, own_ref)):
-        around_ref[i * blocks : (i + 1) * blocks] = ref[:blocks]
-        around_grad_ref[i * blocks : (i + 1) * blocks] = ref[blocks].astype(F32)
+    for i, refs in enumerate(((far_even_ref, far_odd_ref), (near_ref,), (own_ref,))):
+        at = slice(i * blocks, (i + 1) * blocks)
+        around_ref[at] = functools.reduce(jnp.add, [ref[:blocks] for ref in refs])
+        around_grad_ref[at] = functools.reduce(jnp.add, [ref[blocks].astype(F32) for ref in refs])
     first = (lax.axis_index("space") - 2) * blocks
     total_ref[...] = jnp.zeros_like(total_ref)
     curve = jnp.zeros((rows, bs), F32)
+    ids = lambda b, k: ids_ref[k - 1, b] - first
+    side_by_side = lambda b: jnp.concatenate([factor_ref[b, k] for k in range(1, taps)], axis=1)
     for b in range(blocks):
-        chosen = []
-        for k in range(taps):
-            at = 2 * blocks + b if k == 0 else ids_ref[k - 1, b] - first
-            last = jnp.broadcast_to(around_grad_ref[pl.ds(at, 1), :], (tall - count, bs)).astype(BF16)
-            chosen.append(jnp.concatenate([around_ref[at], last], axis=0))
-        side_by_side = jnp.concatenate([factor_ref[b, k] for k in range(taps)], axis=1)
-        image = lax.dot_general(
-            jnp.concatenate(chosen, axis=1), side_by_side, (((1,), (1,)), ((), ())), preferred_element_type=F32
+        chosen = [tall_block(around_ref, around_grad_ref, ids(b, k), tall) for k in range(1, taps)]
+        image = own_image_ref[b] + lax.dot_general(
+            jnp.concatenate(chosen, axis=1), side_by_side(b), (((1,), (1,)), ((), ())), preferred_element_type=F32
         )
         rounded = image.astype(BF16)
         image_ref[b] = rounded
         curve += (image * rounded.astype(F32))[:rows]
     curve_ref[...] = curve
     for b in range(blocks):
-        side_by_side = jnp.concatenate([factor_ref[b, k] for k in range(taps)], axis=1)
-        back = jnp.dot(image_ref[b], side_by_side, preferred_element_type=F32)
-        for k in range(taps):
-            at = 2 * blocks + b if k == 0 else ids_ref[k - 1, b] - first
-            total_ref[at] += back[:rows, k * bs : (k + 1) * bs]
+        back = jnp.dot(image_ref[b], side_by_side(b), preferred_element_type=F32)
+        for k in range(1, taps):
+            total_ref[ids(b, k)] += back[:rows, (k - 1) * bs : k * bs]
     for i, ref in enumerate((back_far_ref, back_near_ref)):
         for b in range(blocks):
             ref[b] = total_ref[i * blocks + b, :count].astype(BF16)
@@ -194,13 +239,16 @@
 
 
 def combine_kernel(
-    rows, own_ref, far_ref, near_ref, curve_ref, dir_ref, terms_ref, probes_ref, map_ref, hess_ref, out_ref, msg_ref
+    rows, own_ref, own_back_ref, even_ref, odd_ref, mate_ref, curve_ref, dir_ref, terms_ref, probes_ref, map_ref,
+    hess_ref, out_ref, msg_ref,
 ):
     _, blocks, bs = terms_ref.shape
     count = probes_ref.shape[0]
     lanes = map_ref.shape[1]
     gradient_ref, weights_ref, inv_diag_ref = terms_ref.at[0], terms_ref.at[1], terms_ref.at[2]
-    from_grad = near_ref[blocks].astype(F32) + far_ref[blocks].astype(F32)
+    own_part = jnp.where(is_even("space"), 1.0, 0.0)
+    arrived = lambda c: even_ref[c].astype(F32) + odd_ref[c].astype(F32) + own_part * mate_ref[c].astype(F32)
+    from_grad = arrived(blocks)
     curve = curve_ref[...]
     cross = jnp.zeros((rows, bs), F32)
     square = jnp.zeros((rows, bs), F32)
@@ -210,14 +258,14 @@
         for c in range(b, b + PAIR):
             came = jnp.concatenate(
                 [
-                    near_ref[c].astype(F32) + far_ref[c].astype(F32),
+                    arrived(c),
                     jnp.broadcast_to(from_grad[c : c + 1], (rows - count, bs)),
                 ],
                 axis=0,
             )
             direction = dir_ref[c]
             weighted = weights_ref[c : c + 1] * direction
-            hess = own_ref[c] + came + weighted
+            hess = own_ref[c] + own_back_ref[c] + came + weighted
             hess_ref[c] = hess
             scaled = hess * inv_diag_ref[c : c + 1]
             curve += weighted * direction
@@ -321,31 +369,34 @@
         ],
     )(*map(in_hbm, (by_block(latent), by_block(responses), by_block(prior_diag), probes, inducing_map, inner_inverse)))
     points = (terms, probes, inducing_map)
-    sums = total(partial, msg, "space")
-    direction, rounded, product, factor = call(
-        functools.partial(direction_kernel, rows),
-        [vmem] * 5 + [pl.ANY],
-        [field, packed, sum_shape, (factor.shape, BF16)],
-        [vmem((blocks, bs), F32), pltpu.SemaphoreType.DMA],
-    )(sums, inner_inverse, *points, in_hbm(factor))
-    far = shifted(rounded, "space", 2)
-    near = shifted(rounded, "space", 1)
-    back_far, back_near, back_own, curve = call(
+    factor = call(load_kernel, [pl.ANY] * 2, [(factor.shape, BF16)], [pltpu.SemaphoreType.DMA])(in_hbm(factor), msg)
+    sums = total(partial, msg, "space", (factor,))
+    direction, rounded, product = call(
+        functools.partial(direction_kernel, rows), [vmem] * 5, [field, packed, sum_shape], [vmem((blocks, bs), F32)]
+    )(sums, inner_inverse, *points)
+    far_odd = shifted(rounded, "space", 2, 1)
+    own_image, again = call(
+        functools.partial(own_image_kernel, tall), [vmem] * 2, [((blocks, tall, bs), F32), packed], [vmem((blocks, bs), F32)]
+    )(rounded, factor)
+    far_even = shifted(again, "space", 2, 0)
+    near = swapped(call(pass_on_kernel, [vmem] * 2, [packed])(rounded, far_odd), "space")
+    back_far, back_near, back_own, curve, image = call(
         functools.partial(hessian_kernel, rows),
-        [smem] + [vmem] * 4,
-        [packed, packed, field, ((rows, bs), F32)],
+        [smem] + [vmem] * 6,
+        [packed, packed, field, ((rows, bs), F32), ((blocks, tall, bs), BF16)],
         [
             vmem((3 * blocks, count, bs), BF16),
             vmem((3 * blocks, bs), F32),
-            vmem((blocks, tall, bs), BF16),
             vmem((3 * blocks, rows, bs), F32),
             vmem((blocks, bs), F32),
         ],
-    )(cond_ids.T, factor, near, far, rounded)
-    from_far = shifted(back_far, "space", -2)
-    from_near = shifted(back_near, "space", -1)
-    hess, partial, msg = call(functools.partial(combine_kernel, rows), [vmem] * 8, [field, sum_shape, sum_msg])(
-        back_own, from_far, from_near, curve, direction, *points
+    )(cond_ids.T, factor, own_image, near, far_even, far_odd, rounded)
+    mate = swapped(back_near, "space")
+    from_even = shifted(back_far, "space", -2, 0)
+    from_odd = shifted(call(join_kernel, [vmem] * 2, [packed])(back_far, mate), "space", -2, 1)
+    own_back = call(functools.partial(own_back_kernel, rows), [vmem] * 2, [field])(image, factor)
+    hess, partial, msg = call(functools.partial(combine_kernel, rows), [vmem] * 10, [field, sum_shape, sum_msg])(
+        back_own, own_back, from_even, from_odd, mate, curve, direction, *points
     )
     hess_sums = total(partial, msg, "space")
     whole = ((count + 1, blocks * bs), F32)

time: 62.9 us -> 57.8 us (0.919)
  waiting for transfers between devices: 27.2 us -> 22 us
  Pallas kernels: 11.6 us -> 13 us
  starting transfers between devices: 23 us -> 21.7 us
    ppermute x12, waiting for transfers between devices: 13.4 us -> 10.6 us  [total(): lax.ppermute(msg, axis, [(i, i ^ d) for i in range(n)])]
    ppermute x4, waiting for transfers between devices: 13.8 us -> 11.2 us  [shifted(): return lax.ppermute(block, axis, route)]
    pallas_call x7 -> x12, Pallas kernels: 7.17 us -> 8.59 us  [the longest x1 3.22 us: body(): call(functools.partial(hessian_kernel, rows), [smem] + [vmem] * 6, [packe...]
    ppermute x4, starting transfers between devices: 6.58 us -> 5.38 us  [shifted(): return lax.ppermute(block, axis, route)]
    ppermute x12, starting transfers between devices: 16.4 us -> 15.7 us  [total(): lax.ppermute(msg, axis, [(i, i ^ d) for i in range(n)])]
    ppermute x0 -> x2, starting transfers between devices: none -> 0.65 us  [swapped(): lax.ppermute(block, axis, [(i, i ^ 1) for i in range(lax.axis_size(axis))])]
  transfers between devices with their start and end apart: 16 -> 18, of which waited for: 11 -> 11; matrix products, arithmetic and copies ran while one was open for 0% -> 0% of each run, Pallas kernels for 0% -> 6%
where the time goes in v5:
time: 57.8 us; the launch traced here: 57.5 us
  waiting for transfers between devices  22 us (38%)
  starting transfers between devices  21.7 us (38%)
  Pallas kernels  13 us (22%)
  between operations  0.76 us (1%)
    ppermute x12, starting transfers between devices, total(): lax.ppermute(msg, axis, [(i, i ^ d) for i in range(n)])  15.7 us
    ppermute x4, waiting for transfers between devices, shifted(): return lax.ppermute(block, axis, route)  11.2 us
    ppermute x12, waiting for transfers between devices, total(): lax.ppermute(msg, axis, [(i, i ^ d) for i in range(n)])  10.6 us
    ppermute x4, starting transfers between devices, shifted(): return lax.ppermute(block, axis, route)  5.38 us
    pallas_call x1, Pallas kernels, body(): call(functools.partial(hessian_kernel, rows), [smem] + [vmem] * 6, [packe...  3.22 us
    pallas_call x1, Pallas kernels, body(): call(functools.partial(finish_kernel, rows), [vmem] * 9, [whole] * 3, kee...  2.27 us
    pallas_call x1, Pallas kernels, body(): call(load_kernel, [pl.ANY] * 2, [(factor.shape, BF16)], [pltpu.SemaphoreT...  2.2 us
    pallas_call x1, Pallas kernels, body(): call(functools.partial(project_kernel, rows), [pl.ANY] * 6, [sum_shape, s...  2.17 us
  transfers between devices with their start and end apart: 18, of which 11 were waited for; matrix products, arithmetic and copies ran while one was open for 0% of the time, Pallas kernels for 6%

profile of v5, /device:TPU:0, one launch (start us, length us, event | category | flops | bytes accessed | tf_op | source)
XLA Modules:
  0.0 57.5 jit_solution(10413918125045855375)
XLA Ops:
  0.6 2.2 %shard_map.103 = (f32[40,256]{1,0:T(8,128)S(1)}, bf16[48,256]{1,0:T(8,128)(2,1)S(1)}, f32[3,32,128]{2,1,0:T(8,128)S(1)}, f32[32,4096]{1,0:T(8,128)S(1)}, bf16[40...) custom-call(f32[32,128]{1,0:T(8,128)} %bitcast.5, s32[32,128]{1,0:T(8,128)} %bitcast.6, f32[32,128]{1,0:T(8,128)} %bitcast.7, ...), custom_call_target="tpu_custom_call" | custom-call | tf_op jit(solution)/shard_map/pallas_call | solution.py:353
  2.8 2.4 %collective-permute-start.2 = (bf16[48,256]{1,0:T(8,128)(2,1)S(1)}, bf16[48,256]{1,0:T(8,128)(2,1)S(1)}, u32[]{:S(2)}, u32[]{:S(2)}) collective-permute-start(bf16[48,256]{1,0:T(8,128)(2,1)S(1)} %get-tuple-element.27.after_ref), channel_id=1, source_target_pairs={{0,3},{1,2},{2,1},{3,0},{4,7},{5,6},{6,5},{7,4},{8,11},{9,10},{10,... | collective-permute-start | bytes 73736 | tf_op jit(solution)/shard_map/ppermute | solution.py:64
  5.3 0.6 %collective-permute-start.1 = (bf16[48,256]{1,0:T(8,128)(2,1)S(1)}, bf16[48,256]{1,0:T(8,128)(2,1)S(1)}, u32[]{:S(2)}, u32[]{:S(2)}) collective-permute-start(bf16[48,256]{1,0:T(8,128)(2,1)S(1)} %get-tuple-element.27.after_ref), channel_id=1, source_target_pairs={{0,2},{1,3},{2,0},{3,1},{4,6},{5,7},{6,4},{7,5},{8,10},{9,11},{10,... | collective-permute-start | bytes 73736 | tf_op jit(solution)/shard_map/ppermute | solution.py:64
  5.9 0.0 collective-permute-start
  5.9 2.2 %shard_map.104.refs_3_.factor_ref = bf16[32,4,128,128]{3,2,1,0:T(8,128)(2,1)S(1)} custom-call(bf16[32,4,128,128]{3,2,1,0:T(8,128)(2,1)} %factor_hbm.1, bf16[48,256]{1,0:T(8,128)(2,1)S(1)} %get-tuple-element.27.after_ref), custom_call_target="tpu_custom_call" | custom-call | tf_op jit(solution)/shard_map/pallas_call | solution.py:372
  8.1 0.0 collective-permute-done.2.refs_2_
  8.1 0.9 %collective-permute-done.1.refs_1_ = bf16[48,256]{1,0:T(8,128)(2,1)S(1)} collective-permute-done((bf16[48,256]{1,0:T(8,128)(2,1)S(1)}, bf16[48,256]{1,0:T(8,128)(2,1)S(1)}, u32[]{:S(2)}, u32[]{:S(2)}) %collective-permute-start.1) | collective-permute-done | bytes 24608 | tf_op jit(solution)/shard_map/ppermute | solution.py:64
  9.1 0.0 collective-permute-done.refs_0_
  9.1 3.7 %collective-permute-start.5 = (bf16[48,256]{1,0:T(8,128)(2,1)S(1)}, bf16[48,256]{1,0:T(8,128)(2,1)S(1)}, u32[]{:S(2)}, u32[]{:S(2)}) collective-permute-start(bf16[48,256]{1,0:T(8,128)(2,1)S(1)} %get-tuple-element.29), channel_id=1, source_target_pairs={{0,12},{1,13},{2,14},{3,15},{4,8},{5,9},{6,10},{7,11},{8,4},{9,5},... | collective-permute-start | bytes 73736 | tf_op jit(solution)/shard_map/ppermute | solution.py:64
  12.8 0.0 collective-permute-start.4
  12.8 0.8 %collective-permute-start.3 = (bf16[48,256]{1,0:T(8,128)(2,1)S(1)}, bf16[48,256]{1,0:T(8,128)(2,1)S(1)}, u32[]{:S(2)}, u32[]{:S(2)}) collective-permute-start(bf16[48,256]{1,0:T(8,128)(2,1)S(1)} %get-tuple-element.29), channel_id=1, source_target_pairs={{0,4},{1,5},{2,6},{3,7},{4,0},{5,1},{6,2},{7,3},{8,12},{9,13},{10,... | collective-permute-start | bytes 73736 | tf_op jit(solution)/shard_map/ppermute | solution.py:64
  13.6 1.5 %collective-permute-done.5.refs_2_ = bf16[48,256]{1,0:T(8,128)(2,1)S(1)} collective-permute-done((bf16[48,256]{1,0:T(8,128)(2,1)S(1)}, bf16[48,256]{1,0:T(8,128)(2,1)S(1)}, u32[]{:S(2)}, u32[]{:S(2)}) %collective-permute-start.5) | collective-permute-done | bytes 24608 | tf_op jit(solution)/shard_map/ppermute | solution.py:64
  15.1 2.4 %collective-permute-done.4.refs_1_ = bf16[48,256]{1,0:T(8,128)(2,1)S(1)} collective-permute-done((bf16[48,256]{1,0:T(8,128)(2,1)S(1)}, bf16[48,256]{1,0:T(8,128)(2,1)S(1)}, u32[]{:S(2)}, u32[]{:S(2)}) %collective-permute-start.4) | collective-permute-done | bytes 24608 | tf_op jit(solution)/shard_map/ppermute | solution.py:64
  17.5 0.0 collective-permute-done.3.refs_0_
  17.5 0.0 copy-start
  17.5 1.1 %shard_map.107 = (f32[32,40,128]{2,1,0:T(8,128)S(1)}, bf16[33,32,128]{2,1,0:T(8,128)(2,1)S(1)}, f32[40,256]{1,0:T(8,128)S(1)}) custom-call(f32[40,256]{1,0:T(8,128)S(1)} %shard_map.106.sums_ref, f32[256,256]{1,0:T(8,128)S(1)} %get-tuple-element.30.inner_ref, f32[3,32,128]{2,1,0:T(8,128)S(1)} %get-tuple-element.31.terms_ref, ...), custom_call_target="tpu_custom_call" | custom-call | tf_op jit(solution)/shard_map/pallas_call | solution.py:374
  18.6 0.7 %collective-permute-start.6 = (bf16[33,32,128]{2,1,0:T(8,128)(2,1)S(1)}, bf16[33,32,128]{2,1,0:T(8,128)(2,1)S(1)}, u32[]{:S(2)}, u32[]{:S(2)}) collective-permute-start(bf16[33,32,128]{2,1,0:T(8,128)(2,1)S(1)} %get-tuple-element.35.own_ref), channel_id=1, source_target_pairs={{1,3},{3,5},{5,7},{7,9},{9,11},{11,13},{13,15},{17,19},{19,21},{21... | collective-permute-start | bytes 811016 | tf_op jit(solution)/shard_map/ppermute | solution.py:18
  19.3 0.8 %shard_map.108 = (f32[32,48,128]{2,1,0:T(8,128)S(1)}, bf16[33,32,128]{2,1,0:T(8,128)(2,1)S(1)}) custom-call(bf16[33,32,128]{2,1,0:T(8,128)(2,1)S(1)} %get-tuple-element.35.own_ref, bf16[32,4,128,128]{3,2,1,0:T(8,128)(2,1)S(1)} %shard_map.104.refs_3_.factor_ref), custom_call_target="tpu_custom_call" | custom-call | tf_op jit(solution)/shard_map/pallas_call | solution.py:378
  20.1 2.7 %collective-permute-start.8 = (bf16[33,32,128]{2,1,0:T(8,128)(2,1)S(1)}, bf16[33,32,128]{2,1,0:T(8,128)(2,1)S(1)}, u32[]{:S(2)}, u32[]{:S(2)}) collective-permute-start(bf16[33,32,128]{2,1,0:T(8,128)(2,1)S(1)} %get-tuple-element.37), channel_id=1, source_target_pairs={{0,2},{2,4},{4,6},{6,8},{8,10},{10,12},{12,14},{16,18},{18,20},{20... | collective-permute-start | bytes 811016 | tf_op jit(solution)/shard_map/ppermute | solution.py:18
  22.9 0.0 collective-permute-done.6.far_ref.far_odd_ref
  22.9 0.6 %collective-permute-start.7 = (bf16[33,32,128]{2,1,0:T(8,128)(2,1)S(1)}, bf16[33,32,128]{2,1,0:T(8,128)(2,1)S(1)}, u32[]{:S(2)}, u32[]{:S(2)}) collective-permute-start(bf16[33,32,128]{2,1,0:T(8,128)(2,1)S(1)} %shard_map.109), channel_id=1, source_target_pairs={{0,1},{1,0},{2,3},{3,2},{4,5},{5,4},{6,7},{7,6},{8,9},{9,8},{10,11... | collective-permute-start | bytes 811016 | tf_op jit(solution)/shard_map/ppermute | solution.py:22
  23.5 3.3 %collective-permute-done.8.far_even_ref = bf16[33,32,128]{2,1,0:T(8,128)(2,1)S(1)} collective-permute-done((bf16[33,32,128]{2,1,0:T(8,128)(2,1)S(1)}, bf16[33,32,128]{2,1,0:T(8,128)(2,1)S(1)}, u32[]{:S(2)}, u32[]{:S(2)}) %collective-permute-start.8) | collective-permute-done | bytes 270368 | tf_op jit(solution)/shard_map/ppermute | solution.py:18
  26.8 0.0 collective-permute-done.7.near_ref
  26.8 0.0 copy-done
  26.8 3.2 %shard_map.110 = (bf16[33,32,128]{2,1,0:T(8,128)(2,1)S(1)}, bf16[33,32,128]{2,1,0:T(8,128)(2,1)S(1)}, f32[32,40,128]{2,1,0:T(8,128)S(1)}, f32[40,128]{1,0:T(8,128)S(1)}, bf16[32,48,128]{2,1,0:T(8,128)(2,1)S(1)}) custom-call(s32[3,32]{1,0:T(4,128)S(1)} %bitcast.4, bf16[32,4,128,128]{3,2,1,0:T(8,128)(2,1)S(1)} %shard_map.104.refs_3_.factor_ref, ...), custom_call_target="tpu_custom_call" | custom-call | tf_op jit(solution)/shard_map/pallas_call | solution.py:383
  30.0 0.1 collective-permute-start.10
  30.1 1.3 %collective-permute-start.9 = (bf16[33,32,128]{2,1,0:T(8,128)(2,1)S(1)}, bf16[33,32,128]{2,1,0:T(8,128)(2,1)S(1)}, u32[]{:S(2)}, u32[]{:S(2)}) collective-permute-start(bf16[33,32,128]{2,1,0:T(8,128)(2,1)S(1)} %get-tuple-element.40.back_far_ref), channel_id=1, source_target_pairs={{2,0},{4,2},{6,4},{8,6},{10,8},{12,10},{14,12},{18,16},{20,18},{22... | collective-permute-start | bytes 811016 | tf_op jit(solution)/shard_map/ppermute | solution.py:18
  31.4 0.2 collective-permute-done.10.got_ref.mate_ref
  31.6 0.1 shard_map.112
  31.7 0.7 %collective-permute-start.11 = (bf16[33,32,128]{2,1,0:T(8,128)(2,1)S(1)}, bf16[33,32,128]{2,1,0:T(8,128)(2,1)S(1)}, u32[]{:S(2)}, u32[]{:S(2)}) collective-permute-start(bf16[33,32,128]{2,1,0:T(8,128)(2,1)S(1)} %shard_map.112), channel_id=1, source_target_pairs={{3,1},{5,3},{7,5},{9,7},{11,9},{13,11},{15,13},{19,17},{21,19},{23... | collective-permute-start | bytes 811016 | tf_op jit(solution)/shard_map/ppermute | solution.py:18
  32.4 0.4 shard_map.111.own_back_ref
  32.8 7.8 %collective-permute-done.9.even_ref = bf16[33,32,128]{2,1,0:T(8,128)(2,1)S(1)} collective-permute-done((bf16[33,32,128]{2,1,0:T(8,128)(2,1)S(1)}, bf16[33,32,128]{2,1,0:T(8,128)(2,1)S(1)}, u32[]{:S(2)}, u32[]{:S(2)}) %collective-permute-start.9) | collective-permute-done | bytes 270368 | tf_op jit(solution)/shard_map/ppermute | solution.py:18
  40.7 0.0 collective-permute-done.11.odd_ref
  40.7 0.7 %shard_map.113 = (f32[32,40,128]{2,1,0:T(8,128)S(1)}, f32[40,256]{1,0:T(8,128)S(1)}, bf16[48,256]{1,0:T(8,128)(2,1)S(1)}) custom-call(f32[32,40,128]{2,1,0:T(8,128)S(1)} %get-tuple-element.38.own_ref, f32[32,40,128]{2,1,0:T(8,128)S(1)} %shard_map.111.own_back_ref, bf16[33,32,128]{2,1,0:T(8,128)(2,1)S(1)} %collective-permute-done.9.even_ref, ...), custom_call_target="tpu_custom_call" | custom-call | tf_op jit(solution)/shard_map/pallas_call | solution.py:398
  41.4 3.5 %collective-permute-start.14 = (bf16[48,256]{1,0:T(8,128)(2,1)S(1)}, bf16[48,256]{1,0:T(8,128)(2,1)S(1)}, u32[]{:S(2)}, u32[]{:S(2)}) collective-permute-start(bf16[48,256]{1,0:T(8,128)(2,1)S(1)} %get-tuple-element.45), channel_id=1, source_target_pairs={{0,3},{1,2},{2,1},{3,0},{4,7},{5,6},{6,5},{7,4},{8,11},{9,10},{10,... | collective-permute-start | bytes 73736 | tf_op jit(solution)/shard_map/ppermute | solution.py:64
  44.8 0.0 collective-permute-start.13
  44.8 0.2 collective-permute-start.12
  45.0 1.4 %collective-permute-done.14.refs_2_ = bf16[48,256]{1,0:T(8,128)(2,1)S(1)} collective-permute-done((bf16[48,256]{1,0:T(8,128)(2,1)S(1)}, bf16[48,256]{1,0:T(8,128)(2,1)S(1)}, u32[]{:S(2)}, u32[]{:S(2)}) %collective-permute-start.14) | collective-permute-done | bytes 24608 | tf_op jit(solution)/shard_map/ppermute | solution.py:64
  46.4 2.2 %collective-permute-done.13.refs_1_ = bf16[48,256]{1,0:T(8,128)(2,1)S(1)} collective-permute-done((bf16[48,256]{1,0:T(8,128)(2,1)S(1)}, bf16[48,256]{1,0:T(8,128)(2,1)S(1)}, u32[]{:S(2)}, u32[]{:S(2)}) %collective-permute-start.13) | collective-permute-done | bytes 24608 | tf_op jit(solution)/shard_map/ppermute | solution.py:64
  48.6 0.0 collective-permute-done.12.refs_0_
  48.7 1.0 %collective-permute-start.17 = (bf16[48,256]{1,0:T(8,128)(2,1)S(1)}, bf16[48,256]{1,0:T(8,128)(2,1)S(1)}, u32[]{:S(2)}, u32[]{:S(2)}) collective-permute-start(bf16[48,256]{1,0:T(8,128)(2,1)S(1)} %get-tuple-element.47), channel_id=1, source_target_pairs={{0,12},{1,13},{2,14},{3,15},{4,8},{5,9},{6,10},{7,11},{8,4},{9,5},... | collective-permute-start | bytes 73736 | tf_op jit(solution)/shard_map/ppermute | solution.py:64
  49.6 1.8 %collective-permute-start.16 = (bf16[48,256]{1,0:T(8,128)(2,1)S(1)}, bf16[48,256]{1,0:T(8,128)(2,1)S(1)}, u32[]{:S(2)}, u32[]{:S(2)}) collective-permute-start(bf16[48,256]{1,0:T(8,128)(2,1)S(1)} %get-tuple-element.47), channel_id=1, source_target_pairs={{0,8},{1,9},{2,10},{3,11},{4,12},{5,13},{6,14},{7,15},{8,0},{9,1},... | collective-permute-start | bytes 73736 | tf_op jit(solution)/shard_map/ppermute | solution.py:64
  51.4 1.7 %collective-permute-start.15 = (bf16[48,256]{1,0:T(8,128)(2,1)S(1)}, bf16[48,256]{1,0:T(8,128)(2,1)S(1)}, u32[]{:S(2)}, u32[]{:S(2)}) collective-permute-start(bf16[48,256]{1,0:T(8,128)(2,1)S(1)} %get-tuple-element.47), channel_id=1, source_target_pairs={{0,4},{1,5},{2,6},{3,7},{4,0},{5,1},{6,2},{7,3},{8,12},{9,13},{10,... | collective-permute-start | bytes 73736 | tf_op jit(solution)/shard_map/ppermute | solution.py:64
  53.1 1.3 %collective-permute-done.17.refs_2_ = bf16[48,256]{1,0:T(8,128)(2,1)S(1)} collective-permute-done((bf16[48,256]{1,0:T(8,128)(2,1)S(1)}, bf16[48,256]{1,0:T(8,128)(2,1)S(1)}, u32[]{:S(2)}, u32[]{:S(2)}) %collective-permute-start.17) | collective-permute-done | bytes 24608 | tf_op jit(solution)/shard_map/ppermute | solution.py:64
  54.5 0.2 collective-permute-done.16.refs_1_
  54.6 0.6 %collective-permute-done.15.refs_0_ = bf16[48,256]{1,0:T(8,128)(2,1)S(1)} collective-permute-done((bf16[48,256]{1,0:T(8,128)(2,1)S(1)}, bf16[48,256]{1,0:T(8,128)(2,1)S(1)}, u32[]{:S(2)}, u32[]{:S(2)}) %collective-permute-start.15) | collective-permute-done | bytes 24608 | tf_op jit(solution)/shard_map/ppermute | solution.py:64
  55.2 2.3 %shard_map.116 = (f32[33,4096]{1,0:T(8,128)}, f32[33,4096]{1,0:T(8,128)}, f32[33,4096]{1,0:T(8,128)}) custom-call(f32[40,256]{1,0:T(8,128)S(1)} %shard_map.106.sums_ref, f32[40,256]{1,0:T(8,128)S(1)} %get-tuple-element.34.product_ref, f32[40,256]{1,0:T(8,128)S(1)} %shard_map.115.hess_sums_ref, f32[256,256]{1,0:T(8,128)S(1)} %get-tuple-element.30.inner_ref, ...), custom_call_target="tpu_custom_call" | custom-call | tf_op jit(solution)/shard_map/pallas_call | solution.py:403
  (5 shorter events, 0.1 us)
Async XLA Ops:
  2.8 5.3 %collective-permute-start.2 = (bf16[48,256]{1,0:T(8,128)(2,1)S(1)}, bf16[48,256]{1,0:T(8,128)(2,1)S(1)}, u32[]{:S(2)}, u32[]{:S(2)}) collective-permute-start(bf16[48,256]{1,0:T(8,128)(2,1)S(1)} %get-tuple-element.27.after_ref), channel_id=1, source_target_pairs={{0,3},{1,2},{2,1},{3,0},{4,7},{5,6},{6,5},{7,4},{8,11},{9,10},{10,... | collective-permute-start | bytes 73736 | tf_op jit(solution)/shard_map/ppermute | solution.py:64
  5.3 3.8 %collective-permute-start.1 = (bf16[48,256]{1,0:T(8,128)(2,1)S(1)}, bf16[48,256]{1,0:T(8,128)(2,1)S(1)}, u32[]{:S(2)}, u32[]{:S(2)}) collective-permute-start(bf16[48,256]{1,0:T(8,128)(2,1)S(1)} %get-tuple-element.27.after_ref), channel_id=1, source_target_pairs={{0,2},{1,3},{2,0},{3,1},{4,6},{5,7},{6,4},{7,5},{8,10},{9,11},{10,... | collective-permute-start | bytes 73736 | tf_op jit(solution)/shard_map/ppermute | solution.py:64
  5.9 3.2 %collective-permute-start = (bf16[48,256]{1,0:T(8,128)(2,1)S(1)}, bf16[48,256]{1,0:T(8,128)(2,1)S(1)}, u32[]{:S(2)}, u32[]{:S(2)}) collective-permute-start(bf16[48,256]{1,0:T(8,128)(2,1)S(1)} %get-tuple-element.27.after_ref), channel_id=1, source_target_pairs={{0,1},{1,0},{2,3},{3,2},{4,5},{5,4},{6,7},{7,6},{8,9},{9,8},{10,11... | collective-permute-start | bytes 73736 | tf_op jit(solution)/shard_map/ppermute | solution.py:64
  9.1 5.9 %collective-permute-start.5 = (bf16[48,256]{1,0:T(8,128)(2,1)S(1)}, bf16[48,256]{1,0:T(8,128)(2,1)S(1)}, u32[]{:S(2)}, u32[]{:S(2)}) collective-permute-start(bf16[48,256]{1,0:T(8,128)(2,1)S(1)} %get-tuple-element.29), channel_id=1, source_target_pairs={{0,12},{1,13},{2,14},{3,15},{4,8},{5,9},{6,10},{7,11},{8,4},{9,5},... | collective-permute-start | bytes 73736 | tf_op jit(solution)/shard_map/ppermute | solution.py:64
  12.8 4.7 %collective-permute-start.4 = (bf16[48,256]{1,0:T(8,128)(2,1)S(1)}, bf16[48,256]{1,0:T(8,128)(2,1)S(1)}, u32[]{:S(2)}, u32[]{:S(2)}) collective-permute-start(bf16[48,256]{1,0:T(8,128)(2,1)S(1)} %get-tuple-element.29), channel_id=1, source_target_pairs={{0,8},{1,9},{2,10},{3,11},{4,12},{5,13},{6,14},{7,15},{8,0},{9,1},... | collective-permute-start | bytes 73736 | tf_op jit(solution)/shard_map/ppermute | solution.py:64
  12.8 4.7 %collective-permute-start.3 = (bf16[48,256]{1,0:T(8,128)(2,1)S(1)}, bf16[48,256]{1,0:T(8,128)(2,1)S(1)}, u32[]{:S(2)}, u32[]{:S(2)}) collective-permute-start(bf16[48,256]{1,0:T(8,128)(2,1)S(1)} %get-tuple-element.29), channel_id=1, source_target_pairs={{0,4},{1,5},{2,6},{3,7},{4,0},{5,1},{6,2},{7,3},{8,12},{9,13},{10,... | collective-permute-start | bytes 73736 | tf_op jit(solution)/shard_map/ppermute | solution.py:64
  17.5 9.3 %copy-start = (s32[32,3]{0,1:T(4,128)S(1)}, s32[32,3]{0,1:T(4,128)}, u32[]{:S(2)}) copy-start(s32[32,3]{0,1:T(4,128)} %param.13) | copy-start | bytes 1156
  18.6 4.3 %collective-permute-start.6 = (bf16[33,32,128]{2,1,0:T(8,128)(2,1)S(1)}, bf16[33,32,128]{2,1,0:T(8,128)(2,1)S(1)}, u32[]{:S(2)}, u32[]{:S(2)}) collective-permute-start(bf16[33,32,128]{2,1,0:T(8,128)(2,1)S(1)} %get-tuple-element.35.own_ref), channel_id=1, source_target_pairs={{1,3},{3,5},{5,7},{7,9},{9,11},{11,13},{13,15},{17,19},{19,21},{21... | collective-permute-start | bytes 811016 | tf_op jit(solution)/shard_map/ppermute | solution.py:18
  20.1 6.7 %collective-permute-start.8 = (bf16[33,32,128]{2,1,0:T(8,128)(2,1)S(1)}, bf16[33,32,128]{2,1,0:T(8,128)(2,1)S(1)}, u32[]{:S(2)}, u32[]{:S(2)}) collective-permute-start(bf16[33,32,128]{2,1,0:T(8,128)(2,1)S(1)} %get-tuple-element.37), channel_id=1, source_target_pairs={{0,2},{2,4},{4,6},{6,8},{8,10},{10,12},{12,14},{16,18},{18,20},{20... | collective-permute-start | bytes 811016 | tf_op jit(solution)/shard_map/ppermute | solution.py:18
  22.9 3.9 %collective-permute-start.7 = (bf16[33,32,128]{2,1,0:T(8,128)(2,1)S(1)}, bf16[33,32,128]{2,1,0:T(8,128)(2,1)S(1)}, u32[]{:S(2)}, u32[]{:S(2)}) collective-permute-start(bf16[33,32,128]{2,1,0:T(8,128)(2,1)S(1)} %shard_map.109), channel_id=1, source_target_pairs={{0,1},{1,0},{2,3},{3,2},{4,5},{5,4},{6,7},{7,6},{8,9},{9,8},{10,11... | collective-permute-start | bytes 811016 | tf_op jit(solution)/shard_map/ppermute | solution.py:22
  30.0 1.6 %collective-permute-start.10 = (bf16[33,32,128]{2,1,0:T(8,128)(2,1)S(1)}, bf16[33,32,128]{2,1,0:T(8,128)(2,1)S(1)}, u32[]{:S(2)}, u32[]{:S(2)}) collective-permute-start(bf16[33,32,128]{2,1,0:T(8,128)(2,1)S(1)} %get-tuple-element.41), channel_id=1, source_target_pairs={{0,1},{1,0},{2,3},{3,2},{4,5},{5,4},{6,7},{7,6},{8,9},{9,8},{10,11... | collective-permute-start | bytes 811016 | tf_op jit(solution)/shard_map/ppermute | solution.py:22
  30.1 10.5 %collective-permute-start.9 = (bf16[33,32,128]{2,1,0:T(8,128)(2,1)S(1)}, bf16[33,32,128]{2,1,0:T(8,128)(2,1)S(1)}, u32[]{:S(2)}, u32[]{:S(2)}) collective-permute-start(bf16[33,32,128]{2,1,0:T(8,128)(2,1)S(1)} %get-tuple-element.40.back_far_ref), channel_id=1, source_target_pairs={{2,0},{4,2},{6,4},{8,6},{10,8},{12,10},{14,12},{18,16},{20,18},{22... | collective-permute-start | bytes 811016 | tf_op jit(solution)/shard_map/ppermute | solution.py:18
  31.7 8.9 %collective-permute-start.11 = (bf16[33,32,128]{2,1,0:T(8,128)(2,1)S(1)}, bf16[33,32,128]{2,1,0:T(8,128)(2,1)S(1)}, u32[]{:S(2)}, u32[]{:S(2)}) collective-permute-start(bf16[33,32,128]{2,1,0:T(8,128)(2,1)S(1)} %shard_map.112), channel_id=1, source_target_pairs={{3,1},{5,3},{7,5},{9,7},{11,9},{13,11},{15,13},{19,17},{21,19},{23... | collective-permute-start | bytes 811016 | tf_op jit(solution)/shard_map/ppermute | solution.py:18
  41.4 5.1 %collective-permute-start.14 = (bf16[48,256]{1,0:T(8,128)(2,1)S(1)}, bf16[48,256]{1,0:T(8,128)(2,1)S(1)}, u32[]{:S(2)}, u32[]{:S(2)}) collective-permute-start(bf16[48,256]{1,0:T(8,128)(2,1)S(1)} %get-tuple-element.45), channel_id=1, source_target_pairs={{0,3},{1,2},{2,1},{3,0},{4,7},{5,6},{6,5},{7,4},{8,11},{9,10},{10,... | collective-permute-start | bytes 73736 | tf_op jit(solution)/shard_map/ppermute | solution.py:64
  44.8 3.8 %collective-permute-start.13 = (bf16[48,256]{1,0:T(8,128)(2,1)S(1)}, bf16[48,256]{1,0:T(8,128)(2,1)S(1)}, u32[]{:S(2)}, u32[]{:S(2)}) collective-permute-start(bf16[48,256]{1,0:T(8,128)(2,1)S(1)} %get-tuple-element.45), channel_id=1, source_target_pairs={{0,2},{1,3},{2,0},{3,1},{4,6},{5,7},{6,4},{7,5},{8,10},{9,11},{10,... | collective-permute-start | bytes 73736 | tf_op jit(solution)/shard_map/ppermute | solution.py:64
  44.8 3.8 %collective-permute-start.12 = (bf16[48,256]{1,0:T(8,128)(2,1)S(1)}, bf16[48,256]{1,0:T(8,128)(2,1)S(1)}, u32[]{:S(2)}, u32[]{:S(2)}) collective-permute-start(bf16[48,256]{1,0:T(8,128)(2,1)S(1)} %get-tuple-element.45), channel_id=1, source_target_pairs={{0,1},{1,0},{2,3},{3,2},{4,5},{5,4},{6,7},{7,6},{8,9},{9,8},{10,11... | collective-permute-start | bytes 73736 | tf_op jit(solution)/shard_map/ppermute | solution.py:64
  48.7 5.8 %collective-permute-start.17 = (bf16[48,256]{1,0:T(8,128)(2,1)S(1)}, bf16[48,256]{1,0:T(8,128)(2,1)S(1)}, u32[]{:S(2)}, u32[]{:S(2)}) collective-permute-start(bf16[48,256]{1,0:T(8,128)(2,1)S(1)} %get-tuple-element.47), channel_id=1, source_target_pairs={{0,12},{1,13},{2,14},{3,15},{4,8},{5,9},{6,10},{7,11},{8,4},{9,5},... | collective-permute-start | bytes 73736 | tf_op jit(solution)/shard_map/ppermute | solution.py:64
  49.6 5.0 %collective-permute-start.16 = (bf16[48,256]{1,0:T(8,128)(2,1)S(1)}, bf16[48,256]{1,0:T(8,128)(2,1)S(1)}, u32[]{:S(2)}, u32[]{:S(2)}) collective-permute-start(bf16[48,256]{1,0:T(8,128)(2,1)S(1)} %get-tuple-element.47), channel_id=1, source_target_pairs={{0,8},{1,9},{2,10},{3,11},{4,12},{5,13},{6,14},{7,15},{8,0},{9,1},... | collective-permute-start | bytes 73736 | tf_op jit(solution)/shard_map/ppermute | solution.py:64
  51.4 3.8 %collective-permute-start.15 = (bf16[48,256]{1,0:T(8,128)(2,1)S(1)}, bf16[48,256]{1,0:T(8,128)(2,1)S(1)}, u32[]{:S(2)}, u32[]{:S(2)}) collective-permute-start(bf16[48,256]{1,0:T(8,128)(2,1)S(1)} %get-tuple-element.47), channel_id=1, source_target_pairs={{0,4},{1,5},{2,6},{3,7},{4,0},{5,1},{6,2},{7,3},{8,12},{9,13},{10,... | collective-permute-start | bytes 73736 | tf_op jit(solution)/shard_map/ppermute | solution.py:64

commit v6 on v5

v6 whole, which is shorter than its diff:
```python
import functools

import jax
import jax.numpy as jnp
from jax import lax
from jax.experimental import pallas as pl
from jax.experimental.pallas import tpu as pltpu
from jax.sharding import PartitionSpec as P

F32, BF16 = jnp.float32, jnp.bfloat16
PAIR = 2
MAP_PARTS = 4
OUT_PARTS = 4


def shifted(block, axis, distance, parity):
    devices = range(lax.axis_size(axis))
    route = [(i - distance, i) for i in devices if i % 2 == parity and i - distance in devices]
    return lax.ppermute(block, axis, route)


def swapped(block, axis):
    return lax.ppermute(block, axis, [(i, i ^ 1) for i in range(lax.axis_size(axis))])


def is_even(axis):
    return lax.rem(lax.axis_index(axis), 2) == 0


def write_message(msg_ref, x):
    top, half = x.shape[0] - 8, x.shape[1] // 2
    value, beside = x[top:, :half], x[top:, half:]
    high = value.astype(BF16).astype(F32)
    middle = (value - high).astype(BF16).astype(F32)
    low = value - high - middle
    row = lax.broadcasted_iota(jnp.int32, value.shape, 0)
    left = jnp.where(row < 4, high, pltpu.roll(low, 3, 0))
    right = jnp.where(row < 1, beside, middle)
    msg_ref[...] = jnp.concatenate([x[:top], jnp.concatenate([left, right], axis=1)], axis=0).astype(BF16)


def read_message(msg_ref):
    x = msg_ref[...].astype(F32)
    top, half = x.shape[0] - 8, x.shape[1] // 2
    left, right = x[top:, :half], x[top:, half:]
    row = lax.broadcasted_iota(jnp.int32, left.shape, 0)
    left = jnp.where(row < 1, left, left + right + pltpu.roll(left, 5, 0))
    return jnp.concatenate([x[:top], jnp.concatenate([left, right], axis=1)], axis=0)


def add_kernel(count, held, x_ref, *refs):
    in_refs, (out_ref, *msg_refs) = refs[: count - 1], refs[count - 1 + held :]
    x = x_ref[...]
    for ref in in_refs:
        x = x + read_message(ref)
    out_ref[...] = x
    for ref in msg_refs:
        write_message(ref, x)


def total(x, msg, axis, beside=()):
    n = lax.axis_size(axis)
    made = ()
    if n & (n - 1):
        for work in beside:
            made = work(msg, *made)
        return lax.psum(x, axis), made
    step = 1
    while step < n:
        partners = [m * step for m in range(1, 4) if m * step < n]
        got = [lax.ppermute(msg, axis, [(i, i ^ d) for i in range(n)]) for d in partners]
        step *= 4
        last = step >= n
        held = ()
        while beside and (last or not held):
            work, *beside = beside
            made = held = work(msg, *made)
        add = functools.partial(add_kernel, len(got) + 1, len(held))
        ins = [pltpu.VMEM] * (len(got) + 1) + [pl.ANY] * len(held)
        outs = [(x.shape, F32)] + [(msg.shape, BF16)] * (not last)
        x, *rest = jax.tree.leaves(call(add, ins, outs)(x, *got, *held))
        msg = rest[0] if rest else None
    return x, made


def eye(rows, lanes):
    return lax.broadcasted_iota(jnp.int32, (rows, lanes), 0) == lax.broadcasted_iota(jnp.int32, (rows, lanes), 1)


def as_row(column, lanes):
    return jnp.sum(jnp.where(eye(column.shape[0], lanes), column, 0.0), axis=0, keepdims=True)


def as_column(row, rows):
    return jnp.sum(jnp.where(eye(rows, row.shape[1]), row, 0.0), axis=1, keepdims=True)


def project_kernel(
    latent_hbm, responses_hbm, prior_hbm, probes_hbm, map_hbm, out_ref, msg_ref, terms_ref, field_ref, map_ref, latent_ref,
    responses_ref, prior_ref, probes_ref, sems,
):
    blocks, bs = latent_ref.shape
    rows = out_ref.shape[0]
    count = probes_ref.shape[0]
    part = map_ref.shape[0] // MAP_PARTS
    cut = lambda ref, i: ref.at[i * part : (i + 1) * part]
    pairs = [(latent_hbm, latent_ref), (responses_hbm, responses_ref), (prior_hbm, prior_ref), (probes_hbm, probes_ref)]
    pairs += [(cut(map_hbm, i), cut(map_ref, i)) for i in range(MAP_PARTS)]
    copies = [pltpu.make_async_copy(a, b, sems.at[i]) for i, (a, b) in enumerate(pairs)]
    for copy in copies:
        copy.start()
    for copy in copies[:3]:
        copy.wait()
    probability = 1.0 / (1.0 + jnp.exp(-latent_ref[...]))
    weights = probability * (1.0 - probability)
    gradient = responses_ref[...].astype(F32) - probability
    inv_diag = 1.0 / (weights + prior_ref[...])
    terms_ref[0] = weights
    terms_ref[1] = inv_diag
    copies[3].wait()
    energy = jnp.zeros((rows, bs), F32)
    scaled = []
    for b in range(blocks):
        at = slice(b * bs, (b + 1) * bs)
        last = jnp.broadcast_to(gradient[b : b + 1], (rows - count, bs))
        field = pltpu.roll(jnp.concatenate([probes_ref[:, at], last], axis=0), 1, 0)
        field_ref[b] = field
        scaled.append(field * inv_diag[b : b + 1])
        energy += field * scaled[-1]
    summed = jnp.zeros(out_ref.shape, F32)
    for b in range(0, blocks, PAIR):
        if b * bs % part == 0:
            copies[4 + b * bs // part].wait()
        both = jnp.concatenate([scaled[b + i].astype(BF16) for i in range(PAIR)], axis=1)
        summed += jnp.dot(both, map_ref[b * bs : (b + PAIR) * bs], preferred_element_type=F32)
    out_ref[...] = summed
    out_ref[count + 1 : count + 2] = as_row(jnp.sum(energy, axis=1, keepdims=True), out_ref.shape[1])
    write_message(msg_ref, out_ref[...])


def direction_kernel(sums_ref, inner_ref, terms_ref, field_ref, map_ref, dir_ref, msg_ref, product_ref, last_ref):
    blocks, _, bs = field_ref.shape
    count = msg_ref.shape[1]
    inv_diag_ref = terms_ref.at[1]
    product = jnp.dot(sums_ref[...], inner_ref[...], precision=lax.Precision.HIGH)
    product_ref[...] = product
    coeffs = product.astype(BF16)
    for b in range(0, blocks, PAIR):
        correction = lax.dot_general(
            coeffs, map_ref[b * bs : (b + PAIR) * bs], (((1,), (1,)), ((), ())), preferred_element_type=F32
        )
        for c in range(b, b + PAIR):
            direction = (field_ref[c] + correction[:, (c - b) * bs : (c - b + 1) * bs]) * inv_diag_ref[c : c + 1]
            dir_ref[c] = direction
            msg_ref[c] = direction[:count].astype(BF16)
            last_ref[c : c + 1] = direction[count : count + 1]
    msg_ref[blocks] = last_ref[...].astype(BF16)


def load_kernel(factor_hbm, inner_hbm, after_ref, factor_ref, inner_ref, sems):
    copies = [
        pltpu.make_async_copy(factor_hbm, factor_ref, sems.at[0]),
        pltpu.make_async_copy(inner_hbm, inner_ref, sems.at[1]),
    ]
    for copy in copies:
        copy.start()
    for copy in copies:
        copy.wait()


def turn_kernel(factor_ref, after_ref, turned_ref):
    blocks, taps, bs, _ = factor_ref.shape
    for b in range(blocks):
        for k in range(taps):
            turned_ref[b, k * bs : (k + 1) * bs] = factor_ref[b, k].T


def tall_block(refs, lasts, at, tall):
    most = refs[at]
    last = jnp.broadcast_to(lasts[pl.ds(at, 1), :], (tall - most.shape[0], most.shape[1]))
    return jnp.concatenate([most, last.astype(BF16)], axis=0)


def own_image_kernel(tall, own_ref, turned_ref, image_ref, again_ref, zeros_ref, last_ref):
    blocks, bs = last_ref.shape
    again_ref[...] = own_ref[...]
    zeros_ref[...] = jnp.zeros_like(zeros_ref)
    last_ref[...] = own_ref[blocks].astype(F32)
    for b in range(blocks):
        image_ref[b] = jnp.dot(tall_block(own_ref, last_ref, b, tall), turned_ref[b, :bs], preferred_element_type=F32)


def pass_on_kernel(own_ref, far_ref, out_ref):
    @pl.when(is_even("space"))
    def _():
        out_ref[...] = own_ref[...]

    @pl.when(jnp.logical_not(is_even("space")))
    def _():
        out_ref[...] = far_ref[...]


def join_kernel(back_far_ref, got_ref, out_ref):
    out_ref[...] = (back_far_ref[...].astype(F32) + got_ref[...].astype(F32)).astype(BF16)


def own_back_kernel(rows, image_ref, factor_ref, out_ref):
    for b in range(factor_ref.shape[0]):
        out_ref[b] = jnp.dot(image_ref[b], factor_ref[b, 0], preferred_element_type=F32)[:rows]


def hessian_kernel(
    rows, ids_ref, factor_ref, turned_ref, own_image_ref, near_ref, far_even_ref, far_odd_ref, own_ref, zeros_ref,
    back_far_ref, back_near_ref, total_ref, curve_ref, image_ref, around_ref, around_last_ref, last_ref,
):
    blocks, taps, bs, _ = factor_ref.shape
    count = around_ref.shape[1]
    tall = image_ref.shape[1]
    for i, refs in enumerate(((far_even_ref, far_odd_ref), (near_ref,), (own_ref,))):
        at = slice(i * blocks, (i + 1) * blocks)
        around_ref[at] = functools.reduce(jnp.add, [ref[:blocks] for ref in refs])
        around_last_ref[at] = functools.reduce(jnp.add, [ref[blocks].astype(F32) for ref in refs])
    first = (lax.axis_index("space") - 2) * blocks
    curve = jnp.zeros((rows, bs), F32)
    ids = lambda b, k: ids_ref[k - 1, b] - first
    side_by_side = lambda b: jnp.concatenate([factor_ref[b, k] for k in range(1, taps)], axis=1)
    for b in range(blocks):
        chosen = [tall_block(around_ref, around_last_ref, ids(b, k), tall) for k in range(1, taps)]
        image = own_image_ref[b] + jnp.dot(
            jnp.concatenate(chosen, axis=1), turned_ref[b, bs:], preferred_element_type=F32
        )
        rounded = image.astype(BF16)
        image_ref[b] = rounded
        curve += (image * rounded.astype(F32))[:rows]
    curve_ref[...] = curve
    for b in range(blocks):
        back = jnp.dot(image_ref[b], side_by_side(b), preferred_element_type=F32)
        for k in range(1, taps):
            total_ref[ids(b, k)] += back[:rows, (k - 1) * bs : k * bs]
    for i, ref in enumerate((back_far_ref, back_near_ref)):
        for b in range(blocks):
            ref[b] = total_ref[i * blocks + b, :count].astype(BF16)
            last_ref[b : b + 1] = total_ref[i * blocks + b, count : count + 1]
        ref[blocks] = last_ref[...].astype(BF16)


def combine_kernel(
    own_ref, own_back_ref, even_ref, odd_ref, mate_ref, curve_ref, dir_ref, terms_ref, field_ref, map_ref, hess_ref,
    out_ref, msg_ref,
):
    blocks, rows, bs = field_ref.shape
    count = mate_ref.shape[1]
    weights_ref, inv_diag_ref = terms_ref.at[0], terms_ref.at[1]
    own_part = jnp.where(is_even("space"), 1.0, 0.0)
    arrived = lambda c: even_ref[c].astype(F32) + odd_ref[c].astype(F32) + own_part * mate_ref[c].astype(F32)
    from_last = arrived(blocks)
    curve = curve_ref[...]
    cross = jnp.zeros((rows, bs), F32)
    square = jnp.zeros((rows, bs), F32)
    summed = jnp.zeros(out_ref.shape, F32)
    for b in range(0, blocks, PAIR):
        parts = []
        for c in range(b, b + PAIR):
            last = jnp.broadcast_to(from_last[c : c + 1], (rows - count, bs))
            direction = dir_ref[c]
            weighted = weights_ref[c : c + 1] * direction
            hess = own_ref[2 * blocks + c] + own_back_ref[c] + jnp.concatenate([arrived(c), last], axis=0) + weighted
            hess_ref[c] = hess
            scaled = hess * inv_diag_ref[c : c + 1]
            curve += weighted * direction
            cross += field_ref[c] * scaled
            square += hess * scaled
            parts.append(scaled.astype(BF16))
        summed += jnp.dot(
            jnp.concatenate(parts, axis=1), map_ref[b * bs : (b + PAIR) * bs], preferred_element_type=F32
        )
    out_ref[...] = summed
    for i, acc in enumerate((curve, cross, square)):
        out_ref[count + 1 + i : count + 2 + i] = as_row(jnp.sum(acc, axis=1, keepdims=True), out_ref.shape[1])
    write_message(msg_ref, out_ref[...])


def finish_kernel(
    sums_ref, product_ref, hess_sums_ref, inner_ref, dir_ref, hess_ref, terms_ref, field_ref, map_ref, solution_hbm,
    residual_hbm, next_hbm, solution_ref, residual_ref, next_ref, sems,
):
    blocks, rows, bs = field_ref.shape
    whole = solution_ref.shape[0]
    inv_diag_ref = terms_ref.at[1]
    sums, product, hess_sums = sums_ref[...], product_ref[...], hess_sums_ref[...]
    column = lambda x, i: as_column(x[whole + i : whole + i + 1], rows)
    coeffs = product.astype(BF16)
    plain = column(sums, 0)
    energy = plain + jnp.sum(coeffs.astype(F32) * sums, axis=1, keepdims=True)
    step = energy / column(hess_sums, 0)
    left = sums - step * hess_sums
    hess_product = jnp.dot(hess_sums, inner_ref[...], precision=lax.Precision.HIGH)
    coeffs = (product - step * hess_product).astype(BF16)
    plain_next = plain - 2.0 * step * column(hess_sums, 1) + step * step * column(hess_sums, 2)
    energy_next = plain_next + jnp.sum(coeffs.astype(F32) * left, axis=1, keepdims=True)
    ratio = energy_next / energy
    part = blocks // OUT_PARTS
    copies = []

    def send(i, ref, hbm):
        at = pl.ds(i * part * bs, part * bs)
        copies.append(pltpu.make_async_copy(ref.at[:, at], hbm.at[:, at], sems.at[len(copies)]))
        copies[-1].start()

    residual_of = lambda c: field_ref[c] - step * hess_ref[c]
    for i in range(OUT_PARTS):
        for c in range(i * part, (i + 1) * part):
            at = slice(c * bs, (c + 1) * bs)
            solution_ref[:, at] = (step * dir_ref[c])[:whole]
            residual_ref[:, at] = residual_of(c)[:whole]
        send(i, solution_ref, solution_hbm)
        send(i, residual_ref, residual_hbm)
    for i in range(OUT_PARTS):
        for b in range(i * part, (i + 1) * part, PAIR):
            correction = lax.dot_general(
                coeffs, map_ref[b * bs : (b + PAIR) * bs], (((1,), (1,)), ((), ())), preferred_element_type=F32
            )
            for c in range(b, b + PAIR):
                smoothed = (residual_of(c) + correction[:, (c - b) * bs : (c - b + 1) * bs]) * inv_diag_ref[c : c + 1]
                next_ref[:, c * bs : (c + 1) * bs] = (smoothed + ratio * dir_ref[c])[:whole]
        send(i, next_ref, next_hbm)
    for copy in copies:
        copy.wait()


def call(kernel, ins, outs, scratch=(), limit=16, keep=True, aliases={}):
    spec = lambda space: pl.BlockSpec(memory_space=space)
    shapes = tuple((pltpu.VMEM if keep else jax.ShapeDtypeStruct)(s, t) for s, t in outs)
    specs = (spec(pltpu.VMEM if keep else pl.ANY),) * len(shapes)
    return pl.pallas_call(
        kernel,
        out_shape=shapes if len(shapes) > 1 else shapes[0],
        in_specs=[spec(space) for space in ins],
        out_specs=specs if len(shapes) > 1 else specs[0],
        scratch_shapes=scratch,
        input_output_aliases=aliases,
        compiler_params=pltpu.CompilerParams(vmem_limit_bytes=limit * 1024 * 1024),
    )


def in_hbm(x):
    return pltpu.with_memory_space_constraint(x, pltpu.HBM)


def in_vmem(x):
    return pltpu.with_memory_space_constraint(x, pltpu.VMEM)


def body(latent, responses, probes, prior_diag, factor, cond_ids, inducing_map, inner_inverse):
    blocks, _, bs, _ = factor.shape
    count = probes.shape[0]
    rows, tall = count + 8, count + 16
    by_block = lambda x: x.reshape(blocks, bs)
    sum_shape = ((rows, inducing_map.shape[1]), F32)
    sum_msg = ((rows, inducing_map.shape[1]), BF16)
    field = ((blocks, rows, bs), F32)
    packed = ((blocks + 1, count, bs), BF16)
    vmem, smem = pltpu.VMEM, pltpu.SMEM
    partial, msg, terms, right_side, inducing_map = call(
        project_kernel,
        [pl.ANY] * 5,
        [sum_shape, sum_msg, ((2, blocks, bs), F32), field, (inducing_map.shape, BF16)],
        [
            vmem((blocks, bs), F32),
            vmem((blocks, bs), jnp.int32),
            vmem((blocks, bs), F32),
            vmem(probes.shape, F32),
            pltpu.SemaphoreType.DMA((4 + MAP_PARTS,)),
        ],
    )(*map(in_hbm, (by_block(latent), by_block(responses), by_block(prior_diag), probes, inducing_map)))
    points = (terms, right_side, inducing_map)

    def load(msg):
        outs = [(factor.shape, BF16), (inner_inverse.shape, F32)]
        return call(load_kernel, [pl.ANY] * 3, outs, [pltpu.SemaphoreType.DMA((2,))])(
            in_hbm(factor), in_hbm(inner_inverse), msg
        )

    def turn(msg, loaded, inner):
        shape = (blocks, factor.shape[1] * bs, bs)
        return loaded, inner, call(turn_kernel, [vmem, pl.ANY], [(shape, BF16)])(loaded, msg)

    sums, (factor, inner_inverse, turned) = total(partial, msg, "space", [load, turn])
    direction, rounded, product = call(
        direction_kernel, [vmem] * 5, [field, packed, sum_shape], [vmem((blocks, bs), F32)]
    )(sums, inner_inverse, *points)
    far_odd = shifted(rounded, "space", 2, 1)
    around = ((3 * blocks, rows, bs), F32)
    own_image, again, zeros = call(
        functools.partial(own_image_kernel, tall),
        [vmem] * 2,
        [((blocks, tall, bs), F32), packed, around],
        [vmem((blocks, bs), F32)],
    )(rounded, turned)
    far_even = shifted(again, "space", 2, 0)
    near = swapped(call(pass_on_kernel, [vmem] * 2, [packed])(rounded, far_odd), "space")
    back_far, back_near, back_own, curve, image = call(
        functools.partial(hessian_kernel, rows),
        [smem] + [vmem] * 8,
        [packed, packed, around, ((rows, bs), F32), ((blocks, tall, bs), BF16)],
        [vmem((3 * blocks, count, bs), BF16), vmem((3 * blocks, bs), F32), vmem((blocks, bs), F32)],
        aliases={8: 2},
    )(cond_ids.T, factor, turned, own_image, near, far_even, far_odd, rounded, zeros)
    mate = swapped(back_near, "space")
    from_even = shifted(back_far, "space", -2, 0)
    from_odd = shifted(call(join_kernel, [vmem] * 2, [packed])(back_far, mate), "space", -2, 1)
    own_back = call(functools.partial(own_back_kernel, rows), [vmem] * 2, [field])(image, factor)
    hess, partial, msg = call(combine_kernel, [vmem] * 10, [field, sum_shape, sum_msg])(
        back_own, own_back, from_even, from_odd, mate, curve, direction, *points
    )
    hess_sums, _ = total(partial, msg, "space")
    whole = ((count + 1, blocks * bs), F32)
    scratch = [vmem(*whole)] * 3 + [pltpu.SemaphoreType.DMA((3 * OUT_PARTS,))]
    return call(finish_kernel, [vmem] * 9, [whole] * 3, scratch, keep=False)(
        *map(in_vmem, (sums, product, hess_sums, inner_inverse, direction, hess, *points))
    )


def solution(mesh):
    return jax.shard_map(
        body,
        mesh=mesh,
        in_specs=(
            P(("groups", "space")),
            P(("groups", "space")),
            P(None, ("groups", "space")),
            P(("groups", "space")),
            P(("groups", "space"), None, None, None),
            P(("groups", "space"), None),
            P(("groups", "space"), None),
            P("groups", None),
        ),
        out_specs=(
            P(None, ("groups", "space")),
            P(None, ("groups", "space")),
            P(None, ("groups", "space")),
        ),
        check_vma=False,
    )
```

time: 57.8 us -> 55.7 us (0.964)
  waiting for transfers between devices: 22 us -> 20.6 us
  Pallas kernels: 13 us -> 12.2 us
    ppermute x12, waiting for transfers between devices: 10.6 us -> 9.19 us  [total(): lax.ppermute(msg, axis, [(i, i ^ d) for i in range(n)])]
    pallas_call x10 -> x11, Pallas kernels: 11.7 us -> 11.2 us  [the longest x1 2.23 us: load(): call(load_kernel, [pl.ANY] * 3, outs, [pltpu.SemaphoreType.DMA((2,))])]
  transfers between devices with their start and end apart: 18 -> 18, of which waited for: 11 -> 10; matrix products, arithmetic and copies ran while one was open for 0% -> 0% of each run, Pallas kernels for 6% -> 8%
where the time goes in v6:
time: 55.7 us; the launch traced here: 55.4 us
  starting transfers between devices  21.8 us (39%)
  waiting for transfers between devices  20.6 us (37%)
  Pallas kernels  12.2 us (22%)
  between operations  0.77 us (1%)
    ppermute x12, starting transfers between devices, total(): lax.ppermute(msg, axis, [(i, i ^ d) for i in range(n)])  15.7 us
    ppermute x4, waiting for transfers between devices, shifted(): return lax.ppermute(block, axis, route)  11.2 us
    ppermute x12, waiting for transfers between devices, total(): lax.ppermute(msg, axis, [(i, i ^ d) for i in range(n)])  9.19 us
    ppermute x4, starting transfers between devices, shifted(): return lax.ppermute(block, axis, route)  5.48 us
    pallas_call x1, Pallas kernels, load(): call(load_kernel, [pl.ANY] * 3, outs, [pltpu.SemaphoreType.DMA((2,))])  2.23 us
    pallas_call x1, Pallas kernels, body(): call(project_kernel, [pl.ANY] * 5, [sum_shape, sum_msg, ((2, blocks, bs),...  2.17 us
    pallas_call x1, Pallas kernels, body(): call(functools.partial(hessian_kernel, rows), [smem] + [vmem] * 8, [packe...  2.13 us
    pallas_call x1, Pallas kernels, body(): call(finish_kernel, [vmem] * 9, [whole] * 3, scratch, keep=False)  1.79 us
  transfers between devices with their start and end apart: 18, of which 10 were waited for; matrix products, arithmetic and copies ran while one was open for 0% of the time, Pallas kernels for 8%

profile of v6, /device:TPU:0, one launch (start us, length us, event | category | flops | bytes accessed | tf_op | source)
XLA Modules:
  0.0 55.4 jit_solution(7397553199868741084)
XLA Ops:
  0.6 2.2 %shard_map.103 = (f32[40,256]{1,0:T(8,128)S(1)}, bf16[40,256]{1,0:T(8,128)(2,1)S(1)}, f32[2,32,128]{2,1,0:T(8,128)S(1)}, f32[32,40,128]{2,1,0:T(8,128)S(1)}, bf16[4096,256]{1,0:T(8,128)(2,1)S(1)}) custom-call(f32[32,128]{1,0:T(8,128)} %bitcast.5, s32[32,128]{1,0:T(8,128)} %bitcast.6, f32[32,128]{1,0:T(8,128)} %bitcast.7, f32[32,4096]{1,0:T(8,128)} %probes_hbm.1, ...), custom_call_target="tpu_custom_call" | custom-call | tf_op jit(solution)/shard_map/pallas_call | solution.py:364
  2.8 2.4 %collective-permute-start.2 = (bf16[40,256]{1,0:T(8,128)(2,1)S(1)}, bf16[40,256]{1,0:T(8,128)(2,1)S(1)}, u32[]{:S(2)}, u32[]{:S(2)}) collective-permute-start(bf16[40,256]{1,0:T(8,128)(2,1)S(1)} %get-tuple-element.29.after_ref), channel_id=1, source_target_pairs={{0,3},{1,2},{2,1},{3,0},{4,7},{5,6},{6,5},{7,4},{8,11},{9,10},{10,... | collective-permute-start | bytes 61448 | tf_op jit(solution)/shard_map/ppermute | solution.py:71
  5.2 0.6 %collective-permute-start.1 = (bf16[40,256]{1,0:T(8,128)(2,1)S(1)}, bf16[40,256]{1,0:T(8,128)(2,1)S(1)}, u32[]{:S(2)}, u32[]{:S(2)}) collective-permute-start(bf16[40,256]{1,0:T(8,128)(2,1)S(1)} %get-tuple-element.29.after_ref), channel_id=1, source_target_pairs={{0,2},{1,3},{2,0},{3,1},{4,6},{5,7},{6,4},{7,5},{8,10},{9,11},{10,... | collective-permute-start | bytes 61448 | tf_op jit(solution)/shard_map/ppermute | solution.py:71
  5.9 0.0 collective-permute-start
  5.9 2.2 %shard_map.104 = (bf16[32,4,128,128]{3,2,1,0:T(8,128)(2,1)S(1)}, f32[256,256]{1,0:T(8,128)S(1)}) custom-call(bf16[32,4,128,128]{3,2,1,0:T(8,128)(2,1)} %factor_hbm.1, f32[256,256]{1,0:T(8,128)} %inner_hbm.1, bf16[40,256]{1,0:T(8,128)(2,1)S(1)} %get-tuple-element.29.after_ref), custom_call_target="tpu_custom_call" | custom-call | tf_op jit(solution)/shard_map/pallas_call | solution.py:380
  8.2 0.0 collective-permute-done.2.refs_2_
  8.2 0.9 %collective-permute-done.1.refs_1_ = bf16[40,256]{1,0:T(8,128)(2,1)S(1)} collective-permute-done((bf16[40,256]{1,0:T(8,128)(2,1)S(1)}, bf16[40,256]{1,0:T(8,128)(2,1)S(1)}, u32[]{:S(2)}, u32[]{:S(2)}) %collective-permute-start.1) | collective-permute-done | bytes 20512 | tf_op jit(solution)/shard_map/ppermute | solution.py:71
  9.0 0.0 collective-permute-done.refs_0_
  9.1 3.7 %collective-permute-start.5 = (bf16[40,256]{1,0:T(8,128)(2,1)S(1)}, bf16[40,256]{1,0:T(8,128)(2,1)S(1)}, u32[]{:S(2)}, u32[]{:S(2)}) collective-permute-start(bf16[40,256]{1,0:T(8,128)(2,1)S(1)} %get-tuple-element.33.after_ref), channel_id=1, source_target_pairs={{0,12},{1,13},{2,14},{3,15},{4,8},{5,9},{6,10},{7,11},{8,4},{9,5},... | collective-permute-start | bytes 61448 | tf_op jit(solution)/shard_map/ppermute | solution.py:71
  12.7 0.0 collective-permute-start.4
  12.7 0.8 %collective-permute-start.3 = (bf16[40,256]{1,0:T(8,128)(2,1)S(1)}, bf16[40,256]{1,0:T(8,128)(2,1)S(1)}, u32[]{:S(2)}, u32[]{:S(2)}) collective-permute-start(bf16[40,256]{1,0:T(8,128)(2,1)S(1)} %get-tuple-element.33.after_ref), channel_id=1, source_target_pairs={{0,4},{1,5},{2,6},{3,7},{4,0},{5,1},{6,2},{7,3},{8,12},{9,13},{10,... | collective-permute-start | bytes 61448 | tf_op jit(solution)/shard_map/ppermute | solution.py:71
  13.5 1.1 %shard_map.106.refs_5_.turned_ref = bf16[32,512,128]{2,1,0:T(8,128)(2,1)S(1)} custom-call(bf16[32,4,128,128]{3,2,1,0:T(8,128)(2,1)S(1)} %get-tuple-element.30.refs_3_.factor_ref, bf16[40,256]{1,0:T(8,128)(2,1)S(1)} %get-tuple-element.33.after_ref), custom_call_target="tpu_custom_call" | custom-call | tf_op jit(solution)/shard_map/pallas_call | solution.py:386
  14.7 0.2 collective-permute-done.5.refs_2_
  14.9 2.6 %collective-permute-done.4.refs_1_ = bf16[40,256]{1,0:T(8,128)(2,1)S(1)} collective-permute-done((bf16[40,256]{1,0:T(8,128)(2,1)S(1)}, bf16[40,256]{1,0:T(8,128)(2,1)S(1)}, u32[]{:S(2)}, u32[]{:S(2)}) %collective-permute-start.4) | collective-permute-done | bytes 20512 | tf_op jit(solution)/shard_map/ppermute | solution.py:71
  17.4 0.0 collective-permute-done.3.refs_0_
  17.4 1.0 %shard_map.108 = (f32[32,40,128]{2,1,0:T(8,128)S(1)}, bf16[33,32,128]{2,1,0:T(8,128)(2,1)S(1)}, f32[40,256]{1,0:T(8,128)S(1)}) custom-call(f32[40,256]{1,0:T(8,128)S(1)} %shard_map.107.sums_ref, f32[256,256]{1,0:T(8,128)S(1)} %get-tuple-element.31.refs_4_.inner_ref, f32[2,32,128]{2,1,0:T(8,128)S(1)} %get-tuple-element.34.terms_ref, ...), custom_call_target="tpu_custom_call" | custom-call | tf_op jit(solution)/shard_map/pallas_call | solution.py:389
  18.4 0.0 copy-start
  18.4 0.7 %collective-permute-start.6 = (bf16[33,32,128]{2,1,0:T(8,128)(2,1)S(1)}, bf16[33,32,128]{2,1,0:T(8,128)(2,1)S(1)}, u32[]{:S(2)}, u32[]{:S(2)}) collective-permute-start(bf16[33,32,128]{2,1,0:T(8,128)(2,1)S(1)} %get-tuple-element.38.own_ref), channel_id=1, source_target_pairs={{1,3},{3,5},{5,7},{7,9},{9,11},{11,13},{13,15},{17,19},{19,21},{21... | collective-permute-start | bytes 811016 | tf_op jit(solution)/shard_map/ppermute | solution.py:19
  19.1 0.5 shard_map.109
  19.6 2.8 %collective-permute-start.8 = (bf16[33,32,128]{2,1,0:T(8,128)(2,1)S(1)}, bf16[33,32,128]{2,1,0:T(8,128)(2,1)S(1)}, u32[]{:S(2)}, u32[]{:S(2)}) collective-permute-start(bf16[33,32,128]{2,1,0:T(8,128)(2,1)S(1)} %get-tuple-element.40), channel_id=1, source_target_pairs={{0,2},{2,4},{4,6},{6,8},{8,10},{10,12},{12,14},{16,18},{18,20},{20... | collective-permute-start | bytes 811016 | tf_op jit(solution)/shard_map/ppermute | solution.py:19
  22.5 0.0 collective-permute-done.6.far_ref.far_odd_ref
  22.5 0.6 %collective-permute-start.7 = (bf16[33,32,128]{2,1,0:T(8,128)(2,1)S(1)}, bf16[33,32,128]{2,1,0:T(8,128)(2,1)S(1)}, u32[]{:S(2)}, u32[]{:S(2)}) collective-permute-start(bf16[33,32,128]{2,1,0:T(8,128)(2,1)S(1)} %shard_map.110), channel_id=1, source_target_pairs={{0,1},{1,0},{2,3},{3,2},{4,5},{5,4},{6,7},{7,6},{8,9},{9,8},{10,11... | collective-permute-start | bytes 811016 | tf_op jit(solution)/shard_map/ppermute | solution.py:23
  23.1 3.3 %collective-permute-done.8.far_even_ref = bf16[33,32,128]{2,1,0:T(8,128)(2,1)S(1)} collective-permute-done((bf16[33,32,128]{2,1,0:T(8,128)(2,1)S(1)}, bf16[33,32,128]{2,1,0:T(8,128)(2,1)S(1)}, u32[]{:S(2)}, u32[]{:S(2)}) %collective-permute-start.8) | collective-permute-done | bytes 270368 | tf_op jit(solution)/shard_map/ppermute | solution.py:19
  26.4 0.0 collective-permute-done.7.near_ref
  26.4 0.0 copy-done
  26.4 2.1 %shard_map.111 = (bf16[33,32,128]{2,1,0:T(8,128)(2,1)S(1)}, bf16[33,32,128]{2,1,0:T(8,128)(2,1)S(1)}, f32[96,40,128]{2,1,0:T(8,128)S(1)}, f32[40,128]{1,0:T(8,128)S(1)}, bf16[32,48,128]{2,1,0:T(8,128)(2,1)S(1)}) custom-call(s32[3,32]{1,0:T(4,128)S(1)} %bitcast.4, ...), custom_call_target="tpu_custom_call", output_to_operand_aliasing={{2}: (8, {})} | custom-call | tf_op jit(solution)/shard_map/pallas_call | solution.py:402
  28.5 0.1 collective-permute-start.10
  28.6 1.3 %collective-permute-start.9 = (bf16[33,32,128]{2,1,0:T(8,128)(2,1)S(1)}, bf16[33,32,128]{2,1,0:T(8,128)(2,1)S(1)}, u32[]{:S(2)}, u32[]{:S(2)}) collective-permute-start(bf16[33,32,128]{2,1,0:T(8,128)(2,1)S(1)} %get-tuple-element.44.back_far_ref), channel_id=1, source_target_pairs={{2,0},{4,2},{6,4},{8,6},{10,8},{12,10},{14,12},{18,16},{20,18},{22... | collective-permute-start | bytes 811016 | tf_op jit(solution)/shard_map/ppermute | solution.py:19
  29.9 0.2 collective-permute-done.10.got_ref.mate_ref
  30.2 0.1 shard_map.113
  30.2 0.7 %collective-permute-start.11 = (bf16[33,32,128]{2,1,0:T(8,128)(2,1)S(1)}, bf16[33,32,128]{2,1,0:T(8,128)(2,1)S(1)}, u32[]{:S(2)}, u32[]{:S(2)}) collective-permute-start(bf16[33,32,128]{2,1,0:T(8,128)(2,1)S(1)} %shard_map.113), channel_id=1, source_target_pairs={{3,1},{5,3},{7,5},{9,7},{11,9},{13,11},{15,13},{19,17},{21,19},{23... | collective-permute-start | bytes 811016 | tf_op jit(solution)/shard_map/ppermute | solution.py:19
  30.9 0.4 shard_map.112.own_back_ref
  31.3 7.9 %collective-permute-done.9.even_ref = bf16[33,32,128]{2,1,0:T(8,128)(2,1)S(1)} collective-permute-done((bf16[33,32,128]{2,1,0:T(8,128)(2,1)S(1)}, bf16[33,32,128]{2,1,0:T(8,128)(2,1)S(1)}, u32[]{:S(2)}, u32[]{:S(2)}) %collective-permute-start.9) | collective-permute-done | bytes 270368 | tf_op jit(solution)/shard_map/ppermute | solution.py:19
  39.2 0.0 collective-permute-done.11.odd_ref
  39.2 0.7 %shard_map.114 = (f32[32,40,128]{2,1,0:T(8,128)S(1)}, f32[40,256]{1,0:T(8,128)S(1)}, bf16[40,256]{1,0:T(8,128)(2,1)S(1)}) custom-call(f32[96,40,128]{2,1,0:T(8,128)S(1)} %get-tuple-element.42.own_ref, f32[32,40,128]{2,1,0:T(8,128)S(1)} %shard_map.112.own_back_ref, bf16[33,32,128]{2,1,0:T(8,128)(2,1)S(1)} %collective-permute-done.9.even_ref, ...), custom_call_target="tpu_custom_call" | custom-call | tf_op jit(solution)/shard_map/pallas_call | solution.py:413
  39.9 3.5 %collective-permute-start.14 = (bf16[40,256]{1,0:T(8,128)(2,1)S(1)}, bf16[40,256]{1,0:T(8,128)(2,1)S(1)}, u32[]{:S(2)}, u32[]{:S(2)}) collective-permute-start(bf16[40,256]{1,0:T(8,128)(2,1)S(1)} %get-tuple-element.49), channel_id=1, source_target_pairs={{0,3},{1,2},{2,1},{3,0},{4,7},{5,6},{6,5},{7,4},{8,11},{9,10},{10,... | collective-permute-start | bytes 61448 | tf_op jit(solution)/shard_map/ppermute | solution.py:71
  43.4 0.0 collective-permute-start.13
  43.4 0.2 collective-permute-start.12
  43.6 1.4 %collective-permute-done.14.refs_2_ = bf16[40,256]{1,0:T(8,128)(2,1)S(1)} collective-permute-done((bf16[40,256]{1,0:T(8,128)(2,1)S(1)}, bf16[40,256]{1,0:T(8,128)(2,1)S(1)}, u32[]{:S(2)}, u32[]{:S(2)}) %collective-permute-start.14) | collective-permute-done | bytes 20512 | tf_op jit(solution)/shard_map/ppermute | solution.py:71
  44.9 2.2 %collective-permute-done.13.refs_1_ = bf16[40,256]{1,0:T(8,128)(2,1)S(1)} collective-permute-done((bf16[40,256]{1,0:T(8,128)(2,1)S(1)}, bf16[40,256]{1,0:T(8,128)(2,1)S(1)}, u32[]{:S(2)}, u32[]{:S(2)}) %collective-permute-start.13) | collective-permute-done | bytes 20512 | tf_op jit(solution)/shard_map/ppermute | solution.py:71
  47.1 0.0 collective-permute-done.12.refs_0_
  47.2 0.8 %collective-permute-start.17 = (bf16[40,256]{1,0:T(8,128)(2,1)S(1)}, bf16[40,256]{1,0:T(8,128)(2,1)S(1)}, u32[]{:S(2)}, u32[]{:S(2)}) collective-permute-start(bf16[40,256]{1,0:T(8,128)(2,1)S(1)} %get-tuple-element.51), channel_id=1, source_target_pairs={{0,12},{1,13},{2,14},{3,15},{4,8},{5,9},{6,10},{7,11},{8,4},{9,5},... | collective-permute-start | bytes 61448 | tf_op jit(solution)/shard_map/ppermute | solution.py:71
  48.0 1.8 %collective-permute-start.16 = (bf16[40,256]{1,0:T(8,128)(2,1)S(1)}, bf16[40,256]{1,0:T(8,128)(2,1)S(1)}, u32[]{:S(2)}, u32[]{:S(2)}) collective-permute-start(bf16[40,256]{1,0:T(8,128)(2,1)S(1)} %get-tuple-element.51), channel_id=1, source_target_pairs={{0,8},{1,9},{2,10},{3,11},{4,12},{5,13},{6,14},{7,15},{8,0},{9,1},... | collective-permute-start | bytes 61448 | tf_op jit(solution)/shard_map/ppermute | solution.py:71
  49.8 1.8 %collective-permute-start.15 = (bf16[40,256]{1,0:T(8,128)(2,1)S(1)}, bf16[40,256]{1,0:T(8,128)(2,1)S(1)}, u32[]{:S(2)}, u32[]{:S(2)}) collective-permute-start(bf16[40,256]{1,0:T(8,128)(2,1)S(1)} %get-tuple-element.51), channel_id=1, source_target_pairs={{0,4},{1,5},{2,6},{3,7},{4,0},{5,1},{6,2},{7,3},{8,12},{9,13},{10,... | collective-permute-start | bytes 61448 | tf_op jit(solution)/shard_map/ppermute | solution.py:71
  51.6 1.3 %collective-permute-done.17.refs_2_ = bf16[40,256]{1,0:T(8,128)(2,1)S(1)} collective-permute-done((bf16[40,256]{1,0:T(8,128)(2,1)S(1)}, bf16[40,256]{1,0:T(8,128)(2,1)S(1)}, u32[]{:S(2)}, u32[]{:S(2)}) %collective-permute-start.17) | collective-permute-done | bytes 20512 | tf_op jit(solution)/shard_map/ppermute | solution.py:71
  52.9 0.0 collective-permute-done.16.refs_1_
  52.9 0.7 %collective-permute-done.15.refs_0_ = bf16[40,256]{1,0:T(8,128)(2,1)S(1)} collective-permute-done((bf16[40,256]{1,0:T(8,128)(2,1)S(1)}, bf16[40,256]{1,0:T(8,128)(2,1)S(1)}, u32[]{:S(2)}, u32[]{:S(2)}) %collective-permute-start.15) | collective-permute-done | bytes 20512 | tf_op jit(solution)/shard_map/ppermute | solution.py:71
  53.6 1.8 %shard_map.117 = (f32[33,4096]{1,0:T(8,128)}, f32[33,4096]{1,0:T(8,128)}, f32[33,4096]{1,0:T(8,128)}) custom-call(f32[40,256]{1,0:T(8,128)S(1)} %shard_map.107.sums_ref, f32[40,256]{1,0:T(8,128)S(1)} %get-tuple-element.37.product_ref, f32[40,256]{1,0:T(8,128)S(1)} %shard_map.116.hess_sums_ref, f32[256,256]{1,0:T(8,128)S(1)} %get-tuple-element.31.refs_4_.inner_ref, ...), custom_call_target="tpu_custom_call" | custom-call | tf_op jit(solution)/shard_map/pallas_call | solution.py:419
  (5 shorter events, 0.1 us)
Async XLA Ops:
  2.8 5.4 %collective-permute-start.2 = (bf16[40,256]{1,0:T(8,128)(2,1)S(1)}, bf16[40,256]{1,0:T(8,128)(2,1)S(1)}, u32[]{:S(2)}, u32[]{:S(2)}) collective-permute-start(bf16[40,256]{1,0:T(8,128)(2,1)S(1)} %get-tuple-element.29.after_ref), channel_id=1, source_target_pairs={{0,3},{1,2},{2,1},{3,0},{4,7},{5,6},{6,5},{7,4},{8,11},{9,10},{10,... | collective-permute-start | bytes 61448 | tf_op jit(solution)/shard_map/ppermute | solution.py:71
  5.2 3.8 %collective-permute-start.1 = (bf16[40,256]{1,0:T(8,128)(2,1)S(1)}, bf16[40,256]{1,0:T(8,128)(2,1)S(1)}, u32[]{:S(2)}, u32[]{:S(2)}) collective-permute-start(bf16[40,256]{1,0:T(8,128)(2,1)S(1)} %get-tuple-element.29.after_ref), channel_id=1, source_target_pairs={{0,2},{1,3},{2,0},{3,1},{4,6},{5,7},{6,4},{7,5},{8,10},{9,11},{10,... | collective-permute-start | bytes 61448 | tf_op jit(solution)/shard_map/ppermute | solution.py:71
  5.9 3.1 %collective-permute-start = (bf16[40,256]{1,0:T(8,128)(2,1)S(1)}, bf16[40,256]{1,0:T(8,128)(2,1)S(1)}, u32[]{:S(2)}, u32[]{:S(2)}) collective-permute-start(bf16[40,256]{1,0:T(8,128)(2,1)S(1)} %get-tuple-element.29.after_ref), channel_id=1, source_target_pairs={{0,1},{1,0},{2,3},{3,2},{4,5},{5,4},{6,7},{7,6},{8,9},{9,8},{10,11... | collective-permute-start | bytes 61448 | tf_op jit(solution)/shard_map/ppermute | solution.py:71
  9.1 5.8 %collective-permute-start.5 = (bf16[40,256]{1,0:T(8,128)(2,1)S(1)}, bf16[40,256]{1,0:T(8,128)(2,1)S(1)}, u32[]{:S(2)}, u32[]{:S(2)}) collective-permute-start(bf16[40,256]{1,0:T(8,128)(2,1)S(1)} %get-tuple-element.33.after_ref), channel_id=1, source_target_pairs={{0,12},{1,13},{2,14},{3,15},{4,8},{5,9},{6,10},{7,11},{8,4},{9,5},... | collective-permute-start | bytes 61448 | tf_op jit(solution)/shard_map/ppermute | solution.py:71
  12.7 4.7 %collective-permute-start.4 = (bf16[40,256]{1,0:T(8,128)(2,1)S(1)}, bf16[40,256]{1,0:T(8,128)(2,1)S(1)}, u32[]{:S(2)}, u32[]{:S(2)}) collective-permute-start(bf16[40,256]{1,0:T(8,128)(2,1)S(1)} %get-tuple-element.33.after_ref), channel_id=1, source_target_pairs={{0,8},{1,9},{2,10},{3,11},{4,12},{5,13},{6,14},{7,15},{8,0},{9,1},... | collective-permute-start | bytes 61448 | tf_op jit(solution)/shard_map/ppermute | solution.py:71
  12.7 4.7 %collective-permute-start.3 = (bf16[40,256]{1,0:T(8,128)(2,1)S(1)}, bf16[40,256]{1,0:T(8,128)(2,1)S(1)}, u32[]{:S(2)}, u32[]{:S(2)}) collective-permute-start(bf16[40,256]{1,0:T(8,128)(2,1)S(1)} %get-tuple-element.33.after_ref), channel_id=1, source_target_pairs={{0,4},{1,5},{2,6},{3,7},{4,0},{5,1},{6,2},{7,3},{8,12},{9,13},{10,... | collective-permute-start | bytes 61448 | tf_op jit(solution)/shard_map/ppermute | solution.py:71
  18.4 8.0 %copy-start = (s32[32,3]{0,1:T(4,128)S(1)}, s32[32,3]{0,1:T(4,128)}, u32[]{:S(2)}) copy-start(s32[32,3]{0,1:T(4,128)} %param.13) | copy-start | bytes 1156
  18.4 4.1 %collective-permute-start.6 = (bf16[33,32,128]{2,1,0:T(8,128)(2,1)S(1)}, bf16[33,32,128]{2,1,0:T(8,128)(2,1)S(1)}, u32[]{:S(2)}, u32[]{:S(2)}) collective-permute-start(bf16[33,32,128]{2,1,0:T(8,128)(2,1)S(1)} %get-tuple-element.38.own_ref), channel_id=1, source_target_pairs={{1,3},{3,5},{5,7},{7,9},{9,11},{11,13},{13,15},{17,19},{19,21},{21... | collective-permute-start | bytes 811016 | tf_op jit(solution)/shard_map/ppermute | solution.py:19
  19.6 6.8 %collective-permute-start.8 = (bf16[33,32,128]{2,1,0:T(8,128)(2,1)S(1)}, bf16[33,32,128]{2,1,0:T(8,128)(2,1)S(1)}, u32[]{:S(2)}, u32[]{:S(2)}) collective-permute-start(bf16[33,32,128]{2,1,0:T(8,128)(2,1)S(1)} %get-tuple-element.40), channel_id=1, source_target_pairs={{0,2},{2,4},{4,6},{6,8},{8,10},{10,12},{12,14},{16,18},{18,20},{20... | collective-permute-start | bytes 811016 | tf_op jit(solution)/shard_map/ppermute | solution.py:19
  22.5 3.9 %collective-permute-start.7 = (bf16[33,32,128]{2,1,0:T(8,128)(2,1)S(1)}, bf16[33,32,128]{2,1,0:T(8,128)(2,1)S(1)}, u32[]{:S(2)}, u32[]{:S(2)}) collective-permute-start(bf16[33,32,128]{2,1,0:T(8,128)(2,1)S(1)} %shard_map.110), channel_id=1, source_target_pairs={{0,1},{1,0},{2,3},{3,2},{4,5},{5,4},{6,7},{7,6},{8,9},{9,8},{10,11... | collective-permute-start | bytes 811016 | tf_op jit(solution)/shard_map/ppermute | solution.py:23
  28.5 1.6 %collective-permute-start.10 = (bf16[33,32,128]{2,1,0:T(8,128)(2,1)S(1)}, bf16[33,32,128]{2,1,0:T(8,128)(2,1)S(1)}, u32[]{:S(2)}, u32[]{:S(2)}) collective-permute-start(bf16[33,32,128]{2,1,0:T(8,128)(2,1)S(1)} %get-tuple-element.45), channel_id=1, source_target_pairs={{0,1},{1,0},{2,3},{3,2},{4,5},{5,4},{6,7},{7,6},{8,9},{9,8},{10,11... | collective-permute-start | bytes 811016 | tf_op jit(solution)/shard_map/ppermute | solution.py:23
  28.6 10.6 %collective-permute-start.9 = (bf16[33,32,128]{2,1,0:T(8,128)(2,1)S(1)}, bf16[33,32,128]{2,1,0:T(8,128)(2,1)S(1)}, u32[]{:S(2)}, u32[]{:S(2)}) collective-permute-start(bf16[33,32,128]{2,1,0:T(8,128)(2,1)S(1)} %get-tuple-element.44.back_far_ref), channel_id=1, source_target_pairs={{2,0},{4,2},{6,4},{8,6},{10,8},{12,10},{14,12},{18,16},{20,18},{22... | collective-permute-start | bytes 811016 | tf_op jit(solution)/shard_map/ppermute | solution.py:19
  30.2 9.0 %collective-permute-start.11 = (bf16[33,32,128]{2,1,0:T(8,128)(2,1)S(1)}, bf16[33,32,128]{2,1,0:T(8,128)(2,1)S(1)}, u32[]{:S(2)}, u32[]{:S(2)}) collective-permute-start(bf16[33,32,128]{2,1,0:T(8,128)(2,1)S(1)} %shard_map.113), channel_id=1, source_target_pairs={{3,1},{5,3},{7,5},{9,7},{11,9},{13,11},{15,13},{19,17},{21,19},{23... | collective-permute-start | bytes 811016 | tf_op jit(solution)/shard_map/ppermute | solution.py:19
  39.9 5.0 %collective-permute-start.14 = (bf16[40,256]{1,0:T(8,128)(2,1)S(1)}, bf16[40,256]{1,0:T(8,128)(2,1)S(1)}, u32[]{:S(2)}, u32[]{:S(2)}) collective-permute-start(bf16[40,256]{1,0:T(8,128)(2,1)S(1)} %get-tuple-element.49), channel_id=1, source_target_pairs={{0,3},{1,2},{2,1},{3,0},{4,7},{5,6},{6,5},{7,4},{8,11},{9,10},{10,... | collective-permute-start | bytes 61448 | tf_op jit(solution)/shard_map/ppermute | solution.py:71
  43.4 3.8 %collective-permute-start.13 = (bf16[40,256]{1,0:T(8,128)(2,1)S(1)}, bf16[40,256]{1,0:T(8,128)(2,1)S(1)}, u32[]{:S(2)}, u32[]{:S(2)}) collective-permute-start(bf16[40,256]{1,0:T(8,128)(2,1)S(1)} %get-tuple-element.49), channel_id=1, source_target_pairs={{0,2},{1,3},{2,0},{3,1},{4,6},{5,7},{6,4},{7,5},{8,10},{9,11},{10,... | collective-permute-start | bytes 61448 | tf_op jit(solution)/shard_map/ppermute | solution.py:71
  43.4 3.8 %collective-permute-start.12 = (bf16[40,256]{1,0:T(8,128)(2,1)S(1)}, bf16[40,256]{1,0:T(8,128)(2,1)S(1)}, u32[]{:S(2)}, u32[]{:S(2)}) collective-permute-start(bf16[40,256]{1,0:T(8,128)(2,1)S(1)} %get-tuple-element.49), channel_id=1, source_target_pairs={{0,1},{1,0},{2,3},{3,2},{4,5},{5,4},{6,7},{7,6},{8,9},{9,8},{10,11... | collective-permute-start | bytes 61448 | tf_op jit(solution)/shard_map/ppermute | solution.py:71
  47.2 5.7 %collective-permute-start.17 = (bf16[40,256]{1,0:T(8,128)(2,1)S(1)}, bf16[40,256]{1,0:T(8,128)(2,1)S(1)}, u32[]{:S(2)}, u32[]{:S(2)}) collective-permute-start(bf16[40,256]{1,0:T(8,128)(2,1)S(1)} %get-tuple-element.51), channel_id=1, source_target_pairs={{0,12},{1,13},{2,14},{3,15},{4,8},{5,9},{6,10},{7,11},{8,4},{9,5},... | collective-permute-start | bytes 61448 | tf_op jit(solution)/shard_map/ppermute | solution.py:71
  48.0 4.9 %collective-permute-start.16 = (bf16[40,256]{1,0:T(8,128)(2,1)S(1)}, bf16[40,256]{1,0:T(8,128)(2,1)S(1)}, u32[]{:S(2)}, u32[]{:S(2)}) collective-permute-start(bf16[40,256]{1,0:T(8,128)(2,1)S(1)} %get-tuple-element.51), channel_id=1, source_target_pairs={{0,8},{1,9},{2,10},{3,11},{4,12},{5,13},{6,14},{7,15},{8,0},{9,1},... | collective-permute-start | bytes 61448 | tf_op jit(solution)/shard_map/ppermute | solution.py:71
  49.8 3.8 %collective-permute-start.15 = (bf16[40,256]{1,0:T(8,128)(2,1)S(1)}, bf16[40,256]{1,0:T(8,128)(2,1)S(1)}, u32[]{:S(2)}, u32[]{:S(2)}) collective-permute-start(bf16[40,256]{1,0:T(8,128)(2,1)S(1)} %get-tuple-element.51), channel_id=1, source_target_pairs={{0,4},{1,5},{2,6},{3,7},{4,0},{5,1},{6,2},{7,3},{8,12},{9,13},{10,... | collective-permute-start | bytes 61448 | tf_op jit(solution)/shard_map/ppermute | solution.py:71

commit v7 on v6

--- a/solution.py
+++ b/solution.py
@@ -52,32 +52,40 @@
     in_refs, (out_ref, *msg_refs) = refs[: count - 1], refs[count - 1 + held :]
     x = x_ref[...]
     for ref in in_refs:
-        x = x + read_message(ref)
+        x = x + (ref[...] if ref.dtype == F32 else read_message(ref))
     out_ref[...] = x
     for ref in msg_refs:
         write_message(ref, x)
 
 
-def total(x, msg, axis, beside=()):
+def rounds_of(n):
+    rounds = [(1,)] + [(3,)] * (n > 2)
+    step = 4
+    while step < n:
+        rounds.append(tuple((m * step) ^ 1 for m in range(1, 4) if m * step < n))
+        step *= 4
+    return rounds
+
+
+def total(x, axis, beside=()):
     n = lax.axis_size(axis)
     made = ()
     if n & (n - 1):
         for work in beside:
-            made = work(msg, *made)
+            made = work(x, *made)
         return lax.psum(x, axis), made
-    step = 1
-    while step < n:
-        partners = [m * step for m in range(1, 4) if m * step < n]
-        got = [lax.ppermute(msg, axis, [(i, i ^ d) for i in range(n)]) for d in partners]
-        step *= 4
-        last = step >= n
+    rounds = rounds_of(n)
+    msg = x
+    for i, partners in enumerate(rounds):
+        got = [lax.ppermute(msg, axis, [(j, j ^ d) for j in range(n)]) for d in partners]
+        last = i + 1 == len(rounds)
         held = ()
-        while beside and (last or not held):
+        while beside and (last or (i > 0 and not held)):
             work, *beside = beside
             made = held = work(msg, *made)
         add = functools.partial(add_kernel, len(got) + 1, len(held))
         ins = [pltpu.VMEM] * (len(got) + 1) + [pl.ANY] * len(held)
-        outs = [(x.shape, F32)] + [(msg.shape, BF16)] * (not last)
+        outs = [(x.shape, F32)] + [(x.shape, BF16)] * (not last)
         x, *rest = jax.tree.leaves(call(add, ins, outs)(x, *got, *held))
         msg = rest[0] if rest else None
     return x, made
@@ -96,7 +104,7 @@
 
 
 def project_kernel(
-    latent_hbm, responses_hbm, prior_hbm, probes_hbm, map_hbm, out_ref, msg_ref, terms_ref, field_ref, map_ref, latent_ref,
+    latent_hbm, responses_hbm, prior_hbm, probes_hbm, map_hbm, out_ref, terms_ref, field_ref, map_ref, latent_ref,
     responses_ref, prior_ref, probes_ref, sems,
 ):
     blocks, bs = latent_ref.shape
@@ -135,7 +143,6 @@
         summed += jnp.dot(both, map_ref[b * bs : (b + PAIR) * bs], preferred_element_type=F32)
     out_ref[...] = summed
     out_ref[count + 1 : count + 2] = as_row(jnp.sum(energy, axis=1, keepdims=True), out_ref.shape[1])
-    write_message(msg_ref, out_ref[...])
 
 
 def direction_kernel(sums_ref, inner_ref, terms_ref, field_ref, map_ref, dir_ref, msg_ref, product_ref, last_ref):
@@ -246,7 +253,7 @@
 
 def combine_kernel(
     own_ref, own_back_ref, even_ref, odd_ref, mate_ref, curve_ref, dir_ref, terms_ref, field_ref, map_ref, hess_ref,
-    out_ref, msg_ref,
+    out_ref,
 ):
     blocks, rows, bs = field_ref.shape
     count = mate_ref.shape[1]
@@ -277,7 +284,6 @@
     out_ref[...] = summed
     for i, acc in enumerate((curve, cross, square)):
         out_ref[count + 1 + i : count + 2 + i] = as_row(jnp.sum(acc, axis=1, keepdims=True), out_ref.shape[1])
-    write_message(msg_ref, out_ref[...])
 
 
 def finish_kernel(
@@ -357,14 +363,13 @@
     rows, tall = count + 8, count + 16
     by_block = lambda x: x.reshape(blocks, bs)
     sum_shape = ((rows, inducing_map.shape[1]), F32)
-    sum_msg = ((rows, inducing_map.shape[1]), BF16)
     field = ((blocks, rows, bs), F32)
     packed = ((blocks + 1, count, bs), BF16)
     vmem, smem = pltpu.VMEM, pltpu.SMEM
-    partial, msg, terms, right_side, inducing_map = call(
+    partial, terms, right_side, inducing_map = call(
         project_kernel,
         [pl.ANY] * 5,
-        [sum_shape, sum_msg, ((2, blocks, bs), F32), field, (inducing_map.shape, BF16)],
+        [sum_shape, ((2, blocks, bs), F32), field, (inducing_map.shape, BF16)],
         [
             vmem((blocks, bs), F32),
             vmem((blocks, bs), jnp.int32),
@@ -385,7 +390,7 @@
         shape = (blocks, factor.shape[1] * bs, bs)
         return loaded, inner, call(turn_kernel, [vmem, pl.ANY], [(shape, BF16)])(loaded, msg)
 
-    sums, (factor, inner_inverse, turned) = total(partial, msg, "space", [load, turn])
+    sums, (factor, inner_inverse, turned) = total(partial, "space", [load, turn])
     direction, rounded, product = call(
         direction_kernel, [vmem] * 5, [field, packed, sum_shape], [vmem((blocks, bs), F32)]
     )(sums, inner_inverse, *points)
@@ -410,10 +415,10 @@
     from_even = shifted(back_far, "space", -2, 0)
     from_odd = shifted(call(join_kernel, [vmem] * 2, [packed])(back_far, mate), "space", -2, 1)
     own_back = call(functools.partial(own_back_kernel, rows), [vmem] * 2, [field])(image, factor)
-    hess, partial, msg = call(combine_kernel, [vmem] * 10, [field, sum_shape, sum_msg])(
+    hess, partial = call(combine_kernel, [vmem] * 10, [field, sum_shape])(
         back_own, own_back, from_even, from_odd, mate, curve, direction, *points
     )
-    hess_sums, _ = total(partial, msg, "space")
+    hess_sums, _ = total(partial, "space")
     whole = ((count + 1, blocks * bs), F32)
     scratch = [vmem(*whole)] * 3 + [pltpu.SemaphoreType.DMA((3 * OUT_PARTS,))]
     return call(finish_kernel, [vmem] * 9, [whole] * 3, scratch, keep=False)(

time: 55.7 us -> 55.4 us (level)
  waiting for transfers between devices: 20.6 us -> 18 us
  starting transfers between devices: 21.8 us -> 24 us
    ppermute x2, starting transfers between devices: 0.67 us -> 3.31 us  [swapped(): lax.ppermute(block, axis, [(i, i ^ 1) for i in range(lax.axis_size(axis))])]
    ppermute x4, waiting for transfers between devices: 11.2 us -> 9.61 us  [shifted(): return lax.ppermute(block, axis, route)]
    ppermute x12 -> x10, waiting for transfers between devices: 9.19 us -> 8.17 us  [total(): lax.ppermute(msg, axis, [(j, j ^ d) for j in range(n)])]
    ppermute x12 -> x10, starting transfers between devices: 15.7 us -> 15.1 us  [total(): lax.ppermute(msg, axis, [(j, j ^ d) for j in range(n)])]
  transfers between devices with their start and end apart: 18 -> 16, of which waited for: 10 -> 9; matrix products, arithmetic and copies ran while one was open for 0% -> 0% of each run, Pallas kernels for 8% -> 8%
where the time goes in v7:
time: 55.4 us; the launch traced here: 55.1 us
  starting transfers between devices  24 us (43%)
  waiting for transfers between devices  18 us (32%)
  Pallas kernels  12.3 us (22%)
  between operations  0.79 us (1%)
    ppermute x10, starting transfers between devices, total(): lax.ppermute(msg, axis, [(j, j ^ d) for j in range(n)])  15.1 us
    ppermute x4, waiting for transfers between devices, shifted(): return lax.ppermute(block, axis, route)  9.61 us
    ppermute x10, waiting for transfers between devices, total(): lax.ppermute(msg, axis, [(j, j ^ d) for j in range(n)])  8.17 us
    ppermute x4, starting transfers between devices, shifted(): return lax.ppermute(block, axis, route)  5.57 us
    ppermute x2, starting transfers between devices, swapped(): lax.ppermute(block, axis, [(i, i ^ 1) for i in range(lax.axis_size(axis))])  3.31 us
    pallas_call x1, Pallas kernels, load(): call(load_kernel, [pl.ANY] * 3, outs, [pltpu.SemaphoreType.DMA((2,))])  2.23 us
    pallas_call x1, Pallas kernels, body(): call(functools.partial(hessian_kernel, rows), [smem] + [vmem] * 8, [packe...  2.16 us
    pallas_call x1, Pallas kernels, body(): call(project_kernel, [pl.ANY] * 5, [sum_shape, ((2, blocks, bs), F32), fi...  2.15 us
  transfers between devices with their start and end apart: 16, of which 9 were waited for; matrix products, arithmetic and copies ran while one was open for 0% of the time, Pallas kernels for 8%

profile of v7, /device:TPU:0, one launch (start us, length us, event | category | flops | bytes accessed | tf_op | source)
XLA Modules:
  0.0 55.1 jit_solution(15961781033873548413)
XLA Ops:
  0.6 2.2 %shard_map.103 = (f32[40,256]{1,0:T(8,128)S(1)}, f32[2,32,128]{2,1,0:T(8,128)S(1)}, f32[32,40,128]{2,1,0:T(8,128)S(1)}, bf16[4096,256]{1,0:T(8,128)(2,1)S(1)}) custom-call(f32[32,128]{1,0:T(8,128)} %bitcast.5, s32[32,128]{1,0:T(8,128)} %bitcast.6, f32[32,128]{1,0:T(8,128)} %bitcast.7, f32[32,4096]{1,0:T(8,128)} %probes_hbm.1, bf16[4096,256]{1,0:T(8,128)(2,1)} %map_hbm.1), custom_call_target="tpu_custom_call" | custom-call | tf_op jit(solution)/shard_map/pallas_call | solution.py:369
  2.8 0.5 collective-permute-start
  3.3 0.9 %collective-permute-done.refs_0_ = f32[40,256]{1,0:T(8,128)S(1)} collective-permute-done((f32[40,256]{1,0:T(8,128)S(1)}, f32[40,256]{1,0:T(8,128)S(1)}, u32[]{:S(2)}, u32[]{:S(2)}) %collective-permute-start) | collective-permute-done | bytes 40992 | tf_op jit(solution)/shard_map/ppermute | solution.py:80
  4.2 2.7 %collective-permute-start.1 = (bf16[40,256]{1,0:T(8,128)(2,1)S(1)}, bf16[40,256]{1,0:T(8,128)(2,1)S(1)}, u32[]{:S(2)}, u32[]{:S(2)}) collective-permute-start(bf16[40,256]{1,0:T(8,128)(2,1)S(1)} %get-tuple-element.32.after_ref), channel_id=1, source_target_pairs={{0,3},{1,2},{2,1},{3,0},{4,7},{5,6},{6,5},{7,4},{8,11},{9,10},{10,... | collective-permute-start | bytes 61448 | tf_op jit(solution)/shard_map/ppermute | solution.py:80
  6.9 2.2 %shard_map.105 = (bf16[32,4,128,128]{3,2,1,0:T(8,128)(2,1)S(1)}, f32[256,256]{1,0:T(8,128)S(1)}) custom-call(bf16[32,4,128,128]{3,2,1,0:T(8,128)(2,1)} %factor_hbm.1, f32[256,256]{1,0:T(8,128)} %inner_hbm.1, bf16[40,256]{1,0:T(8,128)(2,1)S(1)} %get-tuple-element.32.after_ref), custom_call_target="tpu_custom_call" | custom-call | tf_op jit(solution)/shard_map/pallas_call | solution.py:385
  9.1 0.0 collective-permute-done.1.refs_0_
  9.1 3.6 %collective-permute-start.4 = (bf16[40,256]{1,0:T(8,128)(2,1)S(1)}, bf16[40,256]{1,0:T(8,128)(2,1)S(1)}, u32[]{:S(2)}, u32[]{:S(2)}) collective-permute-start(bf16[40,256]{1,0:T(8,128)(2,1)S(1)} %get-tuple-element.36.after_ref), channel_id=1, source_target_pairs={{0,13},{1,12},{2,15},{3,14},{4,9},{5,8},{6,11},{7,10},{8,5},{9,4},... | collective-permute-start | bytes 61448 | tf_op jit(solution)/shard_map/ppermute | solution.py:80
  12.8 0.0 collective-permute-start.3
  12.8 0.5 collective-permute-start.2
  13.3 1.1 %shard_map.107.refs_5_.turned_ref = bf16[32,512,128]{2,1,0:T(8,128)(2,1)S(1)} custom-call(bf16[32,4,128,128]{3,2,1,0:T(8,128)(2,1)S(1)} %get-tuple-element.33.refs_1_.factor_ref.refs_3_, bf16[40,256]{1,0:T(8,128)(2,1)S(1)} %get-tuple-element.36.after_ref), custom_call_target="tpu_custom_call" | custom-call | tf_op jit(solution)/shard_map/pallas_call | solution.py:391
  14.4 0.0 collective-permute-done.4.refs_2_
  14.4 2.5 %collective-permute-done.3.refs_1_ = bf16[40,256]{1,0:T(8,128)(2,1)S(1)} collective-permute-done((bf16[40,256]{1,0:T(8,128)(2,1)S(1)}, bf16[40,256]{1,0:T(8,128)(2,1)S(1)}, u32[]{:S(2)}, u32[]{:S(2)}) %collective-permute-start.3) | collective-permute-done | bytes 20512 | tf_op jit(solution)/shard_map/ppermute | solution.py:80
  16.9 0.0 collective-permute-done.2.refs_0_
  16.9 1.0 %shard_map.109 = (f32[32,40,128]{2,1,0:T(8,128)S(1)}, bf16[33,32,128]{2,1,0:T(8,128)(2,1)S(1)}, f32[40,256]{1,0:T(8,128)S(1)}) custom-call(f32[40,256]{1,0:T(8,128)S(1)} %shard_map.108.sums_ref, f32[256,256]{1,0:T(8,128)S(1)} %get-tuple-element.34.refs_2_.refs_4_.inner_ref, f32[2,32,128]{2,1,0:T(8,128)S(1)} %get-tuple-element.37.terms_ref, ...), custom_call_target="tpu_custom_call" | custom-call | tf_op jit(solution)/shard_map/pallas_call | solution.py:394
  17.9 0.0 copy-start
  17.9 0.7 %collective-permute-start.5 = (bf16[33,32,128]{2,1,0:T(8,128)(2,1)S(1)}, bf16[33,32,128]{2,1,0:T(8,128)(2,1)S(1)}, u32[]{:S(2)}, u32[]{:S(2)}) collective-permute-start(bf16[33,32,128]{2,1,0:T(8,128)(2,1)S(1)} %get-tuple-element.41.own_ref), channel_id=1, source_target_pairs={{1,3},{3,5},{5,7},{7,9},{9,11},{11,13},{13,15},{17,19},{19,21},{21... | collective-permute-start | bytes 811016 | tf_op jit(solution)/shard_map/ppermute | solution.py:19
  18.6 0.5 shard_map.110
  19.1 2.9 %collective-permute-start.7 = (bf16[33,32,128]{2,1,0:T(8,128)(2,1)S(1)}, bf16[33,32,128]{2,1,0:T(8,128)(2,1)S(1)}, u32[]{:S(2)}, u32[]{:S(2)}) collective-permute-start(bf16[33,32,128]{2,1,0:T(8,128)(2,1)S(1)} %get-tuple-element.43), channel_id=1, source_target_pairs={{0,2},{2,4},{4,6},{6,8},{8,10},{10,12},{12,14},{16,18},{18,20},{20... | collective-permute-start | bytes 811016 | tf_op jit(solution)/shard_map/ppermute | solution.py:19
  22.0 0.0 collective-permute-done.5.far_ref.far_odd_ref
  22.1 3.2 %collective-permute-start.6 = (bf16[33,32,128]{2,1,0:T(8,128)(2,1)S(1)}, bf16[33,32,128]{2,1,0:T(8,128)(2,1)S(1)}, u32[]{:S(2)}, u32[]{:S(2)}) collective-permute-start(bf16[33,32,128]{2,1,0:T(8,128)(2,1)S(1)} %shard_map.111), channel_id=1, source_target_pairs={{0,1},{1,0},{2,3},{3,2},{4,5},{5,4},{6,7},{7,6},{8,9},{9,8},{10,11... | collective-permute-start | bytes 811016 | tf_op jit(solution)/shard_map/ppermute | solution.py:23
  25.3 1.7 %collective-permute-done.7.far_even_ref = bf16[33,32,128]{2,1,0:T(8,128)(2,1)S(1)} collective-permute-done((bf16[33,32,128]{2,1,0:T(8,128)(2,1)S(1)}, bf16[33,32,128]{2,1,0:T(8,128)(2,1)S(1)}, u32[]{:S(2)}, u32[]{:S(2)}) %collective-permute-start.7) | collective-permute-done | bytes 270368 | tf_op jit(solution)/shard_map/ppermute | solution.py:19
  27.0 0.0 collective-permute-done.6.near_ref
  27.0 0.0 copy-done
  27.0 2.2 %shard_map.112 = (bf16[33,32,128]{2,1,0:T(8,128)(2,1)S(1)}, bf16[33,32,128]{2,1,0:T(8,128)(2,1)S(1)}, f32[96,40,128]{2,1,0:T(8,128)S(1)}, f32[40,128]{1,0:T(8,128)S(1)}, bf16[32,48,128]{2,1,0:T(8,128)(2,1)S(1)}) custom-call(s32[3,32]{1,0:T(4,128)S(1)} %bitcast.4, ...), custom_call_target="tpu_custom_call", output_to_operand_aliasing={{2}: (8, {})} | custom-call | tf_op jit(solution)/shard_map/pallas_call | solution.py:407
  29.2 0.1 collective-permute-start.9
  29.3 1.3 %collective-permute-start.8 = (bf16[33,32,128]{2,1,0:T(8,128)(2,1)S(1)}, bf16[33,32,128]{2,1,0:T(8,128)(2,1)S(1)}, u32[]{:S(2)}, u32[]{:S(2)}) collective-permute-start(bf16[33,32,128]{2,1,0:T(8,128)(2,1)S(1)} %get-tuple-element.47.back_far_ref), channel_id=1, source_target_pairs={{2,0},{4,2},{6,4},{8,6},{10,8},{12,10},{14,12},{18,16},{20,18},{22... | collective-permute-start | bytes 811016 | tf_op jit(solution)/shard_map/ppermute | solution.py:19
  30.6 0.2 collective-permute-done.9.got_ref.mate_ref
  30.8 0.1 shard_map.114
  30.9 0.7 %collective-permute-start.10 = (bf16[33,32,128]{2,1,0:T(8,128)(2,1)S(1)}, bf16[33,32,128]{2,1,0:T(8,128)(2,1)S(1)}, u32[]{:S(2)}, u32[]{:S(2)}) collective-permute-start(bf16[33,32,128]{2,1,0:T(8,128)(2,1)S(1)} %shard_map.114), channel_id=1, source_target_pairs={{3,1},{5,3},{7,5},{9,7},{11,9},{13,11},{15,13},{19,17},{21,19},{23... | collective-permute-start | bytes 811016 | tf_op jit(solution)/shard_map/ppermute | solution.py:19
  31.6 0.4 shard_map.113.own_back_ref
  32.0 7.9 %collective-permute-done.8.even_ref = bf16[33,32,128]{2,1,0:T(8,128)(2,1)S(1)} collective-permute-done((bf16[33,32,128]{2,1,0:T(8,128)(2,1)S(1)}, bf16[33,32,128]{2,1,0:T(8,128)(2,1)S(1)}, u32[]{:S(2)}, u32[]{:S(2)}) %collective-permute-start.8) | collective-permute-done | bytes 270368 | tf_op jit(solution)/shard_map/ppermute | solution.py:19
  39.9 0.0 collective-permute-done.10.odd_ref
  39.9 0.7 %shard_map.115 = (f32[32,40,128]{2,1,0:T(8,128)S(1)}, f32[40,256]{1,0:T(8,128)S(1)}) custom-call(f32[96,40,128]{2,1,0:T(8,128)S(1)} %get-tuple-element.45.own_ref, f32[32,40,128]{2,1,0:T(8,128)S(1)} %shard_map.113.own_back_ref, bf16[33,32,128]{2,1,0:T(8,128)(2,1)S(1)} %collective-permute-done.8.even_ref, ...), custom_call_target="tpu_custom_call" | custom-call | tf_op jit(solution)/shard_map/pallas_call | solution.py:418
  40.5 0.9 %collective-permute-start.11 = (f32[40,256]{1,0:T(8,128)S(1)}, f32[40,256]{1,0:T(8,128)S(1)}, u32[]{:S(2)}, u32[]{:S(2)}) collective-permute-start(f32[40,256]{1,0:T(8,128)S(1)} %get-tuple-element.51.x_ref), channel_id=1, source_target_pairs={{0,1},{1,0},{2,3},{3,2},{4,5},{5,4},{6,7},{7,6},{8,9},{9,8},{10,11... | collective-permute-start | bytes 122888 | tf_op jit(solution)/shard_map/ppermute | solution.py:80
  41.5 0.9 %collective-permute-done.11.refs_0_ = f32[40,256]{1,0:T(8,128)S(1)} collective-permute-done((f32[40,256]{1,0:T(8,128)S(1)}, f32[40,256]{1,0:T(8,128)S(1)}, u32[]{:S(2)}, u32[]{:S(2)}) %collective-permute-start.11) | collective-permute-done | bytes 40992 | tf_op jit(solution)/shard_map/ppermute | solution.py:80
  42.4 2.9 %collective-permute-start.12 = (bf16[40,256]{1,0:T(8,128)(2,1)S(1)}, bf16[40,256]{1,0:T(8,128)(2,1)S(1)}, u32[]{:S(2)}, u32[]{:S(2)}) collective-permute-start(bf16[40,256]{1,0:T(8,128)(2,1)S(1)} %get-tuple-element.53), channel_id=1, source_target_pairs={{0,3},{1,2},{2,1},{3,0},{4,7},{5,6},{6,5},{7,4},{8,11},{9,10},{10,... | collective-permute-start | bytes 61448 | tf_op jit(solution)/shard_map/ppermute | solution.py:80
  45.3 1.5 %collective-permute-done.12.refs_0_ = bf16[40,256]{1,0:T(8,128)(2,1)S(1)} collective-permute-done((bf16[40,256]{1,0:T(8,128)(2,1)S(1)}, bf16[40,256]{1,0:T(8,128)(2,1)S(1)}, u32[]{:S(2)}, u32[]{:S(2)}) %collective-permute-start.12) | collective-permute-done | bytes 20512 | tf_op jit(solution)/shard_map/ppermute | solution.py:80
  46.8 2.3 %collective-permute-start.15 = (bf16[40,256]{1,0:T(8,128)(2,1)S(1)}, bf16[40,256]{1,0:T(8,128)(2,1)S(1)}, u32[]{:S(2)}, u32[]{:S(2)}) collective-permute-start(bf16[40,256]{1,0:T(8,128)(2,1)S(1)} %get-tuple-element.55), channel_id=1, source_target_pairs={{0,13},{1,12},{2,15},{3,14},{4,9},{5,8},{6,11},{7,10},{8,5},{9,4},... | collective-permute-start | bytes 61448 | tf_op jit(solution)/shard_map/ppermute | solution.py:80
  49.1 0.3 collective-permute-start.14
  49.5 1.3 %collective-permute-start.13 = (bf16[40,256]{1,0:T(8,128)(2,1)S(1)}, bf16[40,256]{1,0:T(8,128)(2,1)S(1)}, u32[]{:S(2)}, u32[]{:S(2)}) collective-permute-start(bf16[40,256]{1,0:T(8,128)(2,1)S(1)} %get-tuple-element.55), channel_id=1, source_target_pairs={{0,5},{1,4},{2,7},{3,6},{4,1},{5,0},{6,3},{7,2},{8,13},{9,12},{10,... | collective-permute-start | bytes 61448 | tf_op jit(solution)/shard_map/ppermute | solution.py:80
  50.7 1.1 %collective-permute-done.15.refs_2_ = bf16[40,256]{1,0:T(8,128)(2,1)S(1)} collective-permute-done((bf16[40,256]{1,0:T(8,128)(2,1)S(1)}, bf16[40,256]{1,0:T(8,128)(2,1)S(1)}, u32[]{:S(2)}, u32[]{:S(2)}) %collective-permute-start.15) | collective-permute-done | bytes 20512 | tf_op jit(solution)/shard_map/ppermute | solution.py:80
  51.9 1.4 %collective-permute-done.14.refs_1_ = bf16[40,256]{1,0:T(8,128)(2,1)S(1)} collective-permute-done((bf16[40,256]{1,0:T(8,128)(2,1)S(1)}, bf16[40,256]{1,0:T(8,128)(2,1)S(1)}, u32[]{:S(2)}, u32[]{:S(2)}) %collective-permute-start.14) | collective-permute-done | bytes 20512 | tf_op jit(solution)/shard_map/ppermute | solution.py:80
  53.2 0.0 collective-permute-done.13.refs_0_
  53.3 1.8 %shard_map.119 = (f32[33,4096]{1,0:T(8,128)}, f32[33,4096]{1,0:T(8,128)}, f32[33,4096]{1,0:T(8,128)}) custom-call(f32[40,256]{1,0:T(8,128)S(1)} %shard_map.108.sums_ref, f32[40,256]{1,0:T(8,128)S(1)} %get-tuple-element.40.product_ref, f32[40,256]{1,0:T(8,128)S(1)} %shard_map.118.hess_sums_ref, f32[256,256]{1,0:T(8,128)S(1)} %get-tuple-element.34.refs_2_.refs_4_.inner_ref, ...), custom_call_target="tpu_custom_call" | custom-call | tf_op jit(solution)/shard_map/pallas_call | solution.py:424
  (7 shorter events, 0.1 us)
Async XLA Ops:
  2.8 1.4 %collective-permute-start = (f32[40,256]{1,0:T(8,128)S(1)}, f32[40,256]{1,0:T(8,128)S(1)}, u32[]{:S(2)}, u32[]{:S(2)}) collective-permute-start(f32[40,256]{1,0:T(8,128)S(1)} %get-tuple-element.30.x_ref), channel_id=1, source_target_pairs={{0,1},{1,0},{2,3},{3,2},{4,5},{5,4},{6,7},{7,6},{8,9},{9,8},{10,11... | collective-permute-start | bytes 122888 | tf_op jit(solution)/shard_map/ppermute | solution.py:80
  4.2 4.9 %collective-permute-start.1 = (bf16[40,256]{1,0:T(8,128)(2,1)S(1)}, bf16[40,256]{1,0:T(8,128)(2,1)S(1)}, u32[]{:S(2)}, u32[]{:S(2)}) collective-permute-start(bf16[40,256]{1,0:T(8,128)(2,1)S(1)} %get-tuple-element.32.after_ref), channel_id=1, source_target_pairs={{0,3},{1,2},{2,1},{3,0},{4,7},{5,6},{6,5},{7,4},{8,11},{9,10},{10,... | collective-permute-start | bytes 61448 | tf_op jit(solution)/shard_map/ppermute | solution.py:80
  9.1 5.3 %collective-permute-start.4 = (bf16[40,256]{1,0:T(8,128)(2,1)S(1)}, bf16[40,256]{1,0:T(8,128)(2,1)S(1)}, u32[]{:S(2)}, u32[]{:S(2)}) collective-permute-start(bf16[40,256]{1,0:T(8,128)(2,1)S(1)} %get-tuple-element.36.after_ref), channel_id=1, source_target_pairs={{0,13},{1,12},{2,15},{3,14},{4,9},{5,8},{6,11},{7,10},{8,5},{9,4},... | collective-permute-start | bytes 61448 | tf_op jit(solution)/shard_map/ppermute | solution.py:80
  12.8 4.1 %collective-permute-start.3 = (bf16[40,256]{1,0:T(8,128)(2,1)S(1)}, bf16[40,256]{1,0:T(8,128)(2,1)S(1)}, u32[]{:S(2)}, u32[]{:S(2)}) collective-permute-start(bf16[40,256]{1,0:T(8,128)(2,1)S(1)} %get-tuple-element.36.after_ref), channel_id=1, source_target_pairs={{0,9},{1,8},{2,11},{3,10},{4,13},{5,12},{6,15},{7,14},{8,1},{9,0},... | collective-permute-start | bytes 61448 | tf_op jit(solution)/shard_map/ppermute | solution.py:80
  12.8 4.1 %collective-permute-start.2 = (bf16[40,256]{1,0:T(8,128)(2,1)S(1)}, bf16[40,256]{1,0:T(8,128)(2,1)S(1)}, u32[]{:S(2)}, u32[]{:S(2)}) collective-permute-start(bf16[40,256]{1,0:T(8,128)(2,1)S(1)} %get-tuple-element.36.after_ref), channel_id=1, source_target_pairs={{0,5},{1,4},{2,7},{3,6},{4,1},{5,0},{6,3},{7,2},{8,13},{9,12},{10,... | collective-permute-start | bytes 61448 | tf_op jit(solution)/shard_map/ppermute | solution.py:80
  17.9 9.2 %copy-start = (s32[32,3]{0,1:T(4,128)S(1)}, s32[32,3]{0,1:T(4,128)}, u32[]{:S(2)}) copy-start(s32[32,3]{0,1:T(4,128)} %param.13) | copy-start | bytes 1156
  17.9 4.2 %collective-permute-start.5 = (bf16[33,32,128]{2,1,0:T(8,128)(2,1)S(1)}, bf16[33,32,128]{2,1,0:T(8,128)(2,1)S(1)}, u32[]{:S(2)}, u32[]{:S(2)}) collective-permute-start(bf16[33,32,128]{2,1,0:T(8,128)(2,1)S(1)} %get-tuple-element.41.own_ref), channel_id=1, source_target_pairs={{1,3},{3,5},{5,7},{7,9},{9,11},{11,13},{13,15},{17,19},{19,21},{21... | collective-permute-start | bytes 811016 | tf_op jit(solution)/shard_map/ppermute | solution.py:19
  19.1 7.9 %collective-permute-start.7 = (bf16[33,32,128]{2,1,0:T(8,128)(2,1)S(1)}, bf16[33,32,128]{2,1,0:T(8,128)(2,1)S(1)}, u32[]{:S(2)}, u32[]{:S(2)}) collective-permute-start(bf16[33,32,128]{2,1,0:T(8,128)(2,1)S(1)} %get-tuple-element.43), channel_id=1, source_target_pairs={{0,2},{2,4},{4,6},{6,8},{8,10},{10,12},{12,14},{16,18},{18,20},{20... | collective-permute-start | bytes 811016 | tf_op jit(solution)/shard_map/ppermute | solution.py:19
  22.1 4.9 %collective-permute-start.6 = (bf16[33,32,128]{2,1,0:T(8,128)(2,1)S(1)}, bf16[33,32,128]{2,1,0:T(8,128)(2,1)S(1)}, u32[]{:S(2)}, u32[]{:S(2)}) collective-permute-start(bf16[33,32,128]{2,1,0:T(8,128)(2,1)S(1)} %shard_map.111), channel_id=1, source_target_pairs={{0,1},{1,0},{2,3},{3,2},{4,5},{5,4},{6,7},{7,6},{8,9},{9,8},{10,11... | collective-permute-start | bytes 811016 | tf_op jit(solution)/shard_map/ppermute | solution.py:23
  29.2 1.6 %collective-permute-start.9 = (bf16[33,32,128]{2,1,0:T(8,128)(2,1)S(1)}, bf16[33,32,128]{2,1,0:T(8,128)(2,1)S(1)}, u32[]{:S(2)}, u32[]{:S(2)}) collective-permute-start(bf16[33,32,128]{2,1,0:T(8,128)(2,1)S(1)} %get-tuple-element.48), channel_id=1, source_target_pairs={{0,1},{1,0},{2,3},{3,2},{4,5},{5,4},{6,7},{7,6},{8,9},{9,8},{10,11... | collective-permute-start | bytes 811016 | tf_op jit(solution)/shard_map/ppermute | solution.py:23
  29.3 10.6 %collective-permute-start.8 = (bf16[33,32,128]{2,1,0:T(8,128)(2,1)S(1)}, bf16[33,32,128]{2,1,0:T(8,128)(2,1)S(1)}, u32[]{:S(2)}, u32[]{:S(2)}) collective-permute-start(bf16[33,32,128]{2,1,0:T(8,128)(2,1)S(1)} %get-tuple-element.47.back_far_ref), channel_id=1, source_target_pairs={{2,0},{4,2},{6,4},{8,6},{10,8},{12,10},{14,12},{18,16},{20,18},{22... | collective-permute-start | bytes 811016 | tf_op jit(solution)/shard_map/ppermute | solution.py:19
  30.9 9.0 %collective-permute-start.10 = (bf16[33,32,128]{2,1,0:T(8,128)(2,1)S(1)}, bf16[33,32,128]{2,1,0:T(8,128)(2,1)S(1)}, u32[]{:S(2)}, u32[]{:S(2)}) collective-permute-start(bf16[33,32,128]{2,1,0:T(8,128)(2,1)S(1)} %shard_map.114), channel_id=1, source_target_pairs={{3,1},{5,3},{7,5},{9,7},{11,9},{13,11},{15,13},{19,17},{21,19},{23... | collective-permute-start | bytes 811016 | tf_op jit(solution)/shard_map/ppermute | solution.py:19
  40.5 1.8 %collective-permute-start.11 = (f32[40,256]{1,0:T(8,128)S(1)}, f32[40,256]{1,0:T(8,128)S(1)}, u32[]{:S(2)}, u32[]{:S(2)}) collective-permute-start(f32[40,256]{1,0:T(8,128)S(1)} %get-tuple-element.51.x_ref), channel_id=1, source_target_pairs={{0,1},{1,0},{2,3},{3,2},{4,5},{5,4},{6,7},{7,6},{8,9},{9,8},{10,11... | collective-permute-start | bytes 122888 | tf_op jit(solution)/shard_map/ppermute | solution.py:80
  42.4 4.4 %collective-permute-start.12 = (bf16[40,256]{1,0:T(8,128)(2,1)S(1)}, bf16[40,256]{1,0:T(8,128)(2,1)S(1)}, u32[]{:S(2)}, u32[]{:S(2)}) collective-permute-start(bf16[40,256]{1,0:T(8,128)(2,1)S(1)} %get-tuple-element.53), channel_id=1, source_target_pairs={{0,3},{1,2},{2,1},{3,0},{4,7},{5,6},{6,5},{7,4},{8,11},{9,10},{10,... | collective-permute-start | bytes 61448 | tf_op jit(solution)/shard_map/ppermute | solution.py:80
  46.8 5.1 %collective-permute-start.15 = (bf16[40,256]{1,0:T(8,128)(2,1)S(1)}, bf16[40,256]{1,0:T(8,128)(2,1)S(1)}, u32[]{:S(2)}, u32[]{:S(2)}) collective-permute-start(bf16[40,256]{1,0:T(8,128)(2,1)S(1)} %get-tuple-element.55), channel_id=1, source_target_pairs={{0,13},{1,12},{2,15},{3,14},{4,9},{5,8},{6,11},{7,10},{8,5},{9,4},... | collective-permute-start | bytes 61448 | tf_op jit(solution)/shard_map/ppermute | solution.py:80
  49.1 4.1 %collective-permute-start.14 = (bf16[40,256]{1,0:T(8,128)(2,1)S(1)}, bf16[40,256]{1,0:T(8,128)(2,1)S(1)}, u32[]{:S(2)}, u32[]{:S(2)}) collective-permute-start(bf16[40,256]{1,0:T(8,128)(2,1)S(1)} %get-tuple-element.55), channel_id=1, source_target_pairs={{0,9},{1,8},{2,11},{3,10},{4,13},{5,12},{6,15},{7,14},{8,1},{9,0},... | collective-permute-start | bytes 61448 | tf_op jit(solution)/shard_map/ppermute | solution.py:80
  49.5 3.8 %collective-permute-start.13 = (bf16[40,256]{1,0:T(8,128)(2,1)S(1)}, bf16[40,256]{1,0:T(8,128)(2,1)S(1)}, u32[]{:S(2)}, u32[]{:S(2)}) collective-permute-start(bf16[40,256]{1,0:T(8,128)(2,1)S(1)} %get-tuple-element.55), channel_id=1, source_target_pairs={{0,5},{1,4},{2,7},{3,6},{4,1},{5,0},{6,3},{7,2},{8,13},{9,12},{10,... | collective-permute-start | bytes 61448 | tf_op jit(solution)/shard_map/ppermute | solution.py:80

commit v8 on v7

--- a/solution.py
+++ b/solution.py
@@ -13,10 +13,9 @@
 OUT_PARTS = 4
 
 
-def shifted(block, axis, distance, parity):
+def sent(block, axis, distance, parities=(0, 1)):
     devices = range(lax.axis_size(axis))
-    route = [(i - distance, i) for i in devices if i % 2 == parity and i - distance in devices]
-    return lax.ppermute(block, axis, route)
+    return lax.ppermute(block, axis, [(i, i + distance) for i in devices if i % 2 in parities and i + distance in devices])
 
 
 def swapped(block, axis):
@@ -67,28 +66,22 @@
     return rounds
 
 
-def total(x, axis, beside=()):
+def total(x, axis, beside=None):
     n = lax.axis_size(axis)
-    made = ()
     if n & (n - 1):
-        for work in beside:
-            made = work(x, *made)
-        return lax.psum(x, axis), made
+        return lax.psum(x, axis), beside(x) if beside else ()
     rounds = rounds_of(n)
     msg = x
     for i, partners in enumerate(rounds):
         got = [lax.ppermute(msg, axis, [(j, j ^ d) for j in range(n)]) for d in partners]
         last = i + 1 == len(rounds)
-        held = ()
-        while beside and (last or (i > 0 and not held)):
-            work, *beside = beside
-            made = held = work(msg, *made)
+        held = beside(msg) if beside and last else ()
         add = functools.partial(add_kernel, len(got) + 1, len(held))
         ins = [pltpu.VMEM] * (len(got) + 1) + [pl.ANY] * len(held)
         outs = [(x.shape, F32)] + [(x.shape, BF16)] * (not last)
         x, *rest = jax.tree.leaves(call(add, ins, outs)(x, *got, *held))
         msg = rest[0] if rest else None
-    return x, made
+    return x, held
 
 
 def eye(rows, lanes):
@@ -188,32 +181,32 @@
     return jnp.concatenate([most, last.astype(BF16)], axis=0)
 
 
-def own_image_kernel(tall, own_ref, turned_ref, image_ref, again_ref, zeros_ref, last_ref):
+def own_image_kernel(tall, own_ref, turned_ref, image_ref, zeros_ref, last_ref):
     blocks, bs = last_ref.shape
-    again_ref[...] = own_ref[...]
     zeros_ref[...] = jnp.zeros_like(zeros_ref)
     last_ref[...] = own_ref[blocks].astype(F32)
     for b in range(blocks):
         image_ref[b] = jnp.dot(tall_block(own_ref, last_ref, b, tall), turned_ref[b, :bs], preferred_element_type=F32)
 
 
-def pass_on_kernel(own_ref, far_ref, out_ref):
-    @pl.when(is_even("space"))
-    def _():
-        out_ref[...] = own_ref[...]
-
-    @pl.when(jnp.logical_not(is_even("space")))
-    def _():
-        out_ref[...] = far_ref[...]
+def pass_on_kernel(near_ref, after_ref, out_ref):
+    out_ref[...] = near_ref[...]
 
 
 def join_kernel(back_far_ref, got_ref, out_ref):
     out_ref[...] = (back_far_ref[...].astype(F32) + got_ref[...].astype(F32)).astype(BF16)
 
 
-def own_back_kernel(rows, image_ref, factor_ref, out_ref):
-    for b in range(factor_ref.shape[0]):
-        out_ref[b] = jnp.dot(image_ref[b], factor_ref[b, 0], preferred_element_type=F32)[:rows]
+def own_back_kernel(rows, image_ref, factor_ref, total_ref, curve_ref, dir_ref, terms_ref, base_ref, curve_out_ref):
+    blocks = factor_ref.shape[0]
+    curve = curve_ref[...]
+    for b in range(blocks):
+        direction = dir_ref[b]
+        weighted = terms_ref[0, b : b + 1] * direction
+        curve += weighted * direction
+        back = jnp.dot(image_ref[b], factor_ref[b, 0], preferred_element_type=F32)[:rows]
+        base_ref[b] = total_ref[2 * blocks + b] + back + weighted
+    curve_out_ref[...] = curve
 
 
 def hessian_kernel(
@@ -252,16 +245,14 @@
 
 
 def combine_kernel(
-    own_ref, own_back_ref, even_ref, odd_ref, mate_ref, curve_ref, dir_ref, terms_ref, field_ref, map_ref, hess_ref,
-    out_ref,
+    base_ref, even_ref, odd_ref, mate_ref, curve_ref, terms_ref, field_ref, map_ref, hess_ref, out_ref
 ):
     blocks, rows, bs = field_ref.shape
     count = mate_ref.shape[1]
-    weights_ref, inv_diag_ref = terms_ref.at[0], terms_ref.at[1]
+    inv_diag_ref = terms_ref.at[1]
     own_part = jnp.where(is_even("space"), 1.0, 0.0)
     arrived = lambda c: even_ref[c].astype(F32) + odd_ref[c].astype(F32) + own_part * mate_ref[c].astype(F32)
     from_last = arrived(blocks)
-    curve = curve_ref[...]
     cross = jnp.zeros((rows, bs), F32)
     square = jnp.zeros((rows, bs), F32)
     summed = jnp.zeros(out_ref.shape, F32)
@@ -269,12 +260,9 @@
         parts = []
         for c in range(b, b + PAIR):
             last = jnp.broadcast_to(from_last[c : c + 1], (rows - count, bs))
-            direction = dir_ref[c]
-            weighted = weights_ref[c : c + 1] * direction
-            hess = own_ref[2 * blocks + c] + own_back_ref[c] + jnp.concatenate([arrived(c), last], axis=0) + weighted
+            hess = base_ref[c] + jnp.concatenate([arrived(c), last], axis=0)
             hess_ref[c] = hess
             scaled = hess * inv_diag_ref[c : c + 1]
-            curve += weighted * direction
             cross += field_ref[c] * scaled
             square += hess * scaled
             parts.append(scaled.astype(BF16))
@@ -282,7 +270,7 @@
             jnp.concatenate(parts, axis=1), map_ref[b * bs : (b + PAIR) * bs], preferred_element_type=F32
         )
     out_ref[...] = summed
-    for i, acc in enumerate((curve, cross, square)):
+    for i, acc in enumerate((curve_ref[...], cross, square)):
         out_ref[count + 1 + i : count + 2 + i] = as_row(jnp.sum(acc, axis=1, keepdims=True), out_ref.shape[1])
 
 
@@ -386,24 +374,21 @@
             in_hbm(factor), in_hbm(inner_inverse), msg
         )
 
-    def turn(msg, loaded, inner):
-        shape = (blocks, factor.shape[1] * bs, bs)
-        return loaded, inner, call(turn_kernel, [vmem, pl.ANY], [(shape, BF16)])(loaded, msg)
-
-    sums, (factor, inner_inverse, turned) = total(partial, "space", [load, turn])
+    sums, (factor, inner_inverse) = total(partial, "space", load)
     direction, rounded, product = call(
         direction_kernel, [vmem] * 5, [field, packed, sum_shape], [vmem((blocks, bs), F32)]
     )(sums, inner_inverse, *points)
-    far_odd = shifted(rounded, "space", 2, 1)
+    near = sent(rounded, "space", 1)
+    far_even = sent(rounded, "space", 2, (0,))
+    turned = call(turn_kernel, [vmem, pl.ANY], [((blocks, factor.shape[1] * bs, bs), BF16)])(factor, rounded)
     around = ((3 * blocks, rows, bs), F32)
-    own_image, again, zeros = call(
+    own_image, zeros = call(
         functools.partial(own_image_kernel, tall),
         [vmem] * 2,
-        [((blocks, tall, bs), F32), packed, around],
+        [((blocks, tall, bs), F32), around],
         [vmem((blocks, bs), F32)],
     )(rounded, turned)
-    far_even = shifted(again, "space", 2, 0)
-    near = swapped(call(pass_on_kernel, [vmem] * 2, [packed])(rounded, far_odd), "space")
+    far_odd = sent(call(pass_on_kernel, [vmem, pl.ANY], [packed])(near, own_image), "space", 1, (0,))
     back_far, back_near, back_own, curve, image = call(
         functools.partial(hessian_kernel, rows),
         [smem] + [vmem] * 8,
@@ -412,12 +397,12 @@
         aliases={8: 2},
     )(cond_ids.T, factor, turned, own_image, near, far_even, far_odd, rounded, zeros)
     mate = swapped(back_near, "space")
-    from_even = shifted(back_far, "space", -2, 0)
-    from_odd = shifted(call(join_kernel, [vmem] * 2, [packed])(back_far, mate), "space", -2, 1)
-    own_back = call(functools.partial(own_back_kernel, rows), [vmem] * 2, [field])(image, factor)
-    hess, partial = call(combine_kernel, [vmem] * 10, [field, sum_shape])(
-        back_own, own_back, from_even, from_odd, mate, curve, direction, *points
+    from_even = sent(back_far, "space", -2, (0,))
+    from_odd = sent(call(join_kernel, [vmem] * 2, [packed])(back_far, mate), "space", -2, (1,))
+    base, curve = call(functools.partial(own_back_kernel, rows), [vmem] * 6, [field, ((rows, bs), F32)])(
+        image, factor, back_own, curve, direction, terms
     )
+    hess, partial = call(combine_kernel, [vmem] * 8, [field, sum_shape])(base, from_even, from_odd, mate, curve, *points)
     hess_sums, _ = total(partial, "space")
     whole = ((count + 1, blocks * bs), F32)
     scratch = [vmem(*whole)] * 3 + [pltpu.SemaphoreType.DMA((3 * OUT_PARTS,))]

time: 55.4 us -> 55.9 us (level)
  starting transfers between devices: 24 us -> 24.6 us
    ppermute x4 -> x5, starting transfers between devices: 5.57 us -> 9.07 us  [sent(): lax.ppermute(block, axis, [(i, i + distance) for i in devices if i % 2 in...]
    ppermute x2 -> x1, starting transfers between devices: 3.31 us -> 0.39 us  [swapped(): lax.ppermute(block, axis, [(i, i ^ 1) for i in range(lax.axis_size(axis))])]
    ppermute x10, waiting for transfers between devices: 8.17 us -> 9.03 us  [total(): lax.ppermute(msg, axis, [(j, j ^ d) for j in range(n)])]
    ppermute x4 -> x5, waiting for transfers between devices: 9.61 us -> 9.04 us  [sent(): lax.ppermute(block, axis, [(i, i + distance) for i in devices if i % 2 in...]
  transfers between devices with their start and end apart: 16 -> 16, of which waited for: 9 -> 10; matrix products, arithmetic and copies ran while one was open for 0% -> 0% of each run, Pallas kernels for 8% -> 8%
where the time goes in v8:
time: 55.9 us; the launch traced here: 55.6 us
  starting transfers between devices  24.6 us (44%)
  waiting for transfers between devices  18.1 us (32%)
  Pallas kernels  12.1 us (22%)
  between operations  0.79 us (1%)
    ppermute x10, starting transfers between devices, total(): lax.ppermute(msg, axis, [(j, j ^ d) for j in range(n)])  15.1 us
    ppermute x5, starting transfers between devices, sent(): lax.ppermute(block, axis, [(i, i + distance) for i in devices if i % 2 in...  9.07 us
    ppermute x5, waiting for transfers between devices, sent(): lax.ppermute(block, axis, [(i, i + distance) for i in devices if i % 2 in...  9.04 us
    ppermute x10, waiting for transfers between devices, total(): lax.ppermute(msg, axis, [(j, j ^ d) for j in range(n)])  9.03 us
    pallas_call x1, Pallas kernels, load(): call(load_kernel, [pl.ANY] * 3, outs, [pltpu.SemaphoreType.DMA((2,))])  2.23 us
    pallas_call x1, Pallas kernels, body(): call(project_kernel, [pl.ANY] * 5, [sum_shape, ((2, blocks, bs), F32), fi...  2.15 us
    pallas_call x1, Pallas kernels, body(): call(functools.partial(hessian_kernel, rows), [smem] + [vmem] * 8, [packe...  2.15 us
    pallas_call x1, Pallas kernels, body(): call(finish_kernel, [vmem] * 9, [whole] * 3, scratch, keep=False)  1.85 us
  transfers between devices with their start and end apart: 16, of which 10 were waited for; matrix products, arithmetic and copies ran while one was open for 0% of the time, Pallas kernels for 8%

profile of v8, /device:TPU:0, one launch (start us, length us, event | category | flops | bytes accessed | tf_op | source)
XLA Modules:
  0.0 55.6 jit_solution(10293928924230569709)
XLA Ops:
  0.6 2.2 %shard_map.103 = (f32[40,256]{1,0:T(8,128)S(1)}, f32[2,32,128]{2,1,0:T(8,128)S(1)}, f32[32,40,128]{2,1,0:T(8,128)S(1)}, bf16[4096,256]{1,0:T(8,128)(2,1)S(1)}) custom-call(f32[32,128]{1,0:T(8,128)} %bitcast.5, s32[32,128]{1,0:T(8,128)} %bitcast.6, f32[32,128]{1,0:T(8,128)} %bitcast.7, f32[32,4096]{1,0:T(8,128)} %probes_hbm.1, bf16[4096,256]{1,0:T(8,128)(2,1)} %map_hbm.1), custom_call_target="tpu_custom_call" | custom-call | tf_op jit(solution)/shard_map/pallas_call | solution.py:357
  2.8 0.5 collective-permute-start
  3.3 0.9 %collective-permute-done.refs_0_ = f32[40,256]{1,0:T(8,128)S(1)} collective-permute-done((f32[40,256]{1,0:T(8,128)S(1)}, f32[40,256]{1,0:T(8,128)S(1)}, u32[]{:S(2)}, u32[]{:S(2)}) %collective-permute-start) | collective-permute-done | bytes 40992 | tf_op jit(solution)/shard_map/ppermute | solution.py:76
  4.2 2.7 %collective-permute-start.1 = (bf16[40,256]{1,0:T(8,128)(2,1)S(1)}, bf16[40,256]{1,0:T(8,128)(2,1)S(1)}, u32[]{:S(2)}, u32[]{:S(2)}) collective-permute-start(bf16[40,256]{1,0:T(8,128)(2,1)S(1)} %get-tuple-element.33), channel_id=1, source_target_pairs={{0,3},{1,2},{2,1},{3,0},{4,7},{5,6},{6,5},{7,4},{8,11},{9,10},{10,... | collective-permute-start | bytes 61448 | tf_op jit(solution)/shard_map/ppermute | solution.py:76
  6.9 1.5 %collective-permute-done.1.refs_0_ = bf16[40,256]{1,0:T(8,128)(2,1)S(1)} collective-permute-done((bf16[40,256]{1,0:T(8,128)(2,1)S(1)}, bf16[40,256]{1,0:T(8,128)(2,1)S(1)}, u32[]{:S(2)}, u32[]{:S(2)}) %collective-permute-start.1) | collective-permute-done | bytes 20512 | tf_op jit(solution)/shard_map/ppermute | solution.py:76
  8.4 3.9 %collective-permute-start.4 = (bf16[40,256]{1,0:T(8,128)(2,1)S(1)}, bf16[40,256]{1,0:T(8,128)(2,1)S(1)}, u32[]{:S(2)}, u32[]{:S(2)}) collective-permute-start(bf16[40,256]{1,0:T(8,128)(2,1)S(1)} %get-tuple-element.35.after_ref), channel_id=1, source_target_pairs={{0,13},{1,12},{2,15},{3,14},{4,9},{5,8},{6,11},{7,10},{8,5},{9,4},... | collective-permute-start | bytes 61448 | tf_op jit(solution)/shard_map/ppermute | solution.py:76
  12.3 0.0 collective-permute-start.3
  12.3 0.6 %collective-permute-start.2 = (bf16[40,256]{1,0:T(8,128)(2,1)S(1)}, bf16[40,256]{1,0:T(8,128)(2,1)S(1)}, u32[]{:S(2)}, u32[]{:S(2)}) collective-permute-start(bf16[40,256]{1,0:T(8,128)(2,1)S(1)} %get-tuple-element.35.after_ref), channel_id=1, source_target_pairs={{0,5},{1,4},{2,7},{3,6},{4,1},{5,0},{6,3},{7,2},{8,13},{9,12},{10,... | collective-permute-start | bytes 61448 | tf_op jit(solution)/shard_map/ppermute | solution.py:76
  12.9 2.2 %shard_map.106 = (bf16[32,4,128,128]{3,2,1,0:T(8,128)(2,1)S(1)}, f32[256,256]{1,0:T(8,128)S(1)}) custom-call(bf16[32,4,128,128]{3,2,1,0:T(8,128)(2,1)} %factor_hbm.1, f32[256,256]{1,0:T(8,128)} %inner_hbm.1, bf16[40,256]{1,0:T(8,128)(2,1)S(1)} %get-tuple-element.35.after_ref), custom_call_target="tpu_custom_call" | custom-call | tf_op jit(solution)/shard_map/pallas_call | solution.py:373
  15.1 0.0 collective-permute-done.4.refs_2_
  15.1 1.3 %collective-permute-done.3.refs_1_ = bf16[40,256]{1,0:T(8,128)(2,1)S(1)} collective-permute-done((bf16[40,256]{1,0:T(8,128)(2,1)S(1)}, bf16[40,256]{1,0:T(8,128)(2,1)S(1)}, u32[]{:S(2)}, u32[]{:S(2)}) %collective-permute-start.3) | collective-permute-done | bytes 20512 | tf_op jit(solution)/shard_map/ppermute | solution.py:76
  16.4 0.0 collective-permute-done.2.refs_0_
  16.4 1.0 %shard_map.108 = (f32[32,40,128]{2,1,0:T(8,128)S(1)}, bf16[33,32,128]{2,1,0:T(8,128)(2,1)S(1)}, f32[40,256]{1,0:T(8,128)S(1)}) custom-call(f32[40,256]{1,0:T(8,128)S(1)} %shard_map.107.sums_ref, f32[256,256]{1,0:T(8,128)S(1)} %get-tuple-element.37.refs_4_.inner_ref, f32[2,32,128]{2,1,0:T(8,128)S(1)} %get-tuple-element.38.terms_ref, ...), custom_call_target="tpu_custom_call" | custom-call | tf_op jit(solution)/shard_map/pallas_call | solution.py:378
  17.4 2.3 %collective-permute-start.5 = (bf16[33,32,128]{2,1,0:T(8,128)(2,1)S(1)}, bf16[33,32,128]{2,1,0:T(8,128)(2,1)S(1)}, u32[]{:S(2)}, u32[]{:S(2)}) collective-permute-start(bf16[33,32,128]{2,1,0:T(8,128)(2,1)S(1)} %get-tuple-element.42.after_ref.own_ref), channel_id=1, source_target_pairs={{0,1},{1,2},{2,3},{3,4},{4,5},{5,6},{6,7},{7,8},{8,9},{9,10},{10,1... | collective-permute-start | bytes 811016 | tf_op jit(solution)/shard_map/ppermute | solution.py:18
  19.6 3.4 %collective-permute-start.6 = (bf16[33,32,128]{2,1,0:T(8,128)(2,1)S(1)}, bf16[33,32,128]{2,1,0:T(8,128)(2,1)S(1)}, u32[]{:S(2)}, u32[]{:S(2)}) collective-permute-start(bf16[33,32,128]{2,1,0:T(8,128)(2,1)S(1)} %get-tuple-element.42.after_ref.own_ref), channel_id=1, source_target_pairs={{0,2},{2,4},{4,6},{6,8},{8,10},{10,12},{12,14},{16,18},{18,20},{20... | collective-permute-start | bytes 811016 | tf_op jit(solution)/shard_map/ppermute | solution.py:18
  23.0 1.1 %shard_map.109.turned_ref = bf16[32,512,128]{2,1,0:T(8,128)(2,1)S(1)} custom-call(bf16[32,4,128,128]{3,2,1,0:T(8,128)(2,1)S(1)} %get-tuple-element.36.refs_3_.factor_ref, bf16[33,32,128]{2,1,0:T(8,128)(2,1)S(1)} %get-tuple-element.42.after_ref.own_ref), custom_call_target="tpu_custom_call" | custom-call | tf_op jit(solution)/shard_map/pallas_call | solution.py:383
  24.2 0.0 copy-start
  24.2 0.5 shard_map.110
  24.7 0.0 collective-permute-done.5.near_ref
  24.8 1.4 %collective-permute-start.7 = (bf16[33,32,128]{2,1,0:T(8,128)(2,1)S(1)}, bf16[33,32,128]{2,1,0:T(8,128)(2,1)S(1)}, u32[]{:S(2)}, u32[]{:S(2)}) collective-permute-start(bf16[33,32,128]{2,1,0:T(8,128)(2,1)S(1)} %shard_map.111), channel_id=1, source_target_pairs={{0,1},{2,3},{4,5},{6,7},{8,9},{10,11},{12,13},{14,15},{16,17},{18,... | collective-permute-start | bytes 811016 | tf_op jit(solution)/shard_map/ppermute | solution.py:18
  26.2 0.8 %collective-permute-done.6.far_even_ref = bf16[33,32,128]{2,1,0:T(8,128)(2,1)S(1)} collective-permute-done((bf16[33,32,128]{2,1,0:T(8,128)(2,1)S(1)}, bf16[33,32,128]{2,1,0:T(8,128)(2,1)S(1)}, u32[]{:S(2)}, u32[]{:S(2)}) %collective-permute-start.6) | collective-permute-done | bytes 270368 | tf_op jit(solution)/shard_map/ppermute | solution.py:18
  27.1 0.3 collective-permute-done.7.far_odd_ref
  27.4 0.0 copy-done
  27.4 2.1 %shard_map.112 = (bf16[33,32,128]{2,1,0:T(8,128)(2,1)S(1)}, bf16[33,32,128]{2,1,0:T(8,128)(2,1)S(1)}, f32[96,40,128]{2,1,0:T(8,128)S(1)}, f32[40,128]{1,0:T(8,128)S(1)}, bf16[32,48,128]{2,1,0:T(8,128)(2,1)S(1)}) custom-call(s32[3,32]{1,0:T(4,128)S(1)} %bitcast.4, ...), custom_call_target="tpu_custom_call", output_to_operand_aliasing={{2}: (8, {})} | custom-call | tf_op jit(solution)/shard_map/pallas_call | solution.py:392
  29.5 0.4 collective-permute-start.9
  29.9 1.3 %collective-permute-start.8 = (bf16[33,32,128]{2,1,0:T(8,128)(2,1)S(1)}, bf16[33,32,128]{2,1,0:T(8,128)(2,1)S(1)}, u32[]{:S(2)}, u32[]{:S(2)}) collective-permute-start(bf16[33,32,128]{2,1,0:T(8,128)(2,1)S(1)} %get-tuple-element.50.back_far_ref), channel_id=1, source_target_pairs={{2,0},{4,2},{6,4},{8,6},{10,8},{12,10},{14,12},{18,16},{20,18},{22... | collective-permute-start | bytes 811016 | tf_op jit(solution)/shard_map/ppermute | solution.py:18
  31.2 0.0 collective-permute-done.9.got_ref.mate_ref
  31.2 0.1 shard_map.114
  31.3 0.7 %collective-permute-start.10 = (bf16[33,32,128]{2,1,0:T(8,128)(2,1)S(1)}, bf16[33,32,128]{2,1,0:T(8,128)(2,1)S(1)}, u32[]{:S(2)}, u32[]{:S(2)}) collective-permute-start(bf16[33,32,128]{2,1,0:T(8,128)(2,1)S(1)} %shard_map.114), channel_id=1, source_target_pairs={{3,1},{5,3},{7,5},{9,7},{11,9},{13,11},{15,13},{19,17},{21,19},{23... | collective-permute-start | bytes 811016 | tf_op jit(solution)/shard_map/ppermute | solution.py:18
  32.0 0.4 shard_map.113
  32.4 7.9 %collective-permute-done.8.even_ref = bf16[33,32,128]{2,1,0:T(8,128)(2,1)S(1)} collective-permute-done((bf16[33,32,128]{2,1,0:T(8,128)(2,1)S(1)}, bf16[33,32,128]{2,1,0:T(8,128)(2,1)S(1)}, u32[]{:S(2)}, u32[]{:S(2)}) %collective-permute-start.8) | collective-permute-done | bytes 270368 | tf_op jit(solution)/shard_map/ppermute | solution.py:18
  40.3 0.0 collective-permute-done.10.odd_ref
  40.3 0.5 shard_map.115
  40.8 0.7 %collective-permute-start.11 = (f32[40,256]{1,0:T(8,128)S(1)}, f32[40,256]{1,0:T(8,128)S(1)}, u32[]{:S(2)}, u32[]{:S(2)}) collective-permute-start(f32[40,256]{1,0:T(8,128)S(1)} %get-tuple-element.53.x_ref), channel_id=1, source_target_pairs={{0,1},{1,0},{2,3},{3,2},{4,5},{5,4},{6,7},{7,6},{8,9},{9,8},{10,11... | collective-permute-start | bytes 122888 | tf_op jit(solution)/shard_map/ppermute | solution.py:76
  41.6 0.9 %collective-permute-done.11.refs_0_ = f32[40,256]{1,0:T(8,128)S(1)} collective-permute-done((f32[40,256]{1,0:T(8,128)S(1)}, f32[40,256]{1,0:T(8,128)S(1)}, u32[]{:S(2)}, u32[]{:S(2)}) %collective-permute-start.11) | collective-permute-done | bytes 40992 | tf_op jit(solution)/shard_map/ppermute | solution.py:76
  42.4 2.7 %collective-permute-start.12 = (bf16[40,256]{1,0:T(8,128)(2,1)S(1)}, bf16[40,256]{1,0:T(8,128)(2,1)S(1)}, u32[]{:S(2)}, u32[]{:S(2)}) collective-permute-start(bf16[40,256]{1,0:T(8,128)(2,1)S(1)} %get-tuple-element.55), channel_id=1, source_target_pairs={{0,3},{1,2},{2,1},{3,0},{4,7},{5,6},{6,5},{7,4},{8,11},{9,10},{10,... | collective-permute-start | bytes 61448 | tf_op jit(solution)/shard_map/ppermute | solution.py:76
  45.2 1.5 %collective-permute-done.12.refs_0_ = bf16[40,256]{1,0:T(8,128)(2,1)S(1)} collective-permute-done((bf16[40,256]{1,0:T(8,128)(2,1)S(1)}, bf16[40,256]{1,0:T(8,128)(2,1)S(1)}, u32[]{:S(2)}, u32[]{:S(2)}) %collective-permute-start.12) | collective-permute-done | bytes 20512 | tf_op jit(solution)/shard_map/ppermute | solution.py:76
  46.7 2.5 %collective-permute-start.15 = (bf16[40,256]{1,0:T(8,128)(2,1)S(1)}, bf16[40,256]{1,0:T(8,128)(2,1)S(1)}, u32[]{:S(2)}, u32[]{:S(2)}) collective-permute-start(bf16[40,256]{1,0:T(8,128)(2,1)S(1)} %get-tuple-element.57), channel_id=1, source_target_pairs={{0,13},{1,12},{2,15},{3,14},{4,9},{5,8},{6,11},{7,10},{8,5},{9,4},... | collective-permute-start | bytes 61448 | tf_op jit(solution)/shard_map/ppermute | solution.py:76
  49.2 0.0 collective-permute-start.14
  49.2 1.4 %collective-permute-start.13 = (bf16[40,256]{1,0:T(8,128)(2,1)S(1)}, bf16[40,256]{1,0:T(8,128)(2,1)S(1)}, u32[]{:S(2)}, u32[]{:S(2)}) collective-permute-start(bf16[40,256]{1,0:T(8,128)(2,1)S(1)} %get-tuple-element.57), channel_id=1, source_target_pairs={{0,5},{1,4},{2,7},{3,6},{4,1},{5,0},{6,3},{7,2},{8,13},{9,12},{10,... | collective-permute-start | bytes 61448 | tf_op jit(solution)/shard_map/ppermute | solution.py:76
  50.6 1.1 %collective-permute-done.15.refs_2_ = bf16[40,256]{1,0:T(8,128)(2,1)S(1)} collective-permute-done((bf16[40,256]{1,0:T(8,128)(2,1)S(1)}, bf16[40,256]{1,0:T(8,128)(2,1)S(1)}, u32[]{:S(2)}, u32[]{:S(2)}) %collective-permute-start.15) | collective-permute-done | bytes 20512 | tf_op jit(solution)/shard_map/ppermute | solution.py:76
  51.8 1.9 %collective-permute-done.14.refs_1_ = bf16[40,256]{1,0:T(8,128)(2,1)S(1)} collective-permute-done((bf16[40,256]{1,0:T(8,128)(2,1)S(1)}, bf16[40,256]{1,0:T(8,128)(2,1)S(1)}, u32[]{:S(2)}, u32[]{:S(2)}) %collective-permute-start.14) | collective-permute-done | bytes 20512 | tf_op jit(solution)/shard_map/ppermute | solution.py:76
  53.7 0.0 collective-permute-done.13.refs_0_
  53.7 1.8 %shard_map.119 = (f32[33,4096]{1,0:T(8,128)}, f32[33,4096]{1,0:T(8,128)}, f32[33,4096]{1,0:T(8,128)}) custom-call(f32[40,256]{1,0:T(8,128)S(1)} %shard_map.107.sums_ref, f32[40,256]{1,0:T(8,128)S(1)} %get-tuple-element.41.product_ref, f32[40,256]{1,0:T(8,128)S(1)} %shard_map.118.hess_sums_ref, f32[256,256]{1,0:T(8,128)S(1)} %get-tuple-element.37.refs_4_.inner_ref, ...), custom_call_target="tpu_custom_call" | custom-call | tf_op jit(solution)/shard_map/pallas_call | solution.py:409
  (7 shorter events, 0.1 us)
Async XLA Ops:
  2.8 1.4 %collective-permute-start = (f32[40,256]{1,0:T(8,128)S(1)}, f32[40,256]{1,0:T(8,128)S(1)}, u32[]{:S(2)}, u32[]{:S(2)}) collective-permute-start(f32[40,256]{1,0:T(8,128)S(1)} %get-tuple-element.31.x_ref), channel_id=1, source_target_pairs={{0,1},{1,0},{2,3},{3,2},{4,5},{5,4},{6,7},{7,6},{8,9},{9,8},{10,11... | collective-permute-start | bytes 122888 | tf_op jit(solution)/shard_map/ppermute | solution.py:76
  4.2 4.1 %collective-permute-start.1 = (bf16[40,256]{1,0:T(8,128)(2,1)S(1)}, bf16[40,256]{1,0:T(8,128)(2,1)S(1)}, u32[]{:S(2)}, u32[]{:S(2)}) collective-permute-start(bf16[40,256]{1,0:T(8,128)(2,1)S(1)} %get-tuple-element.33), channel_id=1, source_target_pairs={{0,3},{1,2},{2,1},{3,0},{4,7},{5,6},{6,5},{7,4},{8,11},{9,10},{10,... | collective-permute-start | bytes 61448 | tf_op jit(solution)/shard_map/ppermute | solution.py:76
  8.4 6.7 %collective-permute-start.4 = (bf16[40,256]{1,0:T(8,128)(2,1)S(1)}, bf16[40,256]{1,0:T(8,128)(2,1)S(1)}, u32[]{:S(2)}, u32[]{:S(2)}) collective-permute-start(bf16[40,256]{1,0:T(8,128)(2,1)S(1)} %get-tuple-element.35.after_ref), channel_id=1, source_target_pairs={{0,13},{1,12},{2,15},{3,14},{4,9},{5,8},{6,11},{7,10},{8,5},{9,4},... | collective-permute-start | bytes 61448 | tf_op jit(solution)/shard_map/ppermute | solution.py:76
  12.3 4.1 %collective-permute-start.3 = (bf16[40,256]{1,0:T(8,128)(2,1)S(1)}, bf16[40,256]{1,0:T(8,128)(2,1)S(1)}, u32[]{:S(2)}, u32[]{:S(2)}) collective-permute-start(bf16[40,256]{1,0:T(8,128)(2,1)S(1)} %get-tuple-element.35.after_ref), channel_id=1, source_target_pairs={{0,9},{1,8},{2,11},{3,10},{4,13},{5,12},{6,15},{7,14},{8,1},{9,0},... | collective-permute-start | bytes 61448 | tf_op jit(solution)/shard_map/ppermute | solution.py:76
  12.3 4.1 %collective-permute-start.2 = (bf16[40,256]{1,0:T(8,128)(2,1)S(1)}, bf16[40,256]{1,0:T(8,128)(2,1)S(1)}, u32[]{:S(2)}, u32[]{:S(2)}) collective-permute-start(bf16[40,256]{1,0:T(8,128)(2,1)S(1)} %get-tuple-element.35.after_ref), channel_id=1, source_target_pairs={{0,5},{1,4},{2,7},{3,6},{4,1},{5,0},{6,3},{7,2},{8,13},{9,12},{10,... | collective-permute-start | bytes 61448 | tf_op jit(solution)/shard_map/ppermute | solution.py:76
  17.4 7.4 %collective-permute-start.5 = (bf16[33,32,128]{2,1,0:T(8,128)(2,1)S(1)}, bf16[33,32,128]{2,1,0:T(8,128)(2,1)S(1)}, u32[]{:S(2)}, u32[]{:S(2)}) collective-permute-start(bf16[33,32,128]{2,1,0:T(8,128)(2,1)S(1)} %get-tuple-element.42.after_ref.own_ref), channel_id=1, source_target_pairs={{0,1},{1,2},{2,3},{3,4},{4,5},{5,6},{6,7},{7,8},{8,9},{9,10},{10,1... | collective-permute-start | bytes 811016 | tf_op jit(solution)/shard_map/ppermute | solution.py:18
  19.6 7.4 %collective-permute-start.6 = (bf16[33,32,128]{2,1,0:T(8,128)(2,1)S(1)}, bf16[33,32,128]{2,1,0:T(8,128)(2,1)S(1)}, u32[]{:S(2)}, u32[]{:S(2)}) collective-permute-start(bf16[33,32,128]{2,1,0:T(8,128)(2,1)S(1)} %get-tuple-element.42.after_ref.own_ref), channel_id=1, source_target_pairs={{0,2},{2,4},{4,6},{6,8},{8,10},{10,12},{12,14},{16,18},{18,20},{20... | collective-permute-start | bytes 811016 | tf_op jit(solution)/shard_map/ppermute | solution.py:18
  24.2 3.2 %copy-start = (s32[32,3]{0,1:T(4,128)S(1)}, s32[32,3]{0,1:T(4,128)}, u32[]{:S(2)}) copy-start(s32[32,3]{0,1:T(4,128)} %param.13) | copy-start | bytes 1156
  24.8 2.6 %collective-permute-start.7 = (bf16[33,32,128]{2,1,0:T(8,128)(2,1)S(1)}, bf16[33,32,128]{2,1,0:T(8,128)(2,1)S(1)}, u32[]{:S(2)}, u32[]{:S(2)}) collective-permute-start(bf16[33,32,128]{2,1,0:T(8,128)(2,1)S(1)} %shard_map.111), channel_id=1, source_target_pairs={{0,1},{2,3},{4,5},{6,7},{8,9},{10,11},{12,13},{14,15},{16,17},{18,... | collective-permute-start | bytes 811016 | tf_op jit(solution)/shard_map/ppermute | solution.py:18
  29.5 1.7 %collective-permute-start.9 = (bf16[33,32,128]{2,1,0:T(8,128)(2,1)S(1)}, bf16[33,32,128]{2,1,0:T(8,128)(2,1)S(1)}, u32[]{:S(2)}, u32[]{:S(2)}) collective-permute-start(bf16[33,32,128]{2,1,0:T(8,128)(2,1)S(1)} %get-tuple-element.51), channel_id=1, source_target_pairs={{0,1},{1,0},{2,3},{3,2},{4,5},{5,4},{6,7},{7,6},{8,9},{9,8},{10,11... | collective-permute-start | bytes 811016 | tf_op jit(solution)/shard_map/ppermute | solution.py:22
  29.9 10.4 %collective-permute-start.8 = (bf16[33,32,128]{2,1,0:T(8,128)(2,1)S(1)}, bf16[33,32,128]{2,1,0:T(8,128)(2,1)S(1)}, u32[]{:S(2)}, u32[]{:S(2)}) collective-permute-start(bf16[33,32,128]{2,1,0:T(8,128)(2,1)S(1)} %get-tuple-element.50.back_far_ref), channel_id=1, source_target_pairs={{2,0},{4,2},{6,4},{8,6},{10,8},{12,10},{14,12},{18,16},{20,18},{22... | collective-permute-start | bytes 811016 | tf_op jit(solution)/shard_map/ppermute | solution.py:18
  31.3 9.0 %collective-permute-start.10 = (bf16[33,32,128]{2,1,0:T(8,128)(2,1)S(1)}, bf16[33,32,128]{2,1,0:T(8,128)(2,1)S(1)}, u32[]{:S(2)}, u32[]{:S(2)}) collective-permute-start(bf16[33,32,128]{2,1,0:T(8,128)(2,1)S(1)} %shard_map.114), channel_id=1, source_target_pairs={{3,1},{5,3},{7,5},{9,7},{11,9},{13,11},{15,13},{19,17},{21,19},{23... | collective-permute-start | bytes 811016 | tf_op jit(solution)/shard_map/ppermute | solution.py:18
  40.8 1.6 %collective-permute-start.11 = (f32[40,256]{1,0:T(8,128)S(1)}, f32[40,256]{1,0:T(8,128)S(1)}, u32[]{:S(2)}, u32[]{:S(2)}) collective-permute-start(f32[40,256]{1,0:T(8,128)S(1)} %get-tuple-element.53.x_ref), channel_id=1, source_target_pairs={{0,1},{1,0},{2,3},{3,2},{4,5},{5,4},{6,7},{7,6},{8,9},{9,8},{10,11... | collective-permute-start | bytes 122888 | tf_op jit(solution)/shard_map/ppermute | solution.py:76
  42.4 4.2 %collective-permute-start.12 = (bf16[40,256]{1,0:T(8,128)(2,1)S(1)}, bf16[40,256]{1,0:T(8,128)(2,1)S(1)}, u32[]{:S(2)}, u32[]{:S(2)}) collective-permute-start(bf16[40,256]{1,0:T(8,128)(2,1)S(1)} %get-tuple-element.55), channel_id=1, source_target_pairs={{0,3},{1,2},{2,1},{3,0},{4,7},{5,6},{6,5},{7,4},{8,11},{9,10},{10,... | collective-permute-start | bytes 61448 | tf_op jit(solution)/shard_map/ppermute | solution.py:76
  46.7 5.1 %collective-permute-start.15 = (bf16[40,256]{1,0:T(8,128)(2,1)S(1)}, bf16[40,256]{1,0:T(8,128)(2,1)S(1)}, u32[]{:S(2)}, u32[]{:S(2)}) collective-permute-start(bf16[40,256]{1,0:T(8,128)(2,1)S(1)} %get-tuple-element.57), channel_id=1, source_target_pairs={{0,13},{1,12},{2,15},{3,14},{4,9},{5,8},{6,11},{7,10},{8,5},{9,4},... | collective-permute-start | bytes 61448 | tf_op jit(solution)/shard_map/ppermute | solution.py:76
  49.2 4.4 %collective-permute-start.14 = (bf16[40,256]{1,0:T(8,128)(2,1)S(1)}, bf16[40,256]{1,0:T(8,128)(2,1)S(1)}, u32[]{:S(2)}, u32[]{:S(2)}) collective-permute-start(bf16[40,256]{1,0:T(8,128)(2,1)S(1)} %get-tuple-element.57), channel_id=1, source_target_pairs={{0,9},{1,8},{2,11},{3,10},{4,13},{5,12},{6,15},{7,14},{8,1},{9,0},... | collective-permute-start | bytes 61448 | tf_op jit(solution)/shard_map/ppermute | solution.py:76
  49.2 4.4 %collective-permute-start.13 = (bf16[40,256]{1,0:T(8,128)(2,1)S(1)}, bf16[40,256]{1,0:T(8,128)(2,1)S(1)}, u32[]{:S(2)}, u32[]{:S(2)}) collective-permute-start(bf16[40,256]{1,0:T(8,128)(2,1)S(1)} %get-tuple-element.57), channel_id=1, source_target_pairs={{0,5},{1,4},{2,7},{3,6},{4,1},{5,0},{6,3},{7,2},{8,13},{9,12},{10,... | collective-permute-start | bytes 61448 | tf_op jit(solution)/shard_map/ppermute | solution.py:76

commit v9 on v8

--- a/solution.py
+++ b/solution.py
@@ -189,8 +189,14 @@
         image_ref[b] = jnp.dot(tall_block(own_ref, last_ref, b, tall), turned_ref[b, :bs], preferred_element_type=F32)
 
 
-def pass_on_kernel(near_ref, after_ref, out_ref):
-    out_ref[...] = near_ref[...]
+def pass_on_kernel(own_ref, far_ref, after_ref, out_ref):
+    @pl.when(is_even("space"))
+    def _():
+        out_ref[...] = own_ref[...]
+
+    @pl.when(jnp.logical_not(is_even("space")))
+    def _():
+        out_ref[...] = far_ref[...]
 
 
 def join_kernel(back_far_ref, got_ref, out_ref):
@@ -378,7 +384,7 @@
     direction, rounded, product = call(
         direction_kernel, [vmem] * 5, [field, packed, sum_shape], [vmem((blocks, bs), F32)]
     )(sums, inner_inverse, *points)
-    near = sent(rounded, "space", 1)
+    far_odd = sent(rounded, "space", 2, (1,))
     far_even = sent(rounded, "space", 2, (0,))
     turned = call(turn_kernel, [vmem, pl.ANY], [((blocks, factor.shape[1] * bs, bs), BF16)])(factor, rounded)
     around = ((3 * blocks, rows, bs), F32)
@@ -388,7 +394,7 @@
         [((blocks, tall, bs), F32), around],
         [vmem((blocks, bs), F32)],
     )(rounded, turned)
-    far_odd = sent(call(pass_on_kernel, [vmem, pl.ANY], [packed])(near, own_image), "space", 1, (0,))
+    near = swapped(call(pass_on_kernel, [vmem, vmem, pl.ANY], [packed])(rounded, far_odd, own_image), "space")
     back_far, back_near, back_own, curve, image = call(
         functools.partial(hessian_kernel, rows),
         [smem] + [vmem] * 8,

time: 55.9 us -> 55.8 us (level)
    ppermute x5 -> x4, starting transfers between devices: 9.07 us -> 6.05 us  [sent(): lax.ppermute(block, axis, [(i, i + distance) for i in devices if i % 2 in...]
    ppermute x1 -> x2, starting transfers between devices: 0.39 us -> 3.03 us  [swapped(): lax.ppermute(block, axis, [(i, i ^ 1) for i in range(lax.axis_size(axis))])]
    ppermute x5 -> x4, waiting for transfers between devices: 9.04 us -> 9.44 us  [sent(): lax.ppermute(block, axis, [(i, i + distance) for i in devices if i % 2 in...]
  transfers between devices with their start and end apart: 16 -> 16, of which waited for: 10 -> 9; matrix products, arithmetic and copies ran while one was open for 0% -> 0% of each run, Pallas kernels for 8% -> 8%
where the time goes in v9:
time: 55.8 us; the launch traced here: 55.5 us
  starting transfers between devices  24.4 us (44%)
  waiting for transfers between devices  18.2 us (33%)
  Pallas kernels  12.1 us (22%)
  between operations  0.78 us (1%)
    ppermute x10, starting transfers between devices, total(): lax.ppermute(msg, axis, [(j, j ^ d) for j in range(n)])  15.4 us
    ppermute x4, waiting for transfers between devices, sent(): lax.ppermute(block, axis, [(i, i + distance) for i in devices if i % 2 in...  9.44 us
    ppermute x10, waiting for transfers between devices, total(): lax.ppermute(msg, axis, [(j, j ^ d) for j in range(n)])  8.71 us
    ppermute x4, starting transfers between devices, sent(): lax.ppermute(block, axis, [(i, i + distance) for i in devices if i % 2 in...  6.05 us
    ppermute x2, starting transfers between devices, swapped(): lax.ppermute(block, axis, [(i, i ^ 1) for i in range(lax.axis_size(axis))])  3.03 us
    pallas_call x1, Pallas kernels, load(): call(load_kernel, [pl.ANY] * 3, outs, [pltpu.SemaphoreType.DMA((2,))])  2.23 us
    pallas_call x1, Pallas kernels, body(): call(functools.partial(hessian_kernel, rows), [smem] + [vmem] * 8, [packe...  2.15 us
    pallas_call x1, Pallas kernels, body(): call(project_kernel, [pl.ANY] * 5, [sum_shape, ((2, blocks, bs), F32), fi...  2.15 us
  transfers between devices with their start and end apart: 16, of which 9 were waited for; matrix products, arithmetic and copies ran while one was open for 0% of the time, Pallas kernels for 8%

profile of v9, /device:TPU:0, one launch (start us, length us, event | category | flops | bytes accessed | tf_op | source)
XLA Modules:
  0.0 55.5 jit_solution(10450920153474347241)
XLA Ops:
  0.6 2.2 %shard_map.103 = (f32[40,256]{1,0:T(8,128)S(1)}, f32[2,32,128]{2,1,0:T(8,128)S(1)}, f32[32,40,128]{2,1,0:T(8,128)S(1)}, bf16[4096,256]{1,0:T(8,128)(2,1)S(1)}) custom-call(f32[32,128]{1,0:T(8,128)} %bitcast.5, s32[32,128]{1,0:T(8,128)} %bitcast.6, f32[32,128]{1,0:T(8,128)} %bitcast.7, f32[32,4096]{1,0:T(8,128)} %probes_hbm.1, bf16[4096,256]{1,0:T(8,128)(2,1)} %map_hbm.1), custom_call_target="tpu_custom_call" | custom-call | tf_op jit(solution)/shard_map/pallas_call | solution.py:363
  2.8 0.5 collective-permute-start
  3.3 0.9 %collective-permute-done.refs_0_ = f32[40,256]{1,0:T(8,128)S(1)} collective-permute-done((f32[40,256]{1,0:T(8,128)S(1)}, f32[40,256]{1,0:T(8,128)S(1)}, u32[]{:S(2)}, u32[]{:S(2)}) %collective-permute-start) | collective-permute-done | bytes 40992 | tf_op jit(solution)/shard_map/ppermute | solution.py:76
  4.2 2.7 %collective-permute-start.1 = (bf16[40,256]{1,0:T(8,128)(2,1)S(1)}, bf16[40,256]{1,0:T(8,128)(2,1)S(1)}, u32[]{:S(2)}, u32[]{:S(2)}) collective-permute-start(bf16[40,256]{1,0:T(8,128)(2,1)S(1)} %get-tuple-element.33), channel_id=1, source_target_pairs={{0,3},{1,2},{2,1},{3,0},{4,7},{5,6},{6,5},{7,4},{8,11},{9,10},{10,... | collective-permute-start | bytes 61448 | tf_op jit(solution)/shard_map/ppermute | solution.py:76
  6.9 1.5 %collective-permute-done.1.refs_0_ = bf16[40,256]{1,0:T(8,128)(2,1)S(1)} collective-permute-done((bf16[40,256]{1,0:T(8,128)(2,1)S(1)}, bf16[40,256]{1,0:T(8,128)(2,1)S(1)}, u32[]{:S(2)}, u32[]{:S(2)}) %collective-permute-start.1) | collective-permute-done | bytes 20512 | tf_op jit(solution)/shard_map/ppermute | solution.py:76
  8.4 3.9 %collective-permute-start.4 = (bf16[40,256]{1,0:T(8,128)(2,1)S(1)}, bf16[40,256]{1,0:T(8,128)(2,1)S(1)}, u32[]{:S(2)}, u32[]{:S(2)}) collective-permute-start(bf16[40,256]{1,0:T(8,128)(2,1)S(1)} %get-tuple-element.35.after_ref), channel_id=1, source_target_pairs={{0,13},{1,12},{2,15},{3,14},{4,9},{5,8},{6,11},{7,10},{8,5},{9,4},... | collective-permute-start | bytes 61448 | tf_op jit(solution)/shard_map/ppermute | solution.py:76
  12.3 0.0 collective-permute-start.3
  12.3 0.6 %collective-permute-start.2 = (bf16[40,256]{1,0:T(8,128)(2,1)S(1)}, bf16[40,256]{1,0:T(8,128)(2,1)S(1)}, u32[]{:S(2)}, u32[]{:S(2)}) collective-permute-start(bf16[40,256]{1,0:T(8,128)(2,1)S(1)} %get-tuple-element.35.after_ref), channel_id=1, source_target_pairs={{0,5},{1,4},{2,7},{3,6},{4,1},{5,0},{6,3},{7,2},{8,13},{9,12},{10,... | collective-permute-start | bytes 61448 | tf_op jit(solution)/shard_map/ppermute | solution.py:76
  12.9 2.2 %shard_map.106 = (bf16[32,4,128,128]{3,2,1,0:T(8,128)(2,1)S(1)}, f32[256,256]{1,0:T(8,128)S(1)}) custom-call(bf16[32,4,128,128]{3,2,1,0:T(8,128)(2,1)} %factor_hbm.1, f32[256,256]{1,0:T(8,128)} %inner_hbm.1, bf16[40,256]{1,0:T(8,128)(2,1)S(1)} %get-tuple-element.35.after_ref), custom_call_target="tpu_custom_call" | custom-call | tf_op jit(solution)/shard_map/pallas_call | solution.py:379
  15.1 0.0 collective-permute-done.4.refs_2_
  15.1 1.3 %collective-permute-done.3.refs_1_ = bf16[40,256]{1,0:T(8,128)(2,1)S(1)} collective-permute-done((bf16[40,256]{1,0:T(8,128)(2,1)S(1)}, bf16[40,256]{1,0:T(8,128)(2,1)S(1)}, u32[]{:S(2)}, u32[]{:S(2)}) %collective-permute-start.3) | collective-permute-done | bytes 20512 | tf_op jit(solution)/shard_map/ppermute | solution.py:76
  16.4 0.0 collective-permute-done.2.refs_0_
  16.4 1.0 %shard_map.108 = (f32[32,40,128]{2,1,0:T(8,128)S(1)}, bf16[33,32,128]{2,1,0:T(8,128)(2,1)S(1)}, f32[40,256]{1,0:T(8,128)S(1)}) custom-call(f32[40,256]{1,0:T(8,128)S(1)} %shard_map.107.sums_ref, f32[256,256]{1,0:T(8,128)S(1)} %get-tuple-element.37.refs_4_.inner_ref, f32[2,32,128]{2,1,0:T(8,128)S(1)} %get-tuple-element.38.terms_ref, ...), custom_call_target="tpu_custom_call" | custom-call | tf_op jit(solution)/shard_map/pallas_call | solution.py:384
  17.4 0.7 %collective-permute-start.5 = (bf16[33,32,128]{2,1,0:T(8,128)(2,1)S(1)}, bf16[33,32,128]{2,1,0:T(8,128)(2,1)S(1)}, u32[]{:S(2)}, u32[]{:S(2)}) collective-permute-start(bf16[33,32,128]{2,1,0:T(8,128)(2,1)S(1)} %get-tuple-element.42.after_ref.own_ref), channel_id=1, source_target_pairs={{1,3},{3,5},{5,7},{7,9},{9,11},{11,13},{13,15},{17,19},{19,21},{21... | collective-permute-start | bytes 811016 | tf_op jit(solution)/shard_map/ppermute | solution.py:18
  18.0 3.4 %collective-permute-start.7 = (bf16[33,32,128]{2,1,0:T(8,128)(2,1)S(1)}, bf16[33,32,128]{2,1,0:T(8,128)(2,1)S(1)}, u32[]{:S(2)}, u32[]{:S(2)}) collective-permute-start(bf16[33,32,128]{2,1,0:T(8,128)(2,1)S(1)} %get-tuple-element.42.after_ref.own_ref), channel_id=1, source_target_pairs={{0,2},{2,4},{4,6},{6,8},{8,10},{10,12},{12,14},{16,18},{18,20},{20... | collective-permute-start | bytes 811016 | tf_op jit(solution)/shard_map/ppermute | solution.py:18
  21.5 1.1 %shard_map.109.turned_ref = bf16[32,512,128]{2,1,0:T(8,128)(2,1)S(1)} custom-call(bf16[32,4,128,128]{3,2,1,0:T(8,128)(2,1)S(1)} %get-tuple-element.36.refs_3_.factor_ref, bf16[33,32,128]{2,1,0:T(8,128)(2,1)S(1)} %get-tuple-element.42.after_ref.own_ref), custom_call_target="tpu_custom_call" | custom-call | tf_op jit(solution)/shard_map/pallas_call | solution.py:389
  22.6 0.0 copy-start
  22.6 0.5 shard_map.110
  23.1 0.0 collective-permute-done.5.far_ref.far_odd_ref
  23.2 2.7 %collective-permute-start.6 = (bf16[33,32,128]{2,1,0:T(8,128)(2,1)S(1)}, bf16[33,32,128]{2,1,0:T(8,128)(2,1)S(1)}, u32[]{:S(2)}, u32[]{:S(2)}) collective-permute-start(bf16[33,32,128]{2,1,0:T(8,128)(2,1)S(1)} %shard_map.111), channel_id=1, source_target_pairs={{0,1},{1,0},{2,3},{3,2},{4,5},{5,4},{6,7},{7,6},{8,9},{9,8},{10,11... | collective-permute-start | bytes 811016 | tf_op jit(solution)/shard_map/ppermute | solution.py:22
  25.9 1.1 %collective-permute-done.7.far_even_ref = bf16[33,32,128]{2,1,0:T(8,128)(2,1)S(1)} collective-permute-done((bf16[33,32,128]{2,1,0:T(8,128)(2,1)S(1)}, bf16[33,32,128]{2,1,0:T(8,128)(2,1)S(1)}, u32[]{:S(2)}, u32[]{:S(2)}) %collective-permute-start.7) | collective-permute-done | bytes 270368 | tf_op jit(solution)/shard_map/ppermute | solution.py:18
  27.0 0.0 collective-permute-done.6.near_ref
  27.0 0.0 copy-done
  27.0 2.2 %shard_map.112 = (bf16[33,32,128]{2,1,0:T(8,128)(2,1)S(1)}, bf16[33,32,128]{2,1,0:T(8,128)(2,1)S(1)}, f32[96,40,128]{2,1,0:T(8,128)S(1)}, f32[40,128]{1,0:T(8,128)S(1)}, bf16[32,48,128]{2,1,0:T(8,128)(2,1)S(1)}) custom-call(s32[3,32]{1,0:T(4,128)S(1)} %bitcast.4, ...), custom_call_target="tpu_custom_call", output_to_operand_aliasing={{2}: (8, {})} | custom-call | tf_op jit(solution)/shard_map/pallas_call | solution.py:398
  29.2 0.4 collective-permute-start.9
  29.6 1.3 %collective-permute-start.8 = (bf16[33,32,128]{2,1,0:T(8,128)(2,1)S(1)}, bf16[33,32,128]{2,1,0:T(8,128)(2,1)S(1)}, u32[]{:S(2)}, u32[]{:S(2)}) collective-permute-start(bf16[33,32,128]{2,1,0:T(8,128)(2,1)S(1)} %get-tuple-element.50.back_far_ref), channel_id=1, source_target_pairs={{2,0},{4,2},{6,4},{8,6},{10,8},{12,10},{14,12},{18,16},{20,18},{22... | collective-permute-start | bytes 811016 | tf_op jit(solution)/shard_map/ppermute | solution.py:18
  30.8 0.0 collective-permute-done.9.got_ref.mate_ref
  30.9 0.1 shard_map.114
  30.9 0.7 %collective-permute-start.10 = (bf16[33,32,128]{2,1,0:T(8,128)(2,1)S(1)}, bf16[33,32,128]{2,1,0:T(8,128)(2,1)S(1)}, u32[]{:S(2)}, u32[]{:S(2)}) collective-permute-start(bf16[33,32,128]{2,1,0:T(8,128)(2,1)S(1)} %shard_map.114), channel_id=1, source_target_pairs={{3,1},{5,3},{7,5},{9,7},{11,9},{13,11},{15,13},{19,17},{21,19},{23... | collective-permute-start | bytes 811016 | tf_op jit(solution)/shard_map/ppermute | solution.py:18
  31.6 0.4 shard_map.113
  32.0 8.3 %collective-permute-done.8.even_ref = bf16[33,32,128]{2,1,0:T(8,128)(2,1)S(1)} collective-permute-done((bf16[33,32,128]{2,1,0:T(8,128)(2,1)S(1)}, bf16[33,32,128]{2,1,0:T(8,128)(2,1)S(1)}, u32[]{:S(2)}, u32[]{:S(2)}) %collective-permute-start.8) | collective-permute-done | bytes 270368 | tf_op jit(solution)/shard_map/ppermute | solution.py:18
  40.3 0.0 collective-permute-done.10.odd_ref
  40.3 0.5 shard_map.115
  40.9 0.8 %collective-permute-start.11 = (f32[40,256]{1,0:T(8,128)S(1)}, f32[40,256]{1,0:T(8,128)S(1)}, u32[]{:S(2)}, u32[]{:S(2)}) collective-permute-start(f32[40,256]{1,0:T(8,128)S(1)} %get-tuple-element.53.x_ref), channel_id=1, source_target_pairs={{0,1},{1,0},{2,3},{3,2},{4,5},{5,4},{6,7},{7,6},{8,9},{9,8},{10,11... | collective-permute-start | bytes 122888 | tf_op jit(solution)/shard_map/ppermute | solution.py:76
  41.7 0.9 %collective-permute-done.11.refs_0_ = f32[40,256]{1,0:T(8,128)S(1)} collective-permute-done((f32[40,256]{1,0:T(8,128)S(1)}, f32[40,256]{1,0:T(8,128)S(1)}, u32[]{:S(2)}, u32[]{:S(2)}) %collective-permute-start.11) | collective-permute-done | bytes 40992 | tf_op jit(solution)/shard_map/ppermute | solution.py:76
  42.6 2.9 %collective-permute-start.12 = (bf16[40,256]{1,0:T(8,128)(2,1)S(1)}, bf16[40,256]{1,0:T(8,128)(2,1)S(1)}, u32[]{:S(2)}, u32[]{:S(2)}) collective-permute-start(bf16[40,256]{1,0:T(8,128)(2,1)S(1)} %get-tuple-element.55), channel_id=1, source_target_pairs={{0,3},{1,2},{2,1},{3,0},{4,7},{5,6},{6,5},{7,4},{8,11},{9,10},{10,... | collective-permute-start | bytes 61448 | tf_op jit(solution)/shard_map/ppermute | solution.py:76
  45.5 1.5 %collective-permute-done.12.refs_0_ = bf16[40,256]{1,0:T(8,128)(2,1)S(1)} collective-permute-done((bf16[40,256]{1,0:T(8,128)(2,1)S(1)}, bf16[40,256]{1,0:T(8,128)(2,1)S(1)}, u32[]{:S(2)}, u32[]{:S(2)}) %collective-permute-start.12) | collective-permute-done | bytes 20512 | tf_op jit(solution)/shard_map/ppermute | solution.py:76
  47.0 2.6 %collective-permute-start.15 = (bf16[40,256]{1,0:T(8,128)(2,1)S(1)}, bf16[40,256]{1,0:T(8,128)(2,1)S(1)}, u32[]{:S(2)}, u32[]{:S(2)}) collective-permute-start(bf16[40,256]{1,0:T(8,128)(2,1)S(1)} %get-tuple-element.57), channel_id=1, source_target_pairs={{0,13},{1,12},{2,15},{3,14},{4,9},{5,8},{6,11},{7,10},{8,5},{9,4},... | collective-permute-start | bytes 61448 | tf_op jit(solution)/shard_map/ppermute | solution.py:76
  49.6 0.0 collective-permute-start.14
  49.6 1.4 %collective-permute-start.13 = (bf16[40,256]{1,0:T(8,128)(2,1)S(1)}, bf16[40,256]{1,0:T(8,128)(2,1)S(1)}, u32[]{:S(2)}, u32[]{:S(2)}) collective-permute-start(bf16[40,256]{1,0:T(8,128)(2,1)S(1)} %get-tuple-element.57), channel_id=1, source_target_pairs={{0,5},{1,4},{2,7},{3,6},{4,1},{5,0},{6,3},{7,2},{8,13},{9,12},{10,... | collective-permute-start | bytes 61448 | tf_op jit(solution)/shard_map/ppermute | solution.py:76
  50.9 1.1 %collective-permute-done.15.refs_2_ = bf16[40,256]{1,0:T(8,128)(2,1)S(1)} collective-permute-done((bf16[40,256]{1,0:T(8,128)(2,1)S(1)}, bf16[40,256]{1,0:T(8,128)(2,1)S(1)}, u32[]{:S(2)}, u32[]{:S(2)}) %collective-permute-start.15) | collective-permute-done | bytes 20512 | tf_op jit(solution)/shard_map/ppermute | solution.py:76
  52.1 1.6 %collective-permute-done.14.refs_1_ = bf16[40,256]{1,0:T(8,128)(2,1)S(1)} collective-permute-done((bf16[40,256]{1,0:T(8,128)(2,1)S(1)}, bf16[40,256]{1,0:T(8,128)(2,1)S(1)}, u32[]{:S(2)}, u32[]{:S(2)}) %collective-permute-start.14) | collective-permute-done | bytes 20512 | tf_op jit(solution)/shard_map/ppermute | solution.py:76
  53.7 0.0 collective-permute-done.13.refs_0_
  53.7 1.8 %shard_map.119 = (f32[33,4096]{1,0:T(8,128)}, f32[33,4096]{1,0:T(8,128)}, f32[33,4096]{1,0:T(8,128)}) custom-call(f32[40,256]{1,0:T(8,128)S(1)} %shard_map.107.sums_ref, f32[40,256]{1,0:T(8,128)S(1)} %get-tuple-element.41.product_ref, f32[40,256]{1,0:T(8,128)S(1)} %shard_map.118.hess_sums_ref, f32[256,256]{1,0:T(8,128)S(1)} %get-tuple-element.37.refs_4_.inner_ref, ...), custom_call_target="tpu_custom_call" | custom-call | tf_op jit(solution)/shard_map/pallas_call | solution.py:415
  (7 shorter events, 0.1 us)
Async XLA Ops:
  2.8 1.4 %collective-permute-start = (f32[40,256]{1,0:T(8,128)S(1)}, f32[40,256]{1,0:T(8,128)S(1)}, u32[]{:S(2)}, u32[]{:S(2)}) collective-permute-start(f32[40,256]{1,0:T(8,128)S(1)} %get-tuple-element.31.x_ref), channel_id=1, source_target_pairs={{0,1},{1,0},{2,3},{3,2},{4,5},{5,4},{6,7},{7,6},{8,9},{9,8},{10,11... | collective-permute-start | bytes 122888 | tf_op jit(solution)/shard_map/ppermute | solution.py:76
  4.2 4.1 %collective-permute-start.1 = (bf16[40,256]{1,0:T(8,128)(2,1)S(1)}, bf16[40,256]{1,0:T(8,128)(2,1)S(1)}, u32[]{:S(2)}, u32[]{:S(2)}) collective-permute-start(bf16[40,256]{1,0:T(8,128)(2,1)S(1)} %get-tuple-element.33), channel_id=1, source_target_pairs={{0,3},{1,2},{2,1},{3,0},{4,7},{5,6},{6,5},{7,4},{8,11},{9,10},{10,... | collective-permute-start | bytes 61448 | tf_op jit(solution)/shard_map/ppermute | solution.py:76
  8.4 6.7 %collective-permute-start.4 = (bf16[40,256]{1,0:T(8,128)(2,1)S(1)}, bf16[40,256]{1,0:T(8,128)(2,1)S(1)}, u32[]{:S(2)}, u32[]{:S(2)}) collective-permute-start(bf16[40,256]{1,0:T(8,128)(2,1)S(1)} %get-tuple-element.35.after_ref), channel_id=1, source_target_pairs={{0,13},{1,12},{2,15},{3,14},{4,9},{5,8},{6,11},{7,10},{8,5},{9,4},... | collective-permute-start | bytes 61448 | tf_op jit(solution)/shard_map/ppermute | solution.py:76
  12.3 4.1 %collective-permute-start.3 = (bf16[40,256]{1,0:T(8,128)(2,1)S(1)}, bf16[40,256]{1,0:T(8,128)(2,1)S(1)}, u32[]{:S(2)}, u32[]{:S(2)}) collective-permute-start(bf16[40,256]{1,0:T(8,128)(2,1)S(1)} %get-tuple-element.35.after_ref), channel_id=1, source_target_pairs={{0,9},{1,8},{2,11},{3,10},{4,13},{5,12},{6,15},{7,14},{8,1},{9,0},... | collective-permute-start | bytes 61448 | tf_op jit(solution)/shard_map/ppermute | solution.py:76
  12.3 4.1 %collective-permute-start.2 = (bf16[40,256]{1,0:T(8,128)(2,1)S(1)}, bf16[40,256]{1,0:T(8,128)(2,1)S(1)}, u32[]{:S(2)}, u32[]{:S(2)}) collective-permute-start(bf16[40,256]{1,0:T(8,128)(2,1)S(1)} %get-tuple-element.35.after_ref), channel_id=1, source_target_pairs={{0,5},{1,4},{2,7},{3,6},{4,1},{5,0},{6,3},{7,2},{8,13},{9,12},{10,... | collective-permute-start | bytes 61448 | tf_op jit(solution)/shard_map/ppermute | solution.py:76
  17.4 5.8 %collective-permute-start.5 = (bf16[33,32,128]{2,1,0:T(8,128)(2,1)S(1)}, bf16[33,32,128]{2,1,0:T(8,128)(2,1)S(1)}, u32[]{:S(2)}, u32[]{:S(2)}) collective-permute-start(bf16[33,32,128]{2,1,0:T(8,128)(2,1)S(1)} %get-tuple-element.42.after_ref.own_ref), channel_id=1, source_target_pairs={{1,3},{3,5},{5,7},{7,9},{9,11},{11,13},{13,15},{17,19},{19,21},{21... | collective-permute-start | bytes 811016 | tf_op jit(solution)/shard_map/ppermute | solution.py:18
  18.0 9.0 %collective-permute-start.7 = (bf16[33,32,128]{2,1,0:T(8,128)(2,1)S(1)}, bf16[33,32,128]{2,1,0:T(8,128)(2,1)S(1)}, u32[]{:S(2)}, u32[]{:S(2)}) collective-permute-start(bf16[33,32,128]{2,1,0:T(8,128)(2,1)S(1)} %get-tuple-element.42.after_ref.own_ref), channel_id=1, source_target_pairs={{0,2},{2,4},{4,6},{6,8},{8,10},{10,12},{12,14},{16,18},{18,20},{20... | collective-permute-start | bytes 811016 | tf_op jit(solution)/shard_map/ppermute | solution.py:18
  22.6 4.4 %copy-start = (s32[32,3]{0,1:T(4,128)S(1)}, s32[32,3]{0,1:T(4,128)}, u32[]{:S(2)}) copy-start(s32[32,3]{0,1:T(4,128)} %param.13) | copy-start | bytes 1156
  23.2 3.8 %collective-permute-start.6 = (bf16[33,32,128]{2,1,0:T(8,128)(2,1)S(1)}, bf16[33,32,128]{2,1,0:T(8,128)(2,1)S(1)}, u32[]{:S(2)}, u32[]{:S(2)}) collective-permute-start(bf16[33,32,128]{2,1,0:T(8,128)(2,1)S(1)} %shard_map.111), channel_id=1, source_target_pairs={{0,1},{1,0},{2,3},{3,2},{4,5},{5,4},{6,7},{7,6},{8,9},{9,8},{10,11... | collective-permute-start | bytes 811016 | tf_op jit(solution)/shard_map/ppermute | solution.py:22
  29.2 1.7 %collective-permute-start.9 = (bf16[33,32,128]{2,1,0:T(8,128)(2,1)S(1)}, bf16[33,32,128]{2,1,0:T(8,128)(2,1)S(1)}, u32[]{:S(2)}, u32[]{:S(2)}) collective-permute-start(bf16[33,32,128]{2,1,0:T(8,128)(2,1)S(1)} %get-tuple-element.51), channel_id=1, source_target_pairs={{0,1},{1,0},{2,3},{3,2},{4,5},{5,4},{6,7},{7,6},{8,9},{9,8},{10,11... | collective-permute-start | bytes 811016 | tf_op jit(solution)/shard_map/ppermute | solution.py:22
  29.6 10.8 %collective-permute-start.8 = (bf16[33,32,128]{2,1,0:T(8,128)(2,1)S(1)}, bf16[33,32,128]{2,1,0:T(8,128)(2,1)S(1)}, u32[]{:S(2)}, u32[]{:S(2)}) collective-permute-start(bf16[33,32,128]{2,1,0:T(8,128)(2,1)S(1)} %get-tuple-element.50.back_far_ref), channel_id=1, source_target_pairs={{2,0},{4,2},{6,4},{8,6},{10,8},{12,10},{14,12},{18,16},{20,18},{22... | collective-permute-start | bytes 811016 | tf_op jit(solution)/shard_map/ppermute | solution.py:18
  30.9 9.4 %collective-permute-start.10 = (bf16[33,32,128]{2,1,0:T(8,128)(2,1)S(1)}, bf16[33,32,128]{2,1,0:T(8,128)(2,1)S(1)}, u32[]{:S(2)}, u32[]{:S(2)}) collective-permute-start(bf16[33,32,128]{2,1,0:T(8,128)(2,1)S(1)} %shard_map.114), channel_id=1, source_target_pairs={{3,1},{5,3},{7,5},{9,7},{11,9},{13,11},{15,13},{19,17},{21,19},{23... | collective-permute-start | bytes 811016 | tf_op jit(solution)/shard_map/ppermute | solution.py:18
  40.9 1.7 %collective-permute-start.11 = (f32[40,256]{1,0:T(8,128)S(1)}, f32[40,256]{1,0:T(8,128)S(1)}, u32[]{:S(2)}, u32[]{:S(2)}) collective-permute-start(f32[40,256]{1,0:T(8,128)S(1)} %get-tuple-element.53.x_ref), channel_id=1, source_target_pairs={{0,1},{1,0},{2,3},{3,2},{4,5},{5,4},{6,7},{7,6},{8,9},{9,8},{10,11... | collective-permute-start | bytes 122888 | tf_op jit(solution)/shard_map/ppermute | solution.py:76
  42.6 4.4 %collective-permute-start.12 = (bf16[40,256]{1,0:T(8,128)(2,1)S(1)}, bf16[40,256]{1,0:T(8,128)(2,1)S(1)}, u32[]{:S(2)}, u32[]{:S(2)}) collective-permute-start(bf16[40,256]{1,0:T(8,128)(2,1)S(1)} %get-tuple-element.55), channel_id=1, source_target_pairs={{0,3},{1,2},{2,1},{3,0},{4,7},{5,6},{6,5},{7,4},{8,11},{9,10},{10,... | collective-permute-start | bytes 61448 | tf_op jit(solution)/shard_map/ppermute | solution.py:76
  47.0 5.1 %collective-permute-start.15 = (bf16[40,256]{1,0:T(8,128)(2,1)S(1)}, bf16[40,256]{1,0:T(8,128)(2,1)S(1)}, u32[]{:S(2)}, u32[]{:S(2)}) collective-permute-start(bf16[40,256]{1,0:T(8,128)(2,1)S(1)} %get-tuple-element.57), channel_id=1, source_target_pairs={{0,13},{1,12},{2,15},{3,14},{4,9},{5,8},{6,11},{7,10},{8,5},{9,4},... | collective-permute-start | bytes 61448 | tf_op jit(solution)/shard_map/ppermute | solution.py:76
  49.6 4.1 %collective-permute-start.14 = (bf16[40,256]{1,0:T(8,128)(2,1)S(1)}, bf16[40,256]{1,0:T(8,128)(2,1)S(1)}, u32[]{:S(2)}, u32[]{:S(2)}) collective-permute-start(bf16[40,256]{1,0:T(8,128)(2,1)S(1)} %get-tuple-element.57), channel_id=1, source_target_pairs={{0,9},{1,8},{2,11},{3,10},{4,13},{5,12},{6,15},{7,14},{8,1},{9,0},... | collective-permute-start | bytes 61448 | tf_op jit(solution)/shard_map/ppermute | solution.py:76
  49.6 4.1 %collective-permute-start.13 = (bf16[40,256]{1,0:T(8,128)(2,1)S(1)}, bf16[40,256]{1,0:T(8,128)(2,1)S(1)}, u32[]{:S(2)}, u32[]{:S(2)}) collective-permute-start(bf16[40,256]{1,0:T(8,128)(2,1)S(1)} %get-tuple-element.57), channel_id=1, source_target_pairs={{0,5},{1,4},{2,7},{3,6},{4,1},{5,0},{6,3},{7,2},{8,13},{9,12},{10,... | collective-permute-start | bytes 61448 | tf_op jit(solution)/shard_map/ppermute | solution.py:76

commit v10 on v9

--- a/solution.py
+++ b/solution.py
@@ -66,22 +66,25 @@
     return rounds
 
 
-def total(x, axis, beside=None):
+def total(x, axis, beside=()):
     n = lax.axis_size(axis)
     if n & (n - 1):
-        return lax.psum(x, axis), beside(x) if beside else ()
+        return lax.psum(x, axis), [work(x) for work in beside]
     rounds = rounds_of(n)
-    msg = x
+    made, todo, msg = [], list(beside), x
     for i, partners in enumerate(rounds):
         got = [lax.ppermute(msg, axis, [(j, j ^ d) for j in range(n)]) for d in partners]
         last = i + 1 == len(rounds)
-        held = beside(msg) if beside and last else ()
+        held = ()
+        while len(todo) >= max(len(rounds) - i, 1):
+            made.append(todo.pop(0)(msg))
+            held += made[-1]
         add = functools.partial(add_kernel, len(got) + 1, len(held))
         ins = [pltpu.VMEM] * (len(got) + 1) + [pl.ANY] * len(held)
         outs = [(x.shape, F32)] + [(x.shape, BF16)] * (not last)
         x, *rest = jax.tree.leaves(call(add, ins, outs)(x, *got, *held))
         msg = rest[0] if rest else None
-    return x, held
+    return x, made
 
 
 def eye(rows, lanes):
@@ -146,15 +149,19 @@
     product_ref[...] = product
     coeffs = product.astype(BF16)
     for b in range(0, blocks, PAIR):
-        correction = lax.dot_general(
-            coeffs, map_ref[b * bs : (b + PAIR) * bs], (((1,), (1,)), ((), ())), preferred_element_type=F32
-        )
+        correction = jnp.dot(coeffs, map_ref[:, b * bs : (b + PAIR) * bs], preferred_element_type=F32)
         for c in range(b, b + PAIR):
             direction = (field_ref[c] + correction[:, (c - b) * bs : (c - b + 1) * bs]) * inv_diag_ref[c : c + 1]
             dir_ref[c] = direction
             msg_ref[c] = direction[:count].astype(BF16)
             last_ref[c : c + 1] = direction[count : count + 1]
     msg_ref[blocks] = last_ref[...].astype(BF16)
+
+
+def turn_map_kernel(map_ref, after_ref, turned_ref):
+    points, inducing = map_ref.shape
+    for i in range(0, points, inducing):
+        turned_ref[:, i : i + inducing] = map_ref[i : i + inducing].T
 
 
 def load_kernel(factor_hbm, inner_hbm, after_ref, factor_ref, inner_ref, sems):
@@ -171,8 +178,8 @@
 def turn_kernel(factor_ref, after_ref, turned_ref):
     blocks, taps, bs, _ = factor_ref.shape
     for b in range(blocks):
-        for k in range(taps):
-            turned_ref[b, k * bs : (k + 1) * bs] = factor_ref[b, k].T
+        for k in range(1, taps):
+            turned_ref[b, (k - 1) * bs : k * bs] = factor_ref[b, k].T
 
 
 def tall_block(refs, lasts, at, tall):
@@ -181,12 +188,18 @@
     return jnp.concatenate([most, last.astype(BF16)], axis=0)
 
 
-def own_image_kernel(tall, own_ref, turned_ref, image_ref, zeros_ref, last_ref):
+def own_image_kernel(tall, own_ref, factor_ref, image_ref, again_ref, zeros_ref, last_ref):
     blocks, bs = last_ref.shape
+    again_ref[...] = own_ref[...]
     zeros_ref[...] = jnp.zeros_like(zeros_ref)
     last_ref[...] = own_ref[blocks].astype(F32)
     for b in range(blocks):
-        image_ref[b] = jnp.dot(tall_block(own_ref, last_ref, b, tall), turned_ref[b, :bs], preferred_element_type=F32)
+        image_ref[b] = lax.dot_general(
+            tall_block(own_ref, last_ref, b, tall),
+            factor_ref[b, 0],
+            (((1,), (1,)), ((), ())),
+            preferred_element_type=F32,
+        )
 
 
 def pass_on_kernel(own_ref, far_ref, after_ref, out_ref):
@@ -233,7 +246,7 @@
     for b in range(blocks):
         chosen = [tall_block(around_ref, around_last_ref, ids(b, k), tall) for k in range(1, taps)]
         image = own_image_ref[b] + jnp.dot(
-            jnp.concatenate(chosen, axis=1), turned_ref[b, bs:], preferred_element_type=F32
+            jnp.concatenate(chosen, axis=1), turned_ref[b], preferred_element_type=F32
         )
         rounded = image.astype(BF16)
         image_ref[b] = rounded
@@ -317,9 +330,7 @@
         send(i, residual_ref, residual_hbm)
     for i in range(OUT_PARTS):
         for b in range(i * part, (i + 1) * part, PAIR):
-            correction = lax.dot_general(
-                coeffs, map_ref[b * bs : (b + PAIR) * bs], (((1,), (1,)), ((), ())), preferred_element_type=F32
-            )
+            correction = jnp.dot(coeffs, map_ref[:, b * bs : (b + PAIR) * bs], preferred_element_type=F32)
             for c in range(b, b + PAIR):
                 smoothed = (residual_of(c) + correction[:, (c - b) * bs : (c - b + 1) * bs]) * inv_diag_ref[c : c + 1]
                 next_ref[:, c * bs : (c + 1) * bs] = (smoothed + ratio * dir_ref[c])[:whole]
@@ -380,21 +391,25 @@
             in_hbm(factor), in_hbm(inner_inverse), msg
         )
 
-    sums, (factor, inner_inverse) = total(partial, "space", load)
+    def turn_map(msg):
+        return (call(turn_map_kernel, [vmem, pl.ANY], [(inducing_map.shape[::-1], BF16)])(inducing_map, msg),)
+
+    sums, ((turned_map,), (factor, inner_inverse)) = total(partial, "space", [turn_map, load])
     direction, rounded, product = call(
         direction_kernel, [vmem] * 5, [field, packed, sum_shape], [vmem((blocks, bs), F32)]
-    )(sums, inner_inverse, *points)
+    )(sums, inner_inverse, terms, right_side, turned_map)
     far_odd = sent(rounded, "space", 2, (1,))
-    far_even = sent(rounded, "space", 2, (0,))
-    turned = call(turn_kernel, [vmem, pl.ANY], [((blocks, factor.shape[1] * bs, bs), BF16)])(factor, rounded)
     around = ((3 * blocks, rows, bs), F32)
-    own_image, zeros = call(
+    own_image, again, zeros = call(
         functools.partial(own_image_kernel, tall),
         [vmem] * 2,
-        [((blocks, tall, bs), F32), around],
+        [((blocks, tall, bs), F32), packed, around],
         [vmem((blocks, bs), F32)],
-    )(rounded, turned)
-    near = swapped(call(pass_on_kernel, [vmem, vmem, pl.ANY], [packed])(rounded, far_odd, own_image), "space")
+    )(rounded, factor)
+    far_even = sent(again, "space", 2, (0,))
+    shape = (blocks, (factor.shape[1] - 1) * bs, bs)
+    turned = call(turn_kernel, [vmem, pl.ANY], [(shape, BF16)])(factor, own_image)
+    near = swapped(call(pass_on_kernel, [vmem, vmem, pl.ANY], [packed])(rounded, far_odd, turned), "space")
     back_far, back_near, back_own, curve, image = call(
         functools.partial(hessian_kernel, rows),
         [smem] + [vmem] * 8,
@@ -413,7 +428,7 @@
     whole = ((count + 1, blocks * bs), F32)
     scratch = [vmem(*whole)] * 3 + [pltpu.SemaphoreType.DMA((3 * OUT_PARTS,))]
     return call(finish_kernel, [vmem] * 9, [whole] * 3, scratch, keep=False)(
-        *map(in_vmem, (sums, product, hess_sums, inner_inverse, direction, hess, *points))
+        *map(in_vmem, (sums, product, hess_sums, inner_inverse, direction, hess, terms, right_side, turned_map))
     )
 
 

time: 55.8 us -> 55.1 us (0.987)
  starting transfers between devices: 24.4 us -> 23.2 us
    ppermute x2, starting transfers between devices: 3.03 us -> 1.63 us  [swapped(): lax.ppermute(block, axis, [(i, i ^ 1) for i in range(lax.axis_size(axis))])]
    ppermute x10, waiting for transfers between devices: 8.71 us -> 8.15 us  [total(): lax.ppermute(msg, axis, [(j, j ^ d) for j in range(n)])]
    pallas_call x1 -> x2, Pallas kernels: 1.13 us -> 1.49 us  [the longest x1 0.86 us: body(): call(turn_kernel, [vmem, pl.ANY], [(shape, BF16)])(factor, own_image)]
  transfers between devices with their start and end apart: 16 -> 16, of which waited for: 9 -> 10; matrix products, arithmetic and copies ran while one was open for 0% -> 0% of each run, Pallas kernels for 8% -> 9%
where the time goes in v10:
time: 55.1 us; the launch traced here: 54.8 us
  starting transfers between devices  23.2 us (42%)
  waiting for transfers between devices  18.4 us (33%)
  Pallas kernels  12.5 us (23%)
  between operations  0.78 us (1%)
    ppermute x10, starting transfers between devices, total(): lax.ppermute(msg, axis, [(j, j ^ d) for j in range(n)])  15.5 us
    ppermute x4, waiting for transfers between devices, sent(): lax.ppermute(block, axis, [(i, i + distance) for i in devices if i % 2 in...  10 us
    ppermute x10, waiting for transfers between devices, total(): lax.ppermute(msg, axis, [(j, j ^ d) for j in range(n)])  8.15 us
    ppermute x4, starting transfers between devices, sent(): lax.ppermute(block, axis, [(i, i + distance) for i in devices if i % 2 in...  6.04 us
    pallas_call x1, Pallas kernels, load(): call(load_kernel, [pl.ANY] * 3, outs, [pltpu.SemaphoreType.DMA((2,))])  2.23 us
    pallas_call x1, Pallas kernels, body(): call(project_kernel, [pl.ANY] * 5, [sum_shape, ((2, blocks, bs), F32), fi...  2.15 us
    pallas_call x1, Pallas kernels, body(): call(functools.partial(hessian_kernel, rows), [smem] + [vmem] * 8, [packe...  2.15 us
    ppermute x2, starting transfers between devices, swapped(): lax.ppermute(block, axis, [(i, i ^ 1) for i in range(lax.axis_size(axis))])  1.63 us
  transfers between devices with their start and end apart: 16, of which 10 were waited for; matrix products, arithmetic and copies ran while one was open for 0% of the time, Pallas kernels for 9%

profile of v10, /device:TPU:0, one launch (start us, length us, event | category | flops | bytes accessed | tf_op | source)
XLA Modules:
  0.0 54.8 jit_solution(13542337092839546628)
XLA Ops:
  0.6 2.2 %shard_map.103 = (f32[40,256]{1,0:T(8,128)S(1)}, f32[2,32,128]{2,1,0:T(8,128)S(1)}, f32[32,40,128]{2,1,0:T(8,128)S(1)}, bf16[4096,256]{1,0:T(8,128)(2,1)S(1)}) custom-call(f32[32,128]{1,0:T(8,128)} %bitcast.5, s32[32,128]{1,0:T(8,128)} %bitcast.6, f32[32,128]{1,0:T(8,128)} %bitcast.7, f32[32,4096]{1,0:T(8,128)} %probes_hbm.1, bf16[4096,256]{1,0:T(8,128)(2,1)} %map_hbm.1), custom_call_target="tpu_custom_call" | custom-call | tf_op jit(solution)/shard_map/pallas_call | solution.py:374
  2.8 0.5 collective-permute-start
  3.3 0.9 %collective-permute-done.refs_0_ = f32[40,256]{1,0:T(8,128)S(1)} collective-permute-done((f32[40,256]{1,0:T(8,128)S(1)}, f32[40,256]{1,0:T(8,128)S(1)}, u32[]{:S(2)}, u32[]{:S(2)}) %collective-permute-start) | collective-permute-done | bytes 40992 | tf_op jit(solution)/shard_map/ppermute | solution.py:76
  4.2 2.7 %collective-permute-start.1 = (bf16[40,256]{1,0:T(8,128)(2,1)S(1)}, bf16[40,256]{1,0:T(8,128)(2,1)S(1)}, u32[]{:S(2)}, u32[]{:S(2)}) collective-permute-start(bf16[40,256]{1,0:T(8,128)(2,1)S(1)} %get-tuple-element.34.after_ref), channel_id=1, source_target_pairs={{0,3},{1,2},{2,1},{3,0},{4,7},{5,6},{6,5},{7,4},{8,11},{9,10},{10,... | collective-permute-start | bytes 61448 | tf_op jit(solution)/shard_map/ppermute | solution.py:76
  6.9 0.6 %shard_map.105.refs_1_.map_ref = bf16[256,4096]{1,0:T(8,128)(2,1)S(1)} custom-call(bf16[4096,256]{1,0:T(8,128)(2,1)S(1)} %get-tuple-element.35.map_ref, bf16[40,256]{1,0:T(8,128)(2,1)S(1)} %get-tuple-element.34.after_ref), custom_call_target="tpu_custom_call" | custom-call | tf_op jit(solution)/shard_map/pallas_call | solution.py:395
  7.5 0.8 %collective-permute-done.1.refs_0_ = bf16[40,256]{1,0:T(8,128)(2,1)S(1)} collective-permute-done((bf16[40,256]{1,0:T(8,128)(2,1)S(1)}, bf16[40,256]{1,0:T(8,128)(2,1)S(1)}, u32[]{:S(2)}, u32[]{:S(2)}) %collective-permute-start.1) | collective-permute-done | bytes 20512 | tf_op jit(solution)/shard_map/ppermute | solution.py:76
  8.4 3.9 %collective-permute-start.4 = (bf16[40,256]{1,0:T(8,128)(2,1)S(1)}, bf16[40,256]{1,0:T(8,128)(2,1)S(1)}, u32[]{:S(2)}, u32[]{:S(2)}) collective-permute-start(bf16[40,256]{1,0:T(8,128)(2,1)S(1)} %get-tuple-element.37.after_ref), channel_id=1, source_target_pairs={{0,13},{1,12},{2,15},{3,14},{4,9},{5,8},{6,11},{7,10},{8,5},{9,4},... | collective-permute-start | bytes 61448 | tf_op jit(solution)/shard_map/ppermute | solution.py:76
  12.3 0.0 collective-permute-start.3
  12.3 0.6 %collective-permute-start.2 = (bf16[40,256]{1,0:T(8,128)(2,1)S(1)}, bf16[40,256]{1,0:T(8,128)(2,1)S(1)}, u32[]{:S(2)}, u32[]{:S(2)}) collective-permute-start(bf16[40,256]{1,0:T(8,128)(2,1)S(1)} %get-tuple-element.37.after_ref), channel_id=1, source_target_pairs={{0,5},{1,4},{2,7},{3,6},{4,1},{5,0},{6,3},{7,2},{8,13},{9,12},{10,... | collective-permute-start | bytes 61448 | tf_op jit(solution)/shard_map/ppermute | solution.py:76
  12.9 2.2 %shard_map.107 = (bf16[32,4,128,128]{3,2,1,0:T(8,128)(2,1)S(1)}, f32[256,256]{1,0:T(8,128)S(1)}) custom-call(bf16[32,4,128,128]{3,2,1,0:T(8,128)(2,1)} %factor_hbm.1, f32[256,256]{1,0:T(8,128)} %inner_hbm.1, bf16[40,256]{1,0:T(8,128)(2,1)S(1)} %get-tuple-element.37.after_ref), custom_call_target="tpu_custom_call" | custom-call | tf_op jit(solution)/shard_map/pallas_call | solution.py:390
  15.1 0.0 collective-permute-done.4.refs_2_
  15.1 1.3 %collective-permute-done.3.refs_1_ = bf16[40,256]{1,0:T(8,128)(2,1)S(1)} collective-permute-done((bf16[40,256]{1,0:T(8,128)(2,1)S(1)}, bf16[40,256]{1,0:T(8,128)(2,1)S(1)}, u32[]{:S(2)}, u32[]{:S(2)}) %collective-permute-start.3) | collective-permute-done | bytes 20512 | tf_op jit(solution)/shard_map/ppermute | solution.py:76
  16.4 0.0 collective-permute-done.2.refs_0_
  16.4 0.8 %shard_map.109 = (f32[32,40,128]{2,1,0:T(8,128)S(1)}, bf16[33,32,128]{2,1,0:T(8,128)(2,1)S(1)}, f32[40,256]{1,0:T(8,128)S(1)}) custom-call(f32[40,256]{1,0:T(8,128)S(1)} %shard_map.108.sums_ref, f32[256,256]{1,0:T(8,128)S(1)} %get-tuple-element.39.refs_4_.inner_ref, f32[2,32,128]{2,1,0:T(8,128)S(1)} %get-tuple-element.40.terms_ref, ...), custom_call_target="tpu_custom_call" | custom-call | tf_op jit(solution)/shard_map/pallas_call | solution.py:398
  17.1 0.7 %collective-permute-start.5 = (bf16[33,32,128]{2,1,0:T(8,128)(2,1)S(1)}, bf16[33,32,128]{2,1,0:T(8,128)(2,1)S(1)}, u32[]{:S(2)}, u32[]{:S(2)}) collective-permute-start(bf16[33,32,128]{2,1,0:T(8,128)(2,1)S(1)} %get-tuple-element.43.own_ref), channel_id=1, source_target_pairs={{1,3},{3,5},{5,7},{7,9},{9,11},{11,13},{13,15},{17,19},{19,21},{21... | collective-permute-start | bytes 811016 | tf_op jit(solution)/shard_map/ppermute | solution.py:18
  17.8 0.9 %shard_map.110 = (f32[32,48,128]{2,1,0:T(8,128)S(1)}, bf16[33,32,128]{2,1,0:T(8,128)(2,1)S(1)}, f32[96,40,128]{2,1,0:T(8,128)S(1)}) custom-call(bf16[33,32,128]{2,1,0:T(8,128)(2,1)S(1)} %get-tuple-element.43.own_ref, bf16[32,4,128,128]{3,2,1,0:T(8,128)(2,1)S(1)} %get-tuple-element.38.refs_3_.factor_ref), custom_call_target="tpu_custom_call" | custom-call | tf_op jit(solution)/shard_map/pallas_call | solution.py:403
  18.8 3.4 %collective-permute-start.7 = (bf16[33,32,128]{2,1,0:T(8,128)(2,1)S(1)}, bf16[33,32,128]{2,1,0:T(8,128)(2,1)S(1)}, u32[]{:S(2)}, u32[]{:S(2)}) collective-permute-start(bf16[33,32,128]{2,1,0:T(8,128)(2,1)S(1)} %get-tuple-element.45), channel_id=1, source_target_pairs={{0,2},{2,4},{4,6},{6,8},{8,10},{10,12},{12,14},{16,18},{18,20},{20... | collective-permute-start | bytes 811016 | tf_op jit(solution)/shard_map/ppermute | solution.py:18
  22.2 0.9 %shard_map.111.after_ref.turned_ref = bf16[32,384,128]{2,1,0:T(8,128)(2,1)S(1)} custom-call(bf16[32,4,128,128]{3,2,1,0:T(8,128)(2,1)S(1)} %get-tuple-element.38.refs_3_.factor_ref, f32[32,48,128]{2,1,0:T(8,128)S(1)} %get-tuple-element.44.after_ref.own_image_ref), custom_call_target="tpu_custom_call" | custom-call | tf_op jit(solution)/shard_map/pallas_call | solution.py:411
  23.1 0.0 copy-start
  23.1 0.0 collective-permute-done.5.far_ref.far_odd_ref
  23.1 1.6 %collective-permute-start.6 = (bf16[33,32,128]{2,1,0:T(8,128)(2,1)S(1)}, bf16[33,32,128]{2,1,0:T(8,128)(2,1)S(1)}, u32[]{:S(2)}, u32[]{:S(2)}) collective-permute-start(bf16[33,32,128]{2,1,0:T(8,128)(2,1)S(1)} %shard_map.112), channel_id=1, source_target_pairs={{0,1},{1,0},{2,3},{3,2},{4,5},{5,4},{6,7},{7,6},{8,9},{9,8},{10,11... | collective-permute-start | bytes 811016 | tf_op jit(solution)/shard_map/ppermute | solution.py:22
  24.7 2.1 %collective-permute-done.7.far_even_ref = bf16[33,32,128]{2,1,0:T(8,128)(2,1)S(1)} collective-permute-done((bf16[33,32,128]{2,1,0:T(8,128)(2,1)S(1)}, bf16[33,32,128]{2,1,0:T(8,128)(2,1)S(1)}, u32[]{:S(2)}, u32[]{:S(2)}) %collective-permute-start.7) | collective-permute-done | bytes 270368 | tf_op jit(solution)/shard_map/ppermute | solution.py:18
  26.8 0.0 collective-permute-done.6.near_ref
  26.8 0.0 copy-done
  26.8 2.2 %shard_map.113 = (bf16[33,32,128]{2,1,0:T(8,128)(2,1)S(1)}, bf16[33,32,128]{2,1,0:T(8,128)(2,1)S(1)}, f32[96,40,128]{2,1,0:T(8,128)S(1)}, f32[40,128]{1,0:T(8,128)S(1)}, bf16[32,48,128]{2,1,0:T(8,128)(2,1)S(1)}) custom-call(s32[3,32]{1,0:T(4,128)S(1)} %bitcast.4, ...), custom_call_target="tpu_custom_call", output_to_operand_aliasing={{2}: (8, {})} | custom-call | tf_op jit(solution)/shard_map/pallas_call | solution.py:413
  28.9 0.1 collective-permute-start.9
  29.0 1.3 %collective-permute-start.8 = (bf16[33,32,128]{2,1,0:T(8,128)(2,1)S(1)}, bf16[33,32,128]{2,1,0:T(8,128)(2,1)S(1)}, u32[]{:S(2)}, u32[]{:S(2)}) collective-permute-start(bf16[33,32,128]{2,1,0:T(8,128)(2,1)S(1)} %get-tuple-element.52.back_far_ref), channel_id=1, source_target_pairs={{2,0},{4,2},{6,4},{8,6},{10,8},{12,10},{14,12},{18,16},{20,18},{22... | collective-permute-start | bytes 811016 | tf_op jit(solution)/shard_map/ppermute | solution.py:18
  30.3 0.2 collective-permute-done.9.got_ref.mate_ref
  30.6 0.1 shard_map.115
  30.6 0.7 %collective-permute-start.10 = (bf16[33,32,128]{2,1,0:T(8,128)(2,1)S(1)}, bf16[33,32,128]{2,1,0:T(8,128)(2,1)S(1)}, u32[]{:S(2)}, u32[]{:S(2)}) collective-permute-start(bf16[33,32,128]{2,1,0:T(8,128)(2,1)S(1)} %shard_map.115), channel_id=1, source_target_pairs={{3,1},{5,3},{7,5},{9,7},{11,9},{13,11},{15,13},{19,17},{21,19},{23... | collective-permute-start | bytes 811016 | tf_op jit(solution)/shard_map/ppermute | solution.py:18
  31.3 0.4 shard_map.114
  31.7 7.9 %collective-permute-done.8.even_ref = bf16[33,32,128]{2,1,0:T(8,128)(2,1)S(1)} collective-permute-done((bf16[33,32,128]{2,1,0:T(8,128)(2,1)S(1)}, bf16[33,32,128]{2,1,0:T(8,128)(2,1)S(1)}, u32[]{:S(2)}, u32[]{:S(2)}) %collective-permute-start.8) | collective-permute-done | bytes 270368 | tf_op jit(solution)/shard_map/ppermute | solution.py:18
  39.6 0.0 collective-permute-done.10.odd_ref
  39.6 0.5 shard_map.116
  40.2 0.9 %collective-permute-start.11 = (f32[40,256]{1,0:T(8,128)S(1)}, f32[40,256]{1,0:T(8,128)S(1)}, u32[]{:S(2)}, u32[]{:S(2)}) collective-permute-start(f32[40,256]{1,0:T(8,128)S(1)} %get-tuple-element.55.x_ref), channel_id=1, source_target_pairs={{0,1},{1,0},{2,3},{3,2},{4,5},{5,4},{6,7},{7,6},{8,9},{9,8},{10,11... | collective-permute-start | bytes 122888 | tf_op jit(solution)/shard_map/ppermute | solution.py:76
  41.1 0.9 %collective-permute-done.11.refs_0_ = f32[40,256]{1,0:T(8,128)S(1)} collective-permute-done((f32[40,256]{1,0:T(8,128)S(1)}, f32[40,256]{1,0:T(8,128)S(1)}, u32[]{:S(2)}, u32[]{:S(2)}) %collective-permute-start.11) | collective-permute-done | bytes 40992 | tf_op jit(solution)/shard_map/ppermute | solution.py:76
  42.0 2.9 %collective-permute-start.12 = (bf16[40,256]{1,0:T(8,128)(2,1)S(1)}, bf16[40,256]{1,0:T(8,128)(2,1)S(1)}, u32[]{:S(2)}, u32[]{:S(2)}) collective-permute-start(bf16[40,256]{1,0:T(8,128)(2,1)S(1)} %get-tuple-element.57), channel_id=1, source_target_pairs={{0,3},{1,2},{2,1},{3,0},{4,7},{5,6},{6,5},{7,4},{8,11},{9,10},{10,... | collective-permute-start | bytes 61448 | tf_op jit(solution)/shard_map/ppermute | solution.py:76
  44.9 1.5 %collective-permute-done.12.refs_0_ = bf16[40,256]{1,0:T(8,128)(2,1)S(1)} collective-permute-done((bf16[40,256]{1,0:T(8,128)(2,1)S(1)}, bf16[40,256]{1,0:T(8,128)(2,1)S(1)}, u32[]{:S(2)}, u32[]{:S(2)}) %collective-permute-start.12) | collective-permute-done | bytes 20512 | tf_op jit(solution)/shard_map/ppermute | solution.py:76
  46.4 2.6 %collective-permute-start.15 = (bf16[40,256]{1,0:T(8,128)(2,1)S(1)}, bf16[40,256]{1,0:T(8,128)(2,1)S(1)}, u32[]{:S(2)}, u32[]{:S(2)}) collective-permute-start(bf16[40,256]{1,0:T(8,128)(2,1)S(1)} %get-tuple-element.59), channel_id=1, source_target_pairs={{0,13},{1,12},{2,15},{3,14},{4,9},{5,8},{6,11},{7,10},{8,5},{9,4},... | collective-permute-start | bytes 61448 | tf_op jit(solution)/shard_map/ppermute | solution.py:76
  49.0 0.0 collective-permute-start.14
  49.0 1.4 %collective-permute-start.13 = (bf16[40,256]{1,0:T(8,128)(2,1)S(1)}, bf16[40,256]{1,0:T(8,128)(2,1)S(1)}, u32[]{:S(2)}, u32[]{:S(2)}) collective-permute-start(bf16[40,256]{1,0:T(8,128)(2,1)S(1)} %get-tuple-element.59), channel_id=1, source_target_pairs={{0,5},{1,4},{2,7},{3,6},{4,1},{5,0},{6,3},{7,2},{8,13},{9,12},{10,... | collective-permute-start | bytes 61448 | tf_op jit(solution)/shard_map/ppermute | solution.py:76
  50.4 1.1 %collective-permute-done.15.refs_2_ = bf16[40,256]{1,0:T(8,128)(2,1)S(1)} collective-permute-done((bf16[40,256]{1,0:T(8,128)(2,1)S(1)}, bf16[40,256]{1,0:T(8,128)(2,1)S(1)}, u32[]{:S(2)}, u32[]{:S(2)}) %collective-permute-start.15) | collective-permute-done | bytes 20512 | tf_op jit(solution)/shard_map/ppermute | solution.py:76
  51.5 1.7 %collective-permute-done.14.refs_1_ = bf16[40,256]{1,0:T(8,128)(2,1)S(1)} collective-permute-done((bf16[40,256]{1,0:T(8,128)(2,1)S(1)}, bf16[40,256]{1,0:T(8,128)(2,1)S(1)}, u32[]{:S(2)}, u32[]{:S(2)}) %collective-permute-start.14) | collective-permute-done | bytes 20512 | tf_op jit(solution)/shard_map/ppermute | solution.py:76
  53.2 0.0 collective-permute-done.13.refs_0_
  53.2 1.6 %shard_map.120 = (f32[33,4096]{1,0:T(8,128)}, f32[33,4096]{1,0:T(8,128)}, f32[33,4096]{1,0:T(8,128)}) custom-call(f32[40,256]{1,0:T(8,128)S(1)} %shard_map.108.sums_ref, f32[40,256]{1,0:T(8,128)S(1)} %get-tuple-element.42.product_ref, f32[40,256]{1,0:T(8,128)S(1)} %shard_map.119.hess_sums_ref, f32[256,256]{1,0:T(8,128)S(1)} %get-tuple-element.39.refs_4_.inner_ref, ...), custom_call_target="tpu_custom_call" | custom-call | tf_op jit(solution)/shard_map/pallas_call | solution.py:430
  (7 shorter events, 0.1 us)
Async XLA Ops:
  2.8 1.4 %collective-permute-start = (f32[40,256]{1,0:T(8,128)S(1)}, f32[40,256]{1,0:T(8,128)S(1)}, u32[]{:S(2)}, u32[]{:S(2)}) collective-permute-start(f32[40,256]{1,0:T(8,128)S(1)} %get-tuple-element.32.x_ref), channel_id=1, source_target_pairs={{0,1},{1,0},{2,3},{3,2},{4,5},{5,4},{6,7},{7,6},{8,9},{9,8},{10,11... | collective-permute-start | bytes 122888 | tf_op jit(solution)/shard_map/ppermute | solution.py:76
  4.2 4.1 %collective-permute-start.1 = (bf16[40,256]{1,0:T(8,128)(2,1)S(1)}, bf16[40,256]{1,0:T(8,128)(2,1)S(1)}, u32[]{:S(2)}, u32[]{:S(2)}) collective-permute-start(bf16[40,256]{1,0:T(8,128)(2,1)S(1)} %get-tuple-element.34.after_ref), channel_id=1, source_target_pairs={{0,3},{1,2},{2,1},{3,0},{4,7},{5,6},{6,5},{7,4},{8,11},{9,10},{10,... | collective-permute-start | bytes 61448 | tf_op jit(solution)/shard_map/ppermute | solution.py:76
  8.4 6.7 %collective-permute-start.4 = (bf16[40,256]{1,0:T(8,128)(2,1)S(1)}, bf16[40,256]{1,0:T(8,128)(2,1)S(1)}, u32[]{:S(2)}, u32[]{:S(2)}) collective-permute-start(bf16[40,256]{1,0:T(8,128)(2,1)S(1)} %get-tuple-element.37.after_ref), channel_id=1, source_target_pairs={{0,13},{1,12},{2,15},{3,14},{4,9},{5,8},{6,11},{7,10},{8,5},{9,4},... | collective-permute-start | bytes 61448 | tf_op jit(solution)/shard_map/ppermute | solution.py:76
  12.3 4.1 %collective-permute-start.3 = (bf16[40,256]{1,0:T(8,128)(2,1)S(1)}, bf16[40,256]{1,0:T(8,128)(2,1)S(1)}, u32[]{:S(2)}, u32[]{:S(2)}) collective-permute-start(bf16[40,256]{1,0:T(8,128)(2,1)S(1)} %get-tuple-element.37.after_ref), channel_id=1, source_target_pairs={{0,9},{1,8},{2,11},{3,10},{4,13},{5,12},{6,15},{7,14},{8,1},{9,0},... | collective-permute-start | bytes 61448 | tf_op jit(solution)/shard_map/ppermute | solution.py:76
  12.3 4.1 %collective-permute-start.2 = (bf16[40,256]{1,0:T(8,128)(2,1)S(1)}, bf16[40,256]{1,0:T(8,128)(2,1)S(1)}, u32[]{:S(2)}, u32[]{:S(2)}) collective-permute-start(bf16[40,256]{1,0:T(8,128)(2,1)S(1)} %get-tuple-element.37.after_ref), channel_id=1, source_target_pairs={{0,5},{1,4},{2,7},{3,6},{4,1},{5,0},{6,3},{7,2},{8,13},{9,12},{10,... | collective-permute-start | bytes 61448 | tf_op jit(solution)/shard_map/ppermute | solution.py:76
  17.1 5.9 %collective-permute-start.5 = (bf16[33,32,128]{2,1,0:T(8,128)(2,1)S(1)}, bf16[33,32,128]{2,1,0:T(8,128)(2,1)S(1)}, u32[]{:S(2)}, u32[]{:S(2)}) collective-permute-start(bf16[33,32,128]{2,1,0:T(8,128)(2,1)S(1)} %get-tuple-element.43.own_ref), channel_id=1, source_target_pairs={{1,3},{3,5},{5,7},{7,9},{9,11},{11,13},{13,15},{17,19},{19,21},{21... | collective-permute-start | bytes 811016 | tf_op jit(solution)/shard_map/ppermute | solution.py:18
  18.8 8.0 %collective-permute-start.7 = (bf16[33,32,128]{2,1,0:T(8,128)(2,1)S(1)}, bf16[33,32,128]{2,1,0:T(8,128)(2,1)S(1)}, u32[]{:S(2)}, u32[]{:S(2)}) collective-permute-start(bf16[33,32,128]{2,1,0:T(8,128)(2,1)S(1)} %get-tuple-element.45), channel_id=1, source_target_pairs={{0,2},{2,4},{4,6},{6,8},{8,10},{10,12},{12,14},{16,18},{18,20},{20... | collective-permute-start | bytes 811016 | tf_op jit(solution)/shard_map/ppermute | solution.py:18
  23.1 3.7 %copy-start = (s32[32,3]{0,1:T(4,128)S(1)}, s32[32,3]{0,1:T(4,128)}, u32[]{:S(2)}) copy-start(s32[32,3]{0,1:T(4,128)} %param.13) | copy-start | bytes 1156
  23.1 3.7 %collective-permute-start.6 = (bf16[33,32,128]{2,1,0:T(8,128)(2,1)S(1)}, bf16[33,32,128]{2,1,0:T(8,128)(2,1)S(1)}, u32[]{:S(2)}, u32[]{:S(2)}) collective-permute-start(bf16[33,32,128]{2,1,0:T(8,128)(2,1)S(1)} %shard_map.112), channel_id=1, source_target_pairs={{0,1},{1,0},{2,3},{3,2},{4,5},{5,4},{6,7},{7,6},{8,9},{9,8},{10,11... | collective-permute-start | bytes 811016 | tf_op jit(solution)/shard_map/ppermute | solution.py:22
  28.9 1.6 %collective-permute-start.9 = (bf16[33,32,128]{2,1,0:T(8,128)(2,1)S(1)}, bf16[33,32,128]{2,1,0:T(8,128)(2,1)S(1)}, u32[]{:S(2)}, u32[]{:S(2)}) collective-permute-start(bf16[33,32,128]{2,1,0:T(8,128)(2,1)S(1)} %get-tuple-element.53), channel_id=1, source_target_pairs={{0,1},{1,0},{2,3},{3,2},{4,5},{5,4},{6,7},{7,6},{8,9},{9,8},{10,11... | collective-permute-start | bytes 811016 | tf_op jit(solution)/shard_map/ppermute | solution.py:22
  29.0 10.6 %collective-permute-start.8 = (bf16[33,32,128]{2,1,0:T(8,128)(2,1)S(1)}, bf16[33,32,128]{2,1,0:T(8,128)(2,1)S(1)}, u32[]{:S(2)}, u32[]{:S(2)}) collective-permute-start(bf16[33,32,128]{2,1,0:T(8,128)(2,1)S(1)} %get-tuple-element.52.back_far_ref), channel_id=1, source_target_pairs={{2,0},{4,2},{6,4},{8,6},{10,8},{12,10},{14,12},{18,16},{20,18},{22... | collective-permute-start | bytes 811016 | tf_op jit(solution)/shard_map/ppermute | solution.py:18
  30.6 9.0 %collective-permute-start.10 = (bf16[33,32,128]{2,1,0:T(8,128)(2,1)S(1)}, bf16[33,32,128]{2,1,0:T(8,128)(2,1)S(1)}, u32[]{:S(2)}, u32[]{:S(2)}) collective-permute-start(bf16[33,32,128]{2,1,0:T(8,128)(2,1)S(1)} %shard_map.115), channel_id=1, source_target_pairs={{3,1},{5,3},{7,5},{9,7},{11,9},{13,11},{15,13},{19,17},{21,19},{23... | collective-permute-start | bytes 811016 | tf_op jit(solution)/shard_map/ppermute | solution.py:18
  40.2 1.8 %collective-permute-start.11 = (f32[40,256]{1,0:T(8,128)S(1)}, f32[40,256]{1,0:T(8,128)S(1)}, u32[]{:S(2)}, u32[]{:S(2)}) collective-permute-start(f32[40,256]{1,0:T(8,128)S(1)} %get-tuple-element.55.x_ref), channel_id=1, source_target_pairs={{0,1},{1,0},{2,3},{3,2},{4,5},{5,4},{6,7},{7,6},{8,9},{9,8},{10,11... | collective-permute-start | bytes 122888 | tf_op jit(solution)/shard_map/ppermute | solution.py:76
  42.0 4.4 %collective-permute-start.12 = (bf16[40,256]{1,0:T(8,128)(2,1)S(1)}, bf16[40,256]{1,0:T(8,128)(2,1)S(1)}, u32[]{:S(2)}, u32[]{:S(2)}) collective-permute-start(bf16[40,256]{1,0:T(8,128)(2,1)S(1)} %get-tuple-element.57), channel_id=1, source_target_pairs={{0,3},{1,2},{2,1},{3,0},{4,7},{5,6},{6,5},{7,4},{8,11},{9,10},{10,... | collective-permute-start | bytes 61448 | tf_op jit(solution)/shard_map/ppermute | solution.py:76
  46.4 5.1 %collective-permute-start.15 = (bf16[40,256]{1,0:T(8,128)(2,1)S(1)}, bf16[40,256]{1,0:T(8,128)(2,1)S(1)}, u32[]{:S(2)}, u32[]{:S(2)}) collective-permute-start(bf16[40,256]{1,0:T(8,128)(2,1)S(1)} %get-tuple-element.59), channel_id=1, source_target_pairs={{0,13},{1,12},{2,15},{3,14},{4,9},{5,8},{6,11},{7,10},{8,5},{9,4},... | collective-permute-start | bytes 61448 | tf_op jit(solution)/shard_map/ppermute | solution.py:76
  49.0 4.2 %collective-permute-start.14 = (bf16[40,256]{1,0:T(8,128)(2,1)S(1)}, bf16[40,256]{1,0:T(8,128)(2,1)S(1)}, u32[]{:S(2)}, u32[]{:S(2)}) collective-permute-start(bf16[40,256]{1,0:T(8,128)(2,1)S(1)} %get-tuple-element.59), channel_id=1, source_target_pairs={{0,9},{1,8},{2,11},{3,10},{4,13},{5,12},{6,15},{7,14},{8,1},{9,0},... | collective-permute-start | bytes 61448 | tf_op jit(solution)/shard_map/ppermute | solution.py:76
  49.0 4.2 %collective-permute-start.13 = (bf16[40,256]{1,0:T(8,128)(2,1)S(1)}, bf16[40,256]{1,0:T(8,128)(2,1)S(1)}, u32[]{:S(2)}, u32[]{:S(2)}) collective-permute-start(bf16[40,256]{1,0:T(8,128)(2,1)S(1)} %get-tuple-element.59), channel_id=1, source_target_pairs={{0,5},{1,4},{2,7},{3,6},{4,1},{5,0},{6,3},{7,2},{8,13},{9,12},{10,... | collective-permute-start | bytes 61448 | tf_op jit(solution)/shard_map/ppermute | solution.py:76

commit v11 on v10

--- a/solution.py
+++ b/solution.py
@@ -212,11 +212,17 @@
         out_ref[...] = far_ref[...]
 
 
+def again_kernel(in_ref, after_ref, out_ref):
+    out_ref[...] = in_ref[...]
+
+
 def join_kernel(back_far_ref, got_ref, out_ref):
     out_ref[...] = (back_far_ref[...].astype(F32) + got_ref[...].astype(F32)).astype(BF16)
 
 
-def own_back_kernel(rows, image_ref, factor_ref, total_ref, curve_ref, dir_ref, terms_ref, base_ref, curve_out_ref):
+def own_back_kernel(
+    rows, image_ref, factor_ref, total_ref, curve_ref, dir_ref, terms_ref, after_ref, base_ref, curve_out_ref
+):
     blocks = factor_ref.shape[0]
     curve = curve_ref[...]
     for b in range(blocks):
@@ -418,11 +424,13 @@
         aliases={8: 2},
     )(cond_ids.T, factor, turned, own_image, near, far_even, far_odd, rounded, zeros)
     mate = swapped(back_near, "space")
-    from_even = sent(back_far, "space", -2, (0,))
-    from_odd = sent(call(join_kernel, [vmem] * 2, [packed])(back_far, mate), "space", -2, (1,))
-    base, curve = call(functools.partial(own_back_kernel, rows), [vmem] * 6, [field, ((rows, bs), F32)])(
-        image, factor, back_own, curve, direction, terms
+    passing = sent(back_far, "space", -1, (0,))
+    joined = call(join_kernel, [vmem] * 2, [packed])(back_far, mate)
+    from_odd = sent(joined, "space", -2, (1,))
+    base, curve = call(functools.partial(own_back_kernel, rows), [vmem] * 6 + [pl.ANY], [field, ((rows, bs), F32)])(
+        image, factor, back_own, curve, direction, terms, joined
     )
+    from_even = sent(call(again_kernel, [vmem, pl.ANY], [packed])(passing, curve), "space", -1, (1,))
     hess, partial = call(combine_kernel, [vmem] * 8, [field, sum_shape])(base, from_even, from_odd, mate, curve, *points)
     hess_sums, _ = total(partial, "space")
     whole = ((count + 1, blocks * bs), F32)

time: 55.1 us -> 57 us (1.034)
  starting transfers between devices: 23.2 us -> 24.3 us
  waiting for transfers between devices: 18.4 us -> 19.2 us
    ppermute x4 -> x5, starting transfers between devices: 6.04 us -> 6.73 us  [sent(): lax.ppermute(block, axis, [(i, i + distance) for i in devices if i % 2 in...]
    ppermute x2, waiting for transfers between devices: 0.24 us -> 0.85 us  [swapped(): lax.ppermute(block, axis, [(i, i ^ 1) for i in range(lax.axis_size(axis))])]
    ppermute x4 -> x5, waiting for transfers between devices: 10 us -> 9.98 us  [sent(): lax.ppermute(block, axis, [(i, i + distance) for i in devices if i % 2 in...]
  transfers between devices with their start and end apart: 16 -> 17, of which waited for: 10 -> 10; matrix products, arithmetic and copies ran while one was open for 0% -> 0% of each run, Pallas kernels for 9% -> 9%
where the time goes in v11:
time: 57 us; the launch traced here: 56.7 us
  starting transfers between devices  24.3 us (43%)
  waiting for transfers between devices  19.2 us (34%)
  Pallas kernels  12.5 us (22%)
  between operations  0.81 us (1%)
    ppermute x10, starting transfers between devices, total(): lax.ppermute(msg, axis, [(j, j ^ d) for j in range(n)])  15.9 us
    ppermute x5, waiting for transfers between devices, sent(): lax.ppermute(block, axis, [(i, i + distance) for i in devices if i % 2 in...  9.98 us
    ppermute x10, waiting for transfers between devices, total(): lax.ppermute(msg, axis, [(j, j ^ d) for j in range(n)])  8.34 us
    ppermute x5, starting transfers between devices, sent(): lax.ppermute(block, axis, [(i, i + distance) for i in devices if i % 2 in...  6.73 us
    pallas_call x1, Pallas kernels, load(): call(load_kernel, [pl.ANY] * 3, outs, [pltpu.SemaphoreType.DMA((2,))])  2.23 us
    pallas_call x1, Pallas kernels, body(): call(project_kernel, [pl.ANY] * 5, [sum_shape, ((2, blocks, bs), F32), fi...  2.14 us
    pallas_call x1, Pallas kernels, body(): call(functools.partial(hessian_kernel, rows), [smem] + [vmem] * 8, [packe...  2.14 us
    ppermute x2, starting transfers between devices, swapped(): lax.ppermute(block, axis, [(i, i ^ 1) for i in range(lax.axis_size(axis))])  1.63 us
  transfers between devices with their start and end apart: 17, of which 10 were waited for; matrix products, arithmetic and copies ran while one was open for 0% of the time, Pallas kernels for 9%

profile of v11, /device:TPU:0, one launch (start us, length us, event | category | flops | bytes accessed | tf_op | source)
XLA Modules:
  0.0 56.7 jit_solution(10876823165276749529)
XLA Ops:
  0.6 2.1 %shard_map.103 = (f32[40,256]{1,0:T(8,128)S(1)}, f32[2,32,128]{2,1,0:T(8,128)S(1)}, f32[32,40,128]{2,1,0:T(8,128)S(1)}, bf16[4096,256]{1,0:T(8,128)(2,1)S(1)}) custom-call(f32[32,128]{1,0:T(8,128)} %bitcast.5, s32[32,128]{1,0:T(8,128)} %bitcast.6, f32[32,128]{1,0:T(8,128)} %bitcast.7, f32[32,4096]{1,0:T(8,128)} %probes_hbm.1, bf16[4096,256]{1,0:T(8,128)(2,1)} %map_hbm.1), custom_call_target="tpu_custom_call" | custom-call | tf_op jit(solution)/shard_map/pallas_call | solution.py:380
  2.8 0.5 collective-permute-start
  3.3 0.9 %collective-permute-done.refs_0_ = f32[40,256]{1,0:T(8,128)S(1)} collective-permute-done((f32[40,256]{1,0:T(8,128)S(1)}, f32[40,256]{1,0:T(8,128)S(1)}, u32[]{:S(2)}, u32[]{:S(2)}) %collective-permute-start) | collective-permute-done | bytes 40992 | tf_op jit(solution)/shard_map/ppermute | solution.py:76
  4.2 2.7 %collective-permute-start.1 = (bf16[40,256]{1,0:T(8,128)(2,1)S(1)}, bf16[40,256]{1,0:T(8,128)(2,1)S(1)}, u32[]{:S(2)}, u32[]{:S(2)}) collective-permute-start(bf16[40,256]{1,0:T(8,128)(2,1)S(1)} %get-tuple-element.34.after_ref), channel_id=1, source_target_pairs={{0,3},{1,2},{2,1},{3,0},{4,7},{5,6},{6,5},{7,4},{8,11},{9,10},{10,... | collective-permute-start | bytes 61448 | tf_op jit(solution)/shard_map/ppermute | solution.py:76
  6.9 0.6 %shard_map.105.refs_1_.map_ref = bf16[256,4096]{1,0:T(8,128)(2,1)S(1)} custom-call(bf16[4096,256]{1,0:T(8,128)(2,1)S(1)} %get-tuple-element.35.map_ref, bf16[40,256]{1,0:T(8,128)(2,1)S(1)} %get-tuple-element.34.after_ref), custom_call_target="tpu_custom_call" | custom-call | tf_op jit(solution)/shard_map/pallas_call | solution.py:401
  7.5 0.8 %collective-permute-done.1.refs_0_ = bf16[40,256]{1,0:T(8,128)(2,1)S(1)} collective-permute-done((bf16[40,256]{1,0:T(8,128)(2,1)S(1)}, bf16[40,256]{1,0:T(8,128)(2,1)S(1)}, u32[]{:S(2)}, u32[]{:S(2)}) %collective-permute-start.1) | collective-permute-done | bytes 20512 | tf_op jit(solution)/shard_map/ppermute | solution.py:76
  8.4 3.9 %collective-permute-start.4 = (bf16[40,256]{1,0:T(8,128)(2,1)S(1)}, bf16[40,256]{1,0:T(8,128)(2,1)S(1)}, u32[]{:S(2)}, u32[]{:S(2)}) collective-permute-start(bf16[40,256]{1,0:T(8,128)(2,1)S(1)} %get-tuple-element.37.after_ref), channel_id=1, source_target_pairs={{0,13},{1,12},{2,15},{3,14},{4,9},{5,8},{6,11},{7,10},{8,5},{9,4},... | collective-permute-start | bytes 61448 | tf_op jit(solution)/shard_map/ppermute | solution.py:76
  12.3 0.0 collective-permute-start.3
  12.3 0.6 %collective-permute-start.2 = (bf16[40,256]{1,0:T(8,128)(2,1)S(1)}, bf16[40,256]{1,0:T(8,128)(2,1)S(1)}, u32[]{:S(2)}, u32[]{:S(2)}) collective-permute-start(bf16[40,256]{1,0:T(8,128)(2,1)S(1)} %get-tuple-element.37.after_ref), channel_id=1, source_target_pairs={{0,5},{1,4},{2,7},{3,6},{4,1},{5,0},{6,3},{7,2},{8,13},{9,12},{10,... | collective-permute-start | bytes 61448 | tf_op jit(solution)/shard_map/ppermute | solution.py:76
  12.9 2.2 %shard_map.107 = (bf16[32,4,128,128]{3,2,1,0:T(8,128)(2,1)S(1)}, f32[256,256]{1,0:T(8,128)S(1)}) custom-call(bf16[32,4,128,128]{3,2,1,0:T(8,128)(2,1)} %factor_hbm.1, f32[256,256]{1,0:T(8,128)} %inner_hbm.1, bf16[40,256]{1,0:T(8,128)(2,1)S(1)} %get-tuple-element.37.after_ref), custom_call_target="tpu_custom_call" | custom-call | tf_op jit(solution)/shard_map/pallas_call | solution.py:396
  15.1 0.0 collective-permute-done.4.refs_2_
  15.1 1.3 %collective-permute-done.3.refs_1_ = bf16[40,256]{1,0:T(8,128)(2,1)S(1)} collective-permute-done((bf16[40,256]{1,0:T(8,128)(2,1)S(1)}, bf16[40,256]{1,0:T(8,128)(2,1)S(1)}, u32[]{:S(2)}, u32[]{:S(2)}) %collective-permute-start.3) | collective-permute-done | bytes 20512 | tf_op jit(solution)/shard_map/ppermute | solution.py:76
  16.4 0.0 collective-permute-done.2.refs_0_
  16.4 0.7 %shard_map.109 = (f32[32,40,128]{2,1,0:T(8,128)S(1)}, bf16[33,32,128]{2,1,0:T(8,128)(2,1)S(1)}, f32[40,256]{1,0:T(8,128)S(1)}) custom-call(f32[40,256]{1,0:T(8,128)S(1)} %shard_map.108.sums_ref, f32[256,256]{1,0:T(8,128)S(1)} %get-tuple-element.39.refs_4_.inner_ref, f32[2,32,128]{2,1,0:T(8,128)S(1)} %get-tuple-element.40.terms_ref, ...), custom_call_target="tpu_custom_call" | custom-call | tf_op jit(solution)/shard_map/pallas_call | solution.py:404
  17.1 0.7 %collective-permute-start.5 = (bf16[33,32,128]{2,1,0:T(8,128)(2,1)S(1)}, bf16[33,32,128]{2,1,0:T(8,128)(2,1)S(1)}, u32[]{:S(2)}, u32[]{:S(2)}) collective-permute-start(bf16[33,32,128]{2,1,0:T(8,128)(2,1)S(1)} %get-tuple-element.43.own_ref), channel_id=1, source_target_pairs={{1,3},{3,5},{5,7},{7,9},{9,11},{11,13},{13,15},{17,19},{19,21},{21... | collective-permute-start | bytes 811016 | tf_op jit(solution)/shard_map/ppermute | solution.py:18
  17.8 0.9 %shard_map.110 = (f32[32,48,128]{2,1,0:T(8,128)S(1)}, bf16[33,32,128]{2,1,0:T(8,128)(2,1)S(1)}, f32[96,40,128]{2,1,0:T(8,128)S(1)}) custom-call(bf16[33,32,128]{2,1,0:T(8,128)(2,1)S(1)} %get-tuple-element.43.own_ref, bf16[32,4,128,128]{3,2,1,0:T(8,128)(2,1)S(1)} %get-tuple-element.38.refs_3_.factor_ref), custom_call_target="tpu_custom_call" | custom-call | tf_op jit(solution)/shard_map/pallas_call | solution.py:409
  18.8 3.4 %collective-permute-start.7 = (bf16[33,32,128]{2,1,0:T(8,128)(2,1)S(1)}, bf16[33,32,128]{2,1,0:T(8,128)(2,1)S(1)}, u32[]{:S(2)}, u32[]{:S(2)}) collective-permute-start(bf16[33,32,128]{2,1,0:T(8,128)(2,1)S(1)} %get-tuple-element.45), channel_id=1, source_target_pairs={{0,2},{2,4},{4,6},{6,8},{8,10},{10,12},{12,14},{16,18},{18,20},{20... | collective-permute-start | bytes 811016 | tf_op jit(solution)/shard_map/ppermute | solution.py:18
  22.2 0.9 %shard_map.111.after_ref.turned_ref = bf16[32,384,128]{2,1,0:T(8,128)(2,1)S(1)} custom-call(bf16[32,4,128,128]{3,2,1,0:T(8,128)(2,1)S(1)} %get-tuple-element.38.refs_3_.factor_ref, f32[32,48,128]{2,1,0:T(8,128)S(1)} %get-tuple-element.44.after_ref.own_image_ref), custom_call_target="tpu_custom_call" | custom-call | tf_op jit(solution)/shard_map/pallas_call | solution.py:417
  23.0 0.0 copy-start
  23.1 0.0 collective-permute-done.5.far_ref.far_odd_ref
  23.1 1.6 %collective-permute-start.6 = (bf16[33,32,128]{2,1,0:T(8,128)(2,1)S(1)}, bf16[33,32,128]{2,1,0:T(8,128)(2,1)S(1)}, u32[]{:S(2)}, u32[]{:S(2)}) collective-permute-start(bf16[33,32,128]{2,1,0:T(8,128)(2,1)S(1)} %shard_map.112), channel_id=1, source_target_pairs={{0,1},{1,0},{2,3},{3,2},{4,5},{5,4},{6,7},{7,6},{8,9},{9,8},{10,11... | collective-permute-start | bytes 811016 | tf_op jit(solution)/shard_map/ppermute | solution.py:22
  24.7 2.1 %collective-permute-done.7.far_even_ref = bf16[33,32,128]{2,1,0:T(8,128)(2,1)S(1)} collective-permute-done((bf16[33,32,128]{2,1,0:T(8,128)(2,1)S(1)}, bf16[33,32,128]{2,1,0:T(8,128)(2,1)S(1)}, u32[]{:S(2)}, u32[]{:S(2)}) %collective-permute-start.7) | collective-permute-done | bytes 270368 | tf_op jit(solution)/shard_map/ppermute | solution.py:18
  26.8 0.0 collective-permute-done.6.near_ref
  26.8 0.0 copy-done
  26.8 2.1 %shard_map.113 = (bf16[33,32,128]{2,1,0:T(8,128)(2,1)S(1)}, bf16[33,32,128]{2,1,0:T(8,128)(2,1)S(1)}, f32[96,40,128]{2,1,0:T(8,128)S(1)}, f32[40,128]{1,0:T(8,128)S(1)}, bf16[32,48,128]{2,1,0:T(8,128)(2,1)S(1)}) custom-call(s32[3,32]{1,0:T(4,128)S(1)} %bitcast.4, ...), custom_call_target="tpu_custom_call", output_to_operand_aliasing={{2}: (8, {})} | custom-call | tf_op jit(solution)/shard_map/pallas_call | solution.py:419
  28.9 0.1 collective-permute-start.8
  29.0 0.7 %collective-permute-start.9 = (bf16[33,32,128]{2,1,0:T(8,128)(2,1)S(1)}, bf16[33,32,128]{2,1,0:T(8,128)(2,1)S(1)}, u32[]{:S(2)}, u32[]{:S(2)}) collective-permute-start(bf16[33,32,128]{2,1,0:T(8,128)(2,1)S(1)} %get-tuple-element.51.back_far_ref), channel_id=1, source_target_pairs={{2,1},{4,3},{6,5},{8,7},{10,9},{12,11},{14,13},{18,17},{20,19},{22... | collective-permute-start | bytes 811016 | tf_op jit(solution)/shard_map/ppermute | solution.py:18
  29.7 0.8 %collective-permute-done.8.got_ref.mate_ref = bf16[33,32,128]{2,1,0:T(8,128)(2,1)S(1)} collective-permute-done((bf16[33,32,128]{2,1,0:T(8,128)(2,1)S(1)}, bf16[33,32,128]{2,1,0:T(8,128)(2,1)S(1)}, u32[]{:S(2)}, u32[]{:S(2)}) %collective-permute-start.8) | collective-permute-done | bytes 270368 | tf_op jit(solution)/shard_map/ppermute | solution.py:22
  30.5 0.1 shard_map.114.after_ref
  30.6 0.7 %collective-permute-start.11 = (bf16[33,32,128]{2,1,0:T(8,128)(2,1)S(1)}, bf16[33,32,128]{2,1,0:T(8,128)(2,1)S(1)}, u32[]{:S(2)}, u32[]{:S(2)}) collective-permute-start(bf16[33,32,128]{2,1,0:T(8,128)(2,1)S(1)} %shard_map.114.after_ref), channel_id=1, source_target_pairs={{3,1},{5,3},{7,5},{9,7},{11,9},{13,11},{15,13},{19,17},{21,19},{23... | collective-permute-start | bytes 811016 | tf_op jit(solution)/shard_map/ppermute | solution.py:18
  31.3 0.4 shard_map.115
  31.7 0.0 collective-permute-done.9.in_ref
  31.7 1.3 %collective-permute-start.10 = (bf16[33,32,128]{2,1,0:T(8,128)(2,1)S(1)}, bf16[33,32,128]{2,1,0:T(8,128)(2,1)S(1)}, u32[]{:S(2)}, u32[]{:S(2)}) collective-permute-start(bf16[33,32,128]{2,1,0:T(8,128)(2,1)S(1)} %shard_map.116), channel_id=1, source_target_pairs={{1,0},{3,2},{5,4},{7,6},{9,8},{11,10},{13,12},{15,14},{17,16},{19,... | collective-permute-start | bytes 811016 | tf_op jit(solution)/shard_map/ppermute | solution.py:18
  33.0 0.0 collective-permute-done.11.odd_ref
  33.1 7.9 %collective-permute-done.10.even_ref = bf16[33,32,128]{2,1,0:T(8,128)(2,1)S(1)} collective-permute-done((bf16[33,32,128]{2,1,0:T(8,128)(2,1)S(1)}, bf16[33,32,128]{2,1,0:T(8,128)(2,1)S(1)}, u32[]{:S(2)}, u32[]{:S(2)}) %collective-permute-start.10) | collective-permute-done | bytes 270368 | tf_op jit(solution)/shard_map/ppermute | solution.py:18
  40.9 0.5 shard_map.117
  41.4 0.2 collective-permute-start.12
  41.6 1.1 %collective-permute-done.12.refs_0_ = f32[40,256]{1,0:T(8,128)S(1)} collective-permute-done((f32[40,256]{1,0:T(8,128)S(1)}, f32[40,256]{1,0:T(8,128)S(1)}, u32[]{:S(2)}, u32[]{:S(2)}) %collective-permute-start.12) | collective-permute-done | bytes 40992 | tf_op jit(solution)/shard_map/ppermute | solution.py:76
  42.7 4.0 %collective-permute-start.13 = (bf16[40,256]{1,0:T(8,128)(2,1)S(1)}, bf16[40,256]{1,0:T(8,128)(2,1)S(1)}, u32[]{:S(2)}, u32[]{:S(2)}) collective-permute-start(bf16[40,256]{1,0:T(8,128)(2,1)S(1)} %get-tuple-element.57), channel_id=1, source_target_pairs={{0,3},{1,2},{2,1},{3,0},{4,7},{5,6},{6,5},{7,4},{8,11},{9,10},{10,... | collective-permute-start | bytes 61448 | tf_op jit(solution)/shard_map/ppermute | solution.py:76
  46.7 1.5 %collective-permute-done.13.refs_0_ = bf16[40,256]{1,0:T(8,128)(2,1)S(1)} collective-permute-done((bf16[40,256]{1,0:T(8,128)(2,1)S(1)}, bf16[40,256]{1,0:T(8,128)(2,1)S(1)}, u32[]{:S(2)}, u32[]{:S(2)}) %collective-permute-start.13) | collective-permute-done | bytes 20512 | tf_op jit(solution)/shard_map/ppermute | solution.py:76
  48.2 2.6 %collective-permute-start.16 = (bf16[40,256]{1,0:T(8,128)(2,1)S(1)}, bf16[40,256]{1,0:T(8,128)(2,1)S(1)}, u32[]{:S(2)}, u32[]{:S(2)}) collective-permute-start(bf16[40,256]{1,0:T(8,128)(2,1)S(1)} %get-tuple-element.59), channel_id=1, source_target_pairs={{0,13},{1,12},{2,15},{3,14},{4,9},{5,8},{6,11},{7,10},{8,5},{9,4},... | collective-permute-start | bytes 61448 | tf_op jit(solution)/shard_map/ppermute | solution.py:76
  50.8 0.0 collective-permute-start.15
  50.8 1.5 %collective-permute-start.14 = (bf16[40,256]{1,0:T(8,128)(2,1)S(1)}, bf16[40,256]{1,0:T(8,128)(2,1)S(1)}, u32[]{:S(2)}, u32[]{:S(2)}) collective-permute-start(bf16[40,256]{1,0:T(8,128)(2,1)S(1)} %get-tuple-element.59), channel_id=1, source_target_pairs={{0,5},{1,4},{2,7},{3,6},{4,1},{5,0},{6,3},{7,2},{8,13},{9,12},{10,... | collective-permute-start | bytes 61448 | tf_op jit(solution)/shard_map/ppermute | solution.py:76
  52.3 1.0 %collective-permute-done.16.refs_2_ = bf16[40,256]{1,0:T(8,128)(2,1)S(1)} collective-permute-done((bf16[40,256]{1,0:T(8,128)(2,1)S(1)}, bf16[40,256]{1,0:T(8,128)(2,1)S(1)}, u32[]{:S(2)}, u32[]{:S(2)}) %collective-permute-start.16) | collective-permute-done | bytes 20512 | tf_op jit(solution)/shard_map/ppermute | solution.py:76
  53.3 1.8 %collective-permute-done.15.refs_1_ = bf16[40,256]{1,0:T(8,128)(2,1)S(1)} collective-permute-done((bf16[40,256]{1,0:T(8,128)(2,1)S(1)}, bf16[40,256]{1,0:T(8,128)(2,1)S(1)}, u32[]{:S(2)}, u32[]{:S(2)}) %collective-permute-start.15) | collective-permute-done | bytes 20512 | tf_op jit(solution)/shard_map/ppermute | solution.py:76
  55.1 0.0 collective-permute-done.14.refs_0_
  55.1 1.6 %shard_map.121 = (f32[33,4096]{1,0:T(8,128)}, f32[33,4096]{1,0:T(8,128)}, f32[33,4096]{1,0:T(8,128)}) custom-call(f32[40,256]{1,0:T(8,128)S(1)} %shard_map.108.sums_ref, f32[40,256]{1,0:T(8,128)S(1)} %get-tuple-element.42.product_ref, f32[40,256]{1,0:T(8,128)S(1)} %shard_map.120.hess_sums_ref, f32[256,256]{1,0:T(8,128)S(1)} %get-tuple-element.39.refs_4_.inner_ref, ...), custom_call_target="tpu_custom_call" | custom-call | tf_op jit(solution)/shard_map/pallas_call | solution.py:438
  (8 shorter events, 0.2 us)
Async XLA Ops:
  2.8 1.4 %collective-permute-start = (f32[40,256]{1,0:T(8,128)S(1)}, f32[40,256]{1,0:T(8,128)S(1)}, u32[]{:S(2)}, u32[]{:S(2)}) collective-permute-start(f32[40,256]{1,0:T(8,128)S(1)} %get-tuple-element.32.x_ref), channel_id=1, source_target_pairs={{0,1},{1,0},{2,3},{3,2},{4,5},{5,4},{6,7},{7,6},{8,9},{9,8},{10,11... | collective-permute-start | bytes 122888 | tf_op jit(solution)/shard_map/ppermute | solution.py:76
  4.2 4.1 %collective-permute-start.1 = (bf16[40,256]{1,0:T(8,128)(2,1)S(1)}, bf16[40,256]{1,0:T(8,128)(2,1)S(1)}, u32[]{:S(2)}, u32[]{:S(2)}) collective-permute-start(bf16[40,256]{1,0:T(8,128)(2,1)S(1)} %get-tuple-element.34.after_ref), channel_id=1, source_target_pairs={{0,3},{1,2},{2,1},{3,0},{4,7},{5,6},{6,5},{7,4},{8,11},{9,10},{10,... | collective-permute-start | bytes 61448 | tf_op jit(solution)/shard_map/ppermute | solution.py:76
  8.4 6.7 %collective-permute-start.4 = (bf16[40,256]{1,0:T(8,128)(2,1)S(1)}, bf16[40,256]{1,0:T(8,128)(2,1)S(1)}, u32[]{:S(2)}, u32[]{:S(2)}) collective-permute-start(bf16[40,256]{1,0:T(8,128)(2,1)S(1)} %get-tuple-element.37.after_ref), channel_id=1, source_target_pairs={{0,13},{1,12},{2,15},{3,14},{4,9},{5,8},{6,11},{7,10},{8,5},{9,4},... | collective-permute-start | bytes 61448 | tf_op jit(solution)/shard_map/ppermute | solution.py:76
  12.3 4.1 %collective-permute-start.3 = (bf16[40,256]{1,0:T(8,128)(2,1)S(1)}, bf16[40,256]{1,0:T(8,128)(2,1)S(1)}, u32[]{:S(2)}, u32[]{:S(2)}) collective-permute-start(bf16[40,256]{1,0:T(8,128)(2,1)S(1)} %get-tuple-element.37.after_ref), channel_id=1, source_target_pairs={{0,9},{1,8},{2,11},{3,10},{4,13},{5,12},{6,15},{7,14},{8,1},{9,0},... | collective-permute-start | bytes 61448 | tf_op jit(solution)/shard_map/ppermute | solution.py:76
  12.3 4.1 %collective-permute-start.2 = (bf16[40,256]{1,0:T(8,128)(2,1)S(1)}, bf16[40,256]{1,0:T(8,128)(2,1)S(1)}, u32[]{:S(2)}, u32[]{:S(2)}) collective-permute-start(bf16[40,256]{1,0:T(8,128)(2,1)S(1)} %get-tuple-element.37.after_ref), channel_id=1, source_target_pairs={{0,5},{1,4},{2,7},{3,6},{4,1},{5,0},{6,3},{7,2},{8,13},{9,12},{10,... | collective-permute-start | bytes 61448 | tf_op jit(solution)/shard_map/ppermute | solution.py:76
  17.1 5.9 %collective-permute-start.5 = (bf16[33,32,128]{2,1,0:T(8,128)(2,1)S(1)}, bf16[33,32,128]{2,1,0:T(8,128)(2,1)S(1)}, u32[]{:S(2)}, u32[]{:S(2)}) collective-permute-start(bf16[33,32,128]{2,1,0:T(8,128)(2,1)S(1)} %get-tuple-element.43.own_ref), channel_id=1, source_target_pairs={{1,3},{3,5},{5,7},{7,9},{9,11},{11,13},{13,15},{17,19},{19,21},{21... | collective-permute-start | bytes 811016 | tf_op jit(solution)/shard_map/ppermute | solution.py:18
  18.8 8.0 %collective-permute-start.7 = (bf16[33,32,128]{2,1,0:T(8,128)(2,1)S(1)}, bf16[33,32,128]{2,1,0:T(8,128)(2,1)S(1)}, u32[]{:S(2)}, u32[]{:S(2)}) collective-permute-start(bf16[33,32,128]{2,1,0:T(8,128)(2,1)S(1)} %get-tuple-element.45), channel_id=1, source_target_pairs={{0,2},{2,4},{4,6},{6,8},{8,10},{10,12},{12,14},{16,18},{18,20},{20... | collective-permute-start | bytes 811016 | tf_op jit(solution)/shard_map/ppermute | solution.py:18
  23.0 3.7 %copy-start = (s32[32,3]{0,1:T(4,128)S(1)}, s32[32,3]{0,1:T(4,128)}, u32[]{:S(2)}) copy-start(s32[32,3]{0,1:T(4,128)} %param.13) | copy-start | bytes 1156
  23.1 3.7 %collective-permute-start.6 = (bf16[33,32,128]{2,1,0:T(8,128)(2,1)S(1)}, bf16[33,32,128]{2,1,0:T(8,128)(2,1)S(1)}, u32[]{:S(2)}, u32[]{:S(2)}) collective-permute-start(bf16[33,32,128]{2,1,0:T(8,128)(2,1)S(1)} %shard_map.112), channel_id=1, source_target_pairs={{0,1},{1,0},{2,3},{3,2},{4,5},{5,4},{6,7},{7,6},{8,9},{9,8},{10,11... | collective-permute-start | bytes 811016 | tf_op jit(solution)/shard_map/ppermute | solution.py:22
  28.9 1.6 %collective-permute-start.8 = (bf16[33,32,128]{2,1,0:T(8,128)(2,1)S(1)}, bf16[33,32,128]{2,1,0:T(8,128)(2,1)S(1)}, u32[]{:S(2)}, u32[]{:S(2)}) collective-permute-start(bf16[33,32,128]{2,1,0:T(8,128)(2,1)S(1)} %get-tuple-element.52), channel_id=1, source_target_pairs={{0,1},{1,0},{2,3},{3,2},{4,5},{5,4},{6,7},{7,6},{8,9},{9,8},{10,11... | collective-permute-start | bytes 811016 | tf_op jit(solution)/shard_map/ppermute | solution.py:22
  29.0 2.7 %collective-permute-start.9 = (bf16[33,32,128]{2,1,0:T(8,128)(2,1)S(1)}, bf16[33,32,128]{2,1,0:T(8,128)(2,1)S(1)}, u32[]{:S(2)}, u32[]{:S(2)}) collective-permute-start(bf16[33,32,128]{2,1,0:T(8,128)(2,1)S(1)} %get-tuple-element.51.back_far_ref), channel_id=1, source_target_pairs={{2,1},{4,3},{6,5},{8,7},{10,9},{12,11},{14,13},{18,17},{20,19},{22... | collective-permute-start | bytes 811016 | tf_op jit(solution)/shard_map/ppermute | solution.py:18
  30.6 2.5 %collective-permute-start.11 = (bf16[33,32,128]{2,1,0:T(8,128)(2,1)S(1)}, bf16[33,32,128]{2,1,0:T(8,128)(2,1)S(1)}, u32[]{:S(2)}, u32[]{:S(2)}) collective-permute-start(bf16[33,32,128]{2,1,0:T(8,128)(2,1)S(1)} %shard_map.114.after_ref), channel_id=1, source_target_pairs={{3,1},{5,3},{7,5},{9,7},{11,9},{13,11},{15,13},{19,17},{21,19},{23... | collective-permute-start | bytes 811016 | tf_op jit(solution)/shard_map/ppermute | solution.py:18
  31.7 9.2 %collective-permute-start.10 = (bf16[33,32,128]{2,1,0:T(8,128)(2,1)S(1)}, bf16[33,32,128]{2,1,0:T(8,128)(2,1)S(1)}, u32[]{:S(2)}, u32[]{:S(2)}) collective-permute-start(bf16[33,32,128]{2,1,0:T(8,128)(2,1)S(1)} %shard_map.116), channel_id=1, source_target_pairs={{1,0},{3,2},{5,4},{7,6},{9,8},{11,10},{13,12},{15,14},{17,16},{19,... | collective-permute-start | bytes 811016 | tf_op jit(solution)/shard_map/ppermute | solution.py:18
  41.4 1.3 %collective-permute-start.12 = (f32[40,256]{1,0:T(8,128)S(1)}, f32[40,256]{1,0:T(8,128)S(1)}, u32[]{:S(2)}, u32[]{:S(2)}) collective-permute-start(f32[40,256]{1,0:T(8,128)S(1)} %get-tuple-element.55.x_ref), channel_id=1, source_target_pairs={{0,1},{1,0},{2,3},{3,2},{4,5},{5,4},{6,7},{7,6},{8,9},{9,8},{10,11... | collective-permute-start | bytes 122888 | tf_op jit(solution)/shard_map/ppermute | solution.py:76
  42.7 5.4 %collective-permute-start.13 = (bf16[40,256]{1,0:T(8,128)(2,1)S(1)}, bf16[40,256]{1,0:T(8,128)(2,1)S(1)}, u32[]{:S(2)}, u32[]{:S(2)}) collective-permute-start(bf16[40,256]{1,0:T(8,128)(2,1)S(1)} %get-tuple-element.57), channel_id=1, source_target_pairs={{0,3},{1,2},{2,1},{3,0},{4,7},{5,6},{6,5},{7,4},{8,11},{9,10},{10,... | collective-permute-start | bytes 61448 | tf_op jit(solution)/shard_map/ppermute | solution.py:76
  48.2 5.1 %collective-permute-start.16 = (bf16[40,256]{1,0:T(8,128)(2,1)S(1)}, bf16[40,256]{1,0:T(8,128)(2,1)S(1)}, u32[]{:S(2)}, u32[]{:S(2)}) collective-permute-start(bf16[40,256]{1,0:T(8,128)(2,1)S(1)} %get-tuple-element.59), channel_id=1, source_target_pairs={{0,13},{1,12},{2,15},{3,14},{4,9},{5,8},{6,11},{7,10},{8,5},{9,4},... | collective-permute-start | bytes 61448 | tf_op jit(solution)/shard_map/ppermute | solution.py:76
  50.8 4.3 %collective-permute-start.15 = (bf16[40,256]{1,0:T(8,128)(2,1)S(1)}, bf16[40,256]{1,0:T(8,128)(2,1)S(1)}, u32[]{:S(2)}, u32[]{:S(2)}) collective-permute-start(bf16[40,256]{1,0:T(8,128)(2,1)S(1)} %get-tuple-element.59), channel_id=1, source_target_pairs={{0,9},{1,8},{2,11},{3,10},{4,13},{5,12},{6,15},{7,14},{8,1},{9,0},... | collective-permute-start | bytes 61448 | tf_op jit(solution)/shard_map/ppermute | solution.py:76
  50.8 4.3 %collective-permute-start.14 = (bf16[40,256]{1,0:T(8,128)(2,1)S(1)}, bf16[40,256]{1,0:T(8,128)(2,1)S(1)}, u32[]{:S(2)}, u32[]{:S(2)}) collective-permute-start(bf16[40,256]{1,0:T(8,128)(2,1)S(1)} %get-tuple-element.59), channel_id=1, source_target_pairs={{0,5},{1,4},{2,7},{3,6},{4,1},{5,0},{6,3},{7,2},{8,13},{9,12},{10,... | collective-permute-start | bytes 61448 | tf_op jit(solution)/shard_map/ppermute | solution.py:76

commit v12 on v10

--- a/solution.py
+++ b/solution.py
@@ -175,11 +175,14 @@
         copy.wait()
 
 
-def turn_kernel(factor_ref, after_ref, turned_ref):
+def turn_kernel(factor_ref, ids_any, after_ref, turned_ref, ids_ref, sem):
+    copy = pltpu.make_async_copy(ids_any, ids_ref, sem)
+    copy.start()
     blocks, taps, bs, _ = factor_ref.shape
     for b in range(blocks):
         for k in range(1, taps):
             turned_ref[b, (k - 1) * bs : k * bs] = factor_ref[b, k].T
+    copy.wait()
 
 
 def tall_block(refs, lasts, at, tall):
@@ -339,10 +342,11 @@
         copy.wait()
 
 
-def call(kernel, ins, outs, scratch=(), limit=16, keep=True, aliases={}):
+def call(kernel, ins, outs, scratch=(), limit=16, keep=True, aliases={}, spaces=None):
     spec = lambda space: pl.BlockSpec(memory_space=space)
-    shapes = tuple((pltpu.VMEM if keep else jax.ShapeDtypeStruct)(s, t) for s, t in outs)
-    specs = (spec(pltpu.VMEM if keep else pl.ANY),) * len(shapes)
+    spaces = spaces or (pltpu.VMEM,) * len(outs)
+    shapes = tuple((space if keep else jax.ShapeDtypeStruct)(s, t) for space, (s, t) in zip(spaces, outs))
+    specs = tuple(spec(space if keep else pl.ANY) for space in spaces)
     return pl.pallas_call(
         kernel,
         out_shape=shapes if len(shapes) > 1 else shapes[0],
@@ -408,7 +412,13 @@
     )(rounded, factor)
     far_even = sent(again, "space", 2, (0,))
     shape = (blocks, (factor.shape[1] - 1) * bs, bs)
-    turned = call(turn_kernel, [vmem, pl.ANY], [(shape, BF16)])(factor, own_image)
+    turned, ids = call(
+        turn_kernel,
+        [vmem, pl.ANY, pl.ANY],
+        [(shape, BF16), (cond_ids.shape[::-1], jnp.int32)],
+        [pltpu.SemaphoreType.DMA],
+        spaces=(vmem, smem),
+    )(factor, cond_ids.T, own_image)
     near = swapped(call(pass_on_kernel, [vmem, vmem, pl.ANY], [packed])(rounded, far_odd, turned), "space")
     back_far, back_near, back_own, curve, image = call(
         functools.partial(hessian_kernel, rows),
@@ -416,7 +426,7 @@
         [packed, packed, around, ((rows, bs), F32), ((blocks, tall, bs), BF16)],
         [vmem((3 * blocks, count, bs), BF16), vmem((3 * blocks, bs), F32), vmem((blocks, bs), F32)],
         aliases={8: 2},
-    )(cond_ids.T, factor, turned, own_image, near, far_even, far_odd, rounded, zeros)
+    )(ids, factor, turned, own_image, near, far_even, far_odd, rounded, zeros)
     mate = swapped(back_near, "space")
     from_even = sent(back_far, "space", -2, (0,))
     from_odd = sent(call(join_kernel, [vmem] * 2, [packed])(back_far, mate), "space", -2, (1,))

time: 55.1 us -> 54.6 us (level)
  Pallas kernels: 12.5 us -> 11.9 us
    pallas_call x1, Pallas kernels: 2.15 us -> 1.58 us  [body(): call(functools.partial(hessian_kernel, rows), [smem] + [vmem] * 8, [packe...]
  transfers between devices with their start and end apart: 16 -> 16, of which waited for: 10 -> 10; matrix products, arithmetic and copies ran while one was open for 0% -> 0% of each run, Pallas kernels for 9% -> 10%
where the time goes in v12:
time: 54.6 us; the launch traced here: 54.4 us
  starting transfers between devices  23.3 us (43%)
  waiting for transfers between devices  18.4 us (34%)
  Pallas kernels  11.9 us (22%)
  between operations  0.78 us (1%)
    ppermute x10, starting transfers between devices, total(): lax.ppermute(msg, axis, [(j, j ^ d) for j in range(n)])  15.5 us
    ppermute x4, waiting for transfers between devices, sent(): lax.ppermute(block, axis, [(i, i + distance) for i in devices if i % 2 in...  9.98 us
    ppermute x10, waiting for transfers between devices, total(): lax.ppermute(msg, axis, [(j, j ^ d) for j in range(n)])  8.16 us
    ppermute x4, starting transfers between devices, sent(): lax.ppermute(block, axis, [(i, i + distance) for i in devices if i % 2 in...  6.18 us
    pallas_call x1, Pallas kernels, load(): call(load_kernel, [pl.ANY] * 3, outs, [pltpu.SemaphoreType.DMA((2,))])  2.23 us
    pallas_call x1, Pallas kernels, body(): call(project_kernel, [pl.ANY] * 5, [sum_shape, ((2, blocks, bs), F32), fi...  2.15 us
    ppermute x2, starting transfers between devices, swapped(): lax.ppermute(block, axis, [(i, i ^ 1) for i in range(lax.axis_size(axis))])  1.61 us
    pallas_call x1, Pallas kernels, body(): call(finish_kernel, [vmem] * 9, [whole] * 3, scratch, keep=False)  1.6 us
  transfers between devices with their start and end apart: 16, of which 10 were waited for; matrix products, arithmetic and copies ran while one was open for 0% of the time, Pallas kernels for 10%

profile of v12, /device:TPU:0, one launch (start us, length us, event | category | flops | bytes accessed | tf_op | source)
XLA Modules:
  0.0 54.4 jit_solution(17467682890518989921)
XLA Ops:
  0.6 2.2 %shard_map.103 = (f32[40,256]{1,0:T(8,128)S(1)}, f32[2,32,128]{2,1,0:T(8,128)S(1)}, f32[32,40,128]{2,1,0:T(8,128)S(1)}, bf16[4096,256]{1,0:T(8,128)(2,1)S(1)}) custom-call(f32[32,128]{1,0:T(8,128)} %bitcast.5, s32[32,128]{1,0:T(8,128)} %bitcast.6, f32[32,128]{1,0:T(8,128)} %bitcast.7, f32[32,4096]{1,0:T(8,128)} %probes_hbm.1, bf16[4096,256]{1,0:T(8,128)(2,1)} %map_hbm.1), custom_call_target="tpu_custom_call" | custom-call | tf_op jit(solution)/shard_map/pallas_call | solution.py:378
  2.8 0.5 collective-permute-start
  3.3 0.9 %collective-permute-done.refs_0_ = f32[40,256]{1,0:T(8,128)S(1)} collective-permute-done((f32[40,256]{1,0:T(8,128)S(1)}, f32[40,256]{1,0:T(8,128)S(1)}, u32[]{:S(2)}, u32[]{:S(2)}) %collective-permute-start) | collective-permute-done | bytes 40992 | tf_op jit(solution)/shard_map/ppermute | solution.py:76
  4.2 2.7 %collective-permute-start.1 = (bf16[40,256]{1,0:T(8,128)(2,1)S(1)}, bf16[40,256]{1,0:T(8,128)(2,1)S(1)}, u32[]{:S(2)}, u32[]{:S(2)}) collective-permute-start(bf16[40,256]{1,0:T(8,128)(2,1)S(1)} %get-tuple-element.36.after_ref), channel_id=1, source_target_pairs={{0,3},{1,2},{2,1},{3,0},{4,7},{5,6},{6,5},{7,4},{8,11},{9,10},{10,... | collective-permute-start | bytes 61448 | tf_op jit(solution)/shard_map/ppermute | solution.py:76
  6.9 0.6 %shard_map.105.refs_1_.map_ref = bf16[256,4096]{1,0:T(8,128)(2,1)S(1)} custom-call(bf16[4096,256]{1,0:T(8,128)(2,1)S(1)} %get-tuple-element.37.map_ref, bf16[40,256]{1,0:T(8,128)(2,1)S(1)} %get-tuple-element.36.after_ref), custom_call_target="tpu_custom_call" | custom-call | tf_op jit(solution)/shard_map/pallas_call | solution.py:399
  7.5 0.8 %collective-permute-done.1.refs_0_ = bf16[40,256]{1,0:T(8,128)(2,1)S(1)} collective-permute-done((bf16[40,256]{1,0:T(8,128)(2,1)S(1)}, bf16[40,256]{1,0:T(8,128)(2,1)S(1)}, u32[]{:S(2)}, u32[]{:S(2)}) %collective-permute-start.1) | collective-permute-done | bytes 20512 | tf_op jit(solution)/shard_map/ppermute | solution.py:76
  8.4 3.9 %collective-permute-start.4 = (bf16[40,256]{1,0:T(8,128)(2,1)S(1)}, bf16[40,256]{1,0:T(8,128)(2,1)S(1)}, u32[]{:S(2)}, u32[]{:S(2)}) collective-permute-start(bf16[40,256]{1,0:T(8,128)(2,1)S(1)} %get-tuple-element.39.after_ref), channel_id=1, source_target_pairs={{0,13},{1,12},{2,15},{3,14},{4,9},{5,8},{6,11},{7,10},{8,5},{9,4},... | collective-permute-start | bytes 61448 | tf_op jit(solution)/shard_map/ppermute | solution.py:76
  12.3 0.0 collective-permute-start.3
  12.3 0.6 %collective-permute-start.2 = (bf16[40,256]{1,0:T(8,128)(2,1)S(1)}, bf16[40,256]{1,0:T(8,128)(2,1)S(1)}, u32[]{:S(2)}, u32[]{:S(2)}) collective-permute-start(bf16[40,256]{1,0:T(8,128)(2,1)S(1)} %get-tuple-element.39.after_ref), channel_id=1, source_target_pairs={{0,5},{1,4},{2,7},{3,6},{4,1},{5,0},{6,3},{7,2},{8,13},{9,12},{10,... | collective-permute-start | bytes 61448 | tf_op jit(solution)/shard_map/ppermute | solution.py:76
  12.9 2.2 %shard_map.107 = (bf16[32,4,128,128]{3,2,1,0:T(8,128)(2,1)S(1)}, f32[256,256]{1,0:T(8,128)S(1)}) custom-call(bf16[32,4,128,128]{3,2,1,0:T(8,128)(2,1)} %factor_hbm.1, f32[256,256]{1,0:T(8,128)} %inner_hbm.1, bf16[40,256]{1,0:T(8,128)(2,1)S(1)} %get-tuple-element.39.after_ref), custom_call_target="tpu_custom_call" | custom-call | tf_op jit(solution)/shard_map/pallas_call | solution.py:394
  15.1 0.0 collective-permute-done.4.refs_2_
  15.1 1.3 %collective-permute-done.3.refs_1_ = bf16[40,256]{1,0:T(8,128)(2,1)S(1)} collective-permute-done((bf16[40,256]{1,0:T(8,128)(2,1)S(1)}, bf16[40,256]{1,0:T(8,128)(2,1)S(1)}, u32[]{:S(2)}, u32[]{:S(2)}) %collective-permute-start.3) | collective-permute-done | bytes 20512 | tf_op jit(solution)/shard_map/ppermute | solution.py:76
  16.4 0.0 collective-permute-done.2.refs_0_
  16.4 0.8 %shard_map.109 = (f32[32,40,128]{2,1,0:T(8,128)S(1)}, bf16[33,32,128]{2,1,0:T(8,128)(2,1)S(1)}, f32[40,256]{1,0:T(8,128)S(1)}) custom-call(f32[40,256]{1,0:T(8,128)S(1)} %shard_map.108.sums_ref, f32[256,256]{1,0:T(8,128)S(1)} %get-tuple-element.41.refs_4_.inner_ref, f32[2,32,128]{2,1,0:T(8,128)S(1)} %get-tuple-element.42.terms_ref, ...), custom_call_target="tpu_custom_call" | custom-call | tf_op jit(solution)/shard_map/pallas_call | solution.py:402
  17.1 0.0 copy-start
  17.2 0.8 %collective-permute-start.5 = (bf16[33,32,128]{2,1,0:T(8,128)(2,1)S(1)}, bf16[33,32,128]{2,1,0:T(8,128)(2,1)S(1)}, u32[]{:S(2)}, u32[]{:S(2)}) collective-permute-start(bf16[33,32,128]{2,1,0:T(8,128)(2,1)S(1)} %get-tuple-element.45.own_ref), channel_id=1, source_target_pairs={{1,3},{3,5},{5,7},{7,9},{9,11},{11,13},{13,15},{17,19},{19,21},{21... | collective-permute-start | bytes 811016 | tf_op jit(solution)/shard_map/ppermute | solution.py:18
  18.0 0.9 %shard_map.110 = (f32[32,48,128]{2,1,0:T(8,128)S(1)}, bf16[33,32,128]{2,1,0:T(8,128)(2,1)S(1)}, f32[96,40,128]{2,1,0:T(8,128)S(1)}) custom-call(bf16[33,32,128]{2,1,0:T(8,128)(2,1)S(1)} %get-tuple-element.45.own_ref, bf16[32,4,128,128]{3,2,1,0:T(8,128)(2,1)S(1)} %get-tuple-element.40.refs_3_.factor_ref), custom_call_target="tpu_custom_call" | custom-call | tf_op jit(solution)/shard_map/pallas_call | solution.py:407
  18.9 3.4 %collective-permute-start.7 = (bf16[33,32,128]{2,1,0:T(8,128)(2,1)S(1)}, bf16[33,32,128]{2,1,0:T(8,128)(2,1)S(1)}, u32[]{:S(2)}, u32[]{:S(2)}) collective-permute-start(bf16[33,32,128]{2,1,0:T(8,128)(2,1)S(1)} %get-tuple-element.49), channel_id=1, source_target_pairs={{0,2},{2,4},{4,6},{6,8},{8,10},{10,12},{12,14},{16,18},{18,20},{20... | collective-permute-start | bytes 811016 | tf_op jit(solution)/shard_map/ppermute | solution.py:18
  22.3 0.0 copy-done
  22.3 0.9 %shard_map.111 = (bf16[32,384,128]{2,1,0:T(8,128)(2,1)S(1)}, s32[3,32]{1,0:T(4,128)S(4)}) custom-call(bf16[32,4,128,128]{3,2,1,0:T(8,128)(2,1)S(1)} %get-tuple-element.40.refs_3_.factor_ref, s32[3,32]{1,0:T(4,128)S(1)} %bitcast.4, f32[32,48,128]{2,1,0:T(8,128)S(1)} %get-tuple-element.46.after_ref.own_image_ref), custom_call_target="tpu_custom_call" | custom-call | tf_op jit(solution)/shard_map/pallas_call | solution.py:415
  23.2 0.0 collective-permute-done.5.far_ref.far_odd_ref
  23.3 1.5 %collective-permute-start.6 = (bf16[33,32,128]{2,1,0:T(8,128)(2,1)S(1)}, bf16[33,32,128]{2,1,0:T(8,128)(2,1)S(1)}, u32[]{:S(2)}, u32[]{:S(2)}) collective-permute-start(bf16[33,32,128]{2,1,0:T(8,128)(2,1)S(1)} %shard_map.112), channel_id=1, source_target_pairs={{0,1},{1,0},{2,3},{3,2},{4,5},{5,4},{6,7},{7,6},{8,9},{9,8},{10,11... | collective-permute-start | bytes 811016 | tf_op jit(solution)/shard_map/ppermute | solution.py:22
  24.8 2.1 %collective-permute-done.7.far_even_ref = bf16[33,32,128]{2,1,0:T(8,128)(2,1)S(1)} collective-permute-done((bf16[33,32,128]{2,1,0:T(8,128)(2,1)S(1)}, bf16[33,32,128]{2,1,0:T(8,128)(2,1)S(1)}, u32[]{:S(2)}, u32[]{:S(2)}) %collective-permute-start.7) | collective-permute-done | bytes 270368 | tf_op jit(solution)/shard_map/ppermute | solution.py:18
  26.9 0.0 collective-permute-done.6.near_ref
  26.9 1.6 %shard_map.113 = (bf16[33,32,128]{2,1,0:T(8,128)(2,1)S(1)}, bf16[33,32,128]{2,1,0:T(8,128)(2,1)S(1)}, f32[96,40,128]{2,1,0:T(8,128)S(1)}, f32[40,128]{1,0:T(8,128)S(1)}, bf16[32,48,128]{2,1,0:T(8,128)(2,1)S(1)}) custom-call(s32[3,32]{1,0:T(4,128)S(4)} %get-tuple-element.47.ids_ref, ...), custom_call_target="tpu_custom_call", output_to_operand_aliasing={{2}: (8, {})} | custom-call | tf_op jit(solution)/shard_map/pallas_call | solution.py:423
  28.5 0.1 collective-permute-start.9
  28.6 1.3 %collective-permute-start.8 = (bf16[33,32,128]{2,1,0:T(8,128)(2,1)S(1)}, bf16[33,32,128]{2,1,0:T(8,128)(2,1)S(1)}, u32[]{:S(2)}, u32[]{:S(2)}) collective-permute-start(bf16[33,32,128]{2,1,0:T(8,128)(2,1)S(1)} %get-tuple-element.56.back_far_ref), channel_id=1, source_target_pairs={{2,0},{4,2},{6,4},{8,6},{10,8},{12,10},{14,12},{18,16},{20,18},{22... | collective-permute-start | bytes 811016 | tf_op jit(solution)/shard_map/ppermute | solution.py:18
  29.9 0.2 collective-permute-done.9.got_ref.mate_ref
  30.1 0.1 shard_map.115
  30.2 0.7 %collective-permute-start.10 = (bf16[33,32,128]{2,1,0:T(8,128)(2,1)S(1)}, bf16[33,32,128]{2,1,0:T(8,128)(2,1)S(1)}, u32[]{:S(2)}, u32[]{:S(2)}) collective-permute-start(bf16[33,32,128]{2,1,0:T(8,128)(2,1)S(1)} %shard_map.115), channel_id=1, source_target_pairs={{3,1},{5,3},{7,5},{9,7},{11,9},{13,11},{15,13},{19,17},{21,19},{23... | collective-permute-start | bytes 811016 | tf_op jit(solution)/shard_map/ppermute | solution.py:18
  30.9 0.4 shard_map.114
  31.3 7.9 %collective-permute-done.8.even_ref = bf16[33,32,128]{2,1,0:T(8,128)(2,1)S(1)} collective-permute-done((bf16[33,32,128]{2,1,0:T(8,128)(2,1)S(1)}, bf16[33,32,128]{2,1,0:T(8,128)(2,1)S(1)}, u32[]{:S(2)}, u32[]{:S(2)}) %collective-permute-start.8) | collective-permute-done | bytes 270368 | tf_op jit(solution)/shard_map/ppermute | solution.py:18
  39.2 0.0 collective-permute-done.10.odd_ref
  39.2 0.5 shard_map.116
  39.7 0.9 %collective-permute-start.11 = (f32[40,256]{1,0:T(8,128)S(1)}, f32[40,256]{1,0:T(8,128)S(1)}, u32[]{:S(2)}, u32[]{:S(2)}) collective-permute-start(f32[40,256]{1,0:T(8,128)S(1)} %get-tuple-element.59.x_ref), channel_id=1, source_target_pairs={{0,1},{1,0},{2,3},{3,2},{4,5},{5,4},{6,7},{7,6},{8,9},{9,8},{10,11... | collective-permute-start | bytes 122888 | tf_op jit(solution)/shard_map/ppermute | solution.py:76
  40.7 0.9 %collective-permute-done.11.refs_0_ = f32[40,256]{1,0:T(8,128)S(1)} collective-permute-done((f32[40,256]{1,0:T(8,128)S(1)}, f32[40,256]{1,0:T(8,128)S(1)}, u32[]{:S(2)}, u32[]{:S(2)}) %collective-permute-start.11) | collective-permute-done | bytes 40992 | tf_op jit(solution)/shard_map/ppermute | solution.py:76
  41.5 2.9 %collective-permute-start.12 = (bf16[40,256]{1,0:T(8,128)(2,1)S(1)}, bf16[40,256]{1,0:T(8,128)(2,1)S(1)}, u32[]{:S(2)}, u32[]{:S(2)}) collective-permute-start(bf16[40,256]{1,0:T(8,128)(2,1)S(1)} %get-tuple-element.61), channel_id=1, source_target_pairs={{0,3},{1,2},{2,1},{3,0},{4,7},{5,6},{6,5},{7,4},{8,11},{9,10},{10,... | collective-permute-start | bytes 61448 | tf_op jit(solution)/shard_map/ppermute | solution.py:76
  44.5 1.5 %collective-permute-done.12.refs_0_ = bf16[40,256]{1,0:T(8,128)(2,1)S(1)} collective-permute-done((bf16[40,256]{1,0:T(8,128)(2,1)S(1)}, bf16[40,256]{1,0:T(8,128)(2,1)S(1)}, u32[]{:S(2)}, u32[]{:S(2)}) %collective-permute-start.12) | collective-permute-done | bytes 20512 | tf_op jit(solution)/shard_map/ppermute | solution.py:76
  46.0 2.6 %collective-permute-start.15 = (bf16[40,256]{1,0:T(8,128)(2,1)S(1)}, bf16[40,256]{1,0:T(8,128)(2,1)S(1)}, u32[]{:S(2)}, u32[]{:S(2)}) collective-permute-start(bf16[40,256]{1,0:T(8,128)(2,1)S(1)} %get-tuple-element.63), channel_id=1, source_target_pairs={{0,13},{1,12},{2,15},{3,14},{4,9},{5,8},{6,11},{7,10},{8,5},{9,4},... | collective-permute-start | bytes 61448 | tf_op jit(solution)/shard_map/ppermute | solution.py:76
  48.5 0.0 collective-permute-start.14
  48.6 1.4 %collective-permute-start.13 = (bf16[40,256]{1,0:T(8,128)(2,1)S(1)}, bf16[40,256]{1,0:T(8,128)(2,1)S(1)}, u32[]{:S(2)}, u32[]{:S(2)}) collective-permute-start(bf16[40,256]{1,0:T(8,128)(2,1)S(1)} %get-tuple-element.63), channel_id=1, source_target_pairs={{0,5},{1,4},{2,7},{3,6},{4,1},{5,0},{6,3},{7,2},{8,13},{9,12},{10,... | collective-permute-start | bytes 61448 | tf_op jit(solution)/shard_map/ppermute | solution.py:76
  49.9 1.1 %collective-permute-done.15.refs_2_ = bf16[40,256]{1,0:T(8,128)(2,1)S(1)} collective-permute-done((bf16[40,256]{1,0:T(8,128)(2,1)S(1)}, bf16[40,256]{1,0:T(8,128)(2,1)S(1)}, u32[]{:S(2)}, u32[]{:S(2)}) %collective-permute-start.15) | collective-permute-done | bytes 20512 | tf_op jit(solution)/shard_map/ppermute | solution.py:76
  51.1 1.7 %collective-permute-done.14.refs_1_ = bf16[40,256]{1,0:T(8,128)(2,1)S(1)} collective-permute-done((bf16[40,256]{1,0:T(8,128)(2,1)S(1)}, bf16[40,256]{1,0:T(8,128)(2,1)S(1)}, u32[]{:S(2)}, u32[]{:S(2)}) %collective-permute-start.14) | collective-permute-done | bytes 20512 | tf_op jit(solution)/shard_map/ppermute | solution.py:76
  52.7 0.0 collective-permute-done.13.refs_0_
  52.8 1.6 %shard_map.120 = (f32[33,4096]{1,0:T(8,128)}, f32[33,4096]{1,0:T(8,128)}, f32[33,4096]{1,0:T(8,128)}) custom-call(f32[40,256]{1,0:T(8,128)S(1)} %shard_map.108.sums_ref, f32[40,256]{1,0:T(8,128)S(1)} %get-tuple-element.44.product_ref, f32[40,256]{1,0:T(8,128)S(1)} %shard_map.119.hess_sums_ref, f32[256,256]{1,0:T(8,128)S(1)} %get-tuple-element.41.refs_4_.inner_ref, ...), custom_call_target="tpu_custom_call" | custom-call | tf_op jit(solution)/shard_map/pallas_call | solution.py:440
  (7 shorter events, 0.1 us)
Async XLA Ops:
  2.8 1.4 %collective-permute-start = (f32[40,256]{1,0:T(8,128)S(1)}, f32[40,256]{1,0:T(8,128)S(1)}, u32[]{:S(2)}, u32[]{:S(2)}) collective-permute-start(f32[40,256]{1,0:T(8,128)S(1)} %get-tuple-element.34.x_ref), channel_id=1, source_target_pairs={{0,1},{1,0},{2,3},{3,2},{4,5},{5,4},{6,7},{7,6},{8,9},{9,8},{10,11... | collective-permute-start | bytes 122888 | tf_op jit(solution)/shard_map/ppermute | solution.py:76
  4.2 4.1 %collective-permute-start.1 = (bf16[40,256]{1,0:T(8,128)(2,1)S(1)}, bf16[40,256]{1,0:T(8,128)(2,1)S(1)}, u32[]{:S(2)}, u32[]{:S(2)}) collective-permute-start(bf16[40,256]{1,0:T(8,128)(2,1)S(1)} %get-tuple-element.36.after_ref), channel_id=1, source_target_pairs={{0,3},{1,2},{2,1},{3,0},{4,7},{5,6},{6,5},{7,4},{8,11},{9,10},{10,... | collective-permute-start | bytes 61448 | tf_op jit(solution)/shard_map/ppermute | solution.py:76
  8.4 6.7 %collective-permute-start.4 = (bf16[40,256]{1,0:T(8,128)(2,1)S(1)}, bf16[40,256]{1,0:T(8,128)(2,1)S(1)}, u32[]{:S(2)}, u32[]{:S(2)}) collective-permute-start(bf16[40,256]{1,0:T(8,128)(2,1)S(1)} %get-tuple-element.39.after_ref), channel_id=1, source_target_pairs={{0,13},{1,12},{2,15},{3,14},{4,9},{5,8},{6,11},{7,10},{8,5},{9,4},... | collective-permute-start | bytes 61448 | tf_op jit(solution)/shard_map/ppermute | solution.py:76
  12.3 4.1 %collective-permute-start.3 = (bf16[40,256]{1,0:T(8,128)(2,1)S(1)}, bf16[40,256]{1,0:T(8,128)(2,1)S(1)}, u32[]{:S(2)}, u32[]{:S(2)}) collective-permute-start(bf16[40,256]{1,0:T(8,128)(2,1)S(1)} %get-tuple-element.39.after_ref), channel_id=1, source_target_pairs={{0,9},{1,8},{2,11},{3,10},{4,13},{5,12},{6,15},{7,14},{8,1},{9,0},... | collective-permute-start | bytes 61448 | tf_op jit(solution)/shard_map/ppermute | solution.py:76
  12.3 4.1 %collective-permute-start.2 = (bf16[40,256]{1,0:T(8,128)(2,1)S(1)}, bf16[40,256]{1,0:T(8,128)(2,1)S(1)}, u32[]{:S(2)}, u32[]{:S(2)}) collective-permute-start(bf16[40,256]{1,0:T(8,128)(2,1)S(1)} %get-tuple-element.39.after_ref), channel_id=1, source_target_pairs={{0,5},{1,4},{2,7},{3,6},{4,1},{5,0},{6,3},{7,2},{8,13},{9,12},{10,... | collective-permute-start | bytes 61448 | tf_op jit(solution)/shard_map/ppermute | solution.py:76
  17.1 5.2 %copy-start = (s32[32,3]{0,1:T(4,128)S(1)}, s32[32,3]{0,1:T(4,128)}, u32[]{:S(2)}) copy-start(s32[32,3]{0,1:T(4,128)} %param.13) | copy-start | bytes 1156
  17.2 6.1 %collective-permute-start.5 = (bf16[33,32,128]{2,1,0:T(8,128)(2,1)S(1)}, bf16[33,32,128]{2,1,0:T(8,128)(2,1)S(1)}, u32[]{:S(2)}, u32[]{:S(2)}) collective-permute-start(bf16[33,32,128]{2,1,0:T(8,128)(2,1)S(1)} %get-tuple-element.45.own_ref), channel_id=1, source_target_pairs={{1,3},{3,5},{5,7},{7,9},{9,11},{11,13},{13,15},{17,19},{19,21},{21... | collective-permute-start | bytes 811016 | tf_op jit(solution)/shard_map/ppermute | solution.py:18
  18.9 8.0 %collective-permute-start.7 = (bf16[33,32,128]{2,1,0:T(8,128)(2,1)S(1)}, bf16[33,32,128]{2,1,0:T(8,128)(2,1)S(1)}, u32[]{:S(2)}, u32[]{:S(2)}) collective-permute-start(bf16[33,32,128]{2,1,0:T(8,128)(2,1)S(1)} %get-tuple-element.49), channel_id=1, source_target_pairs={{0,2},{2,4},{4,6},{6,8},{8,10},{10,12},{12,14},{16,18},{18,20},{20... | collective-permute-start | bytes 811016 | tf_op jit(solution)/shard_map/ppermute | solution.py:18
  23.3 3.6 %collective-permute-start.6 = (bf16[33,32,128]{2,1,0:T(8,128)(2,1)S(1)}, bf16[33,32,128]{2,1,0:T(8,128)(2,1)S(1)}, u32[]{:S(2)}, u32[]{:S(2)}) collective-permute-start(bf16[33,32,128]{2,1,0:T(8,128)(2,1)S(1)} %shard_map.112), channel_id=1, source_target_pairs={{0,1},{1,0},{2,3},{3,2},{4,5},{5,4},{6,7},{7,6},{8,9},{9,8},{10,11... | collective-permute-start | bytes 811016 | tf_op jit(solution)/shard_map/ppermute | solution.py:22
  28.5 1.6 %collective-permute-start.9 = (bf16[33,32,128]{2,1,0:T(8,128)(2,1)S(1)}, bf16[33,32,128]{2,1,0:T(8,128)(2,1)S(1)}, u32[]{:S(2)}, u32[]{:S(2)}) collective-permute-start(bf16[33,32,128]{2,1,0:T(8,128)(2,1)S(1)} %get-tuple-element.57), channel_id=1, source_target_pairs={{0,1},{1,0},{2,3},{3,2},{4,5},{5,4},{6,7},{7,6},{8,9},{9,8},{10,11... | collective-permute-start | bytes 811016 | tf_op jit(solution)/shard_map/ppermute | solution.py:22
  28.6 10.6 %collective-permute-start.8 = (bf16[33,32,128]{2,1,0:T(8,128)(2,1)S(1)}, bf16[33,32,128]{2,1,0:T(8,128)(2,1)S(1)}, u32[]{:S(2)}, u32[]{:S(2)}) collective-permute-start(bf16[33,32,128]{2,1,0:T(8,128)(2,1)S(1)} %get-tuple-element.56.back_far_ref), channel_id=1, source_target_pairs={{2,0},{4,2},{6,4},{8,6},{10,8},{12,10},{14,12},{18,16},{20,18},{22... | collective-permute-start | bytes 811016 | tf_op jit(solution)/shard_map/ppermute | solution.py:18
  30.2 9.0 %collective-permute-start.10 = (bf16[33,32,128]{2,1,0:T(8,128)(2,1)S(1)}, bf16[33,32,128]{2,1,0:T(8,128)(2,1)S(1)}, u32[]{:S(2)}, u32[]{:S(2)}) collective-permute-start(bf16[33,32,128]{2,1,0:T(8,128)(2,1)S(1)} %shard_map.115), channel_id=1, source_target_pairs={{3,1},{5,3},{7,5},{9,7},{11,9},{13,11},{15,13},{19,17},{21,19},{23... | collective-permute-start | bytes 811016 | tf_op jit(solution)/shard_map/ppermute | solution.py:18
  39.7 1.8 %collective-permute-start.11 = (f32[40,256]{1,0:T(8,128)S(1)}, f32[40,256]{1,0:T(8,128)S(1)}, u32[]{:S(2)}, u32[]{:S(2)}) collective-permute-start(f32[40,256]{1,0:T(8,128)S(1)} %get-tuple-element.59.x_ref), channel_id=1, source_target_pairs={{0,1},{1,0},{2,3},{3,2},{4,5},{5,4},{6,7},{7,6},{8,9},{9,8},{10,11... | collective-permute-start | bytes 122888 | tf_op jit(solution)/shard_map/ppermute | solution.py:76
  41.5 4.4 %collective-permute-start.12 = (bf16[40,256]{1,0:T(8,128)(2,1)S(1)}, bf16[40,256]{1,0:T(8,128)(2,1)S(1)}, u32[]{:S(2)}, u32[]{:S(2)}) collective-permute-start(bf16[40,256]{1,0:T(8,128)(2,1)S(1)} %get-tuple-element.61), channel_id=1, source_target_pairs={{0,3},{1,2},{2,1},{3,0},{4,7},{5,6},{6,5},{7,4},{8,11},{9,10},{10,... | collective-permute-start | bytes 61448 | tf_op jit(solution)/shard_map/ppermute | solution.py:76
  46.0 5.1 %collective-permute-start.15 = (bf16[40,256]{1,0:T(8,128)(2,1)S(1)}, bf16[40,256]{1,0:T(8,128)(2,1)S(1)}, u32[]{:S(2)}, u32[]{:S(2)}) collective-permute-start(bf16[40,256]{1,0:T(8,128)(2,1)S(1)} %get-tuple-element.63), channel_id=1, source_target_pairs={{0,13},{1,12},{2,15},{3,14},{4,9},{5,8},{6,11},{7,10},{8,5},{9,4},... | collective-permute-start | bytes 61448 | tf_op jit(solution)/shard_map/ppermute | solution.py:76
  48.5 4.2 %collective-permute-start.14 = (bf16[40,256]{1,0:T(8,128)(2,1)S(1)}, bf16[40,256]{1,0:T(8,128)(2,1)S(1)}, u32[]{:S(2)}, u32[]{:S(2)}) collective-permute-start(bf16[40,256]{1,0:T(8,128)(2,1)S(1)} %get-tuple-element.63), channel_id=1, source_target_pairs={{0,9},{1,8},{2,11},{3,10},{4,13},{5,12},{6,15},{7,14},{8,1},{9,0},... | collective-permute-start | bytes 61448 | tf_op jit(solution)/shard_map/ppermute | solution.py:76
  48.6 4.2 %collective-permute-start.13 = (bf16[40,256]{1,0:T(8,128)(2,1)S(1)}, bf16[40,256]{1,0:T(8,128)(2,1)S(1)}, u32[]{:S(2)}, u32[]{:S(2)}) collective-permute-start(bf16[40,256]{1,0:T(8,128)(2,1)S(1)} %get-tuple-element.63), channel_id=1, source_target_pairs={{0,5},{1,4},{2,7},{3,6},{4,1},{5,0},{6,3},{7,2},{8,13},{9,12},{10,... | collective-permute-start | bytes 61448 | tf_op jit(solution)/shard_map/ppermute | solution.py:76

commit v13 on v12

--- a/solution.py
+++ b/solution.py
@@ -191,9 +191,8 @@
     return jnp.concatenate([most, last.astype(BF16)], axis=0)
 
 
-def own_image_kernel(tall, own_ref, factor_ref, image_ref, again_ref, zeros_ref, last_ref):
+def own_image_kernel(tall, own_ref, factor_ref, image_ref, zeros_ref, last_ref):
     blocks, bs = last_ref.shape
-    again_ref[...] = own_ref[...]
     zeros_ref[...] = jnp.zeros_like(zeros_ref)
     last_ref[...] = own_ref[blocks].astype(F32)
     for b in range(blocks):
@@ -232,16 +231,16 @@
 
 
 def hessian_kernel(
-    rows, ids_ref, factor_ref, turned_ref, own_image_ref, near_ref, far_even_ref, far_odd_ref, own_ref, zeros_ref,
+    rows, ids_ref, factor_ref, turned_ref, own_image_ref, near_ref, far_ref, own_ref, zeros_ref,
     back_far_ref, back_near_ref, total_ref, curve_ref, image_ref, around_ref, around_last_ref, last_ref,
 ):
     blocks, taps, bs, _ = factor_ref.shape
     count = around_ref.shape[1]
     tall = image_ref.shape[1]
-    for i, refs in enumerate(((far_even_ref, far_odd_ref), (near_ref,), (own_ref,))):
+    for i, ref in enumerate((far_ref, near_ref, own_ref)):
         at = slice(i * blocks, (i + 1) * blocks)
-        around_ref[at] = functools.reduce(jnp.add, [ref[:blocks] for ref in refs])
-        around_last_ref[at] = functools.reduce(jnp.add, [ref[blocks].astype(F32) for ref in refs])
+        around_ref[at] = ref[:blocks]
+        around_last_ref[at] = ref[blocks].astype(F32)
     first = (lax.axis_index("space") - 2) * blocks
     curve = jnp.zeros((rows, bs), F32)
     ids = lambda b, k: ids_ref[k - 1, b] - first
@@ -402,15 +401,14 @@
     direction, rounded, product = call(
         direction_kernel, [vmem] * 5, [field, packed, sum_shape], [vmem((blocks, bs), F32)]
     )(sums, inner_inverse, terms, right_side, turned_map)
-    far_odd = sent(rounded, "space", 2, (1,))
+    far = sent(rounded, "space", 2)
     around = ((3 * blocks, rows, bs), F32)
-    own_image, again, zeros = call(
+    own_image, zeros = call(
         functools.partial(own_image_kernel, tall),
         [vmem] * 2,
-        [((blocks, tall, bs), F32), packed, around],
+        [((blocks, tall, bs), F32), around],
         [vmem((blocks, bs), F32)],
     )(rounded, factor)
-    far_even = sent(again, "space", 2, (0,))
     shape = (blocks, (factor.shape[1] - 1) * bs, bs)
     turned, ids = call(
         turn_kernel,
@@ -419,14 +417,14 @@
         [pltpu.SemaphoreType.DMA],
         spaces=(vmem, smem),
     )(factor, cond_ids.T, own_image)
-    near = swapped(call(pass_on_kernel, [vmem, vmem, pl.ANY], [packed])(rounded, far_odd, turned), "space")
+    near = swapped(call(pass_on_kernel, [vmem, vmem, pl.ANY], [packed])(rounded, far, turned), "space")
     back_far, back_near, back_own, curve, image = call(
         functools.partial(hessian_kernel, rows),
-        [smem] + [vmem] * 8,
+        [smem] + [vmem] * 7,
         [packed, packed, around, ((rows, bs), F32), ((blocks, tall, bs), BF16)],
         [vmem((3 * blocks, count, bs), BF16), vmem((3 * blocks, bs), F32), vmem((blocks, bs), F32)],
-        aliases={8: 2},
-    )(ids, factor, turned, own_image, near, far_even, far_odd, rounded, zeros)
+        aliases={7: 2},
+    )(ids, factor, turned, own_image, near, far, rounded, zeros)
     mate = swapped(back_near, "space")
     from_even = sent(back_far, "space", -2, (0,))
     from_odd = sent(call(join_kernel, [vmem] * 2, [packed])(back_far, mate), "space", -2, (1,))

time: 54.6 us -> 56.3 us (1.031)
  waiting for transfers between devices: 18.4 us -> 22.4 us
  starting transfers between devices: 23.3 us -> 21.1 us
    ppermute x4 -> x3, waiting for transfers between devices: 9.98 us -> 12.5 us  [sent(): lax.ppermute(block, axis, [(i, i + distance) for i in devices if i % 2 in...]
    ppermute x2, waiting for transfers between devices: 0.24 us -> 1.72 us  [swapped(): lax.ppermute(block, axis, [(i, i ^ 1) for i in range(lax.axis_size(axis))])]
    ppermute x2, starting transfers between devices: 1.61 us -> 0.21 us  [swapped(): lax.ppermute(block, axis, [(i, i ^ 1) for i in range(lax.axis_size(axis))])]
    ppermute x4 -> x3, starting transfers between devices: 6.18 us -> 5.5 us  [sent(): lax.ppermute(block, axis, [(i, i + distance) for i in devices if i % 2 in...]
  transfers between devices with their start and end apart: 16 -> 15, of which waited for: 10 -> 11; matrix products, arithmetic and copies ran while one was open for 0% -> 0% of each run, Pallas kernels for 10% -> 9%
where the time goes in v13:
time: 56.3 us; the launch traced here: 56.1 us
  waiting for transfers between devices  22.4 us (40%)
  starting transfers between devices  21.1 us (37%)
  Pallas kernels  11.8 us (21%)
  between operations  0.76 us (1%)
    ppermute x10, starting transfers between devices, total(): lax.ppermute(msg, axis, [(j, j ^ d) for j in range(n)])  15.4 us
    ppermute x3, waiting for transfers between devices, sent(): lax.ppermute(block, axis, [(i, i + distance) for i in devices if i % 2 in...  12.5 us
    ppermute x10, waiting for transfers between devices, total(): lax.ppermute(msg, axis, [(j, j ^ d) for j in range(n)])  8.16 us
    ppermute x3, starting transfers between devices, sent(): lax.ppermute(block, axis, [(i, i + distance) for i in devices if i % 2 in...  5.5 us
    pallas_call x1, Pallas kernels, load(): call(load_kernel, [pl.ANY] * 3, outs, [pltpu.SemaphoreType.DMA((2,))])  2.23 us
    pallas_call x1, Pallas kernels, body(): call(project_kernel, [pl.ANY] * 5, [sum_shape, ((2, blocks, bs), F32), fi...  2.15 us
    ppermute x2, waiting for transfers between devices, swapped(): lax.ppermute(block, axis, [(i, i ^ 1) for i in range(lax.axis_size(axis))])  1.72 us
    pallas_call x1, Pallas kernels, body(): call(finish_kernel, [vmem] * 9, [whole] * 3, scratch, keep=False)  1.63 us
  transfers between devices with their start and end apart: 15, of which 11 were waited for; matrix products, arithmetic and copies ran while one was open for 0% of the time, Pallas kernels for 9%

profile of v13, /device:TPU:0, one launch (start us, length us, event | category | flops | bytes accessed | tf_op | source)
XLA Modules:
  0.0 56.1 jit_solution(2171753913930701361)
XLA Ops:
  0.6 2.2 %shard_map.103 = (f32[40,256]{1,0:T(8,128)S(1)}, f32[2,32,128]{2,1,0:T(8,128)S(1)}, f32[32,40,128]{2,1,0:T(8,128)S(1)}, bf16[4096,256]{1,0:T(8,128)(2,1)S(1)}) custom-call(f32[32,128]{1,0:T(8,128)} %bitcast.5, s32[32,128]{1,0:T(8,128)} %bitcast.6, f32[32,128]{1,0:T(8,128)} %bitcast.7, f32[32,4096]{1,0:T(8,128)} %probes_hbm.1, bf16[4096,256]{1,0:T(8,128)(2,1)} %map_hbm.1), custom_call_target="tpu_custom_call" | custom-call | tf_op jit(solution)/shard_map/pallas_call | solution.py:377
  2.8 0.5 collective-permute-start
  3.3 0.9 %collective-permute-done.refs_0_ = f32[40,256]{1,0:T(8,128)S(1)} collective-permute-done((f32[40,256]{1,0:T(8,128)S(1)}, f32[40,256]{1,0:T(8,128)S(1)}, u32[]{:S(2)}, u32[]{:S(2)}) %collective-permute-start) | collective-permute-done | bytes 40992 | tf_op jit(solution)/shard_map/ppermute | solution.py:76
  4.2 2.7 %collective-permute-start.1 = (bf16[40,256]{1,0:T(8,128)(2,1)S(1)}, bf16[40,256]{1,0:T(8,128)(2,1)S(1)}, u32[]{:S(2)}, u32[]{:S(2)}) collective-permute-start(bf16[40,256]{1,0:T(8,128)(2,1)S(1)} %get-tuple-element.35.after_ref), channel_id=1, source_target_pairs={{0,3},{1,2},{2,1},{3,0},{4,7},{5,6},{6,5},{7,4},{8,11},{9,10},{10,... | collective-permute-start | bytes 61448 | tf_op jit(solution)/shard_map/ppermute | solution.py:76
  6.9 0.6 %shard_map.105.refs_1_.map_ref = bf16[256,4096]{1,0:T(8,128)(2,1)S(1)} custom-call(bf16[4096,256]{1,0:T(8,128)(2,1)S(1)} %get-tuple-element.36.map_ref, bf16[40,256]{1,0:T(8,128)(2,1)S(1)} %get-tuple-element.35.after_ref), custom_call_target="tpu_custom_call" | custom-call | tf_op jit(solution)/shard_map/pallas_call | solution.py:398
  7.5 0.8 %collective-permute-done.1.refs_0_ = bf16[40,256]{1,0:T(8,128)(2,1)S(1)} collective-permute-done((bf16[40,256]{1,0:T(8,128)(2,1)S(1)}, bf16[40,256]{1,0:T(8,128)(2,1)S(1)}, u32[]{:S(2)}, u32[]{:S(2)}) %collective-permute-start.1) | collective-permute-done | bytes 20512 | tf_op jit(solution)/shard_map/ppermute | solution.py:76
  8.4 3.9 %collective-permute-start.4 = (bf16[40,256]{1,0:T(8,128)(2,1)S(1)}, bf16[40,256]{1,0:T(8,128)(2,1)S(1)}, u32[]{:S(2)}, u32[]{:S(2)}) collective-permute-start(bf16[40,256]{1,0:T(8,128)(2,1)S(1)} %get-tuple-element.38.after_ref), channel_id=1, source_target_pairs={{0,13},{1,12},{2,15},{3,14},{4,9},{5,8},{6,11},{7,10},{8,5},{9,4},... | collective-permute-start | bytes 61448 | tf_op jit(solution)/shard_map/ppermute | solution.py:76
  12.3 0.0 collective-permute-start.3
  12.3 0.6 %collective-permute-start.2 = (bf16[40,256]{1,0:T(8,128)(2,1)S(1)}, bf16[40,256]{1,0:T(8,128)(2,1)S(1)}, u32[]{:S(2)}, u32[]{:S(2)}) collective-permute-start(bf16[40,256]{1,0:T(8,128)(2,1)S(1)} %get-tuple-element.38.after_ref), channel_id=1, source_target_pairs={{0,5},{1,4},{2,7},{3,6},{4,1},{5,0},{6,3},{7,2},{8,13},{9,12},{10,... | collective-permute-start | bytes 61448 | tf_op jit(solution)/shard_map/ppermute | solution.py:76
  12.9 2.2 %shard_map.107 = (bf16[32,4,128,128]{3,2,1,0:T(8,128)(2,1)S(1)}, f32[256,256]{1,0:T(8,128)S(1)}) custom-call(bf16[32,4,128,128]{3,2,1,0:T(8,128)(2,1)} %factor_hbm.1, f32[256,256]{1,0:T(8,128)} %inner_hbm.1, bf16[40,256]{1,0:T(8,128)(2,1)S(1)} %get-tuple-element.38.after_ref), custom_call_target="tpu_custom_call" | custom-call | tf_op jit(solution)/shard_map/pallas_call | solution.py:393
  15.1 0.0 collective-permute-done.4.refs_2_
  15.1 1.3 %collective-permute-done.3.refs_1_ = bf16[40,256]{1,0:T(8,128)(2,1)S(1)} collective-permute-done((bf16[40,256]{1,0:T(8,128)(2,1)S(1)}, bf16[40,256]{1,0:T(8,128)(2,1)S(1)}, u32[]{:S(2)}, u32[]{:S(2)}) %collective-permute-start.3) | collective-permute-done | bytes 20512 | tf_op jit(solution)/shard_map/ppermute | solution.py:76
  16.4 0.0 collective-permute-done.2.refs_0_
  16.4 0.8 %shard_map.109 = (f32[32,40,128]{2,1,0:T(8,128)S(1)}, bf16[33,32,128]{2,1,0:T(8,128)(2,1)S(1)}, f32[40,256]{1,0:T(8,128)S(1)}) custom-call(f32[40,256]{1,0:T(8,128)S(1)} %shard_map.108.sums_ref, f32[256,256]{1,0:T(8,128)S(1)} %get-tuple-element.40.refs_4_.inner_ref, f32[2,32,128]{2,1,0:T(8,128)S(1)} %get-tuple-element.41.terms_ref, ...), custom_call_target="tpu_custom_call" | custom-call | tf_op jit(solution)/shard_map/pallas_call | solution.py:401
  17.1 0.0 copy-start
  17.2 3.5 %collective-permute-start.5 = (bf16[33,32,128]{2,1,0:T(8,128)(2,1)S(1)}, bf16[33,32,128]{2,1,0:T(8,128)(2,1)S(1)}, u32[]{:S(2)}, u32[]{:S(2)}) collective-permute-start(bf16[33,32,128]{2,1,0:T(8,128)(2,1)S(1)} %get-tuple-element.44.own_ref), channel_id=1, source_target_pairs={{0,2},{1,3},{2,4},{3,5},{4,6},{5,7},{6,8},{7,9},{8,10},{9,11},{10,... | collective-permute-start | bytes 811016 | tf_op jit(solution)/shard_map/ppermute | solution.py:18
  20.7 0.9 %shard_map.110 = (f32[32,48,128]{2,1,0:T(8,128)S(1)}, f32[96,40,128]{2,1,0:T(8,128)S(1)}) custom-call(bf16[33,32,128]{2,1,0:T(8,128)(2,1)S(1)} %get-tuple-element.44.own_ref, bf16[32,4,128,128]{3,2,1,0:T(8,128)(2,1)S(1)} %get-tuple-element.39.refs_3_.factor_ref), custom_call_target="tpu_custom_call" | custom-call | tf_op jit(solution)/shard_map/pallas_call | solution.py:406
  21.6 0.0 copy-done
  21.6 0.9 %shard_map.111 = (bf16[32,384,128]{2,1,0:T(8,128)(2,1)S(1)}, s32[3,32]{1,0:T(4,128)S(4)}) custom-call(bf16[32,4,128,128]{3,2,1,0:T(8,128)(2,1)S(1)} %get-tuple-element.39.refs_3_.factor_ref, s32[3,32]{1,0:T(4,128)S(1)} %bitcast.4, f32[32,48,128]{2,1,0:T(8,128)S(1)} %get-tuple-element.45.after_ref.own_image_ref), custom_call_target="tpu_custom_call" | custom-call | tf_op jit(solution)/shard_map/pallas_call | solution.py:413
  22.5 4.4 %collective-permute-done.5.far_ref = bf16[33,32,128]{2,1,0:T(8,128)(2,1)S(1)} collective-permute-done((bf16[33,32,128]{2,1,0:T(8,128)(2,1)S(1)}, bf16[33,32,128]{2,1,0:T(8,128)(2,1)S(1)}, u32[]{:S(2)}, u32[]{:S(2)}) %collective-permute-start.5) | collective-permute-done | bytes 270368 | tf_op jit(solution)/shard_map/ppermute | solution.py:18
  27.0 0.1 collective-permute-start.6
  27.0 1.5 %collective-permute-done.6.near_ref = bf16[33,32,128]{2,1,0:T(8,128)(2,1)S(1)} collective-permute-done((bf16[33,32,128]{2,1,0:T(8,128)(2,1)S(1)}, bf16[33,32,128]{2,1,0:T(8,128)(2,1)S(1)}, u32[]{:S(2)}, u32[]{:S(2)}) %collective-permute-start.6) | collective-permute-done | bytes 270368 | tf_op jit(solution)/shard_map/ppermute | solution.py:22
  28.6 1.5 %shard_map.113 = (bf16[33,32,128]{2,1,0:T(8,128)(2,1)S(1)}, bf16[33,32,128]{2,1,0:T(8,128)(2,1)S(1)}, f32[96,40,128]{2,1,0:T(8,128)S(1)}, f32[40,128]{1,0:T(8,128)S(1)}, bf16[32,48,128]{2,1,0:T(8,128)(2,1)S(1)}) custom-call(s32[3,32]{1,0:T(4,128)S(4)} %get-tuple-element.46.ids_ref, ...), custom_call_target="tpu_custom_call", output_to_operand_aliasing={{2}: (7, {})} | custom-call | tf_op jit(solution)/shard_map/pallas_call | solution.py:421
  30.1 0.1 collective-permute-start.8
  30.2 1.3 %collective-permute-start.7 = (bf16[33,32,128]{2,1,0:T(8,128)(2,1)S(1)}, bf16[33,32,128]{2,1,0:T(8,128)(2,1)S(1)}, u32[]{:S(2)}, u32[]{:S(2)}) collective-permute-start(bf16[33,32,128]{2,1,0:T(8,128)(2,1)S(1)} %get-tuple-element.54.back_far_ref), channel_id=1, source_target_pairs={{2,0},{4,2},{6,4},{8,6},{10,8},{12,10},{14,12},{18,16},{20,18},{22... | collective-permute-start | bytes 811016 | tf_op jit(solution)/shard_map/ppermute | solution.py:18
  31.5 0.2 collective-permute-done.8.got_ref.mate_ref
  31.7 0.1 shard_map.115
  31.8 0.7 %collective-permute-start.9 = (bf16[33,32,128]{2,1,0:T(8,128)(2,1)S(1)}, bf16[33,32,128]{2,1,0:T(8,128)(2,1)S(1)}, u32[]{:S(2)}, u32[]{:S(2)}) collective-permute-start(bf16[33,32,128]{2,1,0:T(8,128)(2,1)S(1)} %shard_map.115), channel_id=1, source_target_pairs={{3,1},{5,3},{7,5},{9,7},{11,9},{13,11},{15,13},{19,17},{21,19},{23... | collective-permute-start | bytes 811016 | tf_op jit(solution)/shard_map/ppermute | solution.py:18
  32.5 0.4 shard_map.114
  32.9 8.1 %collective-permute-done.7.even_ref = bf16[33,32,128]{2,1,0:T(8,128)(2,1)S(1)} collective-permute-done((bf16[33,32,128]{2,1,0:T(8,128)(2,1)S(1)}, bf16[33,32,128]{2,1,0:T(8,128)(2,1)S(1)}, u32[]{:S(2)}, u32[]{:S(2)}) %collective-permute-start.7) | collective-permute-done | bytes 270368 | tf_op jit(solution)/shard_map/ppermute | solution.py:18
  41.0 0.0 collective-permute-done.9.odd_ref
  41.0 0.5 shard_map.116
  41.5 0.8 %collective-permute-start.10 = (f32[40,256]{1,0:T(8,128)S(1)}, f32[40,256]{1,0:T(8,128)S(1)}, u32[]{:S(2)}, u32[]{:S(2)}) collective-permute-start(f32[40,256]{1,0:T(8,128)S(1)} %get-tuple-element.57.x_ref), channel_id=1, source_target_pairs={{0,1},{1,0},{2,3},{3,2},{4,5},{5,4},{6,7},{7,6},{8,9},{9,8},{10,11... | collective-permute-start | bytes 122888 | tf_op jit(solution)/shard_map/ppermute | solution.py:76
  42.3 0.9 %collective-permute-done.10.refs_0_ = f32[40,256]{1,0:T(8,128)S(1)} collective-permute-done((f32[40,256]{1,0:T(8,128)S(1)}, f32[40,256]{1,0:T(8,128)S(1)}, u32[]{:S(2)}, u32[]{:S(2)}) %collective-permute-start.10) | collective-permute-done | bytes 40992 | tf_op jit(solution)/shard_map/ppermute | solution.py:76
  43.2 2.9 %collective-permute-start.11 = (bf16[40,256]{1,0:T(8,128)(2,1)S(1)}, bf16[40,256]{1,0:T(8,128)(2,1)S(1)}, u32[]{:S(2)}, u32[]{:S(2)}) collective-permute-start(bf16[40,256]{1,0:T(8,128)(2,1)S(1)} %get-tuple-element.59), channel_id=1, source_target_pairs={{0,3},{1,2},{2,1},{3,0},{4,7},{5,6},{6,5},{7,4},{8,11},{9,10},{10,... | collective-permute-start | bytes 61448 | tf_op jit(solution)/shard_map/ppermute | solution.py:76
  46.2 1.5 %collective-permute-done.11.refs_0_ = bf16[40,256]{1,0:T(8,128)(2,1)S(1)} collective-permute-done((bf16[40,256]{1,0:T(8,128)(2,1)S(1)}, bf16[40,256]{1,0:T(8,128)(2,1)S(1)}, u32[]{:S(2)}, u32[]{:S(2)}) %collective-permute-start.11) | collective-permute-done | bytes 20512 | tf_op jit(solution)/shard_map/ppermute | solution.py:76
  47.7 2.6 %collective-permute-start.14 = (bf16[40,256]{1,0:T(8,128)(2,1)S(1)}, bf16[40,256]{1,0:T(8,128)(2,1)S(1)}, u32[]{:S(2)}, u32[]{:S(2)}) collective-permute-start(bf16[40,256]{1,0:T(8,128)(2,1)S(1)} %get-tuple-element.61), channel_id=1, source_target_pairs={{0,13},{1,12},{2,15},{3,14},{4,9},{5,8},{6,11},{7,10},{8,5},{9,4},... | collective-permute-start | bytes 61448 | tf_op jit(solution)/shard_map/ppermute | solution.py:76
  50.2 0.0 collective-permute-start.13
  50.2 1.4 %collective-permute-start.12 = (bf16[40,256]{1,0:T(8,128)(2,1)S(1)}, bf16[40,256]{1,0:T(8,128)(2,1)S(1)}, u32[]{:S(2)}, u32[]{:S(2)}) collective-permute-start(bf16[40,256]{1,0:T(8,128)(2,1)S(1)} %get-tuple-element.61), channel_id=1, source_target_pairs={{0,5},{1,4},{2,7},{3,6},{4,1},{5,0},{6,3},{7,2},{8,13},{9,12},{10,... | collective-permute-start | bytes 61448 | tf_op jit(solution)/shard_map/ppermute | solution.py:76
  51.6 1.1 %collective-permute-done.14.refs_2_ = bf16[40,256]{1,0:T(8,128)(2,1)S(1)} collective-permute-done((bf16[40,256]{1,0:T(8,128)(2,1)S(1)}, bf16[40,256]{1,0:T(8,128)(2,1)S(1)}, u32[]{:S(2)}, u32[]{:S(2)}) %collective-permute-start.14) | collective-permute-done | bytes 20512 | tf_op jit(solution)/shard_map/ppermute | solution.py:76
  52.7 1.7 %collective-permute-done.13.refs_1_ = bf16[40,256]{1,0:T(8,128)(2,1)S(1)} collective-permute-done((bf16[40,256]{1,0:T(8,128)(2,1)S(1)}, bf16[40,256]{1,0:T(8,128)(2,1)S(1)}, u32[]{:S(2)}, u32[]{:S(2)}) %collective-permute-start.13) | collective-permute-done | bytes 20512 | tf_op jit(solution)/shard_map/ppermute | solution.py:76
  54.4 0.0 collective-permute-done.12.refs_0_
  54.4 1.6 %shard_map.120 = (f32[33,4096]{1,0:T(8,128)}, f32[33,4096]{1,0:T(8,128)}, f32[33,4096]{1,0:T(8,128)}) custom-call(f32[40,256]{1,0:T(8,128)S(1)} %shard_map.108.sums_ref, f32[40,256]{1,0:T(8,128)S(1)} %get-tuple-element.43.product_ref, f32[40,256]{1,0:T(8,128)S(1)} %shard_map.119.hess_sums_ref, f32[256,256]{1,0:T(8,128)S(1)} %get-tuple-element.40.refs_4_.inner_ref, ...), custom_call_target="tpu_custom_call" | custom-call | tf_op jit(solution)/shard_map/pallas_call | solution.py:438
  (7 shorter events, 0.1 us)
Async XLA Ops:
  2.8 1.4 %collective-permute-start = (f32[40,256]{1,0:T(8,128)S(1)}, f32[40,256]{1,0:T(8,128)S(1)}, u32[]{:S(2)}, u32[]{:S(2)}) collective-permute-start(f32[40,256]{1,0:T(8,128)S(1)} %get-tuple-element.33.x_ref), channel_id=1, source_target_pairs={{0,1},{1,0},{2,3},{3,2},{4,5},{5,4},{6,7},{7,6},{8,9},{9,8},{10,11... | collective-permute-start | bytes 122888 | tf_op jit(solution)/shard_map/ppermute | solution.py:76
  4.2 4.1 %collective-permute-start.1 = (bf16[40,256]{1,0:T(8,128)(2,1)S(1)}, bf16[40,256]{1,0:T(8,128)(2,1)S(1)}, u32[]{:S(2)}, u32[]{:S(2)}) collective-permute-start(bf16[40,256]{1,0:T(8,128)(2,1)S(1)} %get-tuple-element.35.after_ref), channel_id=1, source_target_pairs={{0,3},{1,2},{2,1},{3,0},{4,7},{5,6},{6,5},{7,4},{8,11},{9,10},{10,... | collective-permute-start | bytes 61448 | tf_op jit(solution)/shard_map/ppermute | solution.py:76
  8.4 6.7 %collective-permute-start.4 = (bf16[40,256]{1,0:T(8,128)(2,1)S(1)}, bf16[40,256]{1,0:T(8,128)(2,1)S(1)}, u32[]{:S(2)}, u32[]{:S(2)}) collective-permute-start(bf16[40,256]{1,0:T(8,128)(2,1)S(1)} %get-tuple-element.38.after_ref), channel_id=1, source_target_pairs={{0,13},{1,12},{2,15},{3,14},{4,9},{5,8},{6,11},{7,10},{8,5},{9,4},... | collective-permute-start | bytes 61448 | tf_op jit(solution)/shard_map/ppermute | solution.py:76
  12.3 4.1 %collective-permute-start.3 = (bf16[40,256]{1,0:T(8,128)(2,1)S(1)}, bf16[40,256]{1,0:T(8,128)(2,1)S(1)}, u32[]{:S(2)}, u32[]{:S(2)}) collective-permute-start(bf16[40,256]{1,0:T(8,128)(2,1)S(1)} %get-tuple-element.38.after_ref), channel_id=1, source_target_pairs={{0,9},{1,8},{2,11},{3,10},{4,13},{5,12},{6,15},{7,14},{8,1},{9,0},... | collective-permute-start | bytes 61448 | tf_op jit(solution)/shard_map/ppermute | solution.py:76
  12.3 4.1 %collective-permute-start.2 = (bf16[40,256]{1,0:T(8,128)(2,1)S(1)}, bf16[40,256]{1,0:T(8,128)(2,1)S(1)}, u32[]{:S(2)}, u32[]{:S(2)}) collective-permute-start(bf16[40,256]{1,0:T(8,128)(2,1)S(1)} %get-tuple-element.38.after_ref), channel_id=1, source_target_pairs={{0,5},{1,4},{2,7},{3,6},{4,1},{5,0},{6,3},{7,2},{8,13},{9,12},{10,... | collective-permute-start | bytes 61448 | tf_op jit(solution)/shard_map/ppermute | solution.py:76
  17.1 4.4 %copy-start = (s32[32,3]{0,1:T(4,128)S(1)}, s32[32,3]{0,1:T(4,128)}, u32[]{:S(2)}) copy-start(s32[32,3]{0,1:T(4,128)} %param.13) | copy-start | bytes 1156
  17.2 9.8 %collective-permute-start.5 = (bf16[33,32,128]{2,1,0:T(8,128)(2,1)S(1)}, bf16[33,32,128]{2,1,0:T(8,128)(2,1)S(1)}, u32[]{:S(2)}, u32[]{:S(2)}) collective-permute-start(bf16[33,32,128]{2,1,0:T(8,128)(2,1)S(1)} %get-tuple-element.44.own_ref), channel_id=1, source_target_pairs={{0,2},{1,3},{2,4},{3,5},{4,6},{5,7},{6,8},{7,9},{8,10},{9,11},{10,... | collective-permute-start | bytes 811016 | tf_op jit(solution)/shard_map/ppermute | solution.py:18
  27.0 1.6 %collective-permute-start.6 = (bf16[33,32,128]{2,1,0:T(8,128)(2,1)S(1)}, bf16[33,32,128]{2,1,0:T(8,128)(2,1)S(1)}, u32[]{:S(2)}, u32[]{:S(2)}) collective-permute-start(bf16[33,32,128]{2,1,0:T(8,128)(2,1)S(1)} %shard_map.112), channel_id=1, source_target_pairs={{0,1},{1,0},{2,3},{3,2},{4,5},{5,4},{6,7},{7,6},{8,9},{9,8},{10,11... | collective-permute-start | bytes 811016 | tf_op jit(solution)/shard_map/ppermute | solution.py:22
  30.1 1.6 %collective-permute-start.8 = (bf16[33,32,128]{2,1,0:T(8,128)(2,1)S(1)}, bf16[33,32,128]{2,1,0:T(8,128)(2,1)S(1)}, u32[]{:S(2)}, u32[]{:S(2)}) collective-permute-start(bf16[33,32,128]{2,1,0:T(8,128)(2,1)S(1)} %get-tuple-element.55), channel_id=1, source_target_pairs={{0,1},{1,0},{2,3},{3,2},{4,5},{5,4},{6,7},{7,6},{8,9},{9,8},{10,11... | collective-permute-start | bytes 811016 | tf_op jit(solution)/shard_map/ppermute | solution.py:22
  30.2 10.8 %collective-permute-start.7 = (bf16[33,32,128]{2,1,0:T(8,128)(2,1)S(1)}, bf16[33,32,128]{2,1,0:T(8,128)(2,1)S(1)}, u32[]{:S(2)}, u32[]{:S(2)}) collective-permute-start(bf16[33,32,128]{2,1,0:T(8,128)(2,1)S(1)} %get-tuple-element.54.back_far_ref), channel_id=1, source_target_pairs={{2,0},{4,2},{6,4},{8,6},{10,8},{12,10},{14,12},{18,16},{20,18},{22... | collective-permute-start | bytes 811016 | tf_op jit(solution)/shard_map/ppermute | solution.py:18
  31.8 9.2 %collective-permute-start.9 = (bf16[33,32,128]{2,1,0:T(8,128)(2,1)S(1)}, bf16[33,32,128]{2,1,0:T(8,128)(2,1)S(1)}, u32[]{:S(2)}, u32[]{:S(2)}) collective-permute-start(bf16[33,32,128]{2,1,0:T(8,128)(2,1)S(1)} %shard_map.115), channel_id=1, source_target_pairs={{3,1},{5,3},{7,5},{9,7},{11,9},{13,11},{15,13},{19,17},{21,19},{23... | collective-permute-start | bytes 811016 | tf_op jit(solution)/shard_map/ppermute | solution.py:18
  41.5 1.7 %collective-permute-start.10 = (f32[40,256]{1,0:T(8,128)S(1)}, f32[40,256]{1,0:T(8,128)S(1)}, u32[]{:S(2)}, u32[]{:S(2)}) collective-permute-start(f32[40,256]{1,0:T(8,128)S(1)} %get-tuple-element.57.x_ref), channel_id=1, source_target_pairs={{0,1},{1,0},{2,3},{3,2},{4,5},{5,4},{6,7},{7,6},{8,9},{9,8},{10,11... | collective-permute-start | bytes 122888 | tf_op jit(solution)/shard_map/ppermute | solution.py:76
  43.2 4.4 %collective-permute-start.11 = (bf16[40,256]{1,0:T(8,128)(2,1)S(1)}, bf16[40,256]{1,0:T(8,128)(2,1)S(1)}, u32[]{:S(2)}, u32[]{:S(2)}) collective-permute-start(bf16[40,256]{1,0:T(8,128)(2,1)S(1)} %get-tuple-element.59), channel_id=1, source_target_pairs={{0,3},{1,2},{2,1},{3,0},{4,7},{5,6},{6,5},{7,4},{8,11},{9,10},{10,... | collective-permute-start | bytes 61448 | tf_op jit(solution)/shard_map/ppermute | solution.py:76
  47.7 5.1 %collective-permute-start.14 = (bf16[40,256]{1,0:T(8,128)(2,1)S(1)}, bf16[40,256]{1,0:T(8,128)(2,1)S(1)}, u32[]{:S(2)}, u32[]{:S(2)}) collective-permute-start(bf16[40,256]{1,0:T(8,128)(2,1)S(1)} %get-tuple-element.61), channel_id=1, source_target_pairs={{0,13},{1,12},{2,15},{3,14},{4,9},{5,8},{6,11},{7,10},{8,5},{9,4},... | collective-permute-start | bytes 61448 | tf_op jit(solution)/shard_map/ppermute | solution.py:76
  50.2 4.2 %collective-permute-start.13 = (bf16[40,256]{1,0:T(8,128)(2,1)S(1)}, bf16[40,256]{1,0:T(8,128)(2,1)S(1)}, u32[]{:S(2)}, u32[]{:S(2)}) collective-permute-start(bf16[40,256]{1,0:T(8,128)(2,1)S(1)} %get-tuple-element.61), channel_id=1, source_target_pairs={{0,9},{1,8},{2,11},{3,10},{4,13},{5,12},{6,15},{7,14},{8,1},{9,0},... | collective-permute-start | bytes 61448 | tf_op jit(solution)/shard_map/ppermute | solution.py:76
  50.2 4.2 %collective-permute-start.12 = (bf16[40,256]{1,0:T(8,128)(2,1)S(1)}, bf16[40,256]{1,0:T(8,128)(2,1)S(1)}, u32[]{:S(2)}, u32[]{:S(2)}) collective-permute-start(bf16[40,256]{1,0:T(8,128)(2,1)S(1)} %get-tuple-element.61), channel_id=1, source_target_pairs={{0,5},{1,4},{2,7},{3,6},{4,1},{5,0},{6,3},{7,2},{8,13},{9,12},{10,... | collective-permute-start | bytes 61448 | tf_op jit(solution)/shard_map/ppermute | solution.py:76

commit v14 on v12

--- a/solution.py
+++ b/solution.py
@@ -191,15 +191,15 @@
     return jnp.concatenate([most, last.astype(BF16)], axis=0)
 
 
-def own_image_kernel(tall, own_ref, factor_ref, image_ref, again_ref, zeros_ref, last_ref):
+def own_image_kernel(tall, first, own_ref, factor_ref, *refs):
+    image_ref, other_ref, last_ref = refs[-3:]
     blocks, bs = last_ref.shape
-    again_ref[...] = own_ref[...]
-    zeros_ref[...] = jnp.zeros_like(zeros_ref)
+    other_ref[...] = jnp.zeros_like(other_ref) if first else own_ref[...]
     last_ref[...] = own_ref[blocks].astype(F32)
-    for b in range(blocks):
+    for b in range(image_ref.shape[0]):
         image_ref[b] = lax.dot_general(
-            tall_block(own_ref, last_ref, b, tall),
-            factor_ref[b, 0],
+            tall_block(own_ref, last_ref, first + b, tall),
+            factor_ref[first + b, 0],
             (((1,), (1,)), ((), ())),
             preferred_element_type=F32,
         )
@@ -232,8 +232,8 @@
 
 
 def hessian_kernel(
-    rows, ids_ref, factor_ref, turned_ref, own_image_ref, near_ref, far_even_ref, far_odd_ref, own_ref, zeros_ref,
-    back_far_ref, back_near_ref, total_ref, curve_ref, image_ref, around_ref, around_last_ref, last_ref,
+    rows, ids_ref, factor_ref, turned_ref, image_one_ref, image_two_ref, near_ref, far_even_ref, far_odd_ref, own_ref,
+    zeros_ref, back_far_ref, back_near_ref, total_ref, curve_ref, image_ref, around_ref, around_last_ref, last_ref,
 ):
     blocks, taps, bs, _ = factor_ref.shape
     count = around_ref.shape[1]
@@ -248,7 +248,9 @@
     side_by_side = lambda b: jnp.concatenate([factor_ref[b, k] for k in range(1, taps)], axis=1)
     for b in range(blocks):
         chosen = [tall_block(around_ref, around_last_ref, ids(b, k), tall) for k in range(1, taps)]
-        image = own_image_ref[b] + jnp.dot(
+        half = image_one_ref.shape[0]
+        own_image = image_one_ref[b] if b < half else image_two_ref[b - half]
+        image = own_image + jnp.dot(
             jnp.concatenate(chosen, axis=1), turned_ref[b], preferred_element_type=F32
         )
         rounded = image.astype(BF16)
@@ -404,13 +406,20 @@
     )(sums, inner_inverse, terms, right_side, turned_map)
     far_odd = sent(rounded, "space", 2, (1,))
     around = ((3 * blocks, rows, bs), F32)
-    own_image, again, zeros = call(
-        functools.partial(own_image_kernel, tall),
-        [vmem] * 2,
-        [((blocks, tall, bs), F32), packed, around],
-        [vmem((blocks, bs), F32)],
-    )(rounded, factor)
+    half = blocks // 2
+
+    def own_image(first, other, *after):
+        count = blocks - half if first else half
+        return call(
+            functools.partial(own_image_kernel, tall, first),
+            [vmem] * 2 + [pl.ANY] * len(after),
+            [((count, tall, bs), F32), other],
+            [vmem((blocks, bs), F32)],
+        )(rounded, factor, *after)
+
+    image_one, again = own_image(0, packed)
     far_even = sent(again, "space", 2, (0,))
+    image_two, zeros = own_image(half, around, image_one)
     shape = (blocks, (factor.shape[1] - 1) * bs, bs)
     turned, ids = call(
         turn_kernel,
@@ -418,15 +427,15 @@
         [(shape, BF16), (cond_ids.shape[::-1], jnp.int32)],
         [pltpu.SemaphoreType.DMA],
         spaces=(vmem, smem),
-    )(factor, cond_ids.T, own_image)
+    )(factor, cond_ids.T, image_two)
     near = swapped(call(pass_on_kernel, [vmem, vmem, pl.ANY], [packed])(rounded, far_odd, turned), "space")
     back_far, back_near, back_own, curve, image = call(
         functools.partial(hessian_kernel, rows),
-        [smem] + [vmem] * 8,
+        [smem] + [vmem] * 9,
         [packed, packed, around, ((rows, bs), F32), ((blocks, tall, bs), BF16)],
         [vmem((3 * blocks, count, bs), BF16), vmem((3 * blocks, bs), F32), vmem((blocks, bs), F32)],
-        aliases={8: 2},
-    )(ids, factor, turned, own_image, near, far_even, far_odd, rounded, zeros)
+        aliases={9: 2},
+    )(ids, factor, turned, image_one, image_two, near, far_even, far_odd, rounded, zeros)
     mate = swapped(back_near, "space")
     from_even = sent(back_far, "space", -2, (0,))
     from_odd = sent(call(join_kernel, [vmem] * 2, [packed])(back_far, mate), "space", -2, (1,))

time: 54.6 us -> 54.5 us (level)
    pallas_call x2 -> x3, Pallas kernels: 2.53 us -> 2.55 us  [the longest x1 1.56 us: body(): call(functools.partial(hessian_kernel, rows), [smem] + [vmem] * 9, [packe...]
where the time goes in v14:
time: 54.5 us; the launch traced here: 54.2 us
  starting transfers between devices  23.4 us (43%)
  waiting for transfers between devices  17.9 us (33%)
  Pallas kernels  11.9 us (22%)
  between operations  0.78 us (1%)
    ppermute x10, starting transfers between devices, total(): lax.ppermute(msg, axis, [(j, j ^ d) for j in range(n)])  15.5 us
    ppermute x4, waiting for transfers between devices, sent(): lax.ppermute(block, axis, [(i, i + distance) for i in devices if i % 2 in...  9.51 us
    ppermute x10, waiting for transfers between devices, total(): lax.ppermute(msg, axis, [(j, j ^ d) for j in range(n)])  8.16 us
    ppermute x4, starting transfers between devices, sent(): lax.ppermute(block, axis, [(i, i + distance) for i in devices if i % 2 in...  6.05 us
    pallas_call x1, Pallas kernels, load(): call(load_kernel, [pl.ANY] * 3, outs, [pltpu.SemaphoreType.DMA((2,))])  2.23 us
    pallas_call x1, Pallas kernels, body(): call(project_kernel, [pl.ANY] * 5, [sum_shape, ((2, blocks, bs), F32), fi...  2.15 us
    ppermute x2, starting transfers between devices, swapped(): lax.ppermute(block, axis, [(i, i ^ 1) for i in range(lax.axis_size(axis))])  1.88 us
    pallas_call x1, Pallas kernels, body(): call(finish_kernel, [vmem] * 9, [whole] * 3, scratch, keep=False)  1.6 us
  transfers between devices with their start and end apart: 16, of which 10 were waited for; matrix products, arithmetic and copies ran while one was open for 0% of the time, Pallas kernels for 10%

profile of v14, /device:TPU:0, one launch (start us, length us, event | category | flops | bytes accessed | tf_op | source)
XLA Modules:
  0.0 54.2 jit_solution(12782319784775076411)
XLA Ops:
  0.6 2.2 %shard_map.103 = (f32[40,256]{1,0:T(8,128)S(1)}, f32[2,32,128]{2,1,0:T(8,128)S(1)}, f32[32,40,128]{2,1,0:T(8,128)S(1)}, bf16[4096,256]{1,0:T(8,128)(2,1)S(1)}) custom-call(f32[32,128]{1,0:T(8,128)} %bitcast.5, s32[32,128]{1,0:T(8,128)} %bitcast.6, f32[32,128]{1,0:T(8,128)} %bitcast.7, f32[32,4096]{1,0:T(8,128)} %probes_hbm.1, bf16[4096,256]{1,0:T(8,128)(2,1)} %map_hbm.1), custom_call_target="tpu_custom_call" | custom-call | tf_op jit(solution)/shard_map/pallas_call | solution.py:380
  2.8 0.5 collective-permute-start
  3.3 0.9 %collective-permute-done.refs_0_ = f32[40,256]{1,0:T(8,128)S(1)} collective-permute-done((f32[40,256]{1,0:T(8,128)S(1)}, f32[40,256]{1,0:T(8,128)S(1)}, u32[]{:S(2)}, u32[]{:S(2)}) %collective-permute-start) | collective-permute-done | bytes 40992 | tf_op jit(solution)/shard_map/ppermute | solution.py:76
  4.2 2.7 %collective-permute-start.1 = (bf16[40,256]{1,0:T(8,128)(2,1)S(1)}, bf16[40,256]{1,0:T(8,128)(2,1)S(1)}, u32[]{:S(2)}, u32[]{:S(2)}) collective-permute-start(bf16[40,256]{1,0:T(8,128)(2,1)S(1)} %get-tuple-element.37.after_ref), channel_id=1, source_target_pairs={{0,3},{1,2},{2,1},{3,0},{4,7},{5,6},{6,5},{7,4},{8,11},{9,10},{10,... | collective-permute-start | bytes 61448 | tf_op jit(solution)/shard_map/ppermute | solution.py:76
  6.9 0.6 %shard_map.105.refs_1_.map_ref = bf16[256,4096]{1,0:T(8,128)(2,1)S(1)} custom-call(bf16[4096,256]{1,0:T(8,128)(2,1)S(1)} %get-tuple-element.38.map_ref, bf16[40,256]{1,0:T(8,128)(2,1)S(1)} %get-tuple-element.37.after_ref), custom_call_target="tpu_custom_call" | custom-call | tf_op jit(solution)/shard_map/pallas_call | solution.py:401
  7.5 0.8 %collective-permute-done.1.refs_0_ = bf16[40,256]{1,0:T(8,128)(2,1)S(1)} collective-permute-done((bf16[40,256]{1,0:T(8,128)(2,1)S(1)}, bf16[40,256]{1,0:T(8,128)(2,1)S(1)}, u32[]{:S(2)}, u32[]{:S(2)}) %collective-permute-start.1) | collective-permute-done | bytes 20512 | tf_op jit(solution)/shard_map/ppermute | solution.py:76
  8.4 3.9 %collective-permute-start.4 = (bf16[40,256]{1,0:T(8,128)(2,1)S(1)}, bf16[40,256]{1,0:T(8,128)(2,1)S(1)}, u32[]{:S(2)}, u32[]{:S(2)}) collective-permute-start(bf16[40,256]{1,0:T(8,128)(2,1)S(1)} %get-tuple-element.40.after_ref), channel_id=1, source_target_pairs={{0,13},{1,12},{2,15},{3,14},{4,9},{5,8},{6,11},{7,10},{8,5},{9,4},... | collective-permute-start | bytes 61448 | tf_op jit(solution)/shard_map/ppermute | solution.py:76
  12.3 0.0 collective-permute-start.3
  12.3 0.6 %collective-permute-start.2 = (bf16[40,256]{1,0:T(8,128)(2,1)S(1)}, bf16[40,256]{1,0:T(8,128)(2,1)S(1)}, u32[]{:S(2)}, u32[]{:S(2)}) collective-permute-start(bf16[40,256]{1,0:T(8,128)(2,1)S(1)} %get-tuple-element.40.after_ref), channel_id=1, source_target_pairs={{0,5},{1,4},{2,7},{3,6},{4,1},{5,0},{6,3},{7,2},{8,13},{9,12},{10,... | collective-permute-start | bytes 61448 | tf_op jit(solution)/shard_map/ppermute | solution.py:76
  12.9 2.2 %shard_map.107 = (bf16[32,4,128,128]{3,2,1,0:T(8,128)(2,1)S(1)}, f32[256,256]{1,0:T(8,128)S(1)}) custom-call(bf16[32,4,128,128]{3,2,1,0:T(8,128)(2,1)} %factor_hbm.1, f32[256,256]{1,0:T(8,128)} %inner_hbm.1, bf16[40,256]{1,0:T(8,128)(2,1)S(1)} %get-tuple-element.40.after_ref), custom_call_target="tpu_custom_call" | custom-call | tf_op jit(solution)/shard_map/pallas_call | solution.py:396
  15.1 0.0 collective-permute-done.4.refs_2_
  15.1 1.3 %collective-permute-done.3.refs_1_ = bf16[40,256]{1,0:T(8,128)(2,1)S(1)} collective-permute-done((bf16[40,256]{1,0:T(8,128)(2,1)S(1)}, bf16[40,256]{1,0:T(8,128)(2,1)S(1)}, u32[]{:S(2)}, u32[]{:S(2)}) %collective-permute-start.3) | collective-permute-done | bytes 20512 | tf_op jit(solution)/shard_map/ppermute | solution.py:76
  16.4 0.0 collective-permute-done.2.refs_0_
  16.4 0.7 %shard_map.109 = (f32[32,40,128]{2,1,0:T(8,128)S(1)}, bf16[33,32,128]{2,1,0:T(8,128)(2,1)S(1)}, f32[40,256]{1,0:T(8,128)S(1)}) custom-call(f32[40,256]{1,0:T(8,128)S(1)} %shard_map.108.sums_ref, f32[256,256]{1,0:T(8,128)S(1)} %get-tuple-element.42.refs_4_.inner_ref, f32[2,32,128]{2,1,0:T(8,128)S(1)} %get-tuple-element.43.terms_ref, ...), custom_call_target="tpu_custom_call" | custom-call | tf_op jit(solution)/shard_map/pallas_call | solution.py:404
  17.1 0.7 %collective-permute-start.5 = (bf16[33,32,128]{2,1,0:T(8,128)(2,1)S(1)}, bf16[33,32,128]{2,1,0:T(8,128)(2,1)S(1)}, u32[]{:S(2)}, u32[]{:S(2)}) collective-permute-start(bf16[33,32,128]{2,1,0:T(8,128)(2,1)S(1)} %get-tuple-element.46.own_ref), channel_id=1, source_target_pairs={{1,3},{3,5},{5,7},{7,9},{9,11},{11,13},{13,15},{17,19},{19,21},{21... | collective-permute-start | bytes 811016 | tf_op jit(solution)/shard_map/ppermute | solution.py:18
  17.8 0.5 shard_map.110
  18.3 3.4 %collective-permute-start.7 = (bf16[33,32,128]{2,1,0:T(8,128)(2,1)S(1)}, bf16[33,32,128]{2,1,0:T(8,128)(2,1)S(1)}, u32[]{:S(2)}, u32[]{:S(2)}) collective-permute-start(bf16[33,32,128]{2,1,0:T(8,128)(2,1)S(1)} %get-tuple-element.51), channel_id=1, source_target_pairs={{0,2},{2,4},{4,6},{6,8},{8,10},{10,12},{12,14},{16,18},{18,20},{20... | collective-permute-start | bytes 811016 | tf_op jit(solution)/shard_map/ppermute | solution.py:18
  21.7 0.0 copy-start
  21.7 0.5 shard_map.111
  22.2 0.1 copy-done
  22.4 0.9 %shard_map.112 = (bf16[32,384,128]{2,1,0:T(8,128)(2,1)S(1)}, s32[3,32]{1,0:T(4,128)S(4)}) custom-call(bf16[32,4,128,128]{3,2,1,0:T(8,128)(2,1)S(1)} %get-tuple-element.41.refs_3_.factor_ref, s32[3,32]{1,0:T(4,128)S(1)} %bitcast.4, f32[16,48,128]{2,1,0:T(8,128)S(1)} %get-tuple-element.48.after_ref.image_two_ref), custom_call_target="tpu_custom_call" | custom-call | tf_op jit(solution)/shard_map/pallas_call | solution.py:424
  23.3 0.0 collective-permute-done.5.far_ref.far_odd_ref
  23.3 1.8 %collective-permute-start.6 = (bf16[33,32,128]{2,1,0:T(8,128)(2,1)S(1)}, bf16[33,32,128]{2,1,0:T(8,128)(2,1)S(1)}, u32[]{:S(2)}, u32[]{:S(2)}) collective-permute-start(bf16[33,32,128]{2,1,0:T(8,128)(2,1)S(1)} %shard_map.113), channel_id=1, source_target_pairs={{0,1},{1,0},{2,3},{3,2},{4,5},{5,4},{6,7},{7,6},{8,9},{9,8},{10,11... | collective-permute-start | bytes 811016 | tf_op jit(solution)/shard_map/ppermute | solution.py:22
  25.1 1.6 %collective-permute-done.7.far_even_ref = bf16[33,32,128]{2,1,0:T(8,128)(2,1)S(1)} collective-permute-done((bf16[33,32,128]{2,1,0:T(8,128)(2,1)S(1)}, bf16[33,32,128]{2,1,0:T(8,128)(2,1)S(1)}, u32[]{:S(2)}, u32[]{:S(2)}) %collective-permute-start.7) | collective-permute-done | bytes 270368 | tf_op jit(solution)/shard_map/ppermute | solution.py:18
  26.8 0.0 collective-permute-done.6.near_ref
  26.8 1.6 %shard_map.114 = (bf16[33,32,128]{2,1,0:T(8,128)(2,1)S(1)}, bf16[33,32,128]{2,1,0:T(8,128)(2,1)S(1)}, f32[96,40,128]{2,1,0:T(8,128)S(1)}, f32[40,128]{1,0:T(8,128)S(1)}, bf16[32,48,128]{2,1,0:T(8,128)(2,1)S(1)}) custom-call(s32[3,32]{1,0:T(4,128)S(4)} %get-tuple-element.49.ids_ref, ...), custom_call_target="tpu_custom_call", output_to_operand_aliasing={{2}: (9, {})} | custom-call | tf_op jit(solution)/shard_map/pallas_call | solution.py:432
  28.3 0.1 collective-permute-start.9
  28.4 1.3 %collective-permute-start.8 = (bf16[33,32,128]{2,1,0:T(8,128)(2,1)S(1)}, bf16[33,32,128]{2,1,0:T(8,128)(2,1)S(1)}, u32[]{:S(2)}, u32[]{:S(2)}) collective-permute-start(bf16[33,32,128]{2,1,0:T(8,128)(2,1)S(1)} %get-tuple-element.58.back_far_ref), channel_id=1, source_target_pairs={{2,0},{4,2},{6,4},{8,6},{10,8},{12,10},{14,12},{18,16},{20,18},{22... | collective-permute-start | bytes 811016 | tf_op jit(solution)/shard_map/ppermute | solution.py:18
  29.7 0.2 collective-permute-done.9.got_ref.mate_ref
  30.0 0.1 shard_map.116
  30.0 0.7 %collective-permute-start.10 = (bf16[33,32,128]{2,1,0:T(8,128)(2,1)S(1)}, bf16[33,32,128]{2,1,0:T(8,128)(2,1)S(1)}, u32[]{:S(2)}, u32[]{:S(2)}) collective-permute-start(bf16[33,32,128]{2,1,0:T(8,128)(2,1)S(1)} %shard_map.116), channel_id=1, source_target_pairs={{3,1},{5,3},{7,5},{9,7},{11,9},{13,11},{15,13},{19,17},{21,19},{23... | collective-permute-start | bytes 811016 | tf_op jit(solution)/shard_map/ppermute | solution.py:18
  30.7 0.4 shard_map.115
  31.2 7.9 %collective-permute-done.8.even_ref = bf16[33,32,128]{2,1,0:T(8,128)(2,1)S(1)} collective-permute-done((bf16[33,32,128]{2,1,0:T(8,128)(2,1)S(1)}, bf16[33,32,128]{2,1,0:T(8,128)(2,1)S(1)}, u32[]{:S(2)}, u32[]{:S(2)}) %collective-permute-start.8) | collective-permute-done | bytes 270368 | tf_op jit(solution)/shard_map/ppermute | solution.py:18
  39.0 0.0 collective-permute-done.10.odd_ref
  39.0 0.5 shard_map.117
  39.6 0.9 %collective-permute-start.11 = (f32[40,256]{1,0:T(8,128)S(1)}, f32[40,256]{1,0:T(8,128)S(1)}, u32[]{:S(2)}, u32[]{:S(2)}) collective-permute-start(f32[40,256]{1,0:T(8,128)S(1)} %get-tuple-element.61.x_ref), channel_id=1, source_target_pairs={{0,1},{1,0},{2,3},{3,2},{4,5},{5,4},{6,7},{7,6},{8,9},{9,8},{10,11... | collective-permute-start | bytes 122888 | tf_op jit(solution)/shard_map/ppermute | solution.py:76
  40.5 0.9 %collective-permute-done.11.refs_0_ = f32[40,256]{1,0:T(8,128)S(1)} collective-permute-done((f32[40,256]{1,0:T(8,128)S(1)}, f32[40,256]{1,0:T(8,128)S(1)}, u32[]{:S(2)}, u32[]{:S(2)}) %collective-permute-start.11) | collective-permute-done | bytes 40992 | tf_op jit(solution)/shard_map/ppermute | solution.py:76
  41.4 2.9 %collective-permute-start.12 = (bf16[40,256]{1,0:T(8,128)(2,1)S(1)}, bf16[40,256]{1,0:T(8,128)(2,1)S(1)}, u32[]{:S(2)}, u32[]{:S(2)}) collective-permute-start(bf16[40,256]{1,0:T(8,128)(2,1)S(1)} %get-tuple-element.63), channel_id=1, source_target_pairs={{0,3},{1,2},{2,1},{3,0},{4,7},{5,6},{6,5},{7,4},{8,11},{9,10},{10,... | collective-permute-start | bytes 61448 | tf_op jit(solution)/shard_map/ppermute | solution.py:76
  44.3 1.5 %collective-permute-done.12.refs_0_ = bf16[40,256]{1,0:T(8,128)(2,1)S(1)} collective-permute-done((bf16[40,256]{1,0:T(8,128)(2,1)S(1)}, bf16[40,256]{1,0:T(8,128)(2,1)S(1)}, u32[]{:S(2)}, u32[]{:S(2)}) %collective-permute-start.12) | collective-permute-done | bytes 20512 | tf_op jit(solution)/shard_map/ppermute | solution.py:76
  45.8 2.6 %collective-permute-start.15 = (bf16[40,256]{1,0:T(8,128)(2,1)S(1)}, bf16[40,256]{1,0:T(8,128)(2,1)S(1)}, u32[]{:S(2)}, u32[]{:S(2)}) collective-permute-start(bf16[40,256]{1,0:T(8,128)(2,1)S(1)} %get-tuple-element.65), channel_id=1, source_target_pairs={{0,13},{1,12},{2,15},{3,14},{4,9},{5,8},{6,11},{7,10},{8,5},{9,4},... | collective-permute-start | bytes 61448 | tf_op jit(solution)/shard_map/ppermute | solution.py:76
  48.4 0.0 collective-permute-start.14
  48.4 1.4 %collective-permute-start.13 = (bf16[40,256]{1,0:T(8,128)(2,1)S(1)}, bf16[40,256]{1,0:T(8,128)(2,1)S(1)}, u32[]{:S(2)}, u32[]{:S(2)}) collective-permute-start(bf16[40,256]{1,0:T(8,128)(2,1)S(1)} %get-tuple-element.65), channel_id=1, source_target_pairs={{0,5},{1,4},{2,7},{3,6},{4,1},{5,0},{6,3},{7,2},{8,13},{9,12},{10,... | collective-permute-start | bytes 61448 | tf_op jit(solution)/shard_map/ppermute | solution.py:76
  49.8 1.1 %collective-permute-done.15.refs_2_ = bf16[40,256]{1,0:T(8,128)(2,1)S(1)} collective-permute-done((bf16[40,256]{1,0:T(8,128)(2,1)S(1)}, bf16[40,256]{1,0:T(8,128)(2,1)S(1)}, u32[]{:S(2)}, u32[]{:S(2)}) %collective-permute-start.15) | collective-permute-done | bytes 20512 | tf_op jit(solution)/shard_map/ppermute | solution.py:76
  50.9 1.7 %collective-permute-done.14.refs_1_ = bf16[40,256]{1,0:T(8,128)(2,1)S(1)} collective-permute-done((bf16[40,256]{1,0:T(8,128)(2,1)S(1)}, bf16[40,256]{1,0:T(8,128)(2,1)S(1)}, u32[]{:S(2)}, u32[]{:S(2)}) %collective-permute-start.14) | collective-permute-done | bytes 20512 | tf_op jit(solution)/shard_map/ppermute | solution.py:76
  52.6 0.0 collective-permute-done.13.refs_0_
  52.6 1.6 %shard_map.121 = (f32[33,4096]{1,0:T(8,128)}, f32[33,4096]{1,0:T(8,128)}, f32[33,4096]{1,0:T(8,128)}) custom-call(f32[40,256]{1,0:T(8,128)S(1)} %shard_map.108.sums_ref, f32[40,256]{1,0:T(8,128)S(1)} %get-tuple-element.45.product_ref, f32[40,256]{1,0:T(8,128)S(1)} %shard_map.120.hess_sums_ref, f32[256,256]{1,0:T(8,128)S(1)} %get-tuple-element.42.refs_4_.inner_ref, ...), custom_call_target="tpu_custom_call" | custom-call | tf_op jit(solution)/shard_map/pallas_call | solution.py:449
  (7 shorter events, 0.1 us)
Async XLA Ops:
  2.8 1.4 %collective-permute-start = (f32[40,256]{1,0:T(8,128)S(1)}, f32[40,256]{1,0:T(8,128)S(1)}, u32[]{:S(2)}, u32[]{:S(2)}) collective-permute-start(f32[40,256]{1,0:T(8,128)S(1)} %get-tuple-element.35.x_ref), channel_id=1, source_target_pairs={{0,1},{1,0},{2,3},{3,2},{4,5},{5,4},{6,7},{7,6},{8,9},{9,8},{10,11... | collective-permute-start | bytes 122888 | tf_op jit(solution)/shard_map/ppermute | solution.py:76
  4.2 4.1 %collective-permute-start.1 = (bf16[40,256]{1,0:T(8,128)(2,1)S(1)}, bf16[40,256]{1,0:T(8,128)(2,1)S(1)}, u32[]{:S(2)}, u32[]{:S(2)}) collective-permute-start(bf16[40,256]{1,0:T(8,128)(2,1)S(1)} %get-tuple-element.37.after_ref), channel_id=1, source_target_pairs={{0,3},{1,2},{2,1},{3,0},{4,7},{5,6},{6,5},{7,4},{8,11},{9,10},{10,... | collective-permute-start | bytes 61448 | tf_op jit(solution)/shard_map/ppermute | solution.py:76
  8.4 6.7 %collective-permute-start.4 = (bf16[40,256]{1,0:T(8,128)(2,1)S(1)}, bf16[40,256]{1,0:T(8,128)(2,1)S(1)}, u32[]{:S(2)}, u32[]{:S(2)}) collective-permute-start(bf16[40,256]{1,0:T(8,128)(2,1)S(1)} %get-tuple-element.40.after_ref), channel_id=1, source_target_pairs={{0,13},{1,12},{2,15},{3,14},{4,9},{5,8},{6,11},{7,10},{8,5},{9,4},... | collective-permute-start | bytes 61448 | tf_op jit(solution)/shard_map/ppermute | solution.py:76
  12.3 4.1 %collective-permute-start.3 = (bf16[40,256]{1,0:T(8,128)(2,1)S(1)}, bf16[40,256]{1,0:T(8,128)(2,1)S(1)}, u32[]{:S(2)}, u32[]{:S(2)}) collective-permute-start(bf16[40,256]{1,0:T(8,128)(2,1)S(1)} %get-tuple-element.40.after_ref), channel_id=1, source_target_pairs={{0,9},{1,8},{2,11},{3,10},{4,13},{5,12},{6,15},{7,14},{8,1},{9,0},... | collective-permute-start | bytes 61448 | tf_op jit(solution)/shard_map/ppermute | solution.py:76
  12.3 4.1 %collective-permute-start.2 = (bf16[40,256]{1,0:T(8,128)(2,1)S(1)}, bf16[40,256]{1,0:T(8,128)(2,1)S(1)}, u32[]{:S(2)}, u32[]{:S(2)}) collective-permute-start(bf16[40,256]{1,0:T(8,128)(2,1)S(1)} %get-tuple-element.40.after_ref), channel_id=1, source_target_pairs={{0,5},{1,4},{2,7},{3,6},{4,1},{5,0},{6,3},{7,2},{8,13},{9,12},{10,... | collective-permute-start | bytes 61448 | tf_op jit(solution)/shard_map/ppermute | solution.py:76
  17.1 6.1 %collective-permute-start.5 = (bf16[33,32,128]{2,1,0:T(8,128)(2,1)S(1)}, bf16[33,32,128]{2,1,0:T(8,128)(2,1)S(1)}, u32[]{:S(2)}, u32[]{:S(2)}) collective-permute-start(bf16[33,32,128]{2,1,0:T(8,128)(2,1)S(1)} %get-tuple-element.46.own_ref), channel_id=1, source_target_pairs={{1,3},{3,5},{5,7},{7,9},{9,11},{11,13},{13,15},{17,19},{19,21},{21... | collective-permute-start | bytes 811016 | tf_op jit(solution)/shard_map/ppermute | solution.py:18
  18.3 8.5 %collective-permute-start.7 = (bf16[33,32,128]{2,1,0:T(8,128)(2,1)S(1)}, bf16[33,32,128]{2,1,0:T(8,128)(2,1)S(1)}, u32[]{:S(2)}, u32[]{:S(2)}) collective-permute-start(bf16[33,32,128]{2,1,0:T(8,128)(2,1)S(1)} %get-tuple-element.51), channel_id=1, source_target_pairs={{0,2},{2,4},{4,6},{6,8},{8,10},{10,12},{12,14},{16,18},{18,20},{20... | collective-permute-start | bytes 811016 | tf_op jit(solution)/shard_map/ppermute | solution.py:18
  21.7 0.7 %copy-start = (s32[32,3]{0,1:T(4,128)S(1)}, s32[32,3]{0,1:T(4,128)}, u32[]{:S(2)}) copy-start(s32[32,3]{0,1:T(4,128)} %param.13) | copy-start | bytes 1156
  23.3 3.4 %collective-permute-start.6 = (bf16[33,32,128]{2,1,0:T(8,128)(2,1)S(1)}, bf16[33,32,128]{2,1,0:T(8,128)(2,1)S(1)}, u32[]{:S(2)}, u32[]{:S(2)}) collective-permute-start(bf16[33,32,128]{2,1,0:T(8,128)(2,1)S(1)} %shard_map.113), channel_id=1, source_target_pairs={{0,1},{1,0},{2,3},{3,2},{4,5},{5,4},{6,7},{7,6},{8,9},{9,8},{10,11... | collective-permute-start | bytes 811016 | tf_op jit(solution)/shard_map/ppermute | solution.py:22
  28.3 1.6 %collective-permute-start.9 = (bf16[33,32,128]{2,1,0:T(8,128)(2,1)S(1)}, bf16[33,32,128]{2,1,0:T(8,128)(2,1)S(1)}, u32[]{:S(2)}, u32[]{:S(2)}) collective-permute-start(bf16[33,32,128]{2,1,0:T(8,128)(2,1)S(1)} %get-tuple-element.59), channel_id=1, source_target_pairs={{0,1},{1,0},{2,3},{3,2},{4,5},{5,4},{6,7},{7,6},{8,9},{9,8},{10,11... | collective-permute-start | bytes 811016 | tf_op jit(solution)/shard_map/ppermute | solution.py:22
  28.4 10.6 %collective-permute-start.8 = (bf16[33,32,128]{2,1,0:T(8,128)(2,1)S(1)}, bf16[33,32,128]{2,1,0:T(8,128)(2,1)S(1)}, u32[]{:S(2)}, u32[]{:S(2)}) collective-permute-start(bf16[33,32,128]{2,1,0:T(8,128)(2,1)S(1)} %get-tuple-element.58.back_far_ref), channel_id=1, source_target_pairs={{2,0},{4,2},{6,4},{8,6},{10,8},{12,10},{14,12},{18,16},{20,18},{22... | collective-permute-start | bytes 811016 | tf_op jit(solution)/shard_map/ppermute | solution.py:18
  30.0 9.0 %collective-permute-start.10 = (bf16[33,32,128]{2,1,0:T(8,128)(2,1)S(1)}, bf16[33,32,128]{2,1,0:T(8,128)(2,1)S(1)}, u32[]{:S(2)}, u32[]{:S(2)}) collective-permute-start(bf16[33,32,128]{2,1,0:T(8,128)(2,1)S(1)} %shard_map.116), channel_id=1, source_target_pairs={{3,1},{5,3},{7,5},{9,7},{11,9},{13,11},{15,13},{19,17},{21,19},{23... | collective-permute-start | bytes 811016 | tf_op jit(solution)/shard_map/ppermute | solution.py:18
  39.6 1.8 %collective-permute-start.11 = (f32[40,256]{1,0:T(8,128)S(1)}, f32[40,256]{1,0:T(8,128)S(1)}, u32[]{:S(2)}, u32[]{:S(2)}) collective-permute-start(f32[40,256]{1,0:T(8,128)S(1)} %get-tuple-element.61.x_ref), channel_id=1, source_target_pairs={{0,1},{1,0},{2,3},{3,2},{4,5},{5,4},{6,7},{7,6},{8,9},{9,8},{10,11... | collective-permute-start | bytes 122888 | tf_op jit(solution)/shard_map/ppermute | solution.py:76
  41.4 4.4 %collective-permute-start.12 = (bf16[40,256]{1,0:T(8,128)(2,1)S(1)}, bf16[40,256]{1,0:T(8,128)(2,1)S(1)}, u32[]{:S(2)}, u32[]{:S(2)}) collective-permute-start(bf16[40,256]{1,0:T(8,128)(2,1)S(1)} %get-tuple-element.63), channel_id=1, source_target_pairs={{0,3},{1,2},{2,1},{3,0},{4,7},{5,6},{6,5},{7,4},{8,11},{9,10},{10,... | collective-permute-start | bytes 61448 | tf_op jit(solution)/shard_map/ppermute | solution.py:76
  45.8 5.1 %collective-permute-start.15 = (bf16[40,256]{1,0:T(8,128)(2,1)S(1)}, bf16[40,256]{1,0:T(8,128)(2,1)S(1)}, u32[]{:S(2)}, u32[]{:S(2)}) collective-permute-start(bf16[40,256]{1,0:T(8,128)(2,1)S(1)} %get-tuple-element.65), channel_id=1, source_target_pairs={{0,13},{1,12},{2,15},{3,14},{4,9},{5,8},{6,11},{7,10},{8,5},{9,4},... | collective-permute-start | bytes 61448 | tf_op jit(solution)/shard_map/ppermute | solution.py:76
  48.4 4.2 %collective-permute-start.14 = (bf16[40,256]{1,0:T(8,128)(2,1)S(1)}, bf16[40,256]{1,0:T(8,128)(2,1)S(1)}, u32[]{:S(2)}, u32[]{:S(2)}) collective-permute-start(bf16[40,256]{1,0:T(8,128)(2,1)S(1)} %get-tuple-element.65), channel_id=1, source_target_pairs={{0,9},{1,8},{2,11},{3,10},{4,13},{5,12},{6,15},{7,14},{8,1},{9,0},... | collective-permute-start | bytes 61448 | tf_op jit(solution)/shard_map/ppermute | solution.py:76
  48.4 4.2 %collective-permute-start.13 = (bf16[40,256]{1,0:T(8,128)(2,1)S(1)}, bf16[40,256]{1,0:T(8,128)(2,1)S(1)}, u32[]{:S(2)}, u32[]{:S(2)}) collective-permute-start(bf16[40,256]{1,0:T(8,128)(2,1)S(1)} %get-tuple-element.65), channel_id=1, source_target_pairs={{0,5},{1,4},{2,7},{3,6},{4,1},{5,0},{6,3},{7,2},{8,13},{9,12},{10,... | collective-permute-start | bytes 61448 | tf_op jit(solution)/shard_map/ppermute | solution.py:76

commit v15 on v14

--- a/solution.py
+++ b/solution.py
@@ -26,35 +26,12 @@
     return lax.rem(lax.axis_index(axis), 2) == 0
 
 
-def write_message(msg_ref, x):
-    top, half = x.shape[0] - 8, x.shape[1] // 2
-    value, beside = x[top:, :half], x[top:, half:]
-    high = value.astype(BF16).astype(F32)
-    middle = (value - high).astype(BF16).astype(F32)
-    low = value - high - middle
-    row = lax.broadcasted_iota(jnp.int32, value.shape, 0)
-    left = jnp.where(row < 4, high, pltpu.roll(low, 3, 0))
-    right = jnp.where(row < 1, beside, middle)
-    msg_ref[...] = jnp.concatenate([x[:top], jnp.concatenate([left, right], axis=1)], axis=0).astype(BF16)
-
-
-def read_message(msg_ref):
-    x = msg_ref[...].astype(F32)
-    top, half = x.shape[0] - 8, x.shape[1] // 2
-    left, right = x[top:, :half], x[top:, half:]
-    row = lax.broadcasted_iota(jnp.int32, left.shape, 0)
-    left = jnp.where(row < 1, left, left + right + pltpu.roll(left, 5, 0))
-    return jnp.concatenate([x[:top], jnp.concatenate([left, right], axis=1)], axis=0)
-
-
 def add_kernel(count, held, x_ref, *refs):
-    in_refs, (out_ref, *msg_refs) = refs[: count - 1], refs[count - 1 + held :]
+    in_refs, out_ref = refs[: count - 1], refs[count - 1 + held]
     x = x_ref[...]
     for ref in in_refs:
-        x = x + (ref[...] if ref.dtype == F32 else read_message(ref))
+        x = x + ref[...]
     out_ref[...] = x
-    for ref in msg_refs:
-        write_message(ref, x)
 
 
 def rounds_of(n):
@@ -71,19 +48,16 @@
     if n & (n - 1):
         return lax.psum(x, axis), [work(x) for work in beside]
     rounds = rounds_of(n)
-    made, todo, msg = [], list(beside), x
+    made, todo = [], list(beside)
     for i, partners in enumerate(rounds):
-        got = [lax.ppermute(msg, axis, [(j, j ^ d) for j in range(n)]) for d in partners]
-        last = i + 1 == len(rounds)
+        got = [lax.ppermute(x, axis, [(j, j ^ d) for j in range(n)]) for d in partners]
         held = ()
         while len(todo) >= max(len(rounds) - i, 1):
-            made.append(todo.pop(0)(msg))
+            made.append(todo.pop(0)(x))
             held += made[-1]
         add = functools.partial(add_kernel, len(got) + 1, len(held))
         ins = [pltpu.VMEM] * (len(got) + 1) + [pl.ANY] * len(held)
-        outs = [(x.shape, F32)] + [(x.shape, BF16)] * (not last)
-        x, *rest = jax.tree.leaves(call(add, ins, outs)(x, *got, *held))
-        msg = rest[0] if rest else None
+        x = call(add, ins, [(x.shape, F32)])(x, *got, *held)
     return x, made
 
 

time: 54.5 us -> 56 us (1.028)
  waiting for transfers between devices: 17.9 us -> 19.7 us
    ppermute x10, waiting for transfers between devices: 8.16 us -> 9.92 us  [total(): lax.ppermute(x, axis, [(j, j ^ d) for j in range(n)])]
  transfers between devices with their start and end apart: 16 -> 16, of which waited for: 10 -> 10; matrix products, arithmetic and copies ran while one was open for 0% -> 0% of each run, Pallas kernels for 10% -> 9%
where the time goes in v15:
time: 56 us; the launch traced here: 55.7 us
  starting transfers between devices  23.1 us (41%)
  waiting for transfers between devices  19.7 us (35%)
  Pallas kernels  11.9 us (21%)
  between operations  0.77 us (1%)
    ppermute x10, starting transfers between devices, total(): lax.ppermute(x, axis, [(j, j ^ d) for j in range(n)])  15.3 us
    ppermute x10, waiting for transfers between devices, total(): lax.ppermute(x, axis, [(j, j ^ d) for j in range(n)])  9.92 us
    ppermute x4, waiting for transfers between devices, sent(): lax.ppermute(block, axis, [(i, i + distance) for i in devices if i % 2 in...  9.58 us
    ppermute x4, starting transfers between devices, sent(): lax.ppermute(block, axis, [(i, i + distance) for i in devices if i % 2 in...  6.04 us
    pallas_call x1, Pallas kernels, load(): call(load_kernel, [pl.ANY] * 3, outs, [pltpu.SemaphoreType.DMA((2,))])  2.23 us
    pallas_call x1, Pallas kernels, body(): call(project_kernel, [pl.ANY] * 5, [sum_shape, ((2, blocks, bs), F32), fi...  2.15 us
    ppermute x2, starting transfers between devices, swapped(): lax.ppermute(block, axis, [(i, i ^ 1) for i in range(lax.axis_size(axis))])  1.74 us
    pallas_call x1, Pallas kernels, body(): call(finish_kernel, [vmem] * 9, [whole] * 3, scratch, keep=False)  1.6 us
  transfers between devices with their start and end apart: 16, of which 10 were waited for; matrix products, arithmetic and copies ran while one was open for 0% of the time, Pallas kernels for 9%

profile of v15, /device:TPU:0, one launch (start us, length us, event | category | flops | bytes accessed | tf_op | source)
XLA Modules:
  0.0 55.7 jit_solution(5823530606168129888)
XLA Ops:
  0.6 2.2 %shard_map.103 = (f32[40,256]{1,0:T(8,128)S(1)}, f32[2,32,128]{2,1,0:T(8,128)S(1)}, f32[32,40,128]{2,1,0:T(8,128)S(1)}, bf16[4096,256]{1,0:T(8,128)(2,1)S(1)}) custom-call(f32[32,128]{1,0:T(8,128)} %bitcast.5, s32[32,128]{1,0:T(8,128)} %bitcast.6, f32[32,128]{1,0:T(8,128)} %bitcast.7, f32[32,4096]{1,0:T(8,128)} %probes_hbm.1, bf16[4096,256]{1,0:T(8,128)(2,1)} %map_hbm.1), custom_call_target="tpu_custom_call" | custom-call | tf_op jit(solution)/shard_map/pallas_call | solution.py:354
  2.8 0.5 collective-permute-start
  3.3 0.9 %collective-permute-done.refs_0_ = f32[40,256]{1,0:T(8,128)S(1)} collective-permute-done((f32[40,256]{1,0:T(8,128)S(1)}, f32[40,256]{1,0:T(8,128)S(1)}, u32[]{:S(2)}, u32[]{:S(2)}) %collective-permute-start) | collective-permute-done | bytes 40992 | tf_op jit(solution)/shard_map/ppermute | solution.py:53
  4.2 2.6 %collective-permute-start.1 = (f32[40,256]{1,0:T(8,128)S(1)}, f32[40,256]{1,0:T(8,128)S(1)}, u32[]{:S(2)}, u32[]{:S(2)}) collective-permute-start(f32[40,256]{1,0:T(8,128)S(1)} %shard_map.104.after_ref.x_ref), channel_id=1, source_target_pairs={{0,3},{1,2},{2,1},{3,0},{4,7},{5,6},{6,5},{7,4},{8,11},{9,10},{10,... | collective-permute-start | bytes 122888 | tf_op jit(solution)/shard_map/ppermute | solution.py:53
  6.8 0.6 %shard_map.105.refs_1_.map_ref = bf16[256,4096]{1,0:T(8,128)(2,1)S(1)} custom-call(bf16[4096,256]{1,0:T(8,128)(2,1)S(1)} %get-tuple-element.28.map_ref, f32[40,256]{1,0:T(8,128)S(1)} %shard_map.104.after_ref.x_ref), custom_call_target="tpu_custom_call" | custom-call | tf_op jit(solution)/shard_map/pallas_call | solution.py:375
  7.4 1.1 %collective-permute-done.1.refs_0_ = f32[40,256]{1,0:T(8,128)S(1)} collective-permute-done((f32[40,256]{1,0:T(8,128)S(1)}, f32[40,256]{1,0:T(8,128)S(1)}, u32[]{:S(2)}, u32[]{:S(2)}) %collective-permute-start.1) | collective-permute-done | bytes 40992 | tf_op jit(solution)/shard_map/ppermute | solution.py:53
  8.5 4.0 %collective-permute-start.4 = (f32[40,256]{1,0:T(8,128)S(1)}, f32[40,256]{1,0:T(8,128)S(1)}, u32[]{:S(2)}, u32[]{:S(2)}) collective-permute-start(f32[40,256]{1,0:T(8,128)S(1)} %shard_map.106.after_ref.x_ref), channel_id=1, source_target_pairs={{0,13},{1,12},{2,15},{3,14},{4,9},{5,8},{6,11},{7,10},{8,5},{9,4},... | collective-permute-start | bytes 122888 | tf_op jit(solution)/shard_map/ppermute | solution.py:53
  12.4 0.0 collective-permute-start.3
  12.4 0.6 %collective-permute-start.2 = (f32[40,256]{1,0:T(8,128)S(1)}, f32[40,256]{1,0:T(8,128)S(1)}, u32[]{:S(2)}, u32[]{:S(2)}) collective-permute-start(f32[40,256]{1,0:T(8,128)S(1)} %shard_map.106.after_ref.x_ref), channel_id=1, source_target_pairs={{0,5},{1,4},{2,7},{3,6},{4,1},{5,0},{6,3},{7,2},{8,13},{9,12},{10,... | collective-permute-start | bytes 122888 | tf_op jit(solution)/shard_map/ppermute | solution.py:53
  13.0 2.2 %shard_map.107 = (bf16[32,4,128,128]{3,2,1,0:T(8,128)(2,1)S(1)}, f32[256,256]{1,0:T(8,128)S(1)}) custom-call(bf16[32,4,128,128]{3,2,1,0:T(8,128)(2,1)} %factor_hbm.1, f32[256,256]{1,0:T(8,128)} %inner_hbm.1, f32[40,256]{1,0:T(8,128)S(1)} %shard_map.106.after_ref.x_ref), custom_call_target="tpu_custom_call" | custom-call | tf_op jit(solution)/shard_map/pallas_call | solution.py:370
  15.3 0.0 collective-permute-done.4.refs_2_
  15.3 1.6 %collective-permute-done.3.refs_1_ = f32[40,256]{1,0:T(8,128)S(1)} collective-permute-done((f32[40,256]{1,0:T(8,128)S(1)}, f32[40,256]{1,0:T(8,128)S(1)}, u32[]{:S(2)}, u32[]{:S(2)}) %collective-permute-start.3) | collective-permute-done | bytes 40992 | tf_op jit(solution)/shard_map/ppermute | solution.py:53
  16.8 0.0 collective-permute-done.2.refs_0_
  16.8 0.7 %shard_map.109 = (f32[32,40,128]{2,1,0:T(8,128)S(1)}, bf16[33,32,128]{2,1,0:T(8,128)(2,1)S(1)}, f32[40,256]{1,0:T(8,128)S(1)}) custom-call(f32[40,256]{1,0:T(8,128)S(1)} %shard_map.108.sums_ref, f32[256,256]{1,0:T(8,128)S(1)} %get-tuple-element.30.refs_4_.inner_ref, f32[2,32,128]{2,1,0:T(8,128)S(1)} %get-tuple-element.31.terms_ref, ...), custom_call_target="tpu_custom_call" | custom-call | tf_op jit(solution)/shard_map/pallas_call | solution.py:378
  17.6 0.7 %collective-permute-start.5 = (bf16[33,32,128]{2,1,0:T(8,128)(2,1)S(1)}, bf16[33,32,128]{2,1,0:T(8,128)(2,1)S(1)}, u32[]{:S(2)}, u32[]{:S(2)}) collective-permute-start(bf16[33,32,128]{2,1,0:T(8,128)(2,1)S(1)} %get-tuple-element.34.own_ref), channel_id=1, source_target_pairs={{1,3},{3,5},{5,7},{7,9},{9,11},{11,13},{13,15},{17,19},{19,21},{21... | collective-permute-start | bytes 811016 | tf_op jit(solution)/shard_map/ppermute | solution.py:18
  18.3 0.5 shard_map.110
  18.7 3.4 %collective-permute-start.7 = (bf16[33,32,128]{2,1,0:T(8,128)(2,1)S(1)}, bf16[33,32,128]{2,1,0:T(8,128)(2,1)S(1)}, u32[]{:S(2)}, u32[]{:S(2)}) collective-permute-start(bf16[33,32,128]{2,1,0:T(8,128)(2,1)S(1)} %get-tuple-element.39), channel_id=1, source_target_pairs={{0,2},{2,4},{4,6},{6,8},{8,10},{10,12},{12,14},{16,18},{18,20},{20... | collective-permute-start | bytes 811016 | tf_op jit(solution)/shard_map/ppermute | solution.py:18
  22.1 0.0 copy-start
  22.2 0.5 shard_map.111
  22.7 0.1 copy-done
  22.8 0.9 %shard_map.112 = (bf16[32,384,128]{2,1,0:T(8,128)(2,1)S(1)}, s32[3,32]{1,0:T(4,128)S(4)}) custom-call(bf16[32,4,128,128]{3,2,1,0:T(8,128)(2,1)S(1)} %get-tuple-element.29.refs_3_.factor_ref, s32[3,32]{1,0:T(4,128)S(1)} %bitcast.4, f32[16,48,128]{2,1,0:T(8,128)S(1)} %get-tuple-element.36.after_ref.image_two_ref), custom_call_target="tpu_custom_call" | custom-call | tf_op jit(solution)/shard_map/pallas_call | solution.py:398
  23.7 0.0 collective-permute-done.5.far_ref.far_odd_ref
  23.8 1.7 %collective-permute-start.6 = (bf16[33,32,128]{2,1,0:T(8,128)(2,1)S(1)}, bf16[33,32,128]{2,1,0:T(8,128)(2,1)S(1)}, u32[]{:S(2)}, u32[]{:S(2)}) collective-permute-start(bf16[33,32,128]{2,1,0:T(8,128)(2,1)S(1)} %shard_map.113), channel_id=1, source_target_pairs={{0,1},{1,0},{2,3},{3,2},{4,5},{5,4},{6,7},{7,6},{8,9},{9,8},{10,11... | collective-permute-start | bytes 811016 | tf_op jit(solution)/shard_map/ppermute | solution.py:22
  25.4 1.7 %collective-permute-done.7.far_even_ref = bf16[33,32,128]{2,1,0:T(8,128)(2,1)S(1)} collective-permute-done((bf16[33,32,128]{2,1,0:T(8,128)(2,1)S(1)}, bf16[33,32,128]{2,1,0:T(8,128)(2,1)S(1)}, u32[]{:S(2)}, u32[]{:S(2)}) %collective-permute-start.7) | collective-permute-done | bytes 270368 | tf_op jit(solution)/shard_map/ppermute | solution.py:18
  27.2 0.0 collective-permute-done.6.near_ref
  27.2 1.6 %shard_map.114 = (bf16[33,32,128]{2,1,0:T(8,128)(2,1)S(1)}, bf16[33,32,128]{2,1,0:T(8,128)(2,1)S(1)}, f32[96,40,128]{2,1,0:T(8,128)S(1)}, f32[40,128]{1,0:T(8,128)S(1)}, bf16[32,48,128]{2,1,0:T(8,128)(2,1)S(1)}) custom-call(s32[3,32]{1,0:T(4,128)S(4)} %get-tuple-element.37.ids_ref, ...), custom_call_target="tpu_custom_call", output_to_operand_aliasing={{2}: (9, {})} | custom-call | tf_op jit(solution)/shard_map/pallas_call | solution.py:406
  28.7 0.1 collective-permute-start.9
  28.8 1.3 %collective-permute-start.8 = (bf16[33,32,128]{2,1,0:T(8,128)(2,1)S(1)}, bf16[33,32,128]{2,1,0:T(8,128)(2,1)S(1)}, u32[]{:S(2)}, u32[]{:S(2)}) collective-permute-start(bf16[33,32,128]{2,1,0:T(8,128)(2,1)S(1)} %get-tuple-element.46.back_far_ref), channel_id=1, source_target_pairs={{2,0},{4,2},{6,4},{8,6},{10,8},{12,10},{14,12},{18,16},{20,18},{22... | collective-permute-start | bytes 811016 | tf_op jit(solution)/shard_map/ppermute | solution.py:18
  30.1 0.2 collective-permute-done.9.got_ref.mate_ref
  30.3 0.1 shard_map.116
  30.4 0.7 %collective-permute-start.10 = (bf16[33,32,128]{2,1,0:T(8,128)(2,1)S(1)}, bf16[33,32,128]{2,1,0:T(8,128)(2,1)S(1)}, u32[]{:S(2)}, u32[]{:S(2)}) collective-permute-start(bf16[33,32,128]{2,1,0:T(8,128)(2,1)S(1)} %shard_map.116), channel_id=1, source_target_pairs={{3,1},{5,3},{7,5},{9,7},{11,9},{13,11},{15,13},{19,17},{21,19},{23... | collective-permute-start | bytes 811016 | tf_op jit(solution)/shard_map/ppermute | solution.py:18
  31.1 0.4 shard_map.115
  31.5 7.9 %collective-permute-done.8.even_ref = bf16[33,32,128]{2,1,0:T(8,128)(2,1)S(1)} collective-permute-done((bf16[33,32,128]{2,1,0:T(8,128)(2,1)S(1)}, bf16[33,32,128]{2,1,0:T(8,128)(2,1)S(1)}, u32[]{:S(2)}, u32[]{:S(2)}) %collective-permute-start.8) | collective-permute-done | bytes 270368 | tf_op jit(solution)/shard_map/ppermute | solution.py:18
  39.4 0.0 collective-permute-done.10.odd_ref
  39.4 0.5 shard_map.117
  39.9 0.9 %collective-permute-start.11 = (f32[40,256]{1,0:T(8,128)S(1)}, f32[40,256]{1,0:T(8,128)S(1)}, u32[]{:S(2)}, u32[]{:S(2)}) collective-permute-start(f32[40,256]{1,0:T(8,128)S(1)} %get-tuple-element.49.x_ref), channel_id=1, source_target_pairs={{0,1},{1,0},{2,3},{3,2},{4,5},{5,4},{6,7},{7,6},{8,9},{9,8},{10,11... | collective-permute-start | bytes 122888 | tf_op jit(solution)/shard_map/ppermute | solution.py:53
  40.9 0.9 %collective-permute-done.11.refs_0_ = f32[40,256]{1,0:T(8,128)S(1)} collective-permute-done((f32[40,256]{1,0:T(8,128)S(1)}, f32[40,256]{1,0:T(8,128)S(1)}, u32[]{:S(2)}, u32[]{:S(2)}) %collective-permute-start.11) | collective-permute-done | bytes 40992 | tf_op jit(solution)/shard_map/ppermute | solution.py:53
  41.7 2.9 %collective-permute-start.12 = (f32[40,256]{1,0:T(8,128)S(1)}, f32[40,256]{1,0:T(8,128)S(1)}, u32[]{:S(2)}, u32[]{:S(2)}) collective-permute-start(f32[40,256]{1,0:T(8,128)S(1)} %shard_map.118.x_ref), channel_id=1, source_target_pairs={{0,3},{1,2},{2,1},{3,0},{4,7},{5,6},{6,5},{7,4},{8,11},{9,10},{10,... | collective-permute-start | bytes 122888 | tf_op jit(solution)/shard_map/ppermute | solution.py:53
  44.6 1.8 %collective-permute-done.12.refs_0_ = f32[40,256]{1,0:T(8,128)S(1)} collective-permute-done((f32[40,256]{1,0:T(8,128)S(1)}, f32[40,256]{1,0:T(8,128)S(1)}, u32[]{:S(2)}, u32[]{:S(2)}) %collective-permute-start.12) | collective-permute-done | bytes 40992 | tf_op jit(solution)/shard_map/ppermute | solution.py:53
  46.4 2.3 %collective-permute-start.15 = (f32[40,256]{1,0:T(8,128)S(1)}, f32[40,256]{1,0:T(8,128)S(1)}, u32[]{:S(2)}, u32[]{:S(2)}) collective-permute-start(f32[40,256]{1,0:T(8,128)S(1)} %shard_map.119.x_ref), channel_id=1, source_target_pairs={{0,13},{1,12},{2,15},{3,14},{4,9},{5,8},{6,11},{7,10},{8,5},{9,4},... | collective-permute-start | bytes 122888 | tf_op jit(solution)/shard_map/ppermute | solution.py:53
  48.7 0.1 collective-permute-start.14
  48.8 1.5 %collective-permute-start.13 = (f32[40,256]{1,0:T(8,128)S(1)}, f32[40,256]{1,0:T(8,128)S(1)}, u32[]{:S(2)}, u32[]{:S(2)}) collective-permute-start(f32[40,256]{1,0:T(8,128)S(1)} %shard_map.119.x_ref), channel_id=1, source_target_pairs={{0,5},{1,4},{2,7},{3,6},{4,1},{5,0},{6,3},{7,2},{8,13},{9,12},{10,... | collective-permute-start | bytes 122888 | tf_op jit(solution)/shard_map/ppermute | solution.py:53
  50.3 1.4 %collective-permute-done.15.refs_2_ = f32[40,256]{1,0:T(8,128)S(1)} collective-permute-done((f32[40,256]{1,0:T(8,128)S(1)}, f32[40,256]{1,0:T(8,128)S(1)}, u32[]{:S(2)}, u32[]{:S(2)}) %collective-permute-start.15) | collective-permute-done | bytes 40992 | tf_op jit(solution)/shard_map/ppermute | solution.py:53
  51.7 2.3 %collective-permute-done.14.refs_1_ = f32[40,256]{1,0:T(8,128)S(1)} collective-permute-done((f32[40,256]{1,0:T(8,128)S(1)}, f32[40,256]{1,0:T(8,128)S(1)}, u32[]{:S(2)}, u32[]{:S(2)}) %collective-permute-start.14) | collective-permute-done | bytes 40992 | tf_op jit(solution)/shard_map/ppermute | solution.py:53
  54.1 0.0 collective-permute-done.13.refs_0_
  54.1 1.6 %shard_map.121 = (f32[33,4096]{1,0:T(8,128)}, f32[33,4096]{1,0:T(8,128)}, f32[33,4096]{1,0:T(8,128)}) custom-call(f32[40,256]{1,0:T(8,128)S(1)} %shard_map.108.sums_ref, f32[40,256]{1,0:T(8,128)S(1)} %get-tuple-element.33.product_ref, f32[40,256]{1,0:T(8,128)S(1)} %shard_map.120.hess_sums_ref, f32[256,256]{1,0:T(8,128)S(1)} %get-tuple-element.30.refs_4_.inner_ref, ...), custom_call_target="tpu_custom_call" | custom-call | tf_op jit(solution)/shard_map/pallas_call | solution.py:423
  (7 shorter events, 0.1 us)
Async XLA Ops:
  2.8 1.4 %collective-permute-start = (f32[40,256]{1,0:T(8,128)S(1)}, f32[40,256]{1,0:T(8,128)S(1)}, u32[]{:S(2)}, u32[]{:S(2)}) collective-permute-start(f32[40,256]{1,0:T(8,128)S(1)} %get-tuple-element.27.x_ref), channel_id=1, source_target_pairs={{0,1},{1,0},{2,3},{3,2},{4,5},{5,4},{6,7},{7,6},{8,9},{9,8},{10,11... | collective-permute-start | bytes 122888 | tf_op jit(solution)/shard_map/ppermute | solution.py:53
  4.2 4.3 %collective-permute-start.1 = (f32[40,256]{1,0:T(8,128)S(1)}, f32[40,256]{1,0:T(8,128)S(1)}, u32[]{:S(2)}, u32[]{:S(2)}) collective-permute-start(f32[40,256]{1,0:T(8,128)S(1)} %shard_map.104.after_ref.x_ref), channel_id=1, source_target_pairs={{0,3},{1,2},{2,1},{3,0},{4,7},{5,6},{6,5},{7,4},{8,11},{9,10},{10,... | collective-permute-start | bytes 122888 | tf_op jit(solution)/shard_map/ppermute | solution.py:53
  8.5 6.8 %collective-permute-start.4 = (f32[40,256]{1,0:T(8,128)S(1)}, f32[40,256]{1,0:T(8,128)S(1)}, u32[]{:S(2)}, u32[]{:S(2)}) collective-permute-start(f32[40,256]{1,0:T(8,128)S(1)} %shard_map.106.after_ref.x_ref), channel_id=1, source_target_pairs={{0,13},{1,12},{2,15},{3,14},{4,9},{5,8},{6,11},{7,10},{8,5},{9,4},... | collective-permute-start | bytes 122888 | tf_op jit(solution)/shard_map/ppermute | solution.py:53
  12.4 4.4 %collective-permute-start.3 = (f32[40,256]{1,0:T(8,128)S(1)}, f32[40,256]{1,0:T(8,128)S(1)}, u32[]{:S(2)}, u32[]{:S(2)}) collective-permute-start(f32[40,256]{1,0:T(8,128)S(1)} %shard_map.106.after_ref.x_ref), channel_id=1, source_target_pairs={{0,9},{1,8},{2,11},{3,10},{4,13},{5,12},{6,15},{7,14},{8,1},{9,0},... | collective-permute-start | bytes 122888 | tf_op jit(solution)/shard_map/ppermute | solution.py:53
  12.4 4.4 %collective-permute-start.2 = (f32[40,256]{1,0:T(8,128)S(1)}, f32[40,256]{1,0:T(8,128)S(1)}, u32[]{:S(2)}, u32[]{:S(2)}) collective-permute-start(f32[40,256]{1,0:T(8,128)S(1)} %shard_map.106.after_ref.x_ref), channel_id=1, source_target_pairs={{0,5},{1,4},{2,7},{3,6},{4,1},{5,0},{6,3},{7,2},{8,13},{9,12},{10,... | collective-permute-start | bytes 122888 | tf_op jit(solution)/shard_map/ppermute | solution.py:53
  17.6 6.1 %collective-permute-start.5 = (bf16[33,32,128]{2,1,0:T(8,128)(2,1)S(1)}, bf16[33,32,128]{2,1,0:T(8,128)(2,1)S(1)}, u32[]{:S(2)}, u32[]{:S(2)}) collective-permute-start(bf16[33,32,128]{2,1,0:T(8,128)(2,1)S(1)} %get-tuple-element.34.own_ref), channel_id=1, source_target_pairs={{1,3},{3,5},{5,7},{7,9},{9,11},{11,13},{13,15},{17,19},{19,21},{21... | collective-permute-start | bytes 811016 | tf_op jit(solution)/shard_map/ppermute | solution.py:18
  18.7 8.4 %collective-permute-start.7 = (bf16[33,32,128]{2,1,0:T(8,128)(2,1)S(1)}, bf16[33,32,128]{2,1,0:T(8,128)(2,1)S(1)}, u32[]{:S(2)}, u32[]{:S(2)}) collective-permute-start(bf16[33,32,128]{2,1,0:T(8,128)(2,1)S(1)} %get-tuple-element.39), channel_id=1, source_target_pairs={{0,2},{2,4},{4,6},{6,8},{8,10},{10,12},{12,14},{16,18},{18,20},{20... | collective-permute-start | bytes 811016 | tf_op jit(solution)/shard_map/ppermute | solution.py:18
  22.1 0.7 %copy-start = (s32[32,3]{0,1:T(4,128)S(1)}, s32[32,3]{0,1:T(4,128)}, u32[]{:S(2)}) copy-start(s32[32,3]{0,1:T(4,128)} %param.13) | copy-start | bytes 1156
  23.8 3.4 %collective-permute-start.6 = (bf16[33,32,128]{2,1,0:T(8,128)(2,1)S(1)}, bf16[33,32,128]{2,1,0:T(8,128)(2,1)S(1)}, u32[]{:S(2)}, u32[]{:S(2)}) collective-permute-start(bf16[33,32,128]{2,1,0:T(8,128)(2,1)S(1)} %shard_map.113), channel_id=1, source_target_pairs={{0,1},{1,0},{2,3},{3,2},{4,5},{5,4},{6,7},{7,6},{8,9},{9,8},{10,11... | collective-permute-start | bytes 811016 | tf_op jit(solution)/shard_map/ppermute | solution.py:22
  28.7 1.6 %collective-permute-start.9 = (bf16[33,32,128]{2,1,0:T(8,128)(2,1)S(1)}, bf16[33,32,128]{2,1,0:T(8,128)(2,1)S(1)}, u32[]{:S(2)}, u32[]{:S(2)}) collective-permute-start(bf16[33,32,128]{2,1,0:T(8,128)(2,1)S(1)} %get-tuple-element.47), channel_id=1, source_target_pairs={{0,1},{1,0},{2,3},{3,2},{4,5},{5,4},{6,7},{7,6},{8,9},{9,8},{10,11... | collective-permute-start | bytes 811016 | tf_op jit(solution)/shard_map/ppermute | solution.py:22
  28.8 10.6 %collective-permute-start.8 = (bf16[33,32,128]{2,1,0:T(8,128)(2,1)S(1)}, bf16[33,32,128]{2,1,0:T(8,128)(2,1)S(1)}, u32[]{:S(2)}, u32[]{:S(2)}) collective-permute-start(bf16[33,32,128]{2,1,0:T(8,128)(2,1)S(1)} %get-tuple-element.46.back_far_ref), channel_id=1, source_target_pairs={{2,0},{4,2},{6,4},{8,6},{10,8},{12,10},{14,12},{18,16},{20,18},{22... | collective-permute-start | bytes 811016 | tf_op jit(solution)/shard_map/ppermute | solution.py:18
  30.4 9.0 %collective-permute-start.10 = (bf16[33,32,128]{2,1,0:T(8,128)(2,1)S(1)}, bf16[33,32,128]{2,1,0:T(8,128)(2,1)S(1)}, u32[]{:S(2)}, u32[]{:S(2)}) collective-permute-start(bf16[33,32,128]{2,1,0:T(8,128)(2,1)S(1)} %shard_map.116), channel_id=1, source_target_pairs={{3,1},{5,3},{7,5},{9,7},{11,9},{13,11},{15,13},{19,17},{21,19},{23... | collective-permute-start | bytes 811016 | tf_op jit(solution)/shard_map/ppermute | solution.py:18
  39.9 1.8 %collective-permute-start.11 = (f32[40,256]{1,0:T(8,128)S(1)}, f32[40,256]{1,0:T(8,128)S(1)}, u32[]{:S(2)}, u32[]{:S(2)}) collective-permute-start(f32[40,256]{1,0:T(8,128)S(1)} %get-tuple-element.49.x_ref), channel_id=1, source_target_pairs={{0,1},{1,0},{2,3},{3,2},{4,5},{5,4},{6,7},{7,6},{8,9},{9,8},{10,11... | collective-permute-start | bytes 122888 | tf_op jit(solution)/shard_map/ppermute | solution.py:53
  41.7 4.6 %collective-permute-start.12 = (f32[40,256]{1,0:T(8,128)S(1)}, f32[40,256]{1,0:T(8,128)S(1)}, u32[]{:S(2)}, u32[]{:S(2)}) collective-permute-start(f32[40,256]{1,0:T(8,128)S(1)} %shard_map.118.x_ref), channel_id=1, source_target_pairs={{0,3},{1,2},{2,1},{3,0},{4,7},{5,6},{6,5},{7,4},{8,11},{9,10},{10,... | collective-permute-start | bytes 122888 | tf_op jit(solution)/shard_map/ppermute | solution.py:53
  46.4 5.3 %collective-permute-start.15 = (f32[40,256]{1,0:T(8,128)S(1)}, f32[40,256]{1,0:T(8,128)S(1)}, u32[]{:S(2)}, u32[]{:S(2)}) collective-permute-start(f32[40,256]{1,0:T(8,128)S(1)} %shard_map.119.x_ref), channel_id=1, source_target_pairs={{0,13},{1,12},{2,15},{3,14},{4,9},{5,8},{6,11},{7,10},{8,5},{9,4},... | collective-permute-start | bytes 122888 | tf_op jit(solution)/shard_map/ppermute | solution.py:53
  48.7 5.4 %collective-permute-start.14 = (f32[40,256]{1,0:T(8,128)S(1)}, f32[40,256]{1,0:T(8,128)S(1)}, u32[]{:S(2)}, u32[]{:S(2)}) collective-permute-start(f32[40,256]{1,0:T(8,128)S(1)} %shard_map.119.x_ref), channel_id=1, source_target_pairs={{0,9},{1,8},{2,11},{3,10},{4,13},{5,12},{6,15},{7,14},{8,1},{9,0},... | collective-permute-start | bytes 122888 | tf_op jit(solution)/shard_map/ppermute | solution.py:53
  48.8 5.3 %collective-permute-start.13 = (f32[40,256]{1,0:T(8,128)S(1)}, f32[40,256]{1,0:T(8,128)S(1)}, u32[]{:S(2)}, u32[]{:S(2)}) collective-permute-start(f32[40,256]{1,0:T(8,128)S(1)} %shard_map.119.x_ref), channel_id=1, source_target_pairs={{0,5},{1,4},{2,7},{3,6},{4,1},{5,0},{6,3},{7,2},{8,13},{9,12},{10,... | collective-permute-start | bytes 122888 | tf_op jit(solution)/shard_map/ppermute | solution.py:53

commit v16 on v14

--- a/solution.py
+++ b/solution.py
@@ -66,7 +66,7 @@
     return rounds
 
 
-def total(x, axis, beside=()):
+def total(x, axis, wire, beside=()):
     n = lax.axis_size(axis)
     if n & (n - 1):
         return lax.psum(x, axis), [work(x) for work in beside]
@@ -81,9 +81,9 @@
             held += made[-1]
         add = functools.partial(add_kernel, len(got) + 1, len(held))
         ins = [pltpu.VMEM] * (len(got) + 1) + [pl.ANY] * len(held)
-        outs = [(x.shape, F32)] + [(x.shape, BF16)] * (not last)
+        outs = [(x.shape, F32)] + [(x.shape, BF16)] * (wire == BF16 and not last)
         x, *rest = jax.tree.leaves(call(add, ins, outs)(x, *got, *held))
-        msg = rest[0] if rest else None
+        msg = rest[0] if rest else x
     return x, made
 
 
@@ -400,7 +400,7 @@
     def turn_map(msg):
         return (call(turn_map_kernel, [vmem, pl.ANY], [(inducing_map.shape[::-1], BF16)])(inducing_map, msg),)
 
-    sums, ((turned_map,), (factor, inner_inverse)) = total(partial, "space", [turn_map, load])
+    sums, ((turned_map,), (factor, inner_inverse)) = total(partial, "space", BF16, [turn_map, load])
     direction, rounded, product = call(
         direction_kernel, [vmem] * 5, [field, packed, sum_shape], [vmem((blocks, bs), F32)]
     )(sums, inner_inverse, terms, right_side, turned_map)
@@ -443,7 +443,7 @@
         image, factor, back_own, curve, direction, terms
     )
     hess, partial = call(combine_kernel, [vmem] * 8, [field, sum_shape])(base, from_even, from_odd, mate, curve, *points)
-    hess_sums, _ = total(partial, "space")
+    hess_sums, _ = total(partial, "space", F32)
     whole = ((count + 1, blocks * bs), F32)
     scratch = [vmem(*whole)] * 3 + [pltpu.SemaphoreType.DMA((3 * OUT_PARTS,))]
     return call(finish_kernel, [vmem] * 9, [whole] * 3, scratch, keep=False)(

time: 54.5 us -> 55.5 us (1.018)
  waiting for transfers between devices: 17.9 us -> 19.1 us
    ppermute x10, waiting for transfers between devices: 8.16 us -> 9.32 us  [total(): lax.ppermute(msg, axis, [(j, j ^ d) for j in range(n)])]
where the time goes in v16:
time: 55.5 us; the launch traced here: 55.2 us
  starting transfers between devices  23.3 us (42%)
  waiting for transfers between devices  19.1 us (34%)
  Pallas kernels  11.9 us (21%)
  between operations  0.78 us (1%)
    ppermute x10, starting transfers between devices, total(): lax.ppermute(msg, axis, [(j, j ^ d) for j in range(n)])  15.4 us
    ppermute x4, waiting for transfers between devices, sent(): lax.ppermute(block, axis, [(i, i + distance) for i in devices if i % 2 in...  9.51 us
    ppermute x10, waiting for transfers between devices, total(): lax.ppermute(msg, axis, [(j, j ^ d) for j in range(n)])  9.32 us
    ppermute x4, starting transfers between devices, sent(): lax.ppermute(block, axis, [(i, i + distance) for i in devices if i % 2 in...  6.05 us
    pallas_call x1, Pallas kernels, load(): call(load_kernel, [pl.ANY] * 3, outs, [pltpu.SemaphoreType.DMA((2,))])  2.23 us
    pallas_call x1, Pallas kernels, body(): call(project_kernel, [pl.ANY] * 5, [sum_shape, ((2, blocks, bs), F32), fi...  2.15 us
    ppermute x2, starting transfers between devices, swapped(): lax.ppermute(block, axis, [(i, i ^ 1) for i in range(lax.axis_size(axis))])  1.88 us
    pallas_call x1, Pallas kernels, body(): call(finish_kernel, [vmem] * 9, [whole] * 3, scratch, keep=False)  1.6 us
  transfers between devices with their start and end apart: 16, of which 10 were waited for; matrix products, arithmetic and copies ran while one was open for 0% of the time, Pallas kernels for 10%

profile of v16, /device:TPU:0, one launch (start us, length us, event | category | flops | bytes accessed | tf_op | source)
XLA Modules:
  0.0 55.2 jit_solution(11822867588269101340)
XLA Ops:
  0.6 2.2 %shard_map.103 = (f32[40,256]{1,0:T(8,128)S(1)}, f32[2,32,128]{2,1,0:T(8,128)S(1)}, f32[32,40,128]{2,1,0:T(8,128)S(1)}, bf16[4096,256]{1,0:T(8,128)(2,1)S(1)}) custom-call(f32[32,128]{1,0:T(8,128)} %bitcast.5, s32[32,128]{1,0:T(8,128)} %bitcast.6, f32[32,128]{1,0:T(8,128)} %bitcast.7, f32[32,4096]{1,0:T(8,128)} %probes_hbm.1, bf16[4096,256]{1,0:T(8,128)(2,1)} %map_hbm.1), custom_call_target="tpu_custom_call" | custom-call | tf_op jit(solution)/shard_map/pallas_call | solution.py:380
  2.8 0.5 collective-permute-start
  3.3 0.9 %collective-permute-done.refs_0_ = f32[40,256]{1,0:T(8,128)S(1)} collective-permute-done((f32[40,256]{1,0:T(8,128)S(1)}, f32[40,256]{1,0:T(8,128)S(1)}, u32[]{:S(2)}, u32[]{:S(2)}) %collective-permute-start) | collective-permute-done | bytes 40992 | tf_op jit(solution)/shard_map/ppermute | solution.py:76
  4.2 2.7 %collective-permute-start.1 = (bf16[40,256]{1,0:T(8,128)(2,1)S(1)}, bf16[40,256]{1,0:T(8,128)(2,1)S(1)}, u32[]{:S(2)}, u32[]{:S(2)}) collective-permute-start(bf16[40,256]{1,0:T(8,128)(2,1)S(1)} %get-tuple-element.33.after_ref), channel_id=1, source_target_pairs={{0,3},{1,2},{2,1},{3,0},{4,7},{5,6},{6,5},{7,4},{8,11},{9,10},{10,... | collective-permute-start | bytes 61448 | tf_op jit(solution)/shard_map/ppermute | solution.py:76
  6.9 0.6 %shard_map.105.refs_1_.map_ref = bf16[256,4096]{1,0:T(8,128)(2,1)S(1)} custom-call(bf16[4096,256]{1,0:T(8,128)(2,1)S(1)} %get-tuple-element.34.map_ref, bf16[40,256]{1,0:T(8,128)(2,1)S(1)} %get-tuple-element.33.after_ref), custom_call_target="tpu_custom_call" | custom-call | tf_op jit(solution)/shard_map/pallas_call | solution.py:401
  7.5 0.8 %collective-permute-done.1.refs_0_ = bf16[40,256]{1,0:T(8,128)(2,1)S(1)} collective-permute-done((bf16[40,256]{1,0:T(8,128)(2,1)S(1)}, bf16[40,256]{1,0:T(8,128)(2,1)S(1)}, u32[]{:S(2)}, u32[]{:S(2)}) %collective-permute-start.1) | collective-permute-done | bytes 20512 | tf_op jit(solution)/shard_map/ppermute | solution.py:76
  8.4 3.9 %collective-permute-start.4 = (bf16[40,256]{1,0:T(8,128)(2,1)S(1)}, bf16[40,256]{1,0:T(8,128)(2,1)S(1)}, u32[]{:S(2)}, u32[]{:S(2)}) collective-permute-start(bf16[40,256]{1,0:T(8,128)(2,1)S(1)} %get-tuple-element.36.after_ref), channel_id=1, source_target_pairs={{0,13},{1,12},{2,15},{3,14},{4,9},{5,8},{6,11},{7,10},{8,5},{9,4},... | collective-permute-start | bytes 61448 | tf_op jit(solution)/shard_map/ppermute | solution.py:76
  12.3 0.0 collective-permute-start.3
  12.3 0.6 %collective-permute-start.2 = (bf16[40,256]{1,0:T(8,128)(2,1)S(1)}, bf16[40,256]{1,0:T(8,128)(2,1)S(1)}, u32[]{:S(2)}, u32[]{:S(2)}) collective-permute-start(bf16[40,256]{1,0:T(8,128)(2,1)S(1)} %get-tuple-element.36.after_ref), channel_id=1, source_target_pairs={{0,5},{1,4},{2,7},{3,6},{4,1},{5,0},{6,3},{7,2},{8,13},{9,12},{10,... | collective-permute-start | bytes 61448 | tf_op jit(solution)/shard_map/ppermute | solution.py:76
  12.9 2.2 %shard_map.107 = (bf16[32,4,128,128]{3,2,1,0:T(8,128)(2,1)S(1)}, f32[256,256]{1,0:T(8,128)S(1)}) custom-call(bf16[32,4,128,128]{3,2,1,0:T(8,128)(2,1)} %factor_hbm.1, f32[256,256]{1,0:T(8,128)} %inner_hbm.1, bf16[40,256]{1,0:T(8,128)(2,1)S(1)} %get-tuple-element.36.after_ref), custom_call_target="tpu_custom_call" | custom-call | tf_op jit(solution)/shard_map/pallas_call | solution.py:396
  15.1 0.0 collective-permute-done.4.refs_2_
  15.1 1.3 %collective-permute-done.3.refs_1_ = bf16[40,256]{1,0:T(8,128)(2,1)S(1)} collective-permute-done((bf16[40,256]{1,0:T(8,128)(2,1)S(1)}, bf16[40,256]{1,0:T(8,128)(2,1)S(1)}, u32[]{:S(2)}, u32[]{:S(2)}) %collective-permute-start.3) | collective-permute-done | bytes 20512 | tf_op jit(solution)/shard_map/ppermute | solution.py:76
  16.4 0.0 collective-permute-done.2.refs_0_
  16.4 0.7 %shard_map.109 = (f32[32,40,128]{2,1,0:T(8,128)S(1)}, bf16[33,32,128]{2,1,0:T(8,128)(2,1)S(1)}, f32[40,256]{1,0:T(8,128)S(1)}) custom-call(f32[40,256]{1,0:T(8,128)S(1)} %shard_map.108.sums_ref, f32[256,256]{1,0:T(8,128)S(1)} %get-tuple-element.38.refs_4_.inner_ref, f32[2,32,128]{2,1,0:T(8,128)S(1)} %get-tuple-element.39.terms_ref, ...), custom_call_target="tpu_custom_call" | custom-call | tf_op jit(solution)/shard_map/pallas_call | solution.py:404
  17.1 0.7 %collective-permute-start.5 = (bf16[33,32,128]{2,1,0:T(8,128)(2,1)S(1)}, bf16[33,32,128]{2,1,0:T(8,128)(2,1)S(1)}, u32[]{:S(2)}, u32[]{:S(2)}) collective-permute-start(bf16[33,32,128]{2,1,0:T(8,128)(2,1)S(1)} %get-tuple-element.42.own_ref), channel_id=1, source_target_pairs={{1,3},{3,5},{5,7},{7,9},{9,11},{11,13},{13,15},{17,19},{19,21},{21... | collective-permute-start | bytes 811016 | tf_op jit(solution)/shard_map/ppermute | solution.py:18
  17.8 0.5 shard_map.110
  18.3 3.4 %collective-permute-start.7 = (bf16[33,32,128]{2,1,0:T(8,128)(2,1)S(1)}, bf16[33,32,128]{2,1,0:T(8,128)(2,1)S(1)}, u32[]{:S(2)}, u32[]{:S(2)}) collective-permute-start(bf16[33,32,128]{2,1,0:T(8,128)(2,1)S(1)} %get-tuple-element.47), channel_id=1, source_target_pairs={{0,2},{2,4},{4,6},{6,8},{8,10},{10,12},{12,14},{16,18},{18,20},{20... | collective-permute-start | bytes 811016 | tf_op jit(solution)/shard_map/ppermute | solution.py:18
  21.7 0.0 copy-start
  21.7 0.5 shard_map.111
  22.2 0.1 copy-done
  22.4 0.9 %shard_map.112 = (bf16[32,384,128]{2,1,0:T(8,128)(2,1)S(1)}, s32[3,32]{1,0:T(4,128)S(4)}) custom-call(bf16[32,4,128,128]{3,2,1,0:T(8,128)(2,1)S(1)} %get-tuple-element.37.refs_3_.factor_ref, s32[3,32]{1,0:T(4,128)S(1)} %bitcast.4, f32[16,48,128]{2,1,0:T(8,128)S(1)} %get-tuple-element.44.after_ref.image_two_ref), custom_call_target="tpu_custom_call" | custom-call | tf_op jit(solution)/shard_map/pallas_call | solution.py:424
  23.3 0.0 collective-permute-done.5.far_ref.far_odd_ref
  23.3 1.8 %collective-permute-start.6 = (bf16[33,32,128]{2,1,0:T(8,128)(2,1)S(1)}, bf16[33,32,128]{2,1,0:T(8,128)(2,1)S(1)}, u32[]{:S(2)}, u32[]{:S(2)}) collective-permute-start(bf16[33,32,128]{2,1,0:T(8,128)(2,1)S(1)} %shard_map.113), channel_id=1, source_target_pairs={{0,1},{1,0},{2,3},{3,2},{4,5},{5,4},{6,7},{7,6},{8,9},{9,8},{10,11... | collective-permute-start | bytes 811016 | tf_op jit(solution)/shard_map/ppermute | solution.py:22
  25.1 1.6 %collective-permute-done.7.far_even_ref = bf16[33,32,128]{2,1,0:T(8,128)(2,1)S(1)} collective-permute-done((bf16[33,32,128]{2,1,0:T(8,128)(2,1)S(1)}, bf16[33,32,128]{2,1,0:T(8,128)(2,1)S(1)}, u32[]{:S(2)}, u32[]{:S(2)}) %collective-permute-start.7) | collective-permute-done | bytes 270368 | tf_op jit(solution)/shard_map/ppermute | solution.py:18
  26.8 0.0 collective-permute-done.6.near_ref
  26.8 1.6 %shard_map.114 = (bf16[33,32,128]{2,1,0:T(8,128)(2,1)S(1)}, bf16[33,32,128]{2,1,0:T(8,128)(2,1)S(1)}, f32[96,40,128]{2,1,0:T(8,128)S(1)}, f32[40,128]{1,0:T(8,128)S(1)}, bf16[32,48,128]{2,1,0:T(8,128)(2,1)S(1)}) custom-call(s32[3,32]{1,0:T(4,128)S(4)} %get-tuple-element.45.ids_ref, ...), custom_call_target="tpu_custom_call", output_to_operand_aliasing={{2}: (9, {})} | custom-call | tf_op jit(solution)/shard_map/pallas_call | solution.py:432
  28.3 0.1 collective-permute-start.9
  28.4 1.3 %collective-permute-start.8 = (bf16[33,32,128]{2,1,0:T(8,128)(2,1)S(1)}, bf16[33,32,128]{2,1,0:T(8,128)(2,1)S(1)}, u32[]{:S(2)}, u32[]{:S(2)}) collective-permute-start(bf16[33,32,128]{2,1,0:T(8,128)(2,1)S(1)} %get-tuple-element.54.back_far_ref), channel_id=1, source_target_pairs={{2,0},{4,2},{6,4},{8,6},{10,8},{12,10},{14,12},{18,16},{20,18},{22... | collective-permute-start | bytes 811016 | tf_op jit(solution)/shard_map/ppermute | solution.py:18
  29.7 0.2 collective-permute-done.9.got_ref.mate_ref
  30.0 0.1 shard_map.116
  30.0 0.7 %collective-permute-start.10 = (bf16[33,32,128]{2,1,0:T(8,128)(2,1)S(1)}, bf16[33,32,128]{2,1,0:T(8,128)(2,1)S(1)}, u32[]{:S(2)}, u32[]{:S(2)}) collective-permute-start(bf16[33,32,128]{2,1,0:T(8,128)(2,1)S(1)} %shard_map.116), channel_id=1, source_target_pairs={{3,1},{5,3},{7,5},{9,7},{11,9},{13,11},{15,13},{19,17},{21,19},{23... | collective-permute-start | bytes 811016 | tf_op jit(solution)/shard_map/ppermute | solution.py:18
  30.7 0.4 shard_map.115
  31.2 7.9 %collective-permute-done.8.even_ref = bf16[33,32,128]{2,1,0:T(8,128)(2,1)S(1)} collective-permute-done((bf16[33,32,128]{2,1,0:T(8,128)(2,1)S(1)}, bf16[33,32,128]{2,1,0:T(8,128)(2,1)S(1)}, u32[]{:S(2)}, u32[]{:S(2)}) %collective-permute-start.8) | collective-permute-done | bytes 270368 | tf_op jit(solution)/shard_map/ppermute | solution.py:18
  39.0 0.0 collective-permute-done.10.odd_ref
  39.0 0.5 shard_map.117
  39.5 0.9 %collective-permute-start.11 = (f32[40,256]{1,0:T(8,128)S(1)}, f32[40,256]{1,0:T(8,128)S(1)}, u32[]{:S(2)}, u32[]{:S(2)}) collective-permute-start(f32[40,256]{1,0:T(8,128)S(1)} %get-tuple-element.57.x_ref), channel_id=1, source_target_pairs={{0,1},{1,0},{2,3},{3,2},{4,5},{5,4},{6,7},{7,6},{8,9},{9,8},{10,11... | collective-permute-start | bytes 122888 | tf_op jit(solution)/shard_map/ppermute | solution.py:76
  40.5 0.9 %collective-permute-done.11.refs_0_ = f32[40,256]{1,0:T(8,128)S(1)} collective-permute-done((f32[40,256]{1,0:T(8,128)S(1)}, f32[40,256]{1,0:T(8,128)S(1)}, u32[]{:S(2)}, u32[]{:S(2)}) %collective-permute-start.11) | collective-permute-done | bytes 40992 | tf_op jit(solution)/shard_map/ppermute | solution.py:76
  41.4 2.9 %collective-permute-start.12 = (f32[40,256]{1,0:T(8,128)S(1)}, f32[40,256]{1,0:T(8,128)S(1)}, u32[]{:S(2)}, u32[]{:S(2)}) collective-permute-start(f32[40,256]{1,0:T(8,128)S(1)} %shard_map.118.x_ref), channel_id=1, source_target_pairs={{0,3},{1,2},{2,1},{3,0},{4,7},{5,6},{6,5},{7,4},{8,11},{9,10},{10,... | collective-permute-start | bytes 122888 | tf_op jit(solution)/shard_map/ppermute | solution.py:76
  44.2 1.8 %collective-permute-done.12.refs_0_ = f32[40,256]{1,0:T(8,128)S(1)} collective-permute-done((f32[40,256]{1,0:T(8,128)S(1)}, f32[40,256]{1,0:T(8,128)S(1)}, u32[]{:S(2)}, u32[]{:S(2)}) %collective-permute-start.12) | collective-permute-done | bytes 40992 | tf_op jit(solution)/shard_map/ppermute | solution.py:76
  46.0 2.4 %collective-permute-start.15 = (f32[40,256]{1,0:T(8,128)S(1)}, f32[40,256]{1,0:T(8,128)S(1)}, u32[]{:S(2)}, u32[]{:S(2)}) collective-permute-start(f32[40,256]{1,0:T(8,128)S(1)} %shard_map.119.x_ref), channel_id=1, source_target_pairs={{0,13},{1,12},{2,15},{3,14},{4,9},{5,8},{6,11},{7,10},{8,5},{9,4},... | collective-permute-start | bytes 122888 | tf_op jit(solution)/shard_map/ppermute | solution.py:76
  48.5 0.0 collective-permute-start.14
  48.5 1.4 %collective-permute-start.13 = (f32[40,256]{1,0:T(8,128)S(1)}, f32[40,256]{1,0:T(8,128)S(1)}, u32[]{:S(2)}, u32[]{:S(2)}) collective-permute-start(f32[40,256]{1,0:T(8,128)S(1)} %shard_map.119.x_ref), channel_id=1, source_target_pairs={{0,5},{1,4},{2,7},{3,6},{4,1},{5,0},{6,3},{7,2},{8,13},{9,12},{10,... | collective-permute-start | bytes 122888 | tf_op jit(solution)/shard_map/ppermute | solution.py:76
  49.9 1.4 %collective-permute-done.15.refs_2_ = f32[40,256]{1,0:T(8,128)S(1)} collective-permute-done((f32[40,256]{1,0:T(8,128)S(1)}, f32[40,256]{1,0:T(8,128)S(1)}, u32[]{:S(2)}, u32[]{:S(2)}) %collective-permute-start.15) | collective-permute-done | bytes 40992 | tf_op jit(solution)/shard_map/ppermute | solution.py:76
  51.3 2.2 %collective-permute-done.14.refs_1_ = f32[40,256]{1,0:T(8,128)S(1)} collective-permute-done((f32[40,256]{1,0:T(8,128)S(1)}, f32[40,256]{1,0:T(8,128)S(1)}, u32[]{:S(2)}, u32[]{:S(2)}) %collective-permute-start.14) | collective-permute-done | bytes 40992 | tf_op jit(solution)/shard_map/ppermute | solution.py:76
  53.6 0.0 collective-permute-done.13.refs_0_
  53.6 1.6 %shard_map.121 = (f32[33,4096]{1,0:T(8,128)}, f32[33,4096]{1,0:T(8,128)}, f32[33,4096]{1,0:T(8,128)}) custom-call(f32[40,256]{1,0:T(8,128)S(1)} %shard_map.108.sums_ref, f32[40,256]{1,0:T(8,128)S(1)} %get-tuple-element.41.product_ref, f32[40,256]{1,0:T(8,128)S(1)} %shard_map.120.hess_sums_ref, f32[256,256]{1,0:T(8,128)S(1)} %get-tuple-element.38.refs_4_.inner_ref, ...), custom_call_target="tpu_custom_call" | custom-call | tf_op jit(solution)/shard_map/pallas_call | solution.py:449
  (7 shorter events, 0.1 us)
Async XLA Ops:
  2.8 1.4 %collective-permute-start = (f32[40,256]{1,0:T(8,128)S(1)}, f32[40,256]{1,0:T(8,128)S(1)}, u32[]{:S(2)}, u32[]{:S(2)}) collective-permute-start(f32[40,256]{1,0:T(8,128)S(1)} %get-tuple-element.31.x_ref), channel_id=1, source_target_pairs={{0,1},{1,0},{2,3},{3,2},{4,5},{5,4},{6,7},{7,6},{8,9},{9,8},{10,11... | collective-permute-start | bytes 122888 | tf_op jit(solution)/shard_map/ppermute | solution.py:76
  4.2 4.1 %collective-permute-start.1 = (bf16[40,256]{1,0:T(8,128)(2,1)S(1)}, bf16[40,256]{1,0:T(8,128)(2,1)S(1)}, u32[]{:S(2)}, u32[]{:S(2)}) collective-permute-start(bf16[40,256]{1,0:T(8,128)(2,1)S(1)} %get-tuple-element.33.after_ref), channel_id=1, source_target_pairs={{0,3},{1,2},{2,1},{3,0},{4,7},{5,6},{6,5},{7,4},{8,11},{9,10},{10,... | collective-permute-start | bytes 61448 | tf_op jit(solution)/shard_map/ppermute | solution.py:76
  8.4 6.7 %collective-permute-start.4 = (bf16[40,256]{1,0:T(8,128)(2,1)S(1)}, bf16[40,256]{1,0:T(8,128)(2,1)S(1)}, u32[]{:S(2)}, u32[]{:S(2)}) collective-permute-start(bf16[40,256]{1,0:T(8,128)(2,1)S(1)} %get-tuple-element.36.after_ref), channel_id=1, source_target_pairs={{0,13},{1,12},{2,15},{3,14},{4,9},{5,8},{6,11},{7,10},{8,5},{9,4},... | collective-permute-start | bytes 61448 | tf_op jit(solution)/shard_map/ppermute | solution.py:76
  12.3 4.1 %collective-permute-start.3 = (bf16[40,256]{1,0:T(8,128)(2,1)S(1)}, bf16[40,256]{1,0:T(8,128)(2,1)S(1)}, u32[]{:S(2)}, u32[]{:S(2)}) collective-permute-start(bf16[40,256]{1,0:T(8,128)(2,1)S(1)} %get-tuple-element.36.after_ref), channel_id=1, source_target_pairs={{0,9},{1,8},{2,11},{3,10},{4,13},{5,12},{6,15},{7,14},{8,1},{9,0},... | collective-permute-start | bytes 61448 | tf_op jit(solution)/shard_map/ppermute | solution.py:76
  12.3 4.1 %collective-permute-start.2 = (bf16[40,256]{1,0:T(8,128)(2,1)S(1)}, bf16[40,256]{1,0:T(8,128)(2,1)S(1)}, u32[]{:S(2)}, u32[]{:S(2)}) collective-permute-start(bf16[40,256]{1,0:T(8,128)(2,1)S(1)} %get-tuple-element.36.after_ref), channel_id=1, source_target_pairs={{0,5},{1,4},{2,7},{3,6},{4,1},{5,0},{6,3},{7,2},{8,13},{9,12},{10,... | collective-permute-start | bytes 61448 | tf_op jit(solution)/shard_map/ppermute | solution.py:76
  17.1 6.1 %collective-permute-start.5 = (bf16[33,32,128]{2,1,0:T(8,128)(2,1)S(1)}, bf16[33,32,128]{2,1,0:T(8,128)(2,1)S(1)}, u32[]{:S(2)}, u32[]{:S(2)}) collective-permute-start(bf16[33,32,128]{2,1,0:T(8,128)(2,1)S(1)} %get-tuple-element.42.own_ref), channel_id=1, source_target_pairs={{1,3},{3,5},{5,7},{7,9},{9,11},{11,13},{13,15},{17,19},{19,21},{21... | collective-permute-start | bytes 811016 | tf_op jit(solution)/shard_map/ppermute | solution.py:18
  18.3 8.5 %collective-permute-start.7 = (bf16[33,32,128]{2,1,0:T(8,128)(2,1)S(1)}, bf16[33,32,128]{2,1,0:T(8,128)(2,1)S(1)}, u32[]{:S(2)}, u32[]{:S(2)}) collective-permute-start(bf16[33,32,128]{2,1,0:T(8,128)(2,1)S(1)} %get-tuple-element.47), channel_id=1, source_target_pairs={{0,2},{2,4},{4,6},{6,8},{8,10},{10,12},{12,14},{16,18},{18,20},{20... | collective-permute-start | bytes 811016 | tf_op jit(solution)/shard_map/ppermute | solution.py:18
  21.7 0.7 %copy-start = (s32[32,3]{0,1:T(4,128)S(1)}, s32[32,3]{0,1:T(4,128)}, u32[]{:S(2)}) copy-start(s32[32,3]{0,1:T(4,128)} %param.13) | copy-start | bytes 1156
  23.3 3.4 %collective-permute-start.6 = (bf16[33,32,128]{2,1,0:T(8,128)(2,1)S(1)}, bf16[33,32,128]{2,1,0:T(8,128)(2,1)S(1)}, u32[]{:S(2)}, u32[]{:S(2)}) collective-permute-start(bf16[33,32,128]{2,1,0:T(8,128)(2,1)S(1)} %shard_map.113), channel_id=1, source_target_pairs={{0,1},{1,0},{2,3},{3,2},{4,5},{5,4},{6,7},{7,6},{8,9},{9,8},{10,11... | collective-permute-start | bytes 811016 | tf_op jit(solution)/shard_map/ppermute | solution.py:22
  28.3 1.6 %collective-permute-start.9 = (bf16[33,32,128]{2,1,0:T(8,128)(2,1)S(1)}, bf16[33,32,128]{2,1,0:T(8,128)(2,1)S(1)}, u32[]{:S(2)}, u32[]{:S(2)}) collective-permute-start(bf16[33,32,128]{2,1,0:T(8,128)(2,1)S(1)} %get-tuple-element.55), channel_id=1, source_target_pairs={{0,1},{1,0},{2,3},{3,2},{4,5},{5,4},{6,7},{7,6},{8,9},{9,8},{10,11... | collective-permute-start | bytes 811016 | tf_op jit(solution)/shard_map/ppermute | solution.py:22
  28.4 10.6 %collective-permute-start.8 = (bf16[33,32,128]{2,1,0:T(8,128)(2,1)S(1)}, bf16[33,32,128]{2,1,0:T(8,128)(2,1)S(1)}, u32[]{:S(2)}, u32[]{:S(2)}) collective-permute-start(bf16[33,32,128]{2,1,0:T(8,128)(2,1)S(1)} %get-tuple-element.54.back_far_ref), channel_id=1, source_target_pairs={{2,0},{4,2},{6,4},{8,6},{10,8},{12,10},{14,12},{18,16},{20,18},{22... | collective-permute-start | bytes 811016 | tf_op jit(solution)/shard_map/ppermute | solution.py:18
  30.0 9.0 %collective-permute-start.10 = (bf16[33,32,128]{2,1,0:T(8,128)(2,1)S(1)}, bf16[33,32,128]{2,1,0:T(8,128)(2,1)S(1)}, u32[]{:S(2)}, u32[]{:S(2)}) collective-permute-start(bf16[33,32,128]{2,1,0:T(8,128)(2,1)S(1)} %shard_map.116), channel_id=1, source_target_pairs={{3,1},{5,3},{7,5},{9,7},{11,9},{13,11},{15,13},{19,17},{21,19},{23... | collective-permute-start | bytes 811016 | tf_op jit(solution)/shard_map/ppermute | solution.py:18
  39.5 1.8 %collective-permute-start.11 = (f32[40,256]{1,0:T(8,128)S(1)}, f32[40,256]{1,0:T(8,128)S(1)}, u32[]{:S(2)}, u32[]{:S(2)}) collective-permute-start(f32[40,256]{1,0:T(8,128)S(1)} %get-tuple-element.57.x_ref), channel_id=1, source_target_pairs={{0,1},{1,0},{2,3},{3,2},{4,5},{5,4},{6,7},{7,6},{8,9},{9,8},{10,11... | collective-permute-start | bytes 122888 | tf_op jit(solution)/shard_map/ppermute | solution.py:76
  41.4 4.6 %collective-permute-start.12 = (f32[40,256]{1,0:T(8,128)S(1)}, f32[40,256]{1,0:T(8,128)S(1)}, u32[]{:S(2)}, u32[]{:S(2)}) collective-permute-start(f32[40,256]{1,0:T(8,128)S(1)} %shard_map.118.x_ref), channel_id=1, source_target_pairs={{0,3},{1,2},{2,1},{3,0},{4,7},{5,6},{6,5},{7,4},{8,11},{9,10},{10,... | collective-permute-start | bytes 122888 | tf_op jit(solution)/shard_map/ppermute | solution.py:76
  46.0 5.3 %collective-permute-start.15 = (f32[40,256]{1,0:T(8,128)S(1)}, f32[40,256]{1,0:T(8,128)S(1)}, u32[]{:S(2)}, u32[]{:S(2)}) collective-permute-start(f32[40,256]{1,0:T(8,128)S(1)} %shard_map.119.x_ref), channel_id=1, source_target_pairs={{0,13},{1,12},{2,15},{3,14},{4,9},{5,8},{6,11},{7,10},{8,5},{9,4},... | collective-permute-start | bytes 122888 | tf_op jit(solution)/shard_map/ppermute | solution.py:76
  48.5 5.1 %collective-permute-start.14 = (f32[40,256]{1,0:T(8,128)S(1)}, f32[40,256]{1,0:T(8,128)S(1)}, u32[]{:S(2)}, u32[]{:S(2)}) collective-permute-start(f32[40,256]{1,0:T(8,128)S(1)} %shard_map.119.x_ref), channel_id=1, source_target_pairs={{0,9},{1,8},{2,11},{3,10},{4,13},{5,12},{6,15},{7,14},{8,1},{9,0},... | collective-permute-start | bytes 122888 | tf_op jit(solution)/shard_map/ppermute | solution.py:76
  48.5 5.1 %collective-permute-start.13 = (f32[40,256]{1,0:T(8,128)S(1)}, f32[40,256]{1,0:T(8,128)S(1)}, u32[]{:S(2)}, u32[]{:S(2)}) collective-permute-start(f32[40,256]{1,0:T(8,128)S(1)} %shard_map.119.x_ref), channel_id=1, source_target_pairs={{0,5},{1,4},{2,7},{3,6},{4,1},{5,0},{6,3},{7,2},{8,13},{9,12},{10,... | collective-permute-start | bytes 122888 | tf_op jit(solution)/shard_map/ppermute | solution.py:76

commit v17 on v14

--- a/solution.py
+++ b/solution.py
@@ -58,11 +58,13 @@
 
 
 def rounds_of(n):
-    rounds = [(1,)] + [(3,)] * (n > 2)
-    step = 4
-    while step < n:
-        rounds.append(tuple((m * step) ^ 1 for m in range(1, 4) if m * step < n))
-        step *= 4
+    rounds, step = [(1,)], n
+    if n.bit_length() % 2:
+        step //= 2
+        rounds.append((step ^ 1,))
+    while step > 2:
+        step //= 4
+        rounds.append(tuple((m * step) ^ 1 for m in range(1, 4)))
     return rounds
 
 

time: 54.5 us -> 53.8 us (0.987)
  waiting for transfers between devices: 17.9 us -> 17.2 us
    ppermute x10, waiting for transfers between devices: 8.16 us -> 7.44 us  [total(): lax.ppermute(msg, axis, [(j, j ^ d) for j in range(n)])]
    ppermute x10, starting transfers between devices: 15.5 us -> 16.2 us  [total(): lax.ppermute(msg, axis, [(j, j ^ d) for j in range(n)])]
    ppermute x4, starting transfers between devices: 6.05 us -> 5.4 us  [sent(): lax.ppermute(block, axis, [(i, i + distance) for i in devices if i % 2 in...]
  transfers between devices with their start and end apart: 16 -> 16, of which waited for: 10 -> 12; matrix products, arithmetic and copies ran while one was open for 0% -> 0% of each run, Pallas kernels for 10% -> 10%
where the time goes in v17:
time: 53.8 us; the launch traced here: 53.5 us
  starting transfers between devices  23.5 us (44%)
  waiting for transfers between devices  17.2 us (32%)
  Pallas kernels  12 us (22%)
  between operations  0.78 us (1%)
    ppermute x10, starting transfers between devices, total(): lax.ppermute(msg, axis, [(j, j ^ d) for j in range(n)])  16.2 us
    ppermute x4, waiting for transfers between devices, sent(): lax.ppermute(block, axis, [(i, i + distance) for i in devices if i % 2 in...  9.49 us
    ppermute x10, waiting for transfers between devices, total(): lax.ppermute(msg, axis, [(j, j ^ d) for j in range(n)])  7.44 us
    ppermute x4, starting transfers between devices, sent(): lax.ppermute(block, axis, [(i, i + distance) for i in devices if i % 2 in...  5.4 us
    pallas_call x1, Pallas kernels, load(): call(load_kernel, [pl.ANY] * 3, outs, [pltpu.SemaphoreType.DMA((2,))])  2.23 us
    pallas_call x1, Pallas kernels, body(): call(project_kernel, [pl.ANY] * 5, [sum_shape, ((2, blocks, bs), F32), fi...  2.15 us
    ppermute x2, starting transfers between devices, swapped(): lax.ppermute(block, axis, [(i, i ^ 1) for i in range(lax.axis_size(axis))])  1.89 us
    pallas_call x1, Pallas kernels, body(): call(finish_kernel, [vmem] * 9, [whole] * 3, scratch, keep=False)  1.6 us
  transfers between devices with their start and end apart: 16, of which 12 were waited for; matrix products, arithmetic and copies ran while one was open for 0% of the time, Pallas kernels for 10%

profile of v17, /device:TPU:0, one launch (start us, length us, event | category | flops | bytes accessed | tf_op | source)
XLA Modules:
  0.0 53.5 jit_solution(14815460595040517393)
XLA Ops:
  0.6 2.2 %shard_map.103 = (f32[40,256]{1,0:T(8,128)S(1)}, f32[2,32,128]{2,1,0:T(8,128)S(1)}, f32[32,40,128]{2,1,0:T(8,128)S(1)}, bf16[4096,256]{1,0:T(8,128)(2,1)S(1)}) custom-call(f32[32,128]{1,0:T(8,128)} %bitcast.5, s32[32,128]{1,0:T(8,128)} %bitcast.6, f32[32,128]{1,0:T(8,128)} %bitcast.7, f32[32,4096]{1,0:T(8,128)} %probes_hbm.1, bf16[4096,256]{1,0:T(8,128)(2,1)} %map_hbm.1), custom_call_target="tpu_custom_call" | custom-call | tf_op jit(solution)/shard_map/pallas_call | solution.py:382
  2.8 0.5 collective-permute-start
  3.3 0.9 %collective-permute-done.refs_0_ = f32[40,256]{1,0:T(8,128)S(1)} collective-permute-done((f32[40,256]{1,0:T(8,128)S(1)}, f32[40,256]{1,0:T(8,128)S(1)}, u32[]{:S(2)}, u32[]{:S(2)}) %collective-permute-start) | collective-permute-done | bytes 40992 | tf_op jit(solution)/shard_map/ppermute | solution.py:78
  4.2 3.8 %collective-permute-start.1 = (bf16[40,256]{1,0:T(8,128)(2,1)S(1)}, bf16[40,256]{1,0:T(8,128)(2,1)S(1)}, u32[]{:S(2)}, u32[]{:S(2)}) collective-permute-start(bf16[40,256]{1,0:T(8,128)(2,1)S(1)} %get-tuple-element.37.after_ref), channel_id=1, source_target_pairs={{0,9},{1,8},{2,11},{3,10},{4,13},{5,12},{6,15},{7,14},{8,1},{9,0},... | collective-permute-start | bytes 61448 | tf_op jit(solution)/shard_map/ppermute | solution.py:78
  8.0 0.6 %shard_map.105.refs_1_.map_ref = bf16[256,4096]{1,0:T(8,128)(2,1)S(1)} custom-call(bf16[4096,256]{1,0:T(8,128)(2,1)S(1)} %get-tuple-element.38.map_ref, bf16[40,256]{1,0:T(8,128)(2,1)S(1)} %get-tuple-element.37.after_ref), custom_call_target="tpu_custom_call" | custom-call | tf_op jit(solution)/shard_map/pallas_call | solution.py:403
  8.6 0.8 %collective-permute-done.1.refs_0_ = bf16[40,256]{1,0:T(8,128)(2,1)S(1)} collective-permute-done((bf16[40,256]{1,0:T(8,128)(2,1)S(1)}, bf16[40,256]{1,0:T(8,128)(2,1)S(1)}, u32[]{:S(2)}, u32[]{:S(2)}) %collective-permute-start.1) | collective-permute-done | bytes 20512 | tf_op jit(solution)/shard_map/ppermute | solution.py:78
  9.5 2.6 %collective-permute-start.4 = (bf16[40,256]{1,0:T(8,128)(2,1)S(1)}, bf16[40,256]{1,0:T(8,128)(2,1)S(1)}, u32[]{:S(2)}, u32[]{:S(2)}) collective-permute-start(bf16[40,256]{1,0:T(8,128)(2,1)S(1)} %get-tuple-element.40.after_ref), channel_id=1, source_target_pairs={{0,7},{1,6},{2,5},{3,4},{4,3},{5,2},{6,1},{7,0},{8,15},{9,14},{10,... | collective-permute-start | bytes 61448 | tf_op jit(solution)/shard_map/ppermute | solution.py:78
  12.1 0.4 collective-permute-start.3
  12.5 0.2 collective-permute-start.2
  12.7 2.2 %shard_map.107 = (bf16[32,4,128,128]{3,2,1,0:T(8,128)(2,1)S(1)}, f32[256,256]{1,0:T(8,128)S(1)}) custom-call(bf16[32,4,128,128]{3,2,1,0:T(8,128)(2,1)} %factor_hbm.1, f32[256,256]{1,0:T(8,128)} %inner_hbm.1, bf16[40,256]{1,0:T(8,128)(2,1)S(1)} %get-tuple-element.40.after_ref), custom_call_target="tpu_custom_call" | custom-call | tf_op jit(solution)/shard_map/pallas_call | solution.py:398
  14.9 0.0 collective-permute-done.4.refs_2_
  14.9 0.4 collective-permute-done.3.refs_1_
  15.3 0.4 collective-permute-done.2.refs_0_
  15.7 0.7 %shard_map.109 = (f32[32,40,128]{2,1,0:T(8,128)S(1)}, bf16[33,32,128]{2,1,0:T(8,128)(2,1)S(1)}, f32[40,256]{1,0:T(8,128)S(1)}) custom-call(f32[40,256]{1,0:T(8,128)S(1)} %shard_map.108.sums_ref, f32[256,256]{1,0:T(8,128)S(1)} %get-tuple-element.42.refs_4_.inner_ref, f32[2,32,128]{2,1,0:T(8,128)S(1)} %get-tuple-element.43.terms_ref, ...), custom_call_target="tpu_custom_call" | custom-call | tf_op jit(solution)/shard_map/pallas_call | solution.py:406
  16.4 0.7 %collective-permute-start.5 = (bf16[33,32,128]{2,1,0:T(8,128)(2,1)S(1)}, bf16[33,32,128]{2,1,0:T(8,128)(2,1)S(1)}, u32[]{:S(2)}, u32[]{:S(2)}) collective-permute-start(bf16[33,32,128]{2,1,0:T(8,128)(2,1)S(1)} %get-tuple-element.46.own_ref), channel_id=1, source_target_pairs={{1,3},{3,5},{5,7},{7,9},{9,11},{11,13},{13,15},{17,19},{19,21},{21... | collective-permute-start | bytes 811016 | tf_op jit(solution)/shard_map/ppermute | solution.py:18
  17.1 0.5 shard_map.110
  17.6 2.8 %collective-permute-start.7 = (bf16[33,32,128]{2,1,0:T(8,128)(2,1)S(1)}, bf16[33,32,128]{2,1,0:T(8,128)(2,1)S(1)}, u32[]{:S(2)}, u32[]{:S(2)}) collective-permute-start(bf16[33,32,128]{2,1,0:T(8,128)(2,1)S(1)} %get-tuple-element.51), channel_id=1, source_target_pairs={{0,2},{2,4},{4,6},{6,8},{8,10},{10,12},{12,14},{16,18},{18,20},{20... | collective-permute-start | bytes 811016 | tf_op jit(solution)/shard_map/ppermute | solution.py:18
  20.4 0.0 copy-start
  20.4 0.5 shard_map.111
  20.9 0.1 copy-done
  21.0 0.9 %shard_map.112 = (bf16[32,384,128]{2,1,0:T(8,128)(2,1)S(1)}, s32[3,32]{1,0:T(4,128)S(4)}) custom-call(bf16[32,4,128,128]{3,2,1,0:T(8,128)(2,1)S(1)} %get-tuple-element.41.refs_3_.factor_ref, s32[3,32]{1,0:T(4,128)S(1)} %bitcast.4, f32[16,48,128]{2,1,0:T(8,128)S(1)} %get-tuple-element.48.after_ref.image_two_ref), custom_call_target="tpu_custom_call" | custom-call | tf_op jit(solution)/shard_map/pallas_call | solution.py:426
  21.9 0.0 collective-permute-done.5.far_ref.far_odd_ref
  22.0 1.8 %collective-permute-start.6 = (bf16[33,32,128]{2,1,0:T(8,128)(2,1)S(1)}, bf16[33,32,128]{2,1,0:T(8,128)(2,1)S(1)}, u32[]{:S(2)}, u32[]{:S(2)}) collective-permute-start(bf16[33,32,128]{2,1,0:T(8,128)(2,1)S(1)} %shard_map.113), channel_id=1, source_target_pairs={{0,1},{1,0},{2,3},{3,2},{4,5},{5,4},{6,7},{7,6},{8,9},{9,8},{10,11... | collective-permute-start | bytes 811016 | tf_op jit(solution)/shard_map/ppermute | solution.py:22
  23.8 1.6 %collective-permute-done.7.far_even_ref = bf16[33,32,128]{2,1,0:T(8,128)(2,1)S(1)} collective-permute-done((bf16[33,32,128]{2,1,0:T(8,128)(2,1)S(1)}, bf16[33,32,128]{2,1,0:T(8,128)(2,1)S(1)}, u32[]{:S(2)}, u32[]{:S(2)}) %collective-permute-start.7) | collective-permute-done | bytes 270368 | tf_op jit(solution)/shard_map/ppermute | solution.py:18
  25.4 0.0 collective-permute-done.6.near_ref
  25.4 1.6 %shard_map.114 = (bf16[33,32,128]{2,1,0:T(8,128)(2,1)S(1)}, bf16[33,32,128]{2,1,0:T(8,128)(2,1)S(1)}, f32[96,40,128]{2,1,0:T(8,128)S(1)}, f32[40,128]{1,0:T(8,128)S(1)}, bf16[32,48,128]{2,1,0:T(8,128)(2,1)S(1)}) custom-call(s32[3,32]{1,0:T(4,128)S(4)} %get-tuple-element.49.ids_ref, ...), custom_call_target="tpu_custom_call", output_to_operand_aliasing={{2}: (9, {})} | custom-call | tf_op jit(solution)/shard_map/pallas_call | solution.py:434
  27.0 0.1 collective-permute-start.9
  27.1 1.3 %collective-permute-start.8 = (bf16[33,32,128]{2,1,0:T(8,128)(2,1)S(1)}, bf16[33,32,128]{2,1,0:T(8,128)(2,1)S(1)}, u32[]{:S(2)}, u32[]{:S(2)}) collective-permute-start(bf16[33,32,128]{2,1,0:T(8,128)(2,1)S(1)} %get-tuple-element.58.back_far_ref), channel_id=1, source_target_pairs={{2,0},{4,2},{6,4},{8,6},{10,8},{12,10},{14,12},{18,16},{20,18},{22... | collective-permute-start | bytes 811016 | tf_op jit(solution)/shard_map/ppermute | solution.py:18
  28.4 0.2 collective-permute-done.9.got_ref.mate_ref
  28.6 0.1 shard_map.116
  28.7 0.7 %collective-permute-start.10 = (bf16[33,32,128]{2,1,0:T(8,128)(2,1)S(1)}, bf16[33,32,128]{2,1,0:T(8,128)(2,1)S(1)}, u32[]{:S(2)}, u32[]{:S(2)}) collective-permute-start(bf16[33,32,128]{2,1,0:T(8,128)(2,1)S(1)} %shard_map.116), channel_id=1, source_target_pairs={{3,1},{5,3},{7,5},{9,7},{11,9},{13,11},{15,13},{19,17},{21,19},{23... | collective-permute-start | bytes 811016 | tf_op jit(solution)/shard_map/ppermute | solution.py:18
  29.4 0.4 shard_map.115
  29.8 7.9 %collective-permute-done.8.even_ref = bf16[33,32,128]{2,1,0:T(8,128)(2,1)S(1)} collective-permute-done((bf16[33,32,128]{2,1,0:T(8,128)(2,1)S(1)}, bf16[33,32,128]{2,1,0:T(8,128)(2,1)S(1)}, u32[]{:S(2)}, u32[]{:S(2)}) %collective-permute-start.8) | collective-permute-done | bytes 270368 | tf_op jit(solution)/shard_map/ppermute | solution.py:18
  37.7 0.0 collective-permute-done.10.odd_ref
  37.7 0.5 shard_map.117
  38.2 0.9 %collective-permute-start.11 = (f32[40,256]{1,0:T(8,128)S(1)}, f32[40,256]{1,0:T(8,128)S(1)}, u32[]{:S(2)}, u32[]{:S(2)}) collective-permute-start(f32[40,256]{1,0:T(8,128)S(1)} %get-tuple-element.61.x_ref), channel_id=1, source_target_pairs={{0,1},{1,0},{2,3},{3,2},{4,5},{5,4},{6,7},{7,6},{8,9},{9,8},{10,11... | collective-permute-start | bytes 122888 | tf_op jit(solution)/shard_map/ppermute | solution.py:78
  39.2 0.9 %collective-permute-done.11.refs_0_ = f32[40,256]{1,0:T(8,128)S(1)} collective-permute-done((f32[40,256]{1,0:T(8,128)S(1)}, f32[40,256]{1,0:T(8,128)S(1)}, u32[]{:S(2)}, u32[]{:S(2)}) %collective-permute-start.11) | collective-permute-done | bytes 40992 | tf_op jit(solution)/shard_map/ppermute | solution.py:78
  40.1 4.7 %collective-permute-start.12 = (bf16[40,256]{1,0:T(8,128)(2,1)S(1)}, bf16[40,256]{1,0:T(8,128)(2,1)S(1)}, u32[]{:S(2)}, u32[]{:S(2)}) collective-permute-start(bf16[40,256]{1,0:T(8,128)(2,1)S(1)} %get-tuple-element.63), channel_id=1, source_target_pairs={{0,9},{1,8},{2,11},{3,10},{4,13},{5,12},{6,15},{7,14},{8,1},{9,0},... | collective-permute-start | bytes 61448 | tf_op jit(solution)/shard_map/ppermute | solution.py:78
  44.8 1.5 %collective-permute-done.12.refs_0_ = bf16[40,256]{1,0:T(8,128)(2,1)S(1)} collective-permute-done((bf16[40,256]{1,0:T(8,128)(2,1)S(1)}, bf16[40,256]{1,0:T(8,128)(2,1)S(1)}, u32[]{:S(2)}, u32[]{:S(2)}) %collective-permute-start.12) | collective-permute-done | bytes 20512 | tf_op jit(solution)/shard_map/ppermute | solution.py:78
  46.3 2.1 %collective-permute-start.15 = (bf16[40,256]{1,0:T(8,128)(2,1)S(1)}, bf16[40,256]{1,0:T(8,128)(2,1)S(1)}, u32[]{:S(2)}, u32[]{:S(2)}) collective-permute-start(bf16[40,256]{1,0:T(8,128)(2,1)S(1)} %get-tuple-element.65), channel_id=1, source_target_pairs={{0,7},{1,6},{2,5},{3,4},{4,3},{5,2},{6,1},{7,0},{8,15},{9,14},{10,... | collective-permute-start | bytes 61448 | tf_op jit(solution)/shard_map/ppermute | solution.py:78
  48.4 0.3 collective-permute-start.14
  48.7 0.6 %collective-permute-start.13 = (bf16[40,256]{1,0:T(8,128)(2,1)S(1)}, bf16[40,256]{1,0:T(8,128)(2,1)S(1)}, u32[]{:S(2)}, u32[]{:S(2)}) collective-permute-start(bf16[40,256]{1,0:T(8,128)(2,1)S(1)} %get-tuple-element.65), channel_id=1, source_target_pairs={{0,3},{1,2},{2,1},{3,0},{4,7},{5,6},{6,5},{7,4},{8,11},{9,10},{10,... | collective-permute-start | bytes 61448 | tf_op jit(solution)/shard_map/ppermute | solution.py:78
  49.3 1.1 %collective-permute-done.15.refs_2_ = bf16[40,256]{1,0:T(8,128)(2,1)S(1)} collective-permute-done((bf16[40,256]{1,0:T(8,128)(2,1)S(1)}, bf16[40,256]{1,0:T(8,128)(2,1)S(1)}, u32[]{:S(2)}, u32[]{:S(2)}) %collective-permute-start.15) | collective-permute-done | bytes 20512 | tf_op jit(solution)/shard_map/ppermute | solution.py:78
  50.4 1.2 %collective-permute-done.14.refs_1_ = bf16[40,256]{1,0:T(8,128)(2,1)S(1)} collective-permute-done((bf16[40,256]{1,0:T(8,128)(2,1)S(1)}, bf16[40,256]{1,0:T(8,128)(2,1)S(1)}, u32[]{:S(2)}, u32[]{:S(2)}) %collective-permute-start.14) | collective-permute-done | bytes 20512 | tf_op jit(solution)/shard_map/ppermute | solution.py:78
  51.6 0.3 collective-permute-done.13.refs_0_
  51.9 1.6 %shard_map.121 = (f32[33,4096]{1,0:T(8,128)}, f32[33,4096]{1,0:T(8,128)}, f32[33,4096]{1,0:T(8,128)}) custom-call(f32[40,256]{1,0:T(8,128)S(1)} %shard_map.108.sums_ref, f32[40,256]{1,0:T(8,128)S(1)} %get-tuple-element.45.product_ref, f32[40,256]{1,0:T(8,128)S(1)} %shard_map.120.hess_sums_ref, f32[256,256]{1,0:T(8,128)S(1)} %get-tuple-element.42.refs_4_.inner_ref, ...), custom_call_target="tpu_custom_call" | custom-call | tf_op jit(solution)/shard_map/pallas_call | solution.py:451
  (7 shorter events, 0.1 us)
Async XLA Ops:
  2.8 1.4 %collective-permute-start = (f32[40,256]{1,0:T(8,128)S(1)}, f32[40,256]{1,0:T(8,128)S(1)}, u32[]{:S(2)}, u32[]{:S(2)}) collective-permute-start(f32[40,256]{1,0:T(8,128)S(1)} %get-tuple-element.35.x_ref), channel_id=1, source_target_pairs={{0,1},{1,0},{2,3},{3,2},{4,5},{5,4},{6,7},{7,6},{8,9},{9,8},{10,11... | collective-permute-start | bytes 122888 | tf_op jit(solution)/shard_map/ppermute | solution.py:78
  4.2 5.2 %collective-permute-start.1 = (bf16[40,256]{1,0:T(8,128)(2,1)S(1)}, bf16[40,256]{1,0:T(8,128)(2,1)S(1)}, u32[]{:S(2)}, u32[]{:S(2)}) collective-permute-start(bf16[40,256]{1,0:T(8,128)(2,1)S(1)} %get-tuple-element.37.after_ref), channel_id=1, source_target_pairs={{0,9},{1,8},{2,11},{3,10},{4,13},{5,12},{6,15},{7,14},{8,1},{9,0},... | collective-permute-start | bytes 61448 | tf_op jit(solution)/shard_map/ppermute | solution.py:78
  9.5 5.5 %collective-permute-start.4 = (bf16[40,256]{1,0:T(8,128)(2,1)S(1)}, bf16[40,256]{1,0:T(8,128)(2,1)S(1)}, u32[]{:S(2)}, u32[]{:S(2)}) collective-permute-start(bf16[40,256]{1,0:T(8,128)(2,1)S(1)} %get-tuple-element.40.after_ref), channel_id=1, source_target_pairs={{0,7},{1,6},{2,5},{3,4},{4,3},{5,2},{6,1},{7,0},{8,15},{9,14},{10,... | collective-permute-start | bytes 61448 | tf_op jit(solution)/shard_map/ppermute | solution.py:78
  12.1 3.2 %collective-permute-start.3 = (bf16[40,256]{1,0:T(8,128)(2,1)S(1)}, bf16[40,256]{1,0:T(8,128)(2,1)S(1)}, u32[]{:S(2)}, u32[]{:S(2)}) collective-permute-start(bf16[40,256]{1,0:T(8,128)(2,1)S(1)} %get-tuple-element.40.after_ref), channel_id=1, source_target_pairs={{0,5},{1,4},{2,7},{3,6},{4,1},{5,0},{6,3},{7,2},{8,13},{9,12},{10,... | collective-permute-start | bytes 61448 | tf_op jit(solution)/shard_map/ppermute | solution.py:78
  12.5 3.2 %collective-permute-start.2 = (bf16[40,256]{1,0:T(8,128)(2,1)S(1)}, bf16[40,256]{1,0:T(8,128)(2,1)S(1)}, u32[]{:S(2)}, u32[]{:S(2)}) collective-permute-start(bf16[40,256]{1,0:T(8,128)(2,1)S(1)} %get-tuple-element.40.after_ref), channel_id=1, source_target_pairs={{0,3},{1,2},{2,1},{3,0},{4,7},{5,6},{6,5},{7,4},{8,11},{9,10},{10,... | collective-permute-start | bytes 61448 | tf_op jit(solution)/shard_map/ppermute | solution.py:78
  16.4 5.5 %collective-permute-start.5 = (bf16[33,32,128]{2,1,0:T(8,128)(2,1)S(1)}, bf16[33,32,128]{2,1,0:T(8,128)(2,1)S(1)}, u32[]{:S(2)}, u32[]{:S(2)}) collective-permute-start(bf16[33,32,128]{2,1,0:T(8,128)(2,1)S(1)} %get-tuple-element.46.own_ref), channel_id=1, source_target_pairs={{1,3},{3,5},{5,7},{7,9},{9,11},{11,13},{13,15},{17,19},{19,21},{21... | collective-permute-start | bytes 811016 | tf_op jit(solution)/shard_map/ppermute | solution.py:18
  17.6 7.8 %collective-permute-start.7 = (bf16[33,32,128]{2,1,0:T(8,128)(2,1)S(1)}, bf16[33,32,128]{2,1,0:T(8,128)(2,1)S(1)}, u32[]{:S(2)}, u32[]{:S(2)}) collective-permute-start(bf16[33,32,128]{2,1,0:T(8,128)(2,1)S(1)} %get-tuple-element.51), channel_id=1, source_target_pairs={{0,2},{2,4},{4,6},{6,8},{8,10},{10,12},{12,14},{16,18},{18,20},{20... | collective-permute-start | bytes 811016 | tf_op jit(solution)/shard_map/ppermute | solution.py:18
  20.4 0.7 %copy-start = (s32[32,3]{0,1:T(4,128)S(1)}, s32[32,3]{0,1:T(4,128)}, u32[]{:S(2)}) copy-start(s32[32,3]{0,1:T(4,128)} %param.13) | copy-start | bytes 1156
  22.0 3.5 %collective-permute-start.6 = (bf16[33,32,128]{2,1,0:T(8,128)(2,1)S(1)}, bf16[33,32,128]{2,1,0:T(8,128)(2,1)S(1)}, u32[]{:S(2)}, u32[]{:S(2)}) collective-permute-start(bf16[33,32,128]{2,1,0:T(8,128)(2,1)S(1)} %shard_map.113), channel_id=1, source_target_pairs={{0,1},{1,0},{2,3},{3,2},{4,5},{5,4},{6,7},{7,6},{8,9},{9,8},{10,11... | collective-permute-start | bytes 811016 | tf_op jit(solution)/shard_map/ppermute | solution.py:22
  27.0 1.6 %collective-permute-start.9 = (bf16[33,32,128]{2,1,0:T(8,128)(2,1)S(1)}, bf16[33,32,128]{2,1,0:T(8,128)(2,1)S(1)}, u32[]{:S(2)}, u32[]{:S(2)}) collective-permute-start(bf16[33,32,128]{2,1,0:T(8,128)(2,1)S(1)} %get-tuple-element.59), channel_id=1, source_target_pairs={{0,1},{1,0},{2,3},{3,2},{4,5},{5,4},{6,7},{7,6},{8,9},{9,8},{10,11... | collective-permute-start | bytes 811016 | tf_op jit(solution)/shard_map/ppermute | solution.py:22
  27.1 10.6 %collective-permute-start.8 = (bf16[33,32,128]{2,1,0:T(8,128)(2,1)S(1)}, bf16[33,32,128]{2,1,0:T(8,128)(2,1)S(1)}, u32[]{:S(2)}, u32[]{:S(2)}) collective-permute-start(bf16[33,32,128]{2,1,0:T(8,128)(2,1)S(1)} %get-tuple-element.58.back_far_ref), channel_id=1, source_target_pairs={{2,0},{4,2},{6,4},{8,6},{10,8},{12,10},{14,12},{18,16},{20,18},{22... | collective-permute-start | bytes 811016 | tf_op jit(solution)/shard_map/ppermute | solution.py:18
  28.7 9.0 %collective-permute-start.10 = (bf16[33,32,128]{2,1,0:T(8,128)(2,1)S(1)}, bf16[33,32,128]{2,1,0:T(8,128)(2,1)S(1)}, u32[]{:S(2)}, u32[]{:S(2)}) collective-permute-start(bf16[33,32,128]{2,1,0:T(8,128)(2,1)S(1)} %shard_map.116), channel_id=1, source_target_pairs={{3,1},{5,3},{7,5},{9,7},{11,9},{13,11},{15,13},{19,17},{21,19},{23... | collective-permute-start | bytes 811016 | tf_op jit(solution)/shard_map/ppermute | solution.py:18
  38.2 1.8 %collective-permute-start.11 = (f32[40,256]{1,0:T(8,128)S(1)}, f32[40,256]{1,0:T(8,128)S(1)}, u32[]{:S(2)}, u32[]{:S(2)}) collective-permute-start(f32[40,256]{1,0:T(8,128)S(1)} %get-tuple-element.61.x_ref), channel_id=1, source_target_pairs={{0,1},{1,0},{2,3},{3,2},{4,5},{5,4},{6,7},{7,6},{8,9},{9,8},{10,11... | collective-permute-start | bytes 122888 | tf_op jit(solution)/shard_map/ppermute | solution.py:78
  40.1 6.2 %collective-permute-start.12 = (bf16[40,256]{1,0:T(8,128)(2,1)S(1)}, bf16[40,256]{1,0:T(8,128)(2,1)S(1)}, u32[]{:S(2)}, u32[]{:S(2)}) collective-permute-start(bf16[40,256]{1,0:T(8,128)(2,1)S(1)} %get-tuple-element.63), channel_id=1, source_target_pairs={{0,9},{1,8},{2,11},{3,10},{4,13},{5,12},{6,15},{7,14},{8,1},{9,0},... | collective-permute-start | bytes 61448 | tf_op jit(solution)/shard_map/ppermute | solution.py:78
  46.3 4.2 %collective-permute-start.15 = (bf16[40,256]{1,0:T(8,128)(2,1)S(1)}, bf16[40,256]{1,0:T(8,128)(2,1)S(1)}, u32[]{:S(2)}, u32[]{:S(2)}) collective-permute-start(bf16[40,256]{1,0:T(8,128)(2,1)S(1)} %get-tuple-element.65), channel_id=1, source_target_pairs={{0,7},{1,6},{2,5},{3,4},{4,3},{5,2},{6,1},{7,0},{8,15},{9,14},{10,... | collective-permute-start | bytes 61448 | tf_op jit(solution)/shard_map/ppermute | solution.py:78
  48.4 3.2 %collective-permute-start.14 = (bf16[40,256]{1,0:T(8,128)(2,1)S(1)}, bf16[40,256]{1,0:T(8,128)(2,1)S(1)}, u32[]{:S(2)}, u32[]{:S(2)}) collective-permute-start(bf16[40,256]{1,0:T(8,128)(2,1)S(1)} %get-tuple-element.65), channel_id=1, source_target_pairs={{0,5},{1,4},{2,7},{3,6},{4,1},{5,0},{6,3},{7,2},{8,13},{9,12},{10,... | collective-permute-start | bytes 61448 | tf_op jit(solution)/shard_map/ppermute | solution.py:78
  48.7 3.2 %collective-permute-start.13 = (bf16[40,256]{1,0:T(8,128)(2,1)S(1)}, bf16[40,256]{1,0:T(8,128)(2,1)S(1)}, u32[]{:S(2)}, u32[]{:S(2)}) collective-permute-start(bf16[40,256]{1,0:T(8,128)(2,1)S(1)} %get-tuple-element.65), channel_id=1, source_target_pairs={{0,3},{1,2},{2,1},{3,0},{4,7},{5,6},{6,5},{7,4},{8,11},{9,10},{10,... | collective-permute-start | bytes 61448 | tf_op jit(solution)/shard_map/ppermute | solution.py:78

commit v18 on v17

--- a/solution.py
+++ b/solution.py
@@ -167,14 +167,22 @@
 
 
 def load_kernel(factor_hbm, inner_hbm, after_ref, factor_ref, inner_ref, sems):
+    half = factor_ref.shape[0] // 2
     copies = [
-        pltpu.make_async_copy(factor_hbm, factor_ref, sems.at[0]),
+        pltpu.make_async_copy(factor_hbm.at[:half], factor_ref.at[:half], sems.at[0]),
         pltpu.make_async_copy(inner_hbm, inner_ref, sems.at[1]),
     ]
     for copy in copies:
         copy.start()
     for copy in copies:
         copy.wait()
+
+
+def load_rest_kernel(factor_hbm, begun_ref, after_ref, factor_ref, sem):
+    half = factor_ref.shape[0] // 2
+    copy = pltpu.make_async_copy(factor_hbm.at[half:], factor_ref.at[half:], sem)
+    copy.start()
+    copy.wait()
 
 
 def turn_kernel(factor_ref, ids_any, after_ref, turned_ref, ids_ref, sem):
@@ -402,7 +410,20 @@
     def turn_map(msg):
         return (call(turn_map_kernel, [vmem, pl.ANY], [(inducing_map.shape[::-1], BF16)])(inducing_map, msg),)
 
-    sums, ((turned_map,), (factor, inner_inverse)) = total(partial, "space", [turn_map, load])
+    begun = []
+
+    def first_step(msg):
+        begun.extend(load(msg))
+        return (*begun, *turn_map(msg))
+
+    def second_step(msg):
+        rest = call(
+            load_rest_kernel, [pl.ANY, vmem, pl.ANY], [(factor.shape, BF16)], [pltpu.SemaphoreType.DMA], aliases={1: 0}
+        )
+        return (rest(in_hbm(factor), begun[0], msg),)
+
+    sums, ((_, inner_inverse, turned_map), (factor_here,)) = total(partial, "space", [first_step, second_step])
+    factor = factor_here
     direction, rounded, product = call(
         direction_kernel, [vmem] * 5, [field, packed, sum_shape], [vmem((blocks, bs), F32)]
     )(sums, inner_inverse, terms, right_side, turned_map)

time: 53.8 us -> 54.3 us (level)
  Pallas kernels: 12 us -> 12.9 us
    pallas_call x0 -> x1, Pallas kernels: none -> 1.6 us  [second_step(): return (rest(in_hbm(factor), begun[0], msg),)]
    pallas_call x1, Pallas kernels: 2.23 us -> 1.61 us  [load(): call(load_kernel, [pl.ANY] * 3, outs, [pltpu.SemaphoreType.DMA((2,))])]
  transfers between devices with their start and end apart: 16 -> 16, of which waited for: 12 -> 11; matrix products, arithmetic and copies ran while one was open for 0% -> 0% of each run, Pallas kernels for 10% -> 12%
where the time goes in v18:
time: 54.3 us; the launch traced here: 53.9 us
  starting transfers between devices  23.3 us (43%)
  waiting for transfers between devices  16.7 us (31%)
  Pallas kernels  12.9 us (24%)
  between operations  0.79 us (1%)
    ppermute x10, starting transfers between devices, total(): lax.ppermute(msg, axis, [(j, j ^ d) for j in range(n)])  16.3 us
    ppermute x4, waiting for transfers between devices, sent(): lax.ppermute(block, axis, [(i, i + distance) for i in devices if i % 2 in...  9.52 us
    ppermute x10, waiting for transfers between devices, total(): lax.ppermute(msg, axis, [(j, j ^ d) for j in range(n)])  6.98 us
    ppermute x4, starting transfers between devices, sent(): lax.ppermute(block, axis, [(i, i + distance) for i in devices if i % 2 in...  5.09 us
    pallas_call x1, Pallas kernels, body(): call(project_kernel, [pl.ANY] * 5, [sum_shape, ((2, blocks, bs), F32), fi...  2.15 us
    ppermute x2, starting transfers between devices, swapped(): lax.ppermute(block, axis, [(i, i ^ 1) for i in range(lax.axis_size(axis))])  1.88 us
    pallas_call x1, Pallas kernels, load(): call(load_kernel, [pl.ANY] * 3, outs, [pltpu.SemaphoreType.DMA((2,))])  1.61 us
    pallas_call x1, Pallas kernels, body(): call(finish_kernel, [vmem] * 9, [whole] * 3, scratch, keep=False)  1.6 us
  transfers between devices with their start and end apart: 16, of which 11 were waited for; matrix products, arithmetic and copies ran while one was open for 0% of the time, Pallas kernels for 12%

profile of v18, /device:TPU:0, one launch (start us, length us, event | category | flops | bytes accessed | tf_op | source)
XLA Modules:
  0.0 53.9 jit_solution(16726450928899818705)
XLA Ops:
  0.6 2.2 %shard_map.103 = (f32[40,256]{1,0:T(8,128)S(1)}, f32[2,32,128]{2,1,0:T(8,128)S(1)}, f32[32,40,128]{2,1,0:T(8,128)S(1)}, bf16[4096,256]{1,0:T(8,128)(2,1)S(1)}) custom-call(f32[32,128]{1,0:T(8,128)} %bitcast.5, s32[32,128]{1,0:T(8,128)} %bitcast.6, f32[32,128]{1,0:T(8,128)} %bitcast.7, f32[32,4096]{1,0:T(8,128)} %probes_hbm.1, bf16[4096,256]{1,0:T(8,128)(2,1)} %map_hbm.1), custom_call_target="tpu_custom_call" | custom-call | tf_op jit(solution)/shard_map/pallas_call | solution.py:390
  2.8 0.5 collective-permute-start
  3.3 0.9 %collective-permute-done.refs_0_ = f32[40,256]{1,0:T(8,128)S(1)} collective-permute-done((f32[40,256]{1,0:T(8,128)S(1)}, f32[40,256]{1,0:T(8,128)S(1)}, u32[]{:S(2)}, u32[]{:S(2)}) %collective-permute-start) | collective-permute-done | bytes 40992 | tf_op jit(solution)/shard_map/ppermute | solution.py:78
  4.2 3.8 %collective-permute-start.1 = (bf16[40,256]{1,0:T(8,128)(2,1)S(1)}, bf16[40,256]{1,0:T(8,128)(2,1)S(1)}, u32[]{:S(2)}, u32[]{:S(2)}) collective-permute-start(bf16[40,256]{1,0:T(8,128)(2,1)S(1)} %get-tuple-element.37.after_ref), channel_id=1, source_target_pairs={{0,9},{1,8},{2,11},{3,10},{4,13},{5,12},{6,15},{7,14},{8,1},{9,0},... | collective-permute-start | bytes 61448 | tf_op jit(solution)/shard_map/ppermute | solution.py:78
  8.0 0.6 %shard_map.106.refs_3_.map_ref = bf16[256,4096]{1,0:T(8,128)(2,1)S(1)} custom-call(bf16[4096,256]{1,0:T(8,128)(2,1)S(1)} %get-tuple-element.40.map_ref, bf16[40,256]{1,0:T(8,128)(2,1)S(1)} %get-tuple-element.37.after_ref), custom_call_target="tpu_custom_call" | custom-call | tf_op jit(solution)/shard_map/pallas_call | solution.py:411
  8.6 1.6 %shard_map.105 = (bf16[32,4,128,128]{3,2,1,0:T(8,128)(2,1)S(1)}, f32[256,256]{1,0:T(8,128)S(1)}) custom-call(bf16[32,4,128,128]{3,2,1,0:T(8,128)(2,1)} %factor_hbm.3, f32[256,256]{1,0:T(8,128)} %inner_hbm.1, bf16[40,256]{1,0:T(8,128)(2,1)S(1)} %get-tuple-element.37.after_ref), custom_call_target="tpu_custom_call" | custom-call | tf_op jit(solution)/shard_map/pallas_call | solution.py:406
  10.2 0.0 collective-permute-done.1.refs_0_
  10.2 2.5 %collective-permute-start.4 = (bf16[40,256]{1,0:T(8,128)(2,1)S(1)}, bf16[40,256]{1,0:T(8,128)(2,1)S(1)}, u32[]{:S(2)}, u32[]{:S(2)}) collective-permute-start(bf16[40,256]{1,0:T(8,128)(2,1)S(1)} %get-tuple-element.42.after_ref), channel_id=1, source_target_pairs={{0,7},{1,6},{2,5},{3,4},{4,3},{5,2},{6,1},{7,0},{8,15},{9,14},{10,... | collective-permute-start | bytes 61448 | tf_op jit(solution)/shard_map/ppermute | solution.py:78
  12.8 0.2 collective-permute-start.3
  13.0 0.5 collective-permute-start.2
  13.5 1.6 %shard_map.108.refs_3_.factor_ref = bf16[32,4,128,128]{3,2,1,0:T(8,128)(2,1)S(1)} custom-call(bf16[32,4,128,128]{3,2,1,0:T(8,128)(2,1)} %factor_hbm.3, bf16[32,4,128,128]{3,2,1,0:T(8,128)(2,1)S(1)} %get-tuple-element.38.refs_1_.begun_ref, bf16[40,256]{1,0:T(8,128)(2,1)S(1)} %get-tuple-element.42.after_ref), custom_call_target="tpu_custom_call", output_to_operand_aliasing={{}: (1, {})} | custom-call | tf_op jit(solution)/shard_map/pallas_call | solution.py:423
  15.1 0.0 collective-permute-done.4.refs_2_
  15.1 0.9 %collective-permute-done.3.refs_1_ = bf16[40,256]{1,0:T(8,128)(2,1)S(1)} collective-permute-done((bf16[40,256]{1,0:T(8,128)(2,1)S(1)}, bf16[40,256]{1,0:T(8,128)(2,1)S(1)}, u32[]{:S(2)}, u32[]{:S(2)}) %collective-permute-start.3) | collective-permute-done | bytes 20512 | tf_op jit(solution)/shard_map/ppermute | solution.py:78
  16.0 0.2 collective-permute-done.2.refs_0_
  16.2 0.7 %shard_map.110 = (f32[32,40,128]{2,1,0:T(8,128)S(1)}, bf16[33,32,128]{2,1,0:T(8,128)(2,1)S(1)}, f32[40,256]{1,0:T(8,128)S(1)}) custom-call(f32[40,256]{1,0:T(8,128)S(1)} %shard_map.109.sums_ref, f32[256,256]{1,0:T(8,128)S(1)} %get-tuple-element.39.refs_2_.inner_ref, f32[2,32,128]{2,1,0:T(8,128)S(1)} %get-tuple-element.43.terms_ref, ...), custom_call_target="tpu_custom_call" | custom-call | tf_op jit(solution)/shard_map/pallas_call | solution.py:427
  17.0 0.7 %collective-permute-start.5 = (bf16[33,32,128]{2,1,0:T(8,128)(2,1)S(1)}, bf16[33,32,128]{2,1,0:T(8,128)(2,1)S(1)}, u32[]{:S(2)}, u32[]{:S(2)}) collective-permute-start(bf16[33,32,128]{2,1,0:T(8,128)(2,1)S(1)} %get-tuple-element.46.own_ref), channel_id=1, source_target_pairs={{1,3},{3,5},{5,7},{7,9},{9,11},{11,13},{13,15},{17,19},{19,21},{21... | collective-permute-start | bytes 811016 | tf_op jit(solution)/shard_map/ppermute | solution.py:18
  17.6 0.5 shard_map.111
  18.1 2.5 %collective-permute-start.7 = (bf16[33,32,128]{2,1,0:T(8,128)(2,1)S(1)}, bf16[33,32,128]{2,1,0:T(8,128)(2,1)S(1)}, u32[]{:S(2)}, u32[]{:S(2)}) collective-permute-start(bf16[33,32,128]{2,1,0:T(8,128)(2,1)S(1)} %get-tuple-element.51), channel_id=1, source_target_pairs={{0,2},{2,4},{4,6},{6,8},{8,10},{10,12},{12,14},{16,18},{18,20},{20... | collective-permute-start | bytes 811016 | tf_op jit(solution)/shard_map/ppermute | solution.py:18
  20.6 0.0 copy-start
  20.6 0.5 shard_map.112
  21.1 0.1 copy-done
  21.3 0.9 %shard_map.113 = (bf16[32,384,128]{2,1,0:T(8,128)(2,1)S(1)}, s32[3,32]{1,0:T(4,128)S(4)}) custom-call(bf16[32,4,128,128]{3,2,1,0:T(8,128)(2,1)S(1)} %shard_map.108.refs_3_.factor_ref, s32[3,32]{1,0:T(4,128)S(1)} %bitcast.4, f32[16,48,128]{2,1,0:T(8,128)S(1)} %get-tuple-element.48.after_ref.image_two_ref), custom_call_target="tpu_custom_call" | custom-call | tf_op jit(solution)/shard_map/pallas_call | solution.py:447
  22.1 0.0 collective-permute-done.5.far_ref.far_odd_ref
  22.2 1.8 %collective-permute-start.6 = (bf16[33,32,128]{2,1,0:T(8,128)(2,1)S(1)}, bf16[33,32,128]{2,1,0:T(8,128)(2,1)S(1)}, u32[]{:S(2)}, u32[]{:S(2)}) collective-permute-start(bf16[33,32,128]{2,1,0:T(8,128)(2,1)S(1)} %shard_map.114), channel_id=1, source_target_pairs={{0,1},{1,0},{2,3},{3,2},{4,5},{5,4},{6,7},{7,6},{8,9},{9,8},{10,11... | collective-permute-start | bytes 811016 | tf_op jit(solution)/shard_map/ppermute | solution.py:22
  24.0 1.6 %collective-permute-done.7.far_even_ref = bf16[33,32,128]{2,1,0:T(8,128)(2,1)S(1)} collective-permute-done((bf16[33,32,128]{2,1,0:T(8,128)(2,1)S(1)}, bf16[33,32,128]{2,1,0:T(8,128)(2,1)S(1)}, u32[]{:S(2)}, u32[]{:S(2)}) %collective-permute-start.7) | collective-permute-done | bytes 270368 | tf_op jit(solution)/shard_map/ppermute | solution.py:18
  25.6 0.0 collective-permute-done.6.near_ref
  25.6 1.6 %shard_map.115 = (bf16[33,32,128]{2,1,0:T(8,128)(2,1)S(1)}, bf16[33,32,128]{2,1,0:T(8,128)(2,1)S(1)}, f32[96,40,128]{2,1,0:T(8,128)S(1)}, f32[40,128]{1,0:T(8,128)S(1)}, bf16[32,48,128]{2,1,0:T(8,128)(2,1)S(1)}) custom-call(s32[3,32]{1,0:T(4,128)S(4)} %get-tuple-element.49.ids_ref, ...), custom_call_target="tpu_custom_call", output_to_operand_aliasing={{2}: (9, {})} | custom-call | tf_op jit(solution)/shard_map/pallas_call | solution.py:455
  27.2 0.1 collective-permute-start.9
  27.3 1.3 %collective-permute-start.8 = (bf16[33,32,128]{2,1,0:T(8,128)(2,1)S(1)}, bf16[33,32,128]{2,1,0:T(8,128)(2,1)S(1)}, u32[]{:S(2)}, u32[]{:S(2)}) collective-permute-start(bf16[33,32,128]{2,1,0:T(8,128)(2,1)S(1)} %get-tuple-element.58.back_far_ref), channel_id=1, source_target_pairs={{2,0},{4,2},{6,4},{8,6},{10,8},{12,10},{14,12},{18,16},{20,18},{22... | collective-permute-start | bytes 811016 | tf_op jit(solution)/shard_map/ppermute | solution.py:18
  28.6 0.2 collective-permute-done.9.got_ref.mate_ref
  28.8 0.1 shard_map.117
  28.9 0.7 %collective-permute-start.10 = (bf16[33,32,128]{2,1,0:T(8,128)(2,1)S(1)}, bf16[33,32,128]{2,1,0:T(8,128)(2,1)S(1)}, u32[]{:S(2)}, u32[]{:S(2)}) collective-permute-start(bf16[33,32,128]{2,1,0:T(8,128)(2,1)S(1)} %shard_map.117), channel_id=1, source_target_pairs={{3,1},{5,3},{7,5},{9,7},{11,9},{13,11},{15,13},{19,17},{21,19},{23... | collective-permute-start | bytes 811016 | tf_op jit(solution)/shard_map/ppermute | solution.py:18
  29.6 0.4 shard_map.116
  30.0 7.9 %collective-permute-done.8.even_ref = bf16[33,32,128]{2,1,0:T(8,128)(2,1)S(1)} collective-permute-done((bf16[33,32,128]{2,1,0:T(8,128)(2,1)S(1)}, bf16[33,32,128]{2,1,0:T(8,128)(2,1)S(1)}, u32[]{:S(2)}, u32[]{:S(2)}) %collective-permute-start.8) | collective-permute-done | bytes 270368 | tf_op jit(solution)/shard_map/ppermute | solution.py:18
  37.9 0.0 collective-permute-done.10.odd_ref
  37.9 0.5 shard_map.118
  38.4 0.9 %collective-permute-start.11 = (f32[40,256]{1,0:T(8,128)S(1)}, f32[40,256]{1,0:T(8,128)S(1)}, u32[]{:S(2)}, u32[]{:S(2)}) collective-permute-start(f32[40,256]{1,0:T(8,128)S(1)} %get-tuple-element.61.x_ref), channel_id=1, source_target_pairs={{0,1},{1,0},{2,3},{3,2},{4,5},{5,4},{6,7},{7,6},{8,9},{9,8},{10,11... | collective-permute-start | bytes 122888 | tf_op jit(solution)/shard_map/ppermute | solution.py:78
  39.4 0.9 %collective-permute-done.11.refs_0_ = f32[40,256]{1,0:T(8,128)S(1)} collective-permute-done((f32[40,256]{1,0:T(8,128)S(1)}, f32[40,256]{1,0:T(8,128)S(1)}, u32[]{:S(2)}, u32[]{:S(2)}) %collective-permute-start.11) | collective-permute-done | bytes 40992 | tf_op jit(solution)/shard_map/ppermute | solution.py:78
  40.3 4.5 %collective-permute-start.12 = (bf16[40,256]{1,0:T(8,128)(2,1)S(1)}, bf16[40,256]{1,0:T(8,128)(2,1)S(1)}, u32[]{:S(2)}, u32[]{:S(2)}) collective-permute-start(bf16[40,256]{1,0:T(8,128)(2,1)S(1)} %get-tuple-element.63), channel_id=1, source_target_pairs={{0,9},{1,8},{2,11},{3,10},{4,13},{5,12},{6,15},{7,14},{8,1},{9,0},... | collective-permute-start | bytes 61448 | tf_op jit(solution)/shard_map/ppermute | solution.py:78
  44.8 1.5 %collective-permute-done.12.refs_0_ = bf16[40,256]{1,0:T(8,128)(2,1)S(1)} collective-permute-done((bf16[40,256]{1,0:T(8,128)(2,1)S(1)}, bf16[40,256]{1,0:T(8,128)(2,1)S(1)}, u32[]{:S(2)}, u32[]{:S(2)}) %collective-permute-start.12) | collective-permute-done | bytes 20512 | tf_op jit(solution)/shard_map/ppermute | solution.py:78
  46.3 2.1 %collective-permute-start.15 = (bf16[40,256]{1,0:T(8,128)(2,1)S(1)}, bf16[40,256]{1,0:T(8,128)(2,1)S(1)}, u32[]{:S(2)}, u32[]{:S(2)}) collective-permute-start(bf16[40,256]{1,0:T(8,128)(2,1)S(1)} %get-tuple-element.65), channel_id=1, source_target_pairs={{0,7},{1,6},{2,5},{3,4},{4,3},{5,2},{6,1},{7,0},{8,15},{9,14},{10,... | collective-permute-start | bytes 61448 | tf_op jit(solution)/shard_map/ppermute | solution.py:78
  48.4 0.7 %collective-permute-start.14 = (bf16[40,256]{1,0:T(8,128)(2,1)S(1)}, bf16[40,256]{1,0:T(8,128)(2,1)S(1)}, u32[]{:S(2)}, u32[]{:S(2)}) collective-permute-start(bf16[40,256]{1,0:T(8,128)(2,1)S(1)} %get-tuple-element.65), channel_id=1, source_target_pairs={{0,5},{1,4},{2,7},{3,6},{4,1},{5,0},{6,3},{7,2},{8,13},{9,12},{10,... | collective-permute-start | bytes 61448 | tf_op jit(solution)/shard_map/ppermute | solution.py:78
  49.1 0.6 %collective-permute-start.13 = (bf16[40,256]{1,0:T(8,128)(2,1)S(1)}, bf16[40,256]{1,0:T(8,128)(2,1)S(1)}, u32[]{:S(2)}, u32[]{:S(2)}) collective-permute-start(bf16[40,256]{1,0:T(8,128)(2,1)S(1)} %get-tuple-element.65), channel_id=1, source_target_pairs={{0,3},{1,2},{2,1},{3,0},{4,7},{5,6},{6,5},{7,4},{8,11},{9,10},{10,... | collective-permute-start | bytes 61448 | tf_op jit(solution)/shard_map/ppermute | solution.py:78
  49.6 0.8 %collective-permute-done.15.refs_2_ = bf16[40,256]{1,0:T(8,128)(2,1)S(1)} collective-permute-done((bf16[40,256]{1,0:T(8,128)(2,1)S(1)}, bf16[40,256]{1,0:T(8,128)(2,1)S(1)}, u32[]{:S(2)}, u32[]{:S(2)}) %collective-permute-start.15) | collective-permute-done | bytes 20512 | tf_op jit(solution)/shard_map/ppermute | solution.py:78
  50.4 1.2 %collective-permute-done.14.refs_1_ = bf16[40,256]{1,0:T(8,128)(2,1)S(1)} collective-permute-done((bf16[40,256]{1,0:T(8,128)(2,1)S(1)}, bf16[40,256]{1,0:T(8,128)(2,1)S(1)}, u32[]{:S(2)}, u32[]{:S(2)}) %collective-permute-start.14) | collective-permute-done | bytes 20512 | tf_op jit(solution)/shard_map/ppermute | solution.py:78
  51.6 0.7 %collective-permute-done.13.refs_0_ = bf16[40,256]{1,0:T(8,128)(2,1)S(1)} collective-permute-done((bf16[40,256]{1,0:T(8,128)(2,1)S(1)}, bf16[40,256]{1,0:T(8,128)(2,1)S(1)}, u32[]{:S(2)}, u32[]{:S(2)}) %collective-permute-start.13) | collective-permute-done | bytes 20512 | tf_op jit(solution)/shard_map/ppermute | solution.py:78
  52.3 1.6 %shard_map.122 = (f32[33,4096]{1,0:T(8,128)}, f32[33,4096]{1,0:T(8,128)}, f32[33,4096]{1,0:T(8,128)}) custom-call(f32[40,256]{1,0:T(8,128)S(1)} %shard_map.109.sums_ref, f32[40,256]{1,0:T(8,128)S(1)} %get-tuple-element.45.product_ref, f32[40,256]{1,0:T(8,128)S(1)} %shard_map.121.hess_sums_ref, f32[256,256]{1,0:T(8,128)S(1)} %get-tuple-element.39.refs_2_.inner_ref, ...), custom_call_target="tpu_custom_call" | custom-call | tf_op jit(solution)/shard_map/pallas_call | solution.py:472
  (7 shorter events, 0.1 us)
Async XLA Ops:
  2.8 1.4 %collective-permute-start = (f32[40,256]{1,0:T(8,128)S(1)}, f32[40,256]{1,0:T(8,128)S(1)}, u32[]{:S(2)}, u32[]{:S(2)}) collective-permute-start(f32[40,256]{1,0:T(8,128)S(1)} %get-tuple-element.35.x_ref), channel_id=1, source_target_pairs={{0,1},{1,0},{2,3},{3,2},{4,5},{5,4},{6,7},{7,6},{8,9},{9,8},{10,11... | collective-permute-start | bytes 122888 | tf_op jit(solution)/shard_map/ppermute | solution.py:78
  4.2 6.0 %collective-permute-start.1 = (bf16[40,256]{1,0:T(8,128)(2,1)S(1)}, bf16[40,256]{1,0:T(8,128)(2,1)S(1)}, u32[]{:S(2)}, u32[]{:S(2)}) collective-permute-start(bf16[40,256]{1,0:T(8,128)(2,1)S(1)} %get-tuple-element.37.after_ref), channel_id=1, source_target_pairs={{0,9},{1,8},{2,11},{3,10},{4,13},{5,12},{6,15},{7,14},{8,1},{9,0},... | collective-permute-start | bytes 61448 | tf_op jit(solution)/shard_map/ppermute | solution.py:78
  10.2 4.8 %collective-permute-start.4 = (bf16[40,256]{1,0:T(8,128)(2,1)S(1)}, bf16[40,256]{1,0:T(8,128)(2,1)S(1)}, u32[]{:S(2)}, u32[]{:S(2)}) collective-permute-start(bf16[40,256]{1,0:T(8,128)(2,1)S(1)} %get-tuple-element.42.after_ref), channel_id=1, source_target_pairs={{0,7},{1,6},{2,5},{3,4},{4,3},{5,2},{6,1},{7,0},{8,15},{9,14},{10,... | collective-permute-start | bytes 61448 | tf_op jit(solution)/shard_map/ppermute | solution.py:78
  12.8 3.2 %collective-permute-start.3 = (bf16[40,256]{1,0:T(8,128)(2,1)S(1)}, bf16[40,256]{1,0:T(8,128)(2,1)S(1)}, u32[]{:S(2)}, u32[]{:S(2)}) collective-permute-start(bf16[40,256]{1,0:T(8,128)(2,1)S(1)} %get-tuple-element.42.after_ref), channel_id=1, source_target_pairs={{0,5},{1,4},{2,7},{3,6},{4,1},{5,0},{6,3},{7,2},{8,13},{9,12},{10,... | collective-permute-start | bytes 61448 | tf_op jit(solution)/shard_map/ppermute | solution.py:78
  13.0 3.2 %collective-permute-start.2 = (bf16[40,256]{1,0:T(8,128)(2,1)S(1)}, bf16[40,256]{1,0:T(8,128)(2,1)S(1)}, u32[]{:S(2)}, u32[]{:S(2)}) collective-permute-start(bf16[40,256]{1,0:T(8,128)(2,1)S(1)} %get-tuple-element.42.after_ref), channel_id=1, source_target_pairs={{0,3},{1,2},{2,1},{3,0},{4,7},{5,6},{6,5},{7,4},{8,11},{9,10},{10,... | collective-permute-start | bytes 61448 | tf_op jit(solution)/shard_map/ppermute | solution.py:78
  17.0 5.2 %collective-permute-start.5 = (bf16[33,32,128]{2,1,0:T(8,128)(2,1)S(1)}, bf16[33,32,128]{2,1,0:T(8,128)(2,1)S(1)}, u32[]{:S(2)}, u32[]{:S(2)}) collective-permute-start(bf16[33,32,128]{2,1,0:T(8,128)(2,1)S(1)} %get-tuple-element.46.own_ref), channel_id=1, source_target_pairs={{1,3},{3,5},{5,7},{7,9},{9,11},{11,13},{13,15},{17,19},{19,21},{21... | collective-permute-start | bytes 811016 | tf_op jit(solution)/shard_map/ppermute | solution.py:18
  18.1 7.5 %collective-permute-start.7 = (bf16[33,32,128]{2,1,0:T(8,128)(2,1)S(1)}, bf16[33,32,128]{2,1,0:T(8,128)(2,1)S(1)}, u32[]{:S(2)}, u32[]{:S(2)}) collective-permute-start(bf16[33,32,128]{2,1,0:T(8,128)(2,1)S(1)} %get-tuple-element.51), channel_id=1, source_target_pairs={{0,2},{2,4},{4,6},{6,8},{8,10},{10,12},{12,14},{16,18},{18,20},{20... | collective-permute-start | bytes 811016 | tf_op jit(solution)/shard_map/ppermute | solution.py:18
  20.6 0.7 %copy-start = (s32[32,3]{0,1:T(4,128)S(1)}, s32[32,3]{0,1:T(4,128)}, u32[]{:S(2)}) copy-start(s32[32,3]{0,1:T(4,128)} %param.13) | copy-start | bytes 1156
  22.2 3.5 %collective-permute-start.6 = (bf16[33,32,128]{2,1,0:T(8,128)(2,1)S(1)}, bf16[33,32,128]{2,1,0:T(8,128)(2,1)S(1)}, u32[]{:S(2)}, u32[]{:S(2)}) collective-permute-start(bf16[33,32,128]{2,1,0:T(8,128)(2,1)S(1)} %shard_map.114), channel_id=1, source_target_pairs={{0,1},{1,0},{2,3},{3,2},{4,5},{5,4},{6,7},{7,6},{8,9},{9,8},{10,11... | collective-permute-start | bytes 811016 | tf_op jit(solution)/shard_map/ppermute | solution.py:22
  27.2 1.6 %collective-permute-start.9 = (bf16[33,32,128]{2,1,0:T(8,128)(2,1)S(1)}, bf16[33,32,128]{2,1,0:T(8,128)(2,1)S(1)}, u32[]{:S(2)}, u32[]{:S(2)}) collective-permute-start(bf16[33,32,128]{2,1,0:T(8,128)(2,1)S(1)} %get-tuple-element.59), channel_id=1, source_target_pairs={{0,1},{1,0},{2,3},{3,2},{4,5},{5,4},{6,7},{7,6},{8,9},{9,8},{10,11... | collective-permute-start | bytes 811016 | tf_op jit(solution)/shard_map/ppermute | solution.py:22
  27.3 10.6 %collective-permute-start.8 = (bf16[33,32,128]{2,1,0:T(8,128)(2,1)S(1)}, bf16[33,32,128]{2,1,0:T(8,128)(2,1)S(1)}, u32[]{:S(2)}, u32[]{:S(2)}) collective-permute-start(bf16[33,32,128]{2,1,0:T(8,128)(2,1)S(1)} %get-tuple-element.58.back_far_ref), channel_id=1, source_target_pairs={{2,0},{4,2},{6,4},{8,6},{10,8},{12,10},{14,12},{18,16},{20,18},{22... | collective-permute-start | bytes 811016 | tf_op jit(solution)/shard_map/ppermute | solution.py:18
  28.9 9.0 %collective-permute-start.10 = (bf16[33,32,128]{2,1,0:T(8,128)(2,1)S(1)}, bf16[33,32,128]{2,1,0:T(8,128)(2,1)S(1)}, u32[]{:S(2)}, u32[]{:S(2)}) collective-permute-start(bf16[33,32,128]{2,1,0:T(8,128)(2,1)S(1)} %shard_map.117), channel_id=1, source_target_pairs={{3,1},{5,3},{7,5},{9,7},{11,9},{13,11},{15,13},{19,17},{21,19},{23... | collective-permute-start | bytes 811016 | tf_op jit(solution)/shard_map/ppermute | solution.py:18
  38.4 1.8 %collective-permute-start.11 = (f32[40,256]{1,0:T(8,128)S(1)}, f32[40,256]{1,0:T(8,128)S(1)}, u32[]{:S(2)}, u32[]{:S(2)}) collective-permute-start(f32[40,256]{1,0:T(8,128)S(1)} %get-tuple-element.61.x_ref), channel_id=1, source_target_pairs={{0,1},{1,0},{2,3},{3,2},{4,5},{5,4},{6,7},{7,6},{8,9},{9,8},{10,11... | collective-permute-start | bytes 122888 | tf_op jit(solution)/shard_map/ppermute | solution.py:78
  40.3 6.0 %collective-permute-start.12 = (bf16[40,256]{1,0:T(8,128)(2,1)S(1)}, bf16[40,256]{1,0:T(8,128)(2,1)S(1)}, u32[]{:S(2)}, u32[]{:S(2)}) collective-permute-start(bf16[40,256]{1,0:T(8,128)(2,1)S(1)} %get-tuple-element.63), channel_id=1, source_target_pairs={{0,9},{1,8},{2,11},{3,10},{4,13},{5,12},{6,15},{7,14},{8,1},{9,0},... | collective-permute-start | bytes 61448 | tf_op jit(solution)/shard_map/ppermute | solution.py:78
  46.3 4.2 %collective-permute-start.15 = (bf16[40,256]{1,0:T(8,128)(2,1)S(1)}, bf16[40,256]{1,0:T(8,128)(2,1)S(1)}, u32[]{:S(2)}, u32[]{:S(2)}) collective-permute-start(bf16[40,256]{1,0:T(8,128)(2,1)S(1)} %get-tuple-element.65), channel_id=1, source_target_pairs={{0,7},{1,6},{2,5},{3,4},{4,3},{5,2},{6,1},{7,0},{8,15},{9,14},{10,... | collective-permute-start | bytes 61448 | tf_op jit(solution)/shard_map/ppermute | solution.py:78
  48.4 3.2 %collective-permute-start.14 = (bf16[40,256]{1,0:T(8,128)(2,1)S(1)}, bf16[40,256]{1,0:T(8,128)(2,1)S(1)}, u32[]{:S(2)}, u32[]{:S(2)}) collective-permute-start(bf16[40,256]{1,0:T(8,128)(2,1)S(1)} %get-tuple-element.65), channel_id=1, source_target_pairs={{0,5},{1,4},{2,7},{3,6},{4,1},{5,0},{6,3},{7,2},{8,13},{9,12},{10,... | collective-permute-start | bytes 61448 | tf_op jit(solution)/shard_map/ppermute | solution.py:78
  49.1 3.2 %collective-permute-start.13 = (bf16[40,256]{1,0:T(8,128)(2,1)S(1)}, bf16[40,256]{1,0:T(8,128)(2,1)S(1)}, u32[]{:S(2)}, u32[]{:S(2)}) collective-permute-start(bf16[40,256]{1,0:T(8,128)(2,1)S(1)} %get-tuple-element.65), channel_id=1, source_target_pairs={{0,3},{1,2},{2,1},{3,0},{4,7},{5,6},{6,5},{7,4},{8,11},{9,10},{10,... | collective-permute-start | bytes 61448 | tf_op jit(solution)/shard_map/ppermute | solution.py:78
